TPU v7x, 32 devices: a whole 2x2x4 slice. The times are simulated.
32 devices in a mesh: row: 4 (over x, core), col: 8 (over z, y).
Axes of the slice: x: 2, y: 2, z: 4, core: 2. Of those that a mesh axis runs over, the one named last changes fastest.
Arguments:
- covariance: float32 [8192, 8192], P('row', 'col'), may hold values from -12 to 12, as said below
- noise_var: float32 [64, 128], P('row'), may hold values from 0.1 to 1
- wind_table: float32 [16, 2], replicated, may hold values from -0.7 to 0.7
- diffusivity: float32 [16], replicated, may hold values from 0.01 to 0.05
- wind_index: int32 [3, 64], replicated, may hold values from 0 to 15
Outputs:
- predicted_spread_matrix: float32 [8192, 8192], P('row', 'col')
- operator_times_prior: bfloat16 [8192, 8192], P('row', 'col')
Inputs may be any that keep to these rules, and one draw needn't show every extreme that they name: covariance is symmetric: entry (a, b) equals entry (b, a) exactly.
All inputs are finite; a program needn't handle non-finite values.
Results may differ from a plain program's by a relative error of at most 0.0025.
Values may be sent and summed in bfloat16 or wider, within the bound.
No kernel may reach another device: no remote copies, remote signals or barrier semaphores. Data moves between devices by JAX's collectives and lax.ppermute only.
A program may use at most 192 MiB of HBM per device.

v0:
```python
import functools

import jax
import jax.numpy as jnp
from jax import lax
from jax.experimental import pallas as pl
from jax.experimental.pallas import tpu as pltpu
from jax.sharding import PartitionSpec as P

F32 = jnp.float32
BF16 = jnp.bfloat16
VMEM_LIMIT = 63 * 1024 * 1024


def params():
    return pltpu.CompilerParams(vmem_limit_bytes=VMEM_LIMIT)


def cost(work):
    return pl.CostEstimate(flops=work, bytes_accessed=work, transcendentals=0)


def stencil_terms(zonal_cour, merid_cour, diffuse):
    middle_weight = 1.0 - zonal_cour * zonal_cour - merid_cour * merid_cour - 4.0 * diffuse
    eastward_weight = 0.5 * zonal_cour * zonal_cour - 0.5 * zonal_cour + diffuse
    west_w = 0.5 * zonal_cour * zonal_cour + 0.5 * zonal_cour + diffuse
    north_w = 0.5 * merid_cour * merid_cour - 0.5 * merid_cour + diffuse
    south_w = 0.5 * merid_cour * merid_cour + 0.5 * merid_cour + diffuse
    return jnp.stack([middle_weight, eastward_weight, west_w, north_w, south_w])


def looked_up(wind_table, diffusivity, wind_index):
    table_ids = jnp.arange(wind_table.shape[0], dtype=jnp.int32)
    one_hot = (wind_index[:, :, None] == table_ids[None, None, :]).astype(F32)
    courant = jnp.einsum("sly,yc->slc", one_hot, wind_table, precision=lax.Precision.HIGHEST)
    diffuse = jnp.einsum("sly,y->sl", one_hot, diffusivity, precision=lax.Precision.HIGHEST)
    return stencil_terms(courant[..., 0], courant[..., 1], diffuse)


def split(values):
    high = values.astype(BF16)
    return high, (values - high.astype(F32)).astype(BF16)


def circulant(row):
    size = row.shape[1]
    return pltpu.roll(jnp.broadcast_to(row, (size, size)), 0, 1, stride=1, stride_axis=0)


def product(left, right):
    return jnp.dot(left, right, preferred_element_type=F32)


def composed(weight_ref, steps, lats):
    nlon = weight_ref.shape[-1]
    padded = lats + 2 * steps
    lane = lax.broadcasted_iota(jnp.int32, (padded, nlon), 1)
    rows = {0: (lane == 0).astype(F32)}
    for step_no in range(steps):
        low, high = step_no + 1, padded - step_no - 1
        c, e, w, n, s = [weight_ref[member * steps + step_no, low:high, :] for member in range(5)]
        size = high - low
        fresh = {}
        for d in range(-step_no - 1, step_no + 2):
            terms = []
            if d in rows:
                here = rows[d][1 : 1 + size]
                terms += [c * here, e * pltpu.roll(here, 1, 1), w * pltpu.roll(here, nlon - 1, 1)]
            if d - 1 in rows:
                terms.append(n * rows[d - 1][2 : 2 + size])
            if d + 1 in rows:
                terms.append(s * rows[d + 1][0:size])
            fresh[d] = functools.reduce(lambda x, y: x + y, terms)
        rows = fresh
    return rows


def stencil_rows(row_seights, col_seights, steps, lat_rows, lats, nlon):
    def kernel(row_ref, col_ref, row_out, col_out):
        for ref, out, size in ((row_ref, row_out, lat_rows), (col_ref, col_out, lats)):
            for d, value in composed(ref, steps, size).items():
                out[d + steps] = value

    return pl.pallas_call(
        kernel,
        out_shape=[
            jax.ShapeDtypeStruct((2 * steps + 1, size, nlon), F32) for size in (lat_rows, lats)
        ],
        compiler_params=params(),
        cost_estimate=cost(1),
        name="stencil_rows",
    )(row_seights, col_seights)


def pack(covariance, where, near, own, halo, nlon):
    rows, cols = covariance.shape
    wide = halo * nlon
    outer, span = near * nlon, own * nlon
    direct = [(0, outer, 0, 0), (0, outer, outer, rows - outer), (2, span, 0, None)]
    made_shapes = [(2 * outer, wide)] * 2 + [(span, wide)] * 4 + [(wide, cols)] * 2
    got_shapes = [(size, wide) for _, size, _, _ in direct for _ in range(2)]
    got_shapes += [(wide, span)] * 2 + [(wide, cols)] * 2

    def kernel(where_ref, p_ref, *refs):
        outs, got, made, in_sem, out_sem = refs[:8], refs[8:18], refs[18:26], refs[26], refs[27]
        lat = lambda k: pl.multiple_of(where_ref[k] * nlon, nlon)
        sources = []
        for _, size, _, start in direct:
            at = pl.ds(lat(0) if start is None else start, size)
            sources += [p_ref.at[at, pl.ds(lane, wide)] for lane in (0, cols - wide)]
        sources += [p_ref.at[pl.ds(lat(k), wide), pl.ds(lat(3), span)] for k in (1, 2)]
        sources += [p_ref.at[pl.ds(start, wide), :] for start in (0, rows - wide)]
        loads = [
            pltpu.make_async_copy(source, got[k], in_sem.at[k]) for k, source in enumerate(sources)
        ]
        for load in loads:
            load.start()
        stores = []

        def store(k, row, size):
            at = pl.ds(row, size)
            stores.append(
                pltpu.make_async_copy(made[k].at[at, :], outs[k].at[at, :], out_sem.at[len(stores)])
            )
            stores[-1].start()

        for k, (first_out, size, row, _) in enumerate(direct):
            for side in range(2):
                loads[2 * k + side].wait()
                made[first_out + side][row : row + size, :] = got[2 * k + side][...].astype(BF16)
                store(first_out + side, row, size)
        for k in range(2):
            loads[6 + k].wait()
            for j in range(halo):
                for a in range(own):
                    block = got[6 + k][j * nlon : (j + 1) * nlon, a * nlon : (a + 1) * nlon]
                    made[4 + k][a * nlon : (a + 1) * nlon, j * nlon : (j + 1) * nlon] = block.T.astype(BF16)
            store(4 + k, 0, span)
        for k in range(2):
            loads[8 + k].wait()
            made[6 + k][...] = got[8 + k][...].astype(BF16)
            store(6 + k, 0, wide)
        for copy in stores:
            copy.wait()

    return pl.pallas_call(
        kernel,
        in_specs=[pl.BlockSpec(memory_space=pltpu.SMEM), pl.BlockSpec(memory_space=pl.ANY)],
        out_specs=[pl.BlockSpec(memory_space=pl.ANY)] * 8,
        out_shape=[jax.ShapeDtypeStruct(shape, BF16) for shape in made_shapes],
        scratch_shapes=[pltpu.VMEM(shape, F32) for shape in got_shapes]
        + [pltpu.VMEM(shape, BF16) for shape in made_shapes]
        + [pltpu.SemaphoreType.DMA((10,)), pltpu.SemaphoreType.DMA((10,))],
        compiler_params=params(),
        cost_estimate=cost(1),
        name="pack",
    )(where, covariance)


def columns_operator(
    covariance, left, right, stencil, where, unit, steps, nlon, count, block_at, held=None, work=1
):
    rows, cols = covariance.shape
    lats = cols // nlon
    wide = steps * nlon
    size = unit * nlon
    span = 2 * steps * nlon
    pairs = lats // 2

    def kernel(where_ref, stencil_ref, p_ref, left_ref, right_ref, *rest):
        outs, (data_ref, b_high, b_low) = rest[:-3], rest[-3:]
        if held is not None:
            outs = outs[1:]
        t_ref = outs[0]
        i = pl.program_id(0)

        @pl.when(i == 0)
        def _():
            data_ref[size:, :wide] = jnp.zeros((size, wide), BF16)
            data_ref[size:, wide + cols :] = jnp.zeros((size, wide), BF16)
            for q in range(pairs):
                for a in range(2):
                    for k in range(2 * steps):
                        d = k - (steps - 1) - a
                        high, low = split(circulant(stencil_ref[d + steps, 2 * q + a : 2 * q + a + 1, :]))
                        at = pl.ds(q * span + k * nlon, nlon)
                        b_high[at, a * nlon : (a + 1) * nlon] = high
                        b_low[at, a * nlon : (a + 1) * nlon] = low

        data_ref[:size, :wide] = left_ref[...]
        data_ref[:size, wide + cols :] = right_ref[...]
        data_ref[:size, wide : wide + cols], data_ref[size:, wide : wide + cols] = split(p_ref[...])
        for q in range(pairs):
            window = slice((2 * q + 1) * nlon, (2 * q + 1) * nlon + span)
            of = pl.ds(q * span, span)
            both = product(data_ref[:, window], b_high[of, :])
            total = both[:size] + both[size:] + product(data_ref[:size, window], b_low[of, :])
            for a, k, d in ((0, 2 * q, -steps), (1, 2 * q + 2 * steps + 1, steps)):
                far = slice(k * nlon, (k + 1) * nlon)
                weight = jnp.sum(stencil_ref[d + steps, 2 * q + a : 2 * q + a + 1, :], axis=1, keepdims=True)
                far_values = data_ref[:size, far].astype(F32) + data_ref[size:, far].astype(F32)
                value = total[:, a * nlon : (a + 1) * nlon] + weight * far_values
                t_ref[:, (2 * q + a) * nlon : (2 * q + a + 1) * nlon] = value.astype(BF16)
        if held is None:

            @pl.when(i == 0)
            def _():
                outs[1][...] = t_ref[:wide, :]

            @pl.when(i == count - 1)
            def _():
                outs[2][...] = t_ref[size - wide :, :]

    in_specs = [
        pl.BlockSpec(stencil.shape, lambda i, at: (0, 0, 0)),
        pl.BlockSpec((size, cols), lambda i, at: (block_at(i, at), 0)),
        pl.BlockSpec((size, wide), lambda i, at: (i, 0)),
        pl.BlockSpec((size, wide), lambda i, at: (i, 0)),
    ]
    out_specs = [pl.BlockSpec((size, cols), lambda i, at: (block_at(i, at), 0))]
    out_shape = [jax.ShapeDtypeStruct((rows, cols), BF16)]
    operands = [where, stencil, covariance, left, right]
    aliases = {}
    if held is None:
        out_specs += [pl.BlockSpec((wide, cols), lambda i, at: (0, 0))] * 2
        out_shape += [jax.ShapeDtypeStruct((wide, cols), BF16)] * 2
    else:
        in_specs.append(pl.BlockSpec(memory_space=pl.ANY))
        operands.append(held)
        aliases = {5: 0}
    return pl.pallas_call(
        kernel,
        grid_spec=pltpu.PrefetchScalarGridSpec(
            num_scalar_prefetch=1,
            grid=(count,),
            in_specs=in_specs,
            out_specs=out_specs,
            scratch_shapes=[pltpu.VMEM((2 * size, cols + 2 * wide), BF16)]
            + [pltpu.VMEM((pairs * span, size), BF16)] * 2,
        ),
        out_shape=out_shape,
        input_output_aliases=aliases,
        compiler_params=params(),
        cost_estimate=cost(work),
        name="columns_operator",
    )(*operands)


def rows_operator(values, top, bottom, stencil, steps, nlon, out_dtype, noise=None, diagonal=None):
    rows, cols = values.shape
    lat_rows = rows // nlon
    wide = steps * nlon
    size = 2 * nlon
    span = 2 * steps * nlon
    pairs = lat_rows // 2
    ahead = (steps + 1) // 2
    exact = values.dtype == BF16
    chunk = min(cols, 256)

    def kernel(stencil_ref, x_ref, top_ref, bottom_ref, *rest):
        extra, rest = (rest[:2], rest[2:]) if noise is not None else ((), rest)
        out_ref, a_ref, high_ref = rest[:3]
        low_ref = None if exact else rest[3]
        g = pl.program_id(0)

        @pl.when(g == 0)
        def _():
            high_ref[:wide, :] = top_ref[...]
            high_ref[wide + rows :, :] = bottom_ref[...]
            if not exact:
                low_ref[:wide, :] = jnp.zeros((wide, cols), BF16)
                low_ref[wide + rows :, :] = jnp.zeros((wide, cols), BF16)

        @pl.when(g < pairs)
        def _():
            at = pl.ds(pl.multiple_of(wide + g * size, nlon), size)
            if exact:
                high_ref[at, :] = x_ref[...]
            else:
                high_ref[at, :], low_ref[at, :] = split(x_ref[...])

        @pl.when(g >= ahead)
        def _():
            p = g - ahead
            row = lambda d, a: stencil_ref[d + steps, pl.ds(2 * p + a, 1), :]
            for a in range(2):
                for k in range(2 * steps):
                    high, low = split(circulant(row(k - (steps - 1) - a, a)))
                    a_ref[a * nlon : (a + 1) * nlon, k * nlon : (k + 1) * nlon] = high
                    a_ref[size + a * nlon : size + (a + 1) * nlon, k * nlon : (k + 1) * nlon] = low
            unit = lambda k: pl.multiple_of((2 * p + k) * nlon, nlon)
            for lane in range(0, cols, chunk):
                lanes = slice(lane, lane + chunk)
                window = high_ref[pl.ds(unit(1), span), lanes]
                both = product(a_ref[...], window)
                total = both[:size] + both[size:]
                if not exact:
                    total += product(a_ref[:size, :], low_ref[pl.ds(unit(1), span), lanes])
                for a, k, d in ((0, 0, -steps), (1, 2 * steps + 1, steps)):
                    far = high_ref[pl.ds(unit(k), nlon), lanes].astype(F32)
                    if not exact:
                        far += low_ref[pl.ds(unit(k), nlon), lanes].astype(F32)
                    weight = jnp.sum(row(d, a), axis=1, keepdims=True)
                    value = total[a * nlon : (a + 1) * nlon, :] + weight * far
                    out_ref[a * nlon : (a + 1) * nlon, lanes] = value.astype(out_dtype)
            if noise is not None:
                diagonal_ref, noise_ref = extra
                for a in range(2):
                    lat = 2 * p + a - diagonal_ref[0]

                    @pl.when(jnp.logical_and(lat >= 0, lat < cols // nlon))
                    def _(a=a, lat=lat):
                        lanes = pl.ds(pl.multiple_of(lat * nlon, nlon), nlon)
                        eye = lax.broadcasted_iota(jnp.int32, (nlon, nlon), 0) == lax.broadcasted_iota(
                            jnp.int32, (nlon, nlon), 1
                        )
                        added = jnp.where(eye, noise_ref[pl.ds(2 * p + a, 1), :], 0.0)
                        out_ref[a * nlon : (a + 1) * nlon, lanes] += added

    in_specs = [
        pl.BlockSpec(stencil.shape, lambda g: (0, 0, 0)),
        pl.BlockSpec((size, cols), lambda g: (jnp.minimum(g, pairs - 1), 0)),
        pl.BlockSpec((wide, cols), lambda g: (0, 0)),
        pl.BlockSpec((wide, cols), lambda g: (0, 0)),
    ]
    operands = [stencil, values, top, bottom]
    if noise is not None:
        in_specs += [pl.BlockSpec(memory_space=pltpu.SMEM), pl.BlockSpec(noise.shape, lambda g: (0, 0))]
        operands += [diagonal, noise]
    return pl.pallas_call(
        kernel,
        grid=(pairs + ahead,),
        in_specs=in_specs,
        out_specs=pl.BlockSpec((size, cols), lambda g: (jnp.maximum(g - ahead, 0), 0)),
        out_shape=jax.ShapeDtypeStruct((rows, cols), out_dtype),
        scratch_shapes=[pltpu.VMEM((2 * size, span), BF16)]
        + [pltpu.VMEM((rows + 2 * wide, cols), BF16)] * (1 if exact else 2),
        compiler_params=params(),
        cost_estimate=cost(1),
        name="rows_operator",
    )(*operands)


def shifted(block, axis, by):
    size = lax.axis_size(axis)
    pairs = [(i, i + by) for i in range(size) if 0 <= i + by < size]
    return lax.ppermute(block, axis, pairs)


def gathered(first, last, axis, dim, unit, halo, own):
    before, after = [], []
    need, hop = halo, 1
    while need > 0:
        take = min(own, need)
        size = first.shape[dim]
        before.insert(0, shifted(lax.slice_in_dim(last, size - take * unit, size, axis=dim), axis, hop))
        after.append(shifted(lax.slice_in_dim(first, 0, take * unit, axis=dim), axis, -hop))
        need, hop = need - take, hop + 1
    join = lambda parts: parts[0] if len(parts) == 1 else jnp.concatenate(parts, axis=dim)
    return join(before), join(after)


def mirror_pairs(n_row, n_col, side):
    pairs = []
    for a in range(n_row):
        for b in range(n_col):
            to = 2 * a + (1 - b % 2) + side
            if 0 <= to < n_col:
                pairs.append((a * n_col + b, (b // 2) * n_col + to))
    return pairs


def device_stencils(wind_table, diffusivity, wind_index, lat_rows, lats, nlon):
    steps = wind_index.shape[0]
    weights = looked_up(wind_table, diffusivity, wind_index)
    padded = jnp.pad(weights, ((0, 0), (0, 0), (steps, steps)))
    turned = padded[jnp.array([0, 2, 1, 3, 4])]

    def local(of, axis, count):
        part = lax.dynamic_slice_in_dim(of, lax.axis_index(axis) * count, count + 2 * steps, 2)
        part = part.reshape(5 * steps, count + 2 * steps, 1)
        return jnp.broadcast_to(part, part.shape[:2] + (nlon,))

    return stencil_rows(local(padded, "row", lat_rows), local(turned, "col", lats), steps, lat_rows, lats, nlon)


def body(covariance, noise_var, wind_table, diffusivity, wind_index):
    rows_dev, cols_dev = covariance.shape
    lat_rows, nlon = noise_var.shape
    steps, nlat = wind_index.shape
    lats = cols_dev // nlon
    n_row, n_col = lax.axis_size("row"), lax.axis_size("col")
    row_id, col_id = lax.axis_index("row"), lax.axis_index("col")
    own = lat_rows // 4
    mirrored = lat_rows == 2 * lats and own % 2 == 0 and own >= steps and own <= lats - steps

    if not mirrored:
        return plain_body(covariance, noise_var, wind_table, diffusivity, wind_index)

    near = lat_rows // 2 - own
    middle = lat_rows // 2
    parity = col_id % 2
    by_parity = lambda even, odd: jnp.where(parity == 0, even, odd).astype(jnp.int32)
    mirror_at = by_parity(middle - own, middle).reshape(1)
    direct_at = by_parity(middle, middle - own).reshape(1)
    base = (1 - parity) * lats
    sources = jnp.stack([mirror_at[0], base + lats - steps, base, by_parity(lats - own, 0)]).astype(jnp.int32)
    first, last, first_inner, last_inner, left_m, right_m, top, bottom = pack(
        covariance, sources, near, own, steps, nlon
    )
    left = shifted(last, "col", 1)
    right = shifted(first, "col", -1)
    p_top = shifted(bottom, "row", 1)
    p_bottom = shifted(top, "row", -1)
    left_m, right_m, p_top, wind_index = lax.optimization_barrier((left_m, right_m, p_top, wind_index))
    left_m = lax.ppermute(left_m, ("row", "col"), mirror_pairs(n_row, n_col, 1))
    right_m = lax.ppermute(right_m, ("row", "col"), mirror_pairs(n_row, n_col, -1))

    row_s, col_s = device_stencils(wind_table, diffusivity, wind_index, lat_rows, lats, nlon)

    operator_times_prior = rows_operator(covariance, p_top, p_bottom, row_s, steps, nlon, BF16)
    operator_times_prior, left, right, first_inner, last_inner = lax.optimization_barrier(
        (operator_times_prior, left, right, first_inner, last_inner)
    )
    left_inner = shifted(last_inner, "col", 1)
    right_inner = shifted(first_inner, "col", -1)
    mirror, t_first, t_last = columns_operator(
        covariance, left, right, col_s, mirror_at, near, steps, nlon, 2, lambda i, at: i * (lat_rows // near - 1)
    )
    t_top = shifted(t_last, "row", 1)
    t_first, left_m = lax.optimization_barrier((t_first, left_m))
    t_bottom = shifted(t_first, "row", -1)
    inner_at = lambda i, at: at[0] // own + i
    (mirror,) = columns_operator(
        covariance, left_m, right_m, col_s, mirror_at, own, steps, nlon, 1, inner_at, mirror
    )
    (mirror,) = columns_operator(
        covariance, left_inner, right_inner, col_s, direct_at, own, steps, nlon, 1, inner_at, mirror, 10 ** 13
    )
    diagonal = (col_id * lats - row_id * lat_rows).astype(jnp.int32).reshape(1)
    predicted_spread_matrix = rows_operator(
        mirror, t_top, t_bottom, row_s, steps, nlon, F32, noise_var, diagonal
    )
    return (predicted_spread_matrix, operator_times_prior)


def plain_body(covariance, noise_var, wind_table, diffusivity, wind_index):
    rows_dev, cols_dev = covariance.shape
    lat_rows, nlon = noise_var.shape
    steps, nlat = wind_index.shape
    lats = cols_dev // nlon
    row_id, col_id = lax.axis_index("row"), lax.axis_index("col")
    sent = covariance.astype(BF16)
    left, right = gathered(sent, sent, "col", 1, nlon, steps, lats)
    p_top, p_bottom = gathered(sent, sent, "row", 0, nlon, steps, lat_rows)
    row_s, col_s = device_stencils(wind_table, diffusivity, wind_index, lat_rows, lats, nlon)
    operator_times_prior = rows_operator(covariance, p_top, p_bottom, row_s, steps, nlon, BF16)
    unused = jnp.zeros((1,), jnp.int32)
    held = jnp.zeros((rows_dev, cols_dev), BF16)
    (mirror,) = columns_operator(
        covariance, left, right, col_s, unused, 2, steps, nlon, lat_rows // 2, lambda i, at: i, held
    )
    t_top, t_bottom = gathered(mirror, mirror, "row", 0, nlon, steps, lat_rows)
    diagonal = (col_id * lats - row_id * lat_rows).astype(jnp.int32).reshape(1)
    predicted_spread_matrix = rows_operator(
        mirror, t_top, t_bottom, row_s, steps, nlon, F32, noise_var, diagonal
    )
    return (predicted_spread_matrix, operator_times_prior)


def solution(mesh):
    in_specs = (P("row", "col"), P("row", None), P(), P(), P())
    out_specs = (P("row", "col"), P("row", "col"))
    return jax.shard_map(body, mesh=mesh, in_specs=in_specs, out_specs=out_specs, check_vma=False)
```

profile of v0, /device:TPU:9, one launch (start us, length us, event | category | flops | bytes accessed | tf_op | source)
XLA Modules:
  0.0 100.3 jit_solution(9371647325573372391)
XLA Ops:
  0.6 0.0 copy-start
  0.7 0.7 pad_add_fusion.where_ref
  1.3 0.0 copy-start.3
  1.3 0.0 copy-start.2
  1.3 0.0 copy-start.4
  1.3 6.8 %pack.1 = (bf16[1024,384]{1,0:T(8,128)(2,1)}, bf16[1024,384]{1,0:T(8,128)(2,1)}, bf16[512,384]{1,0:T(8,128)(2,1)}, bf16[512,384]{1,0:T(8,128)(2,1)}, bf16[512,38...) custom-call(s32[4]{0:T(128)} %pad_add_fusion.where_ref, ...), custom_call_target="tpu_custom_call" | custom-call | flops 1 | bytes 1 | tf_op jit(solution)/shard_map/pack/pallas_call | solution.py:146
  8.2 3.7 %collective-permute-start = (bf16[384,1024]{1,0:T(8,128)(2,1)}, bf16[384,1024]{1,0:T(8,128)(2,1)}, u32[]{:S(2)}, u32[]{:S(2)}) collective-permute-start(bf16[384,1024]{1,0:T(8,128)(2,1)} %get-tuple-element.28), channel_id=1, source_target_pairs={{0,8},{8,16},{16,24},{1,9},{9,17},{17,25},{2,10},{10,18},{18,26},{... | collective-permute-start | bytes 2359304 | tf_op jit(solution)/shard_map/ppermute | solution.py:347
  11.9 1.9 %collective-permute-start.1 = (bf16[384,1024]{1,0:T(8,128)(2,1)}, bf16[384,1024]{1,0:T(8,128)(2,1)}, u32[]{:S(2)}, u32[]{:S(2)}) collective-permute-start(bf16[384,1024]{1,0:T(8,128)(2,1)} %get-tuple-element.33), channel_id=1, source_target_pairs={{8,0},{16,8},{24,16},{9,1},{17,9},{25,17},{10,2},{18,10},{26,18},{... | collective-permute-start | bytes 2359304 | tf_op jit(solution)/shard_map/ppermute | solution.py:347
  13.8 3.1 %collective-permute-start.2 = (bf16[1024,384]{1,0:T(8,128)(2,1)}, bf16[1024,384]{1,0:T(8,128)(2,1)S(1)}, u32[]{:S(2)}, u32[]{:S(2)}) collective-permute-start(bf16[1024,384]{1,0:T(8,128)(2,1)} %get-tuple-element.34), channel_id=1, source_target_pairs={{0,1},{1,2},{2,3},{3,4},{4,5},{5,6},{6,7},{8,9},{9,10},{10,11},{11... | collective-permute-start | bytes 2359304 | tf_op jit(solution)/shard_map/ppermute | solution.py:347
  16.9 3.0 %collective-permute-start.3 = (bf16[1024,384]{1,0:T(8,128)(2,1)}, bf16[1024,384]{1,0:T(8,128)(2,1)}, u32[]{:S(2)}, u32[]{:S(2)}) collective-permute-start(bf16[1024,384]{1,0:T(8,128)(2,1)} %get-tuple-element.35), channel_id=1, source_target_pairs={{1,0},{2,1},{3,2},{4,3},{5,4},{6,5},{7,6},{9,8},{10,9},{11,10},{12... | collective-permute-start | bytes 2359304 | tf_op jit(solution)/shard_map/ppermute | solution.py:347
  20.0 0.0 copy-done.3
  20.0 1.1 %collective-permute-done.top_ref = bf16[384,1024]{1,0:T(8,128)(2,1)} collective-permute-done((bf16[384,1024]{1,0:T(8,128)(2,1)}, bf16[384,1024]{1,0:T(8,128)(2,1)}, u32[]{:S(2)}, u32[]{:S(2)}) %collective-permute-start) | collective-permute-done | bytes 786464 | tf_op jit(solution)/shard_map/ppermute | solution.py:347
  21.1 0.0 copy-done.2
  21.1 0.0 copy-done.4
  21.1 0.1 fusion
  21.2 0.0 copy-done
  21.2 0.1 fusion.1
  21.4 0.6 gather_fusion
  22.0 0.1 pad_dynamic-slice_fusion.1
  22.1 0.1 pad_dynamic-slice_fusion
  22.2 3.2 %collective-permute-start.6 = (bf16[512,384]{1,0:T(8,128)(2,1)}, bf16[512,384]{1,0:T(8,128)(2,1)}, u32[]{:S(2)}, u32[]{:S(2)}) collective-permute-start(bf16[512,384]{1,0:T(8,128)(2,1)} %get-tuple-element.43), channel_id=1, source_target_pairs={{0,2},{1,1},{2,10},{3,9},{4,18},{5,17},{6,26},{7,25},{8,4},{9,3},{... | collective-permute-start | bytes 1179656 | tf_op jit(solution)/shard_map/ppermute | solution.py:416
  25.4 4.5 %collective-permute-start.7 = (bf16[512,384]{1,0:T(8,128)(2,1)}, bf16[512,384]{1,0:T(8,128)(2,1)}, u32[]{:S(2)}, u32[]{:S(2)}) collective-permute-start(bf16[512,384]{1,0:T(8,128)(2,1)} %get-tuple-element.45), channel_id=1, source_target_pairs={{0,0},{2,8},{4,16},{6,24},{8,2},{9,1},{10,10},{11,9},{12,18},{13,1... | collective-permute-start | bytes 1179656 | tf_op jit(solution)/shard_map/ppermute | solution.py:417
  29.9 0.8 broadcast_in_dim.23.col_ref
  30.7 0.8 broadcast_in_dim.20.row_ref
  31.5 1.9 %stencil_rows.1 = (f32[7,16,128]{2,1,0:T(8,128)}, f32[7,8,128]{2,1,0:T(8,128)}) custom-call(f32[15,22,128]{2,1,0:T(8,128)} %broadcast_in_dim.20.row_ref, f32[15,14,128]{2,1,0:T(8,128)} %broadcast_in_dim.23.col_ref), custom_call_target="tpu_custom_call" | custom-call | flops 1 | bytes 1 | tf_op jit(solution)/shard_map/stencil_rows/pallas_call | solution.py:84
  33.3 0.0 collective-permute-done.1.bottom_ref
  33.3 17.0 %rows_operator.2 = bf16[2048,1024]{1,0:T(8,128)(2,1)} custom-call(f32[7,16,128]{2,1,0:T(8,128)} %get-tuple-element.30.stencil_ref, f32[2048,1024]{1,0:T(8,128)} %p_ref.7, bf16[384,1024]{1,0:T(8,128)(2,1)} %collective-permute-done.top_ref, bf16[384,1024]{1,0:T(8,128)(2,1)} %collective-permute-done.1.bottom_ref), custom_call_target="tpu_custom_call" | custom-call | flops 1 | bytes 1 | tf_op jit(solution)/shard_map/rows_operator/pallas_call | solution.py:330
  50.3 0.6 collective-permute-done.2.left_ref
  50.9 0.0 copy-start.1
  50.9 1.8 %collective-permute-done.3.right_ref = bf16[1024,384]{1,0:T(8,128)(2,1)} collective-permute-done((bf16[1024,384]{1,0:T(8,128)(2,1)}, bf16[1024,384]{1,0:T(8,128)(2,1)}, u32[]{:S(2)}, u32[]{:S(2)}) %collective-permute-start.3) | collective-permute-done | bytes 786464 | tf_op jit(solution)/shard_map/ppermute | solution.py:347
  52.8 2.3 %collective-permute-start.4 = (bf16[512,384]{1,0:T(8,128)(2,1)}, bf16[512,384]{1,0:T(8,128)(2,1)}, u32[]{:S(2)}, u32[]{:S(2)}) collective-permute-start(bf16[512,384]{1,0:T(8,128)(2,1)} %get-tuple-element.38), channel_id=1, source_target_pairs={{0,1},{1,2},{2,3},{3,4},{4,5},{5,6},{6,7},{8,9},{9,10},{10,11},{11... | collective-permute-start | bytes 1179656 | tf_op jit(solution)/shard_map/ppermute | solution.py:347
  55.0 3.9 %collective-permute-start.5 = (bf16[512,384]{1,0:T(8,128)(2,1)}, bf16[512,384]{1,0:T(8,128)(2,1)}, u32[]{:S(2)}, u32[]{:S(2)}) collective-permute-start(bf16[512,384]{1,0:T(8,128)(2,1)} %get-tuple-element.39), channel_id=1, source_target_pairs={{1,0},{2,1},{3,2},{4,3},{5,4},{6,5},{7,6},{9,8},{10,9},{11,10},{12... | collective-permute-start | bytes 1179656 | tf_op jit(solution)/shard_map/ppermute | solution.py:347
  58.9 0.0 copy-done.1
  59.0 9.8 %columns_operator.3 = (bf16[2048,1024]{1,0:T(8,128)(2,1)}, bf16[384,1024]{1,0:T(8,128)(2,1)}, bf16[384,1024]{1,0:T(8,128)(2,1)}) custom-call(s32[1]{0:T(128)} %bitcast.where_ref, f32[7,8,128]{2,1,0:T(8,128)} %get-tuple-element.31.stencil_ref, f32[2048,1024]{1,0:T(8,128)} %p_ref.7, bf16[1024,384]{1,0:T(8,128)(2,1)} %copy-done.1, ...), custom_call_target="tpu_custom_call" | custom-call | flops 1 | bytes 1 | tf_op jit(solution)/shard_map/columns_operator/pallas_call | solution.py:231
  68.8 4.3 %collective-permute-start.8 = (bf16[384,1024]{1,0:T(8,128)(2,1)}, bf16[384,1024]{1,0:T(8,128)(2,1)}, u32[]{:S(2)}, u32[]{:S(2)}) collective-permute-start(bf16[384,1024]{1,0:T(8,128)(2,1)} %get-tuple-element.47), channel_id=1, source_target_pairs={{0,8},{8,16},{16,24},{1,9},{9,17},{17,25},{2,10},{10,18},{18,26},{... | collective-permute-start | bytes 2359304 | tf_op jit(solution)/shard_map/ppermute | solution.py:347
  73.1 0.0 collective-permute-done.6.left_ref
  73.1 2.1 %collective-permute-start.9 = (bf16[384,1024]{1,0:T(8,128)(2,1)}, bf16[384,1024]{1,0:T(8,128)(2,1)}, u32[]{:S(2)}, u32[]{:S(2)}) collective-permute-start(bf16[384,1024]{1,0:T(8,128)(2,1)} %get-tuple-element.48), channel_id=1, source_target_pairs={{8,0},{16,8},{24,16},{9,1},{17,9},{25,17},{10,2},{18,10},{26,18},{... | collective-permute-start | bytes 2359304 | tf_op jit(solution)/shard_map/ppermute | solution.py:347
  75.2 0.0 collective-permute-done.7.right_ref
  75.2 5.8 %columns_operator.4.rest_0_ = bf16[2048,1024]{1,0:T(8,128)(2,1)} custom-call(s32[1]{0:T(128)} %bitcast.where_ref, f32[7,8,128]{2,1,0:T(8,128)} %get-tuple-element.31.stencil_ref, f32[2048,1024]{1,0:T(8,128)} %p_ref.7, bf16[512,384]{1,0:T(8,128)(2,1)} %collective-permute-done.6.left_ref, ...), custom_call_target="tpu_custom_call", output_to_operand_aliasing={{}: (5, {})} | custom-call | flops 1 | bytes 1 | tf_op jit(solution)/shard_map/columns_operator/pallas_call | solution.py:231
  81.0 0.0 collective-permute-done.4.left_ref
  81.0 0.0 collective-permute-done.5.right_ref
  81.0 5.8 %columns_operator.5.x_ref = bf16[2048,1024]{1,0:T(8,128)(2,1)} custom-call(s32[1]{0:T(128)} %bitcast.13.where_ref, f32[7,8,128]{2,1,0:T(8,128)} %get-tuple-element.31.stencil_ref, f32[2048,1024]{1,0:T(8,128)} %p_ref.7, bf16[512,384]{1,0:T(8,128)(2,1)} %collective-permute-done.4.left_ref, ...), custom_call_target="tpu_custom_call", output_to_operand_aliasing={{}: (5, {})} | custom-call | flops 9999999827968 | bytes 9999999827968 | tf_op jit(solution)/shard_map/columns_operator/pallas_call | solution.py:231
  86.8 0.0 collective-permute-done.8.top_ref
  86.9 0.0 collective-permute-done.9.bottom_ref
  86.9 13.4 %rows_operator.3 = f32[2048,1024]{1,0:T(8,128)} custom-call(f32[7,16,128]{2,1,0:T(8,128)} %get-tuple-element.30.stencil_ref, bf16[2048,1024]{1,0:T(8,128)(2,1)} %columns_operator.5.x_ref, bf16[384,1024]{1,0:T(8,128)(2,1)} %collective-permute-done.8.top_ref, bf16[384,1024]{1,0:T(8,128)(2,1)} %collective-permute-done.9.bottom_ref, s32[1]{0:T(128)} %bitcast.14.rest_0_, ...), custom_call_target="tpu_custom_call" | custom-call | flops 1 | bytes 1 | tf_op jit(solution)/shard_map/rows_operator/pallas_call | solution.py:330
  (9 shorter events, 0.1 us)
Async XLA Ops:
  0.6 20.6 %copy-start = (f32[16,2]{0,1:T(2,128)S(1)}, f32[16,2]{0,1:T(2,128)}, u32[]{:S(2)}) copy-start(f32[16,2]{0,1:T(2,128)} %param.8) | copy-start | bytes 388
  1.3 18.7 %copy-start.3 = (s32[5]{0:T(128)S(1)}, s32[5]{0:T(128)}, u32[]{:S(2)}) copy-start(s32[5]{0:T(128)} %constant.56) | copy-start | bytes 64
  1.3 19.8 %copy-start.2 = (s32[3,64]{1,0:T(4,128)S(1)}, s32[3,64]{1,0:T(4,128)}, u32[]{:S(2)}) copy-start(s32[3,64]{1,0:T(4,128)} %param.10) | copy-start | bytes 2308
  1.3 19.8 %copy-start.4 = (f32[16]{0:T(128)S(1)}, f32[16]{0:T(128)}, u32[]{:S(2)}) copy-start(f32[16]{0:T(128)} %param.9) | copy-start | bytes 196
  8.2 12.9 %collective-permute-start = (bf16[384,1024]{1,0:T(8,128)(2,1)}, bf16[384,1024]{1,0:T(8,128)(2,1)}, u32[]{:S(2)}, u32[]{:S(2)}) collective-permute-start(bf16[384,1024]{1,0:T(8,128)(2,1)} %get-tuple-element.28), channel_id=1, source_target_pairs={{0,8},{8,16},{16,24},{1,9},{9,17},{17,25},{2,10},{10,18},{18,26},{... | collective-permute-start | bytes 2359304 | tf_op jit(solution)/shard_map/ppermute | solution.py:347
  11.9 21.5 %collective-permute-start.1 = (bf16[384,1024]{1,0:T(8,128)(2,1)}, bf16[384,1024]{1,0:T(8,128)(2,1)}, u32[]{:S(2)}, u32[]{:S(2)}) collective-permute-start(bf16[384,1024]{1,0:T(8,128)(2,1)} %get-tuple-element.33), channel_id=1, source_target_pairs={{8,0},{16,8},{24,16},{9,1},{17,9},{25,17},{10,2},{18,10},{26,18},{... | collective-permute-start | bytes 2359304 | tf_op jit(solution)/shard_map/ppermute | solution.py:347
  13.8 37.1 %collective-permute-start.2 = (bf16[1024,384]{1,0:T(8,128)(2,1)}, bf16[1024,384]{1,0:T(8,128)(2,1)S(1)}, u32[]{:S(2)}, u32[]{:S(2)}) collective-permute-start(bf16[1024,384]{1,0:T(8,128)(2,1)} %get-tuple-element.34), channel_id=1, source_target_pairs={{0,1},{1,2},{2,3},{3,4},{4,5},{5,6},{6,7},{8,9},{9,10},{10,11},{11... | collective-permute-start | bytes 2359304 | tf_op jit(solution)/shard_map/ppermute | solution.py:347
  16.9 35.8 %collective-permute-start.3 = (bf16[1024,384]{1,0:T(8,128)(2,1)}, bf16[1024,384]{1,0:T(8,128)(2,1)}, u32[]{:S(2)}, u32[]{:S(2)}) collective-permute-start(bf16[1024,384]{1,0:T(8,128)(2,1)} %get-tuple-element.35), channel_id=1, source_target_pairs={{1,0},{2,1},{3,2},{4,3},{5,4},{6,5},{7,6},{9,8},{10,9},{11,10},{12... | collective-permute-start | bytes 2359304 | tf_op jit(solution)/shard_map/ppermute | solution.py:347
  22.2 50.9 %collective-permute-start.6 = (bf16[512,384]{1,0:T(8,128)(2,1)}, bf16[512,384]{1,0:T(8,128)(2,1)}, u32[]{:S(2)}, u32[]{:S(2)}) collective-permute-start(bf16[512,384]{1,0:T(8,128)(2,1)} %get-tuple-element.43), channel_id=1, source_target_pairs={{0,2},{1,1},{2,10},{3,9},{4,18},{5,17},{6,26},{7,25},{8,4},{9,3},{... | collective-permute-start | bytes 1179656 | tf_op jit(solution)/shard_map/ppermute | solution.py:416
  25.4 49.8 %collective-permute-start.7 = (bf16[512,384]{1,0:T(8,128)(2,1)}, bf16[512,384]{1,0:T(8,128)(2,1)}, u32[]{:S(2)}, u32[]{:S(2)}) collective-permute-start(bf16[512,384]{1,0:T(8,128)(2,1)} %get-tuple-element.45), channel_id=1, source_target_pairs={{0,0},{2,8},{4,16},{6,24},{8,2},{9,1},{10,10},{11,9},{12,18},{13,1... | collective-permute-start | bytes 1179656 | tf_op jit(solution)/shard_map/ppermute | solution.py:417
  50.9 8.0 %copy-start.1 = (bf16[1024,384]{1,0:T(8,128)(2,1)}, bf16[1024,384]{1,0:T(8,128)(2,1)S(1)}, u32[]{:S(2)}) copy-start(bf16[1024,384]{1,0:T(8,128)(2,1)S(1)} %collective-permute-done.2.left_ref) | copy-start | bytes 2359300
  52.8 28.3 %collective-permute-start.4 = (bf16[512,384]{1,0:T(8,128)(2,1)}, bf16[512,384]{1,0:T(8,128)(2,1)}, u32[]{:S(2)}, u32[]{:S(2)}) collective-permute-start(bf16[512,384]{1,0:T(8,128)(2,1)} %get-tuple-element.38), channel_id=1, source_target_pairs={{0,1},{1,2},{2,3},{3,4},{4,5},{5,6},{6,7},{8,9},{9,10},{10,11},{11... | collective-permute-start | bytes 1179656 | tf_op jit(solution)/shard_map/ppermute | solution.py:347
  55.0 26.0 %collective-permute-start.5 = (bf16[512,384]{1,0:T(8,128)(2,1)}, bf16[512,384]{1,0:T(8,128)(2,1)}, u32[]{:S(2)}, u32[]{:S(2)}) collective-permute-start(bf16[512,384]{1,0:T(8,128)(2,1)} %get-tuple-element.39), channel_id=1, source_target_pairs={{1,0},{2,1},{3,2},{4,3},{5,4},{6,5},{7,6},{9,8},{10,9},{11,10},{12... | collective-permute-start | bytes 1179656 | tf_op jit(solution)/shard_map/ppermute | solution.py:347
  68.8 18.1 %collective-permute-start.8 = (bf16[384,1024]{1,0:T(8,128)(2,1)}, bf16[384,1024]{1,0:T(8,128)(2,1)}, u32[]{:S(2)}, u32[]{:S(2)}) collective-permute-start(bf16[384,1024]{1,0:T(8,128)(2,1)} %get-tuple-element.47), channel_id=1, source_target_pairs={{0,8},{8,16},{16,24},{1,9},{9,17},{17,25},{2,10},{10,18},{18,26},{... | collective-permute-start | bytes 2359304 | tf_op jit(solution)/shard_map/ppermute | solution.py:347
  73.1 13.8 %collective-permute-start.9 = (bf16[384,1024]{1,0:T(8,128)(2,1)}, bf16[384,1024]{1,0:T(8,128)(2,1)}, u32[]{:S(2)}, u32[]{:S(2)}) collective-permute-start(bf16[384,1024]{1,0:T(8,128)(2,1)} %get-tuple-element.48), channel_id=1, source_target_pairs={{8,0},{16,8},{24,16},{9,1},{17,9},{25,17},{10,2},{18,10},{26,18},{... | collective-permute-start | bytes 2359304 | tf_op jit(solution)/shard_map/ppermute | solution.py:347
where the time goes:
time: 101 us; the launch traced here: 100 us
  Pallas kernels  60.6 us (60%)
  starting transfers between devices  32 us (32%)
  waiting for transfers between devices  3.52 us (3%)
  local copies, waits for them, and re-layouts  2.34 us (2%)
    pallas_call x2, Pallas kernels, rows_operator(): pl.pallas_call(kernel, grid=(pairs + ahead,), in_specs=in_specs, out_spec...  30.4 us
    ppermute x8, starting transfers between devices, shifted(): return lax.ppermute(block, axis, pairs)  24.3 us
    pallas_call x3, Pallas kernels, columns_operator(): pl.pallas_call(kernel, grid_spec=pltpu.PrefetchScalarGridSpec(num_scalar_...  21.5 us
    pallas_call x1, Pallas kernels, pack(): pl.pallas_call(kernel, in_specs=[pl.BlockSpec(memory_space=pltpu.SMEM), p...  6.83 us
    ppermute x1, starting transfers between devices, body(): lax.ppermute(right_m, ('row', 'col'), mirror_pairs(n_row, n_col, -1))  4.5 us
    ppermute x8, waiting for transfers between devices, shifted(): return lax.ppermute(block, axis, pairs)  3.51 us
    ppermute x1, starting transfers between devices, body(): left_m = lax.ppermute(left_m, ('row', 'col'), mirror_pairs(n_row, n_col, 1))  3.2 us
  transfers between devices with their start and end apart: 10, of which 3 were waited for; matrix products, arithmetic and copies ran while one was open for 3% of the time, Pallas kernels for 40%

commit v1 on v0

v1 whole, which is shorter than its diff:
```python
import functools

import jax
import jax.numpy as jnp
from jax import lax
from jax.experimental import pallas as pl
from jax.experimental.pallas import tpu as pltpu
from jax.sharding import PartitionSpec as P

F32 = jnp.float32
BF16 = jnp.bfloat16
VMEM_LIMIT = 63 * 1024 * 1024


def params():
    return pltpu.CompilerParams(vmem_limit_bytes=VMEM_LIMIT)


def cost(work):
    return pl.CostEstimate(flops=work, bytes_accessed=work, transcendentals=0)


def stencil_terms(zonal_cour, merid_cour, diffuse):
    middle_weight = 1.0 - zonal_cour * zonal_cour - merid_cour * merid_cour - 4.0 * diffuse
    eastward_weight = 0.5 * zonal_cour * zonal_cour - 0.5 * zonal_cour + diffuse
    west_w = 0.5 * zonal_cour * zonal_cour + 0.5 * zonal_cour + diffuse
    north_w = 0.5 * merid_cour * merid_cour - 0.5 * merid_cour + diffuse
    south_w = 0.5 * merid_cour * merid_cour + 0.5 * merid_cour + diffuse
    return middle_weight, eastward_weight, west_w, north_w, south_w


def split(values):
    high = values.astype(BF16)
    return high, (values - high.astype(F32)).astype(BF16)


def circulant(row):
    size, group = row.shape[1], 8
    first = pltpu.roll(jnp.broadcast_to(row, (group, size)), 0, 1, stride=1, stride_axis=0)
    return jnp.concatenate([first] + [pltpu.roll(first, at, 1) for at in range(group, size, group)], axis=0)


def product(left, right):
    return jnp.dot(left, right, preferred_element_type=F32)


def composed(terms, lats, nlon):
    steps = len(terms)
    padded = lats + 2 * steps
    lane = lax.broadcasted_iota(jnp.int32, (padded, nlon), 1)
    rows = {0: (lane == 0).astype(F32)}
    for step_no in range(steps):
        low, high = step_no + 1, padded - step_no - 1
        c, e, w, n, s = [term[low:high] for term in terms[step_no]]
        size = high - low
        fresh = {}
        for d in range(-step_no - 1, step_no + 2):
            parts = []
            if d in rows:
                here = rows[d][1 : 1 + size]
                parts += [c * here, e * pltpu.roll(here, 1, 1), w * pltpu.roll(here, nlon - 1, 1)]
            if d - 1 in rows:
                parts.append(n * rows[d - 1][2 : 2 + size])
            if d + 1 in rows:
                parts.append(s * rows[d + 1][0:size])
            fresh[d] = functools.reduce(lambda x, y: x + y, parts)
        rows = fresh
    return rows


def stencil_rows(wind_table, diffusivity, wind_index, row_lat, col_lat, lat_rows, lats, nlon):
    steps = wind_index.shape[0]
    table = wind_table.shape[0]
    padded = jnp.pad(wind_index, ((0, 0), (steps, steps)), constant_values=-1)

    def local(first, count):
        part = lax.dynamic_slice_in_dim(padded, first, count + 2 * steps, 1)
        return jnp.broadcast_to(part[:, :, None], part.shape + (nlon,))

    def kernel(table_ref, diffuse_ref, row_ref, col_ref, row_out, col_out):
        for ref, out, size, turned in ((row_ref, row_out, lat_rows, False), (col_ref, col_out, lats, True)):
            terms = []
            for step_no in range(steps):
                index = ref[step_no]
                zonal = merid = diffuse = jnp.zeros(index.shape, F32)
                for entry in range(table):
                    here = index == entry
                    zonal = jnp.where(here, table_ref[2 * entry], zonal)
                    merid = jnp.where(here, table_ref[2 * entry + 1], merid)
                    diffuse = jnp.where(here, diffuse_ref[entry], diffuse)
                c, e, w, n, s = [
                    jnp.where(index >= 0, term, 0.0) for term in stencil_terms(zonal, merid, diffuse)
                ]
                terms.append((c, w, e, n, s) if turned else (c, e, w, n, s))
            for d, value in composed(terms, size, nlon).items():
                out[d + steps] = value

    return pl.pallas_call(
        kernel,
        in_specs=[pl.BlockSpec(memory_space=pltpu.SMEM)] * 2 + [pl.BlockSpec(memory_space=pltpu.VMEM)] * 2,
        out_shape=[
            jax.ShapeDtypeStruct((2 * steps + 1, size, nlon), F32) for size in (lat_rows, lats)
        ],
        compiler_params=params(),
        cost_estimate=cost(1),
        name="stencil_rows",
    )(wind_table.reshape(-1), diffusivity, local(row_lat, lat_rows), local(col_lat, lats))


def packed(covariance, where, pieces):
    outs = 1 + max(piece[4] for piece in pieces)

    def placed(piece):
        _, size, _, width, _, _, turn = piece
        return (width, size) if turn else (size, width)

    out_shapes = [None] * outs
    for piece in pieces:
        shape = placed(piece)
        out_shapes[piece[4]] = (max(piece[5] + shape[0], (out_shapes[piece[4]] or (0,))[0]), shape[1])

    def kernel(where_ref, p_ref, *refs):
        count = len(pieces)
        results, got, made = refs[:outs], refs[outs : outs + count], refs[outs + count : outs + 2 * count]
        in_sem, out_sem = refs[outs + 2 * count :]
        start = lambda at: pl.multiple_of(where_ref[at[0]], 128) if isinstance(at, tuple) else at
        loads = []
        for k, (row, size, col, width, _, _, _) in enumerate(pieces):
            source = p_ref.at[pl.ds(start(row), size), pl.ds(start(col), width)]
            loads.append(pltpu.make_async_copy(source, got[k], in_sem.at[k]))
            loads[-1].start()
        stores = []
        for k, piece in enumerate(pieces):
            loads[k].wait()
            turn, shape = piece[6], placed(piece)
            if turn:
                for a in range(0, shape[0], turn):
                    for b in range(0, shape[1], turn):
                        made[k][a : a + turn, b : b + turn] = got[k][b : b + turn, a : a + turn].T.astype(BF16)
            else:
                made[k][...] = got[k][...].astype(BF16)
            target = results[piece[4]].at[pl.ds(piece[5], shape[0]), :]
            stores.append(pltpu.make_async_copy(made[k], target, out_sem.at[k]))
            stores[-1].start()
        for copy in stores:
            copy.wait()

    return pl.pallas_call(
        kernel,
        in_specs=[pl.BlockSpec(memory_space=pltpu.SMEM), pl.BlockSpec(memory_space=pl.ANY)],
        out_specs=[pl.BlockSpec(memory_space=pl.ANY)] * outs,
        out_shape=[jax.ShapeDtypeStruct(shape, BF16) for shape in out_shapes],
        scratch_shapes=[pltpu.VMEM(piece[1:4:2], F32) for piece in pieces]
        + [pltpu.VMEM(placed(piece), BF16) for piece in pieces]
        + [pltpu.SemaphoreType.DMA((len(pieces),)), pltpu.SemaphoreType.DMA((len(pieces),))],
        compiler_params=params(),
        cost_estimate=cost(1),
        name="packed",
    )(where, covariance)


def columns_operator(
    covariance, left, right, stencil, where, unit, steps, nlon, count, block_at, held=None, work=1
):
    rows, cols = covariance.shape
    lats = cols // nlon
    wide = steps * nlon
    size = unit * nlon
    span = 2 * steps * nlon
    pairs = lats // 2

    def kernel(where_ref, stencil_ref, p_ref, left_ref, right_ref, *rest):
        outs, (data_ref, b_high, b_low) = rest[:-3], rest[-3:]
        if held is not None:
            outs = outs[1:]
        t_ref = outs[0]
        i = pl.program_id(0)

        @pl.when(i == 0)
        def _():
            data_ref[size:, :wide] = jnp.zeros((size, wide), BF16)
            data_ref[size:, wide + cols :] = jnp.zeros((size, wide), BF16)
            for q in range(pairs):
                for a in range(2):
                    for k in range(2 * steps):
                        d = k - (steps - 1) - a
                        high, low = split(circulant(stencil_ref[d + steps, 2 * q + a : 2 * q + a + 1, :]))
                        at = pl.ds(q * span + k * nlon, nlon)
                        b_high[at, a * nlon : (a + 1) * nlon] = high
                        b_low[at, a * nlon : (a + 1) * nlon] = low

        data_ref[:size, :wide] = left_ref[...]
        data_ref[:size, wide + cols :] = right_ref[...]
        data_ref[:size, wide : wide + cols], data_ref[size:, wide : wide + cols] = split(p_ref[...])
        for q in range(pairs):
            window = slice((2 * q + 1) * nlon, (2 * q + 1) * nlon + span)
            of = pl.ds(q * span, span)
            both = product(data_ref[:, window], b_high[of, :])
            total = both[:size] + both[size:] + product(data_ref[:size, window], b_low[of, :])
            for a, k, d in ((0, 2 * q, -steps), (1, 2 * q + 2 * steps + 1, steps)):
                far = slice(k * nlon, (k + 1) * nlon)
                weight = jnp.sum(stencil_ref[d + steps, 2 * q + a : 2 * q + a + 1, :], axis=1, keepdims=True)
                far_values = data_ref[:size, far].astype(F32) + data_ref[size:, far].astype(F32)
                value = total[:, a * nlon : (a + 1) * nlon] + weight * far_values
                t_ref[:, (2 * q + a) * nlon : (2 * q + a + 1) * nlon] = value.astype(BF16)
        if held is None:

            @pl.when(i == 0)
            def _():
                outs[1][...] = t_ref[:wide, :]

            @pl.when(i == count - 1)
            def _():
                outs[2][...] = t_ref[size - wide :, :]

    in_specs = [
        pl.BlockSpec(stencil.shape, lambda i, at: (0, 0, 0)),
        pl.BlockSpec((size, cols), lambda i, at: (block_at(i, at), 0)),
        pl.BlockSpec((size, wide), lambda i, at: (i, 0)),
        pl.BlockSpec((size, wide), lambda i, at: (i, 0)),
    ]
    out_specs = [pl.BlockSpec((size, cols), lambda i, at: (block_at(i, at), 0))]
    out_shape = [jax.ShapeDtypeStruct((rows, cols), BF16)]
    operands = [where, stencil, covariance, left, right]
    aliases = {}
    if held is None:
        out_specs += [pl.BlockSpec((wide, cols), lambda i, at: (0, 0))] * 2
        out_shape += [jax.ShapeDtypeStruct((wide, cols), BF16)] * 2
    else:
        in_specs.append(pl.BlockSpec(memory_space=pl.ANY))
        operands.append(held)
        aliases = {5: 0}
    return pl.pallas_call(
        kernel,
        grid_spec=pltpu.PrefetchScalarGridSpec(
            num_scalar_prefetch=1,
            grid=(count,),
            in_specs=in_specs,
            out_specs=out_specs,
            scratch_shapes=[pltpu.VMEM((2 * size, cols + 2 * wide), BF16)]
            + [pltpu.VMEM((pairs * span, size), BF16)] * 2,
        ),
        out_shape=out_shape,
        input_output_aliases=aliases,
        compiler_params=params(),
        cost_estimate=cost(work),
        name="columns_operator",
    )(*operands)


def rows_operator(values, top, bottom, stencil, steps, nlon, out_dtype, noise=None, diagonal=None):
    rows, cols = values.shape
    lat_rows = rows // nlon
    wide = steps * nlon
    size = 2 * nlon
    span = 2 * steps * nlon
    pairs = lat_rows // 2
    ahead = min((steps + 1) // 2, pairs - 1)
    exact = values.dtype == BF16
    chunk = min(cols, 256)

    def kernel(stencil_ref, x_ref, top_ref, bottom_ref, *rest):
        extra, rest = (rest[:2], rest[2:]) if noise is not None else ((), rest)
        out_ref, a_ref, high_ref, sem = rest[:4]
        raw_ref, low_ref = (None, None) if exact else rest[4:]
        p = pl.program_id(0)

        def load(q):
            here = pl.ds(pl.multiple_of(q * size, size), size)
            there = pl.ds(pl.multiple_of(wide + q * size, nlon), size)
            target = high_ref.at[there, :] if exact else raw_ref.at[here, :]
            return pltpu.make_async_copy(x_ref.at[here, :], target, sem.at[q])

        def ready(q):
            load(q).wait()
            if not exact:
                there = pl.ds(pl.multiple_of(wide + q * size, nlon), size)
                here = pl.ds(pl.multiple_of(q * size, size), size)
                high_ref[there, :], low_ref[there, :] = split(raw_ref[here, :])

        @pl.when(p == 0)
        def _():
            halos = [
                pltpu.make_async_copy(top_ref, high_ref.at[:wide, :], sem.at[pairs]),
                pltpu.make_async_copy(bottom_ref, high_ref.at[wide + rows :, :], sem.at[pairs + 1]),
            ]
            for halo in halos:
                halo.start()
            for q in range(pairs):
                load(q).start()
            if not exact:
                low_ref[:wide, :] = jnp.zeros((wide, cols), BF16)
                low_ref[wide + rows :, :] = jnp.zeros((wide, cols), BF16)
            for halo in halos:
                halo.wait()
            for q in range(ahead):
                ready(q)

        @pl.when(p + ahead < pairs)
        def _():
            ready(p + ahead)

        row = lambda d, a: stencil_ref[d + steps, pl.ds(2 * p + a, 1), :]
        for a in range(2):
            for k in range(2 * steps):
                high, low = split(circulant(row(k - (steps - 1) - a, a)))
                a_ref[a * nlon : (a + 1) * nlon, k * nlon : (k + 1) * nlon] = high
                a_ref[size + a * nlon : size + (a + 1) * nlon, k * nlon : (k + 1) * nlon] = low
        unit = lambda k: pl.multiple_of((2 * p + k) * nlon, nlon)
        for lane in range(0, cols, chunk):
            lanes = slice(lane, lane + chunk)
            window = high_ref[pl.ds(unit(1), span), lanes]
            both = product(a_ref[...], window)
            total = both[:size] + both[size:]
            if not exact:
                total += product(a_ref[:size, :], low_ref[pl.ds(unit(1), span), lanes])
            for a, k, d in ((0, 0, -steps), (1, 2 * steps + 1, steps)):
                far = high_ref[pl.ds(unit(k), nlon), lanes].astype(F32)
                if not exact:
                    far += low_ref[pl.ds(unit(k), nlon), lanes].astype(F32)
                weight = jnp.sum(row(d, a), axis=1, keepdims=True)
                value = total[a * nlon : (a + 1) * nlon, :] + weight * far
                out_ref[a * nlon : (a + 1) * nlon, lanes] = value.astype(out_dtype)
        if noise is not None:
            diagonal_ref, noise_ref = extra
            for a in range(2):
                lat = 2 * p + a - diagonal_ref[0]

                @pl.when(jnp.logical_and(lat >= 0, lat < cols // nlon))
                def _(a=a, lat=lat):
                    lanes = pl.ds(pl.multiple_of(lat * nlon, nlon), nlon)
                    eye = lax.broadcasted_iota(jnp.int32, (nlon, nlon), 0) == lax.broadcasted_iota(
                        jnp.int32, (nlon, nlon), 1
                    )
                    added = jnp.where(eye, noise_ref[pl.ds(2 * p + a, 1), :], 0.0)
                    out_ref[a * nlon : (a + 1) * nlon, lanes] += added

    in_specs = [
        pl.BlockSpec(stencil.shape, lambda g: (0, 0, 0)),
        pl.BlockSpec(memory_space=pl.ANY),
        pl.BlockSpec(memory_space=pl.ANY),
        pl.BlockSpec(memory_space=pl.ANY),
    ]
    operands = [stencil, values, top, bottom]
    if noise is not None:
        in_specs += [pl.BlockSpec(memory_space=pltpu.SMEM), pl.BlockSpec(noise.shape, lambda g: (0, 0))]
        operands += [diagonal, noise]
    return pl.pallas_call(
        kernel,
        grid=(pairs,),
        in_specs=in_specs,
        out_specs=pl.BlockSpec((size, cols), lambda g: (g, 0)),
        out_shape=jax.ShapeDtypeStruct((rows, cols), out_dtype),
        scratch_shapes=[pltpu.VMEM((2 * size, span), BF16)]
        + [pltpu.VMEM((rows + 2 * wide, cols), BF16), pltpu.SemaphoreType.DMA((pairs + 2,))]
        + ([] if exact else [pltpu.VMEM((rows, cols), F32), pltpu.VMEM((rows + 2 * wide, cols), BF16)]),
        compiler_params=params(),
        cost_estimate=cost(1),
        name="rows_operator",
    )(*operands)


def shifted(block, axis, by):
    size = lax.axis_size(axis)
    pairs = [(i, i + by) for i in range(size) if 0 <= i + by < size]
    return lax.ppermute(block, axis, pairs)


def gathered(first, last, axis, dim, unit, halo, own):
    before, after = [], []
    need, hop = halo, 1
    while need > 0:
        take = min(own, need)
        size = first.shape[dim]
        before.insert(0, shifted(lax.slice_in_dim(last, size - take * unit, size, axis=dim), axis, hop))
        after.append(shifted(lax.slice_in_dim(first, 0, take * unit, axis=dim), axis, -hop))
        need, hop = need - take, hop + 1
    join = lambda parts: parts[0] if len(parts) == 1 else jnp.concatenate(parts, axis=dim)
    return join(before), join(after)


def mirror_pairs(n_row, n_col, side):
    pairs = []
    for a in range(n_row):
        for b in range(n_col):
            to = 2 * a + (1 - b % 2) + side
            if 0 <= to < n_col:
                pairs.append((a * n_col + b, (b // 2) * n_col + to))
    return pairs


def body(covariance, noise_var, wind_table, diffusivity, wind_index):
    rows_dev, cols_dev = covariance.shape
    lat_rows, nlon = noise_var.shape
    steps, nlat = wind_index.shape
    lats = cols_dev // nlon
    n_row, n_col = lax.axis_size("row"), lax.axis_size("col")
    row_id, col_id = lax.axis_index("row"), lax.axis_index("col")
    own = lat_rows // 4
    mirrored = lat_rows == 2 * lats and own % 2 == 0 and own >= steps and own <= lats - steps

    if not mirrored:
        return plain_body(covariance, noise_var, wind_table, diffusivity, wind_index)

    near = lat_rows // 2 - own
    middle = lat_rows // 2
    parity = col_id % 2
    by_parity = lambda even, odd: jnp.where(parity == 0, even, odd).astype(jnp.int32)
    mirror_at = by_parity(middle - own, middle).reshape(1)
    direct_at = by_parity(middle, middle - own).reshape(1)
    base = (1 - parity) * lats
    sources = nlon * jnp.stack([mirror_at[0], base + lats - steps, base, by_parity(lats - own, 0)]).astype(jnp.int32)
    outer, inner, wide = near * nlon, own * nlon, steps * nlon
    ends = (0, cols_dev - wide)
    pieces = [
        (row, outer, lane, wide, k, there, 0)
        for row, there in ((0, 0), (rows_dev - outer, outer))
        for k, lane in enumerate(ends)
    ]
    pieces += [(row, wide, 0, cols_dev, k + 2, 0, 0) for k, row in enumerate((0, rows_dev - wide))]
    pieces += [((k + 1,), wide, (3,), inner, k + 4, 0, nlon) for k in range(2)]
    pieces += [((0,), inner, lane, wide, k + 6, 0, 0) for k, lane in enumerate(ends)]
    first, last, top, bottom, left_m, right_m, first_inner, last_inner = packed(covariance, sources, pieces)
    left = shifted(last, "col", 1)
    right = shifted(first, "col", -1)
    p_top = shifted(bottom, "row", 1)
    p_bottom = shifted(top, "row", -1)
    left_m, right_m, first_inner, wind_index, p_top = lax.optimization_barrier(
        (left_m, right_m, first_inner, wind_index, p_top)
    )
    left_m = lax.ppermute(left_m, ("row", "col"), mirror_pairs(n_row, n_col, 1))
    right_m = lax.ppermute(right_m, ("row", "col"), mirror_pairs(n_row, n_col, -1))
    right_inner = shifted(first_inner, "col", -1)

    row_s, col_s = stencil_rows(
        wind_table, diffusivity, wind_index, row_id * lat_rows, col_id * lats, lat_rows, lats, nlon
    )

    operator_times_prior = rows_operator(covariance, p_top, p_bottom, row_s, steps, nlon, BF16)
    operator_times_prior, left, right, last_inner = lax.optimization_barrier(
        (operator_times_prior, left, right, last_inner)
    )
    left_inner = shifted(last_inner, "col", 1)
    mirror, t_first, t_last = columns_operator(
        covariance, left, right, col_s, mirror_at, near, steps, nlon, 2, lambda i, at: i * (lat_rows // near - 1)
    )
    t_top = shifted(t_last, "row", 1)
    t_first, left_m = lax.optimization_barrier((t_first, left_m))
    t_bottom = shifted(t_first, "row", -1)
    inner_at = lambda i, at: at[0] // own + i
    (mirror,) = columns_operator(
        covariance, left_m, right_m, col_s, mirror_at, own, steps, nlon, 1, inner_at, mirror
    )
    (mirror,) = columns_operator(
        covariance, left_inner, right_inner, col_s, direct_at, own, steps, nlon, 1, inner_at, mirror, 10 ** 13
    )
    diagonal = (col_id * lats - row_id * lat_rows).astype(jnp.int32).reshape(1)
    predicted_spread_matrix = rows_operator(
        mirror, t_top, t_bottom, row_s, steps, nlon, F32, noise_var, diagonal
    )
    return (predicted_spread_matrix, operator_times_prior)


def plain_body(covariance, noise_var, wind_table, diffusivity, wind_index):
    rows_dev, cols_dev = covariance.shape
    lat_rows, nlon = noise_var.shape
    steps, nlat = wind_index.shape
    lats = cols_dev // nlon
    row_id, col_id = lax.axis_index("row"), lax.axis_index("col")
    sent = covariance.astype(BF16)
    left, right = gathered(sent, sent, "col", 1, nlon, steps, lats)
    p_top, p_bottom = gathered(sent, sent, "row", 0, nlon, steps, lat_rows)
    row_s, col_s = stencil_rows(
        wind_table, diffusivity, wind_index, row_id * lat_rows, col_id * lats, lat_rows, lats, nlon
    )
    operator_times_prior = rows_operator(covariance, p_top, p_bottom, row_s, steps, nlon, BF16)
    unused = jnp.zeros((1,), jnp.int32)
    held = jnp.zeros((rows_dev, cols_dev), BF16)
    (mirror,) = columns_operator(
        covariance, left, right, col_s, unused, 2, steps, nlon, lat_rows // 2, lambda i, at: i, held
    )
    t_top, t_bottom = gathered(mirror, mirror, "row", 0, nlon, steps, lat_rows)
    diagonal = (col_id * lats - row_id * lat_rows).astype(jnp.int32).reshape(1)
    predicted_spread_matrix = rows_operator(
        mirror, t_top, t_bottom, row_s, steps, nlon, F32, noise_var, diagonal
    )
    return (predicted_spread_matrix, operator_times_prior)


def solution(mesh):
    in_specs = (P("row", "col"), P("row", None), P(), P(), P())
    out_specs = (P("row", "col"), P("row", "col"))
    return jax.shard_map(body, mesh=mesh, in_specs=in_specs, out_specs=out_specs, check_vma=False)
```

time: 101 us -> 109 us (1.079)
  the two profiles are of different devices: /device:TPU:9 before, /device:TPU:1 now
where the time goes in v1:
time: 109 us
  Pallas kernels  63.5 us (58%)
  starting transfers between devices  30.3 us (28%)
  waiting for transfers between devices  11 us (10%)
  local copies, waits for them, and re-layouts  2.24 us (2%)
    pallas_call x2, Pallas kernels, rows_operator(): pl.pallas_call(kernel, grid=(pairs,), in_specs=in_specs, out_specs=pl.Blo...  30.8 us
    pallas_call x3, Pallas kernels, columns_operator(): pl.pallas_call(kernel, grid_spec=pltpu.PrefetchScalarGridSpec(num_scalar_...  24.4 us
    ppermute x8, starting transfers between devices, shifted(): return lax.ppermute(block, axis, pairs)  23 us
    ppermute x8, waiting for transfers between devices, shifted(): return lax.ppermute(block, axis, pairs)  11 us
    pallas_call x1, Pallas kernels, packed(): pl.pallas_call(kernel, in_specs=[pl.BlockSpec(memory_space=pltpu.SMEM), p...  6.62 us
    ppermute x1, starting transfers between devices, body(): left_m = lax.ppermute(left_m, ('row', 'col'), mirror_pairs(n_row, n_col, 1))  5.21 us
  transfers between devices with their start and end apart: 10, of which 2 were waited for; matrix products, arithmetic and copies ran while one was open for 2% of the time, Pallas kernels for 40%

profile of v1, /device:TPU:1, one launch (start us, length us, event | category | flops | bytes accessed | tf_op | source)
XLA Modules:
  0.0 108.6 jit_solution(14749605617104146101)
XLA Ops:
  0.6 0.6 add_multiply_fusion.where_ref
  1.2 0.0 copy-start.2
  1.2 0.0 copy-start.1
  1.2 6.6 %packed.1 = (bf16[1024,384]{1,0:T(8,128)(2,1)}, bf16[1024,384]{1,0:T(8,128)(2,1)}, bf16[384,1024]{1,0:T(8,128)(2,1)}, bf16[384,1024]{1,0:T(8,128)(2,1)}, bf16[51...) custom-call(s32[4]{0:T(128)} %add_multiply_fusion.where_ref, ...), custom_call_target="tpu_custom_call" | custom-call | flops 1 | bytes 1 | tf_op jit(solution)/shard_map/packed/pallas_call | solution.py:148
  7.8 4.5 %collective-permute-start = (bf16[384,1024]{1,0:T(8,128)(2,1)}, bf16[384,1024]{1,0:T(8,128)(2,1)}, u32[]{:S(2)}, u32[]{:S(2)}) collective-permute-start(bf16[384,1024]{1,0:T(8,128)(2,1)} %get-tuple-element.29), channel_id=1, source_target_pairs={{0,8},{8,16},{16,24},{1,9},{9,17},{17,25},{2,10},{10,18},{18,26},{... | collective-permute-start | bytes 2359304 | tf_op jit(solution)/shard_map/ppermute | solution.py:366
  12.4 1.9 %collective-permute-start.1 = (bf16[384,1024]{1,0:T(8,128)(2,1)}, bf16[384,1024]{1,0:T(8,128)(2,1)}, u32[]{:S(2)}, u32[]{:S(2)}) collective-permute-start(bf16[384,1024]{1,0:T(8,128)(2,1)} %get-tuple-element.34), channel_id=1, source_target_pairs={{8,0},{16,8},{24,16},{9,1},{17,9},{25,17},{10,2},{18,10},{26,18},{... | collective-permute-start | bytes 2359304 | tf_op jit(solution)/shard_map/ppermute | solution.py:366
  14.3 3.2 %collective-permute-start.2 = (bf16[1024,384]{1,0:T(8,128)(2,1)}, bf16[1024,384]{1,0:T(8,128)(2,1)S(1)}, u32[]{:S(2)}, u32[]{:S(2)}) collective-permute-start(bf16[1024,384]{1,0:T(8,128)(2,1)} %get-tuple-element.35), channel_id=1, source_target_pairs={{0,1},{1,2},{2,3},{3,4},{4,5},{5,6},{6,7},{8,9},{9,10},{10,11},{11... | collective-permute-start | bytes 2359304 | tf_op jit(solution)/shard_map/ppermute | solution.py:366
  17.5 1.3 %collective-permute-start.3 = (bf16[1024,384]{1,0:T(8,128)(2,1)}, bf16[1024,384]{1,0:T(8,128)(2,1)}, u32[]{:S(2)}, u32[]{:S(2)}) collective-permute-start(bf16[1024,384]{1,0:T(8,128)(2,1)} %get-tuple-element.36), channel_id=1, source_target_pairs={{1,0},{2,1},{3,2},{4,3},{5,4},{6,5},{7,6},{9,8},{10,9},{11,10},{12... | collective-permute-start | bytes 2359304 | tf_op jit(solution)/shard_map/ppermute | solution.py:366
  18.8 0.0 copy-done.2
  18.8 0.1 copy.10
  18.9 0.6 reshape.16.table_ref
  19.5 2.1 %collective-permute-done.top_ref = bf16[384,1024]{1,0:T(8,128)(2,1)} collective-permute-done((bf16[384,1024]{1,0:T(8,128)(2,1)}, bf16[384,1024]{1,0:T(8,128)(2,1)}, u32[]{:S(2)}, u32[]{:S(2)}) %collective-permute-start) | collective-permute-done | bytes 786464 | tf_op jit(solution)/shard_map/ppermute | solution.py:366
  21.6 1.3 %collective-permute-start.5 = (bf16[512,384]{1,0:T(8,128)(2,1)}, bf16[512,384]{1,0:T(8,128)(2,1)}, u32[]{:S(2)}, u32[]{:S(2)}) collective-permute-start(bf16[512,384]{1,0:T(8,128)(2,1)} %get-tuple-element.39), channel_id=1, source_target_pairs={{1,0},{2,1},{3,2},{4,3},{5,4},{6,5},{7,6},{9,8},{10,9},{11,10},{12... | collective-permute-start | bytes 1179656 | tf_op jit(solution)/shard_map/ppermute | solution.py:366
  22.9 5.2 %collective-permute-start.6 = (bf16[512,384]{1,0:T(8,128)(2,1)}, bf16[512,384]{1,0:T(8,128)(2,1)}, u32[]{:S(2)}, u32[]{:S(2)}) collective-permute-start(bf16[512,384]{1,0:T(8,128)(2,1)} %get-tuple-element.43), channel_id=1, source_target_pairs={{0,2},{1,1},{2,10},{3,9},{4,18},{5,17},{6,26},{7,25},{8,4},{9,3},{... | collective-permute-start | bytes 1179656 | tf_op jit(solution)/shard_map/ppermute | solution.py:431
  28.1 0.0 copy-done.1
  28.1 0.1 pad_dynamic-slice_fusion
  28.2 0.1 pad_dynamic-slice_fusion.1
  28.3 0.7 broadcast_in_dim.5.col_ref
  28.9 0.7 broadcast_in_dim.4.row_ref
  29.6 1.7 %stencil_rows.1 = (f32[7,16,128]{2,1,0:T(8,128)}, f32[7,8,128]{2,1,0:T(8,128)}) custom-call(f32[32]{0:T(128)} %reshape.16.table_ref, f32[16]{0:T(128)} %diffuse_ref.1, s32[3,22,128]{2,1,0:T(8,128)} %broadcast_in_dim.4.row_ref, s32[3,14,128]{2,1,0:T(8,128)} %broadcast_in_dim.5.col_ref), custom_call_target="tpu_custom_call" | custom-call | flops 1 | bytes 1 | tf_op jit(solution)/shard_map/stencil_rows/pallas_call | solution.py:98
  31.4 0.0 collective-permute-done.1.bottom_ref
  31.4 2.1 %collective-permute-start.7 = (bf16[512,384]{1,0:T(8,128)(2,1)}, bf16[512,384]{1,0:T(8,128)(2,1)}, u32[]{:S(2)}, u32[]{:S(2)}) collective-permute-start(bf16[512,384]{1,0:T(8,128)(2,1)} %get-tuple-element.45), channel_id=1, source_target_pairs={{0,0},{2,8},{4,16},{6,24},{8,2},{9,1},{10,10},{11,9},{12,18},{13,1... | collective-permute-start | bytes 1179656 | tf_op jit(solution)/shard_map/ppermute | solution.py:432
  33.4 17.5 %rows_operator.2 = bf16[2048,1024]{1,0:T(8,128)(2,1)} custom-call(f32[7,16,128]{2,1,0:T(8,128)} %get-tuple-element.31.stencil_ref, f32[2048,1024]{1,0:T(8,128)} %p_ref.7, bf16[384,1024]{1,0:T(8,128)(2,1)} %collective-permute-done.top_ref, bf16[384,1024]{1,0:T(8,128)(2,1)} %collective-permute-done.1.bottom_ref), custom_call_target="tpu_custom_call" | custom-call | flops 1 | bytes 1 | tf_op jit(solution)/shard_map/rows_operator/pallas_call | solution.py:348
  51.0 8.9 %collective-permute-done.2.left_ref = bf16[1024,384]{1,0:T(8,128)(2,1)S(1)} collective-permute-done((bf16[1024,384]{1,0:T(8,128)(2,1)}, bf16[1024,384]{1,0:T(8,128)(2,1)S(1)}, u32[]{:S(2)}, u32[]{:S(2)}) %collective-permute-start.2) | collective-permute-done | bytes 786464 | tf_op jit(solution)/shard_map/ppermute | solution.py:366
  59.9 0.0 copy-start
  59.9 0.0 collective-permute-done.3.right_ref
  59.9 4.5 %collective-permute-start.4 = (bf16[512,384]{1,0:T(8,128)(2,1)}, bf16[512,384]{1,0:T(8,128)(2,1)}, u32[]{:S(2)}, u32[]{:S(2)}) collective-permute-start(bf16[512,384]{1,0:T(8,128)(2,1)} %get-tuple-element.38), channel_id=1, source_target_pairs={{0,1},{1,2},{2,3},{3,4},{4,5},{5,6},{6,7},{8,9},{9,10},{10,11},{11... | collective-permute-start | bytes 1179656 | tf_op jit(solution)/shard_map/ppermute | solution.py:366
  64.3 0.0 copy-done
  64.4 12.4 %columns_operator.3 = (bf16[2048,1024]{1,0:T(8,128)(2,1)}, bf16[384,1024]{1,0:T(8,128)(2,1)}, bf16[384,1024]{1,0:T(8,128)(2,1)}) custom-call(s32[1]{0:T(128)} %bitcast.where_ref, f32[7,8,128]{2,1,0:T(8,128)} %get-tuple-element.32.stencil_ref, f32[2048,1024]{1,0:T(8,128)} %p_ref.7, bf16[1024,384]{1,0:T(8,128)(2,1)} %copy-done, ...), custom_call_target="tpu_custom_call" | custom-call | flops 1 | bytes 1 | tf_op jit(solution)/shard_map/columns_operator/pallas_call | solution.py:233
  76.8 4.3 %collective-permute-start.8 = (bf16[384,1024]{1,0:T(8,128)(2,1)}, bf16[384,1024]{1,0:T(8,128)(2,1)}, u32[]{:S(2)}, u32[]{:S(2)}) collective-permute-start(bf16[384,1024]{1,0:T(8,128)(2,1)} %get-tuple-element.47), channel_id=1, source_target_pairs={{0,8},{8,16},{16,24},{1,9},{9,17},{17,25},{2,10},{10,18},{18,26},{... | collective-permute-start | bytes 2359304 | tf_op jit(solution)/shard_map/ppermute | solution.py:366
  81.0 0.0 collective-permute-done.6.left_ref
  81.0 2.1 %collective-permute-start.9 = (bf16[384,1024]{1,0:T(8,128)(2,1)}, bf16[384,1024]{1,0:T(8,128)(2,1)}, u32[]{:S(2)}, u32[]{:S(2)}) collective-permute-start(bf16[384,1024]{1,0:T(8,128)(2,1)} %get-tuple-element.48), channel_id=1, source_target_pairs={{8,0},{16,8},{24,16},{9,1},{17,9},{25,17},{10,2},{18,10},{26,18},{... | collective-permute-start | bytes 2359304 | tf_op jit(solution)/shard_map/ppermute | solution.py:366
  83.2 0.0 collective-permute-done.7.right_ref
  83.2 6.0 %columns_operator.4.rest_0_ = bf16[2048,1024]{1,0:T(8,128)(2,1)} custom-call(s32[1]{0:T(128)} %bitcast.where_ref, f32[7,8,128]{2,1,0:T(8,128)} %get-tuple-element.32.stencil_ref, f32[2048,1024]{1,0:T(8,128)} %p_ref.7, bf16[512,384]{1,0:T(8,128)(2,1)} %collective-permute-done.6.left_ref, ...), custom_call_target="tpu_custom_call", output_to_operand_aliasing={{}: (5, {})} | custom-call | flops 1 | bytes 1 | tf_op jit(solution)/shard_map/columns_operator/pallas_call | solution.py:233
  89.2 0.0 collective-permute-done.5.right_ref
  89.2 0.0 collective-permute-done.4.left_ref
  89.2 6.0 %columns_operator.5.x_ref = bf16[2048,1024]{1,0:T(8,128)(2,1)} custom-call(s32[1]{0:T(128)} %bitcast.4.where_ref, f32[7,8,128]{2,1,0:T(8,128)} %get-tuple-element.32.stencil_ref, f32[2048,1024]{1,0:T(8,128)} %p_ref.7, bf16[512,384]{1,0:T(8,128)(2,1)} %collective-permute-done.4.left_ref, ...), custom_call_target="tpu_custom_call", output_to_operand_aliasing={{}: (5, {})} | custom-call | flops 9999999827968 | bytes 9999999827968 | tf_op jit(solution)/shard_map/columns_operator/pallas_call | solution.py:233
  95.1 0.0 collective-permute-done.8.top_ref
  95.1 0.0 collective-permute-done.9.bottom_ref
  95.1 13.3 %rows_operator.3 = f32[2048,1024]{1,0:T(8,128)} custom-call(f32[7,16,128]{2,1,0:T(8,128)} %get-tuple-element.31.stencil_ref, bf16[2048,1024]{1,0:T(8,128)(2,1)} %columns_operator.5.x_ref, bf16[384,1024]{1,0:T(8,128)(2,1)} %collective-permute-done.8.top_ref, bf16[384,1024]{1,0:T(8,128)(2,1)} %collective-permute-done.9.bottom_ref, s32[1]{0:T(128)} %bitcast.5.rest_0_, ...), custom_call_target="tpu_custom_call" | custom-call | flops 1 | bytes 1 | tf_op jit(solution)/shard_map/rows_operator/pallas_call | solution.py:348
Async XLA Ops:
  1.2 17.6 %copy-start.2 = (f32[16,2]{0,1:T(2,128)S(1)}, f32[16,2]{0,1:T(2,128)}, u32[]{:S(2)}) copy-start(f32[16,2]{0,1:T(2,128)} %param.7) | copy-start | bytes 388
  1.2 26.9 %copy-start.1 = (s32[3,64]{1,0:T(4,128)S(1)}, s32[3,64]{1,0:T(4,128)}, u32[]{:S(2)}) copy-start(s32[3,64]{1,0:T(4,128)} %param.9) | copy-start | bytes 2308
  7.8 13.7 %collective-permute-start = (bf16[384,1024]{1,0:T(8,128)(2,1)}, bf16[384,1024]{1,0:T(8,128)(2,1)}, u32[]{:S(2)}, u32[]{:S(2)}) collective-permute-start(bf16[384,1024]{1,0:T(8,128)(2,1)} %get-tuple-element.29), channel_id=1, source_target_pairs={{0,8},{8,16},{16,24},{1,9},{9,17},{17,25},{2,10},{10,18},{18,26},{... | collective-permute-start | bytes 2359304 | tf_op jit(solution)/shard_map/ppermute | solution.py:366
  12.4 19.0 %collective-permute-start.1 = (bf16[384,1024]{1,0:T(8,128)(2,1)}, bf16[384,1024]{1,0:T(8,128)(2,1)}, u32[]{:S(2)}, u32[]{:S(2)}) collective-permute-start(bf16[384,1024]{1,0:T(8,128)(2,1)} %get-tuple-element.34), channel_id=1, source_target_pairs={{8,0},{16,8},{24,16},{9,1},{17,9},{25,17},{10,2},{18,10},{26,18},{... | collective-permute-start | bytes 2359304 | tf_op jit(solution)/shard_map/ppermute | solution.py:366
  14.3 45.6 %collective-permute-start.2 = (bf16[1024,384]{1,0:T(8,128)(2,1)}, bf16[1024,384]{1,0:T(8,128)(2,1)S(1)}, u32[]{:S(2)}, u32[]{:S(2)}) collective-permute-start(bf16[1024,384]{1,0:T(8,128)(2,1)} %get-tuple-element.35), channel_id=1, source_target_pairs={{0,1},{1,2},{2,3},{3,4},{4,5},{5,6},{6,7},{8,9},{9,10},{10,11},{11... | collective-permute-start | bytes 2359304 | tf_op jit(solution)/shard_map/ppermute | solution.py:366
  17.5 42.4 %collective-permute-start.3 = (bf16[1024,384]{1,0:T(8,128)(2,1)}, bf16[1024,384]{1,0:T(8,128)(2,1)}, u32[]{:S(2)}, u32[]{:S(2)}) collective-permute-start(bf16[1024,384]{1,0:T(8,128)(2,1)} %get-tuple-element.36), channel_id=1, source_target_pairs={{1,0},{2,1},{3,2},{4,3},{5,4},{6,5},{7,6},{9,8},{10,9},{11,10},{12... | collective-permute-start | bytes 2359304 | tf_op jit(solution)/shard_map/ppermute | solution.py:366
  21.6 67.6 %collective-permute-start.5 = (bf16[512,384]{1,0:T(8,128)(2,1)}, bf16[512,384]{1,0:T(8,128)(2,1)}, u32[]{:S(2)}, u32[]{:S(2)}) collective-permute-start(bf16[512,384]{1,0:T(8,128)(2,1)} %get-tuple-element.39), channel_id=1, source_target_pairs={{1,0},{2,1},{3,2},{4,3},{5,4},{6,5},{7,6},{9,8},{10,9},{11,10},{12... | collective-permute-start | bytes 1179656 | tf_op jit(solution)/shard_map/ppermute | solution.py:366
  22.9 58.2 %collective-permute-start.6 = (bf16[512,384]{1,0:T(8,128)(2,1)}, bf16[512,384]{1,0:T(8,128)(2,1)}, u32[]{:S(2)}, u32[]{:S(2)}) collective-permute-start(bf16[512,384]{1,0:T(8,128)(2,1)} %get-tuple-element.43), channel_id=1, source_target_pairs={{0,2},{1,1},{2,10},{3,9},{4,18},{5,17},{6,26},{7,25},{8,4},{9,3},{... | collective-permute-start | bytes 1179656 | tf_op jit(solution)/shard_map/ppermute | solution.py:431
  31.4 51.8 %collective-permute-start.7 = (bf16[512,384]{1,0:T(8,128)(2,1)}, bf16[512,384]{1,0:T(8,128)(2,1)}, u32[]{:S(2)}, u32[]{:S(2)}) collective-permute-start(bf16[512,384]{1,0:T(8,128)(2,1)} %get-tuple-element.45), channel_id=1, source_target_pairs={{0,0},{2,8},{4,16},{6,24},{8,2},{9,1},{10,10},{11,9},{12,18},{13,1... | collective-permute-start | bytes 1179656 | tf_op jit(solution)/shard_map/ppermute | solution.py:432
  59.9 4.5 %copy-start = (bf16[1024,384]{1,0:T(8,128)(2,1)}, bf16[1024,384]{1,0:T(8,128)(2,1)S(1)}, u32[]{:S(2)}) copy-start(bf16[1024,384]{1,0:T(8,128)(2,1)S(1)} %collective-permute-done.2.left_ref) | copy-start | bytes 2359300
  59.9 29.3 %collective-permute-start.4 = (bf16[512,384]{1,0:T(8,128)(2,1)}, bf16[512,384]{1,0:T(8,128)(2,1)}, u32[]{:S(2)}, u32[]{:S(2)}) collective-permute-start(bf16[512,384]{1,0:T(8,128)(2,1)} %get-tuple-element.38), channel_id=1, source_target_pairs={{0,1},{1,2},{2,3},{3,4},{4,5},{5,6},{6,7},{8,9},{9,10},{10,11},{11... | collective-permute-start | bytes 1179656 | tf_op jit(solution)/shard_map/ppermute | solution.py:366
  76.8 18.4 %collective-permute-start.8 = (bf16[384,1024]{1,0:T(8,128)(2,1)}, bf16[384,1024]{1,0:T(8,128)(2,1)}, u32[]{:S(2)}, u32[]{:S(2)}) collective-permute-start(bf16[384,1024]{1,0:T(8,128)(2,1)} %get-tuple-element.47), channel_id=1, source_target_pairs={{0,8},{8,16},{16,24},{1,9},{9,17},{17,25},{2,10},{10,18},{18,26},{... | collective-permute-start | bytes 2359304 | tf_op jit(solution)/shard_map/ppermute | solution.py:366
  81.0 14.1 %collective-permute-start.9 = (bf16[384,1024]{1,0:T(8,128)(2,1)}, bf16[384,1024]{1,0:T(8,128)(2,1)}, u32[]{:S(2)}, u32[]{:S(2)}) collective-permute-start(bf16[384,1024]{1,0:T(8,128)(2,1)} %get-tuple-element.48), channel_id=1, source_target_pairs={{8,0},{16,8},{24,16},{9,1},{17,9},{25,17},{10,2},{18,10},{26,18},{... | collective-permute-start | bytes 2359304 | tf_op jit(solution)/shard_map/ppermute | solution.py:366

commit v2 on v1

--- a/solution.py
+++ b/solution.py
@@ -160,7 +160,7 @@
 
 
 def columns_operator(
-    covariance, left, right, stencil, where, unit, steps, nlon, count, block_at, held=None, work=1
+    covariance, left, right, stencil, where, unit, steps, nlon, count, block_at, held=None, ends=False, work=1
 ):
     rows, cols = covariance.shape
     lats = cols // nlon
@@ -170,7 +170,7 @@
     pairs = lats // 2
 
     def kernel(where_ref, stencil_ref, p_ref, left_ref, right_ref, *rest):
-        outs, (data_ref, b_high, b_low) = rest[:-3], rest[-3:]
+        outs, (data_ref, b_ref) = rest[:-2], rest[-2:]
         if held is not None:
             outs = outs[1:]
         t_ref = outs[0]
@@ -185,25 +185,24 @@
                     for k in range(2 * steps):
                         d = k - (steps - 1) - a
                         high, low = split(circulant(stencil_ref[d + steps, 2 * q + a : 2 * q + a + 1, :]))
-                        at = pl.ds(q * span + k * nlon, nlon)
-                        b_high[at, a * nlon : (a + 1) * nlon] = high
-                        b_low[at, a * nlon : (a + 1) * nlon] = low
+                        for part, value in enumerate((high, high, low)):
+                            at = pl.ds((3 * q + part) * span + k * nlon, nlon)
+                            b_ref[at, a * nlon : (a + 1) * nlon] = value
 
         data_ref[:size, :wide] = left_ref[...]
         data_ref[:size, wide + cols :] = right_ref[...]
         data_ref[:size, wide : wide + cols], data_ref[size:, wide : wide + cols] = split(p_ref[...])
         for q in range(pairs):
             window = slice((2 * q + 1) * nlon, (2 * q + 1) * nlon + span)
-            of = pl.ds(q * span, span)
-            both = product(data_ref[:, window], b_high[of, :])
-            total = both[:size] + both[size:] + product(data_ref[:size, window], b_low[of, :])
+            high, low = data_ref[:size, window], data_ref[size:, window]
+            total = product(jnp.concatenate([high, low, high], axis=1), b_ref[pl.ds(3 * q * span, 3 * span), :])
             for a, k, d in ((0, 2 * q, -steps), (1, 2 * q + 2 * steps + 1, steps)):
                 far = slice(k * nlon, (k + 1) * nlon)
                 weight = jnp.sum(stencil_ref[d + steps, 2 * q + a : 2 * q + a + 1, :], axis=1, keepdims=True)
                 far_values = data_ref[:size, far].astype(F32) + data_ref[size:, far].astype(F32)
                 value = total[:, a * nlon : (a + 1) * nlon] + weight * far_values
                 t_ref[:, (2 * q + a) * nlon : (2 * q + a + 1) * nlon] = value.astype(BF16)
-        if held is None:
+        if ends:
 
             @pl.when(i == 0)
             def _():
@@ -223,10 +222,10 @@
     out_shape = [jax.ShapeDtypeStruct((rows, cols), BF16)]
     operands = [where, stencil, covariance, left, right]
     aliases = {}
-    if held is None:
+    if ends:
         out_specs += [pl.BlockSpec((wide, cols), lambda i, at: (0, 0))] * 2
         out_shape += [jax.ShapeDtypeStruct((wide, cols), BF16)] * 2
-    else:
+    if held is not None:
         in_specs.append(pl.BlockSpec(memory_space=pl.ANY))
         operands.append(held)
         aliases = {5: 0}
@@ -238,7 +237,7 @@
             in_specs=in_specs,
             out_specs=out_specs,
             scratch_shapes=[pltpu.VMEM((2 * size, cols + 2 * wide), BF16)]
-            + [pltpu.VMEM((pairs * span, size), BF16)] * 2,
+            + [pltpu.VMEM((3 * pairs * span, 2 * nlon), BF16)],
         ),
         out_shape=out_shape,
         input_output_aliases=aliases,
@@ -257,7 +256,7 @@
     pairs = lat_rows // 2
     ahead = min((steps + 1) // 2, pairs - 1)
     exact = values.dtype == BF16
-    chunk = min(cols, 256)
+    chunk = min(cols, 512)
 
     def kernel(stencil_ref, x_ref, top_ref, bottom_ref, *rest):
         extra, rest = (rest[:2], rest[2:]) if noise is not None else ((), rest)
@@ -304,16 +303,17 @@
         for a in range(2):
             for k in range(2 * steps):
                 high, low = split(circulant(row(k - (steps - 1) - a, a)))
-                a_ref[a * nlon : (a + 1) * nlon, k * nlon : (k + 1) * nlon] = high
-                a_ref[size + a * nlon : size + (a + 1) * nlon, k * nlon : (k + 1) * nlon] = low
+                for part, value in enumerate((high, low) if exact else (high, low, high)):
+                    lane = part * span + k * nlon
+                    a_ref[a * nlon : (a + 1) * nlon, lane : lane + nlon] = value
         unit = lambda k: pl.multiple_of((2 * p + k) * nlon, nlon)
         for lane in range(0, cols, chunk):
             lanes = slice(lane, lane + chunk)
             window = high_ref[pl.ds(unit(1), span), lanes]
-            both = product(a_ref[...], window)
-            total = both[:size] + both[size:]
+            parts = [window, window]
             if not exact:
-                total += product(a_ref[:size, :], low_ref[pl.ds(unit(1), span), lanes])
+                parts.append(low_ref[pl.ds(unit(1), span), lanes])
+            total = product(a_ref[...], jnp.concatenate(parts, axis=0))
             for a, k, d in ((0, 0, -steps), (1, 2 * steps + 1, steps)):
                 far = high_ref[pl.ds(unit(k), nlon), lanes].astype(F32)
                 if not exact:
@@ -351,7 +351,7 @@
         in_specs=in_specs,
         out_specs=pl.BlockSpec((size, cols), lambda g: (g, 0)),
         out_shape=jax.ShapeDtypeStruct((rows, cols), out_dtype),
-        scratch_shapes=[pltpu.VMEM((2 * size, span), BF16)]
+        scratch_shapes=[pltpu.VMEM((size, (2 if exact else 3) * span), BF16)]
         + [pltpu.VMEM((rows + 2 * wide, cols), BF16), pltpu.SemaphoreType.DMA((pairs + 2,))]
         + ([] if exact else [pltpu.VMEM((rows, cols), F32), pltpu.VMEM((rows + 2 * wide, cols), BF16)]),
         compiler_params=params(),
@@ -425,34 +425,34 @@
     right = shifted(first, "col", -1)
     p_top = shifted(bottom, "row", 1)
     p_bottom = shifted(top, "row", -1)
-    left_m, right_m, first_inner, wind_index, p_top = lax.optimization_barrier(
-        (left_m, right_m, first_inner, wind_index, p_top)
-    )
+    left_m, right_m, wind_index, p_top = lax.optimization_barrier((left_m, right_m, wind_index, p_top))
     left_m = lax.ppermute(left_m, ("row", "col"), mirror_pairs(n_row, n_col, 1))
     right_m = lax.ppermute(right_m, ("row", "col"), mirror_pairs(n_row, n_col, -1))
-    right_inner = shifted(first_inner, "col", -1)
 
     row_s, col_s = stencil_rows(
         wind_table, diffusivity, wind_index, row_id * lat_rows, col_id * lats, lat_rows, lats, nlon
     )
 
     operator_times_prior = rows_operator(covariance, p_top, p_bottom, row_s, steps, nlon, BF16)
-    operator_times_prior, left, right, last_inner = lax.optimization_barrier(
-        (operator_times_prior, left, right, last_inner)
-    )
-    left_inner = shifted(last_inner, "col", 1)
-    mirror, t_first, t_last = columns_operator(
-        covariance, left, right, col_s, mirror_at, near, steps, nlon, 2, lambda i, at: i * (lat_rows // near - 1)
-    )
-    t_top = shifted(t_last, "row", 1)
-    t_first, left_m = lax.optimization_barrier((t_first, left_m))
-    t_bottom = shifted(t_first, "row", -1)
+    operator_times_prior, left_m = lax.optimization_barrier((operator_times_prior, left_m))
     inner_at = lambda i, at: at[0] // own + i
     (mirror,) = columns_operator(
-        covariance, left_m, right_m, col_s, mirror_at, own, steps, nlon, 1, inner_at, mirror
-    )
+        covariance, left_m, right_m, col_s, mirror_at, own, steps, nlon, 1, inner_at
+    )
+    mirror, left, right, first_inner, last_inner = lax.optimization_barrier(
+        (mirror, left, right, first_inner, last_inner)
+    )
+    left_inner = shifted(last_inner, "col", 1)
+    right_inner = shifted(first_inner, "col", -1)
+    mirror, t_first, t_last = columns_operator(
+        covariance, left, right, col_s, mirror_at, near, steps, nlon, 2,
+        lambda i, at: i * (lat_rows // near - 1), mirror, True,
+    )
+    t_top = shifted(t_last, "row", 1)
+    t_bottom = shifted(t_first, "row", -1)
     (mirror,) = columns_operator(
-        covariance, left_inner, right_inner, col_s, direct_at, own, steps, nlon, 1, inner_at, mirror, 10 ** 13
+        covariance, left_inner, right_inner, col_s, direct_at, own, steps, nlon, 1, inner_at, mirror, False,
+        10 ** 13,
     )
     diagonal = (col_id * lats - row_id * lat_rows).astype(jnp.int32).reshape(1)
     predicted_spread_matrix = rows_operator(

time: 109 us -> 121 us (1.11)
  the two profiles are of different devices: /device:TPU:1 before, /device:TPU:5 now
where the time goes in v2:
time: 121 us; the launch traced here: 120 us
  Pallas kernels  65.4 us (54%)
  starting transfers between devices  43.2 us (36%)
  waiting for transfers between devices  7.3 us (6%)
  local copies, waits for them, and re-layouts  2.19 us (2%)
    ppermute x8, starting transfers between devices, shifted(): return lax.ppermute(block, axis, pairs)  39.2 us
    pallas_call x2, Pallas kernels, rows_operator(): pl.pallas_call(kernel, grid=(pairs,), in_specs=in_specs, out_specs=pl.Blo...  32.3 us
    pallas_call x3, Pallas kernels, columns_operator(): pl.pallas_call(kernel, grid_spec=pltpu.PrefetchScalarGridSpec(num_scalar_...  24.7 us
    ppermute x8, waiting for transfers between devices, shifted(): return lax.ppermute(block, axis, pairs)  7.3 us
    pallas_call x1, Pallas kernels, packed(): pl.pallas_call(kernel, in_specs=[pl.BlockSpec(memory_space=pltpu.SMEM), p...  6.62 us
  transfers between devices with their start and end apart: 10, of which 3 were waited for; matrix products, arithmetic and copies ran while one was open for 2% of the time, Pallas kernels for 37%

profile of v2, /device:TPU:5, one launch (start us, length us, event | category | flops | bytes accessed | tf_op | source)
XLA Modules:
  0.0 119.8 jit_solution(18393226576005572255)
XLA Ops:
  0.6 0.7 add_multiply_fusion.where_ref
  1.3 0.0 copy-start.2
  1.3 0.0 copy-start.1
  1.3 6.6 %packed.1 = (bf16[1024,384]{1,0:T(8,128)(2,1)}, bf16[1024,384]{1,0:T(8,128)(2,1)}, bf16[384,1024]{1,0:T(8,128)(2,1)}, bf16[384,1024]{1,0:T(8,128)(2,1)}, bf16[51...) custom-call(s32[4]{0:T(128)} %add_multiply_fusion.where_ref, ...), custom_call_target="tpu_custom_call" | custom-call | flops 1 | bytes 1 | tf_op jit(solution)/shard_map/packed/pallas_call | solution.py:148
  7.9 3.7 %collective-permute-start = (bf16[384,1024]{1,0:T(8,128)(2,1)}, bf16[384,1024]{1,0:T(8,128)(2,1)}, u32[]{:S(2)}, u32[]{:S(2)}) collective-permute-start(bf16[384,1024]{1,0:T(8,128)(2,1)} %get-tuple-element.28), channel_id=1, source_target_pairs={{0,8},{8,16},{16,24},{1,9},{9,17},{17,25},{2,10},{10,18},{18,26},{... | collective-permute-start | bytes 2359304 | tf_op jit(solution)/shard_map/ppermute | solution.py:366
  11.6 1.9 %collective-permute-start.1 = (bf16[384,1024]{1,0:T(8,128)(2,1)}, bf16[384,1024]{1,0:T(8,128)(2,1)}, u32[]{:S(2)}, u32[]{:S(2)}) collective-permute-start(bf16[384,1024]{1,0:T(8,128)(2,1)} %get-tuple-element.33), channel_id=1, source_target_pairs={{8,0},{16,8},{24,16},{9,1},{17,9},{25,17},{10,2},{18,10},{26,18},{... | collective-permute-start | bytes 2359304 | tf_op jit(solution)/shard_map/ppermute | solution.py:366
  13.6 3.1 %collective-permute-start.4 = (bf16[1024,384]{1,0:T(8,128)(2,1)}, bf16[1024,384]{1,0:T(8,128)(2,1)S(1)}, u32[]{:S(2)}, u32[]{:S(2)}) collective-permute-start(bf16[1024,384]{1,0:T(8,128)(2,1)} %get-tuple-element.37), channel_id=1, source_target_pairs={{0,1},{1,2},{2,3},{3,4},{4,5},{5,6},{6,7},{8,9},{9,10},{10,11},{11... | collective-permute-start | bytes 2359304 | tf_op jit(solution)/shard_map/ppermute | solution.py:366
  16.7 2.2 %collective-permute-start.5 = (bf16[1024,384]{1,0:T(8,128)(2,1)}, bf16[1024,384]{1,0:T(8,128)(2,1)}, u32[]{:S(2)}, u32[]{:S(2)}) collective-permute-start(bf16[1024,384]{1,0:T(8,128)(2,1)} %get-tuple-element.38), channel_id=1, source_target_pairs={{1,0},{2,1},{3,2},{4,3},{5,4},{6,5},{7,6},{9,8},{10,9},{11,10},{12... | collective-permute-start | bytes 2359304 | tf_op jit(solution)/shard_map/ppermute | solution.py:366
  18.9 2.0 %collective-permute-done.top_ref = bf16[384,1024]{1,0:T(8,128)(2,1)} collective-permute-done((bf16[384,1024]{1,0:T(8,128)(2,1)}, bf16[384,1024]{1,0:T(8,128)(2,1)}, u32[]{:S(2)}, u32[]{:S(2)}) %collective-permute-start) | collective-permute-done | bytes 786464 | tf_op jit(solution)/shard_map/ppermute | solution.py:366
  20.9 1.9 %collective-permute-start.2 = (bf16[512,384]{1,0:T(8,128)(2,1)}, bf16[512,384]{1,0:T(8,128)(2,1)}, u32[]{:S(2)}, u32[]{:S(2)}) collective-permute-start(bf16[512,384]{1,0:T(8,128)(2,1)} %get-tuple-element.34), channel_id=1, source_target_pairs={{0,2},{1,1},{2,10},{3,9},{4,18},{5,17},{6,26},{7,25},{8,4},{9,3},{... | collective-permute-start | bytes 1179656 | tf_op jit(solution)/shard_map/ppermute | solution.py:429
  22.8 2.1 %collective-permute-start.3 = (bf16[512,384]{1,0:T(8,128)(2,1)}, bf16[512,384]{1,0:T(8,128)(2,1)}, u32[]{:S(2)}, u32[]{:S(2)}) collective-permute-start(bf16[512,384]{1,0:T(8,128)(2,1)} %get-tuple-element.36), channel_id=1, source_target_pairs={{0,0},{2,8},{4,16},{6,24},{8,2},{9,1},{10,10},{11,9},{12,18},{13,1... | collective-permute-start | bytes 1179656 | tf_op jit(solution)/shard_map/ppermute | solution.py:430
  24.9 0.0 copy-done.2
  24.9 0.1 copy.10
  25.0 0.6 reshape.16.table_ref
  25.5 0.0 copy-done.1
  25.5 0.1 pad_dynamic-slice_fusion
  25.6 0.1 pad_dynamic-slice_fusion.1
  25.7 0.7 broadcast_in_dim.5.col_ref
  26.4 0.7 broadcast_in_dim.4.row_ref
  27.1 1.7 %stencil_rows.1 = (f32[7,16,128]{2,1,0:T(8,128)}, f32[7,8,128]{2,1,0:T(8,128)}) custom-call(f32[32]{0:T(128)} %reshape.16.table_ref, f32[16]{0:T(128)} %diffuse_ref.1, s32[3,22,128]{2,1,0:T(8,128)} %broadcast_in_dim.4.row_ref, s32[3,14,128]{2,1,0:T(8,128)} %broadcast_in_dim.5.col_ref), custom_call_target="tpu_custom_call" | custom-call | flops 1 | bytes 1 | tf_op jit(solution)/shard_map/stencil_rows/pallas_call | solution.py:98
  28.8 0.0 collective-permute-done.1.bottom_ref
  28.8 18.3 %rows_operator.2 = bf16[2048,1024]{1,0:T(8,128)(2,1)} custom-call(f32[7,16,128]{2,1,0:T(8,128)} %get-tuple-element.30.stencil_ref, f32[2048,1024]{1,0:T(8,128)} %p_ref.7, bf16[384,1024]{1,0:T(8,128)(2,1)} %collective-permute-done.top_ref, bf16[384,1024]{1,0:T(8,128)(2,1)} %collective-permute-done.1.bottom_ref), custom_call_target="tpu_custom_call" | custom-call | flops 1 | bytes 1 | tf_op jit(solution)/shard_map/rows_operator/pallas_call | solution.py:348
  47.1 0.0 collective-permute-done.2.left_ref
  47.1 0.0 collective-permute-done.3.right_ref
  47.2 6.1 %columns_operator.3.rest_0_ = bf16[2048,1024]{1,0:T(8,128)(2,1)} custom-call(s32[1]{0:T(128)} %bitcast.where_ref, f32[7,8,128]{2,1,0:T(8,128)} %get-tuple-element.31.stencil_ref, f32[2048,1024]{1,0:T(8,128)} %p_ref.7, bf16[512,384]{1,0:T(8,128)(2,1)} %collective-permute-done.2.left_ref, bf16[512,384]{1,0:T(8,128)(2,1)} %collective-permute-done.3.right_ref), custom_call_target="tpu_custom_call" | custom-call | flops 1 | bytes 1 | tf_op jit(solution)/shard_map/columns_operator/pallas_call | solution.py:232
  53.3 0.0 collective-permute-done.4.left_ref
  53.3 0.0 copy-start
  53.3 0.0 collective-permute-done.5.right_ref
  53.3 6.9 %collective-permute-start.6 = (bf16[512,384]{1,0:T(8,128)(2,1)}, bf16[512,384]{1,0:T(8,128)(2,1)}, u32[]{:S(2)}, u32[]{:S(2)}) collective-permute-start(bf16[512,384]{1,0:T(8,128)(2,1)} %get-tuple-element.41), channel_id=1, source_target_pairs={{0,1},{1,2},{2,3},{3,4},{4,5},{5,6},{6,7},{8,9},{9,10},{10,11},{11... | collective-permute-start | bytes 1179656 | tf_op jit(solution)/shard_map/ppermute | solution.py:366
  60.2 1.9 %collective-permute-start.7 = (bf16[512,384]{1,0:T(8,128)(2,1)}, bf16[512,384]{1,0:T(8,128)(2,1)}, u32[]{:S(2)}, u32[]{:S(2)}) collective-permute-start(bf16[512,384]{1,0:T(8,128)(2,1)} %get-tuple-element.42), channel_id=1, source_target_pairs={{1,0},{2,1},{3,2},{4,3},{5,4},{6,5},{7,6},{9,8},{10,9},{11,10},{12... | collective-permute-start | bytes 1179656 | tf_op jit(solution)/shard_map/ppermute | solution.py:366
  62.1 0.0 copy-done
  62.1 12.4 %columns_operator.4 = (bf16[2048,1024]{1,0:T(8,128)(2,1)}, bf16[384,1024]{1,0:T(8,128)(2,1)}, bf16[384,1024]{1,0:T(8,128)(2,1)}) custom-call(s32[1]{0:T(128)} %bitcast.where_ref, f32[7,8,128]{2,1,0:T(8,128)} %get-tuple-element.31.stencil_ref, f32[2048,1024]{1,0:T(8,128)} %p_ref.7, bf16[1024,384]{1,0:T(8,128)(2,1)} %copy-done, ...), custom_call_target="tpu_custom_call", output_to_operand_aliasing={{0}: (5, {})} | custom-call | flops 1 | bytes 1 | tf_op jit(solution)/shard_map/columns_operator/pallas_call | solution.py:232
  74.5 17.4 %collective-permute-start.8 = (bf16[384,1024]{1,0:T(8,128)(2,1)}, bf16[384,1024]{1,0:T(8,128)(2,1)}, u32[]{:S(2)}, u32[]{:S(2)}) collective-permute-start(bf16[384,1024]{1,0:T(8,128)(2,1)} %get-tuple-element.47), channel_id=1, source_target_pairs={{0,8},{8,16},{16,24},{1,9},{9,17},{17,25},{2,10},{10,18},{18,26},{... | collective-permute-start | bytes 2359304 | tf_op jit(solution)/shard_map/ppermute | solution.py:366
  92.0 2.1 %collective-permute-start.9 = (bf16[384,1024]{1,0:T(8,128)(2,1)}, bf16[384,1024]{1,0:T(8,128)(2,1)}, u32[]{:S(2)}, u32[]{:S(2)}) collective-permute-start(bf16[384,1024]{1,0:T(8,128)(2,1)} %get-tuple-element.48), channel_id=1, source_target_pairs={{8,0},{16,8},{24,16},{9,1},{17,9},{25,17},{10,2},{18,10},{26,18},{... | collective-permute-start | bytes 2359304 | tf_op jit(solution)/shard_map/ppermute | solution.py:366
  94.1 0.0 collective-permute-done.6.left_ref
  94.1 0.0 collective-permute-done.7.right_ref
  94.1 6.2 %columns_operator.5.x_ref = bf16[2048,1024]{1,0:T(8,128)(2,1)} custom-call(s32[1]{0:T(128)} %bitcast.4.where_ref, f32[7,8,128]{2,1,0:T(8,128)} %get-tuple-element.31.stencil_ref, f32[2048,1024]{1,0:T(8,128)} %p_ref.7, bf16[512,384]{1,0:T(8,128)(2,1)} %collective-permute-done.6.left_ref, ...), custom_call_target="tpu_custom_call", output_to_operand_aliasing={{}: (5, {})} | custom-call | flops 9999999827968 | bytes 9999999827968 | tf_op jit(solution)/shard_map/columns_operator/pallas_call | solution.py:232
  100.2 0.9 collective-permute-done.8.top_ref
  101.2 4.4 %collective-permute-done.9.bottom_ref = bf16[384,1024]{1,0:T(8,128)(2,1)} collective-permute-done((bf16[384,1024]{1,0:T(8,128)(2,1)}, bf16[384,1024]{1,0:T(8,128)(2,1)}, u32[]{:S(2)}, u32[]{:S(2)}) %collective-permute-start.9) | collective-permute-done | bytes 786464 | tf_op jit(solution)/shard_map/ppermute | solution.py:366
  105.6 14.0 %rows_operator.3 = f32[2048,1024]{1,0:T(8,128)} custom-call(f32[7,16,128]{2,1,0:T(8,128)} %get-tuple-element.30.stencil_ref, bf16[2048,1024]{1,0:T(8,128)(2,1)} %columns_operator.5.x_ref, bf16[384,1024]{1,0:T(8,128)(2,1)} %collective-permute-done.8.top_ref, bf16[384,1024]{1,0:T(8,128)(2,1)} %collective-permute-done.9.bottom_ref, s32[1]{0:T(128)} %bitcast.5.rest_0_, ...), custom_call_target="tpu_custom_call" | custom-call | flops 1 | bytes 1 | tf_op jit(solution)/shard_map/rows_operator/pallas_call | solution.py:348
Async XLA Ops:
  1.3 23.6 %copy-start.2 = (f32[16,2]{0,1:T(2,128)S(1)}, f32[16,2]{0,1:T(2,128)}, u32[]{:S(2)}) copy-start(f32[16,2]{0,1:T(2,128)} %param.7) | copy-start | bytes 388
  1.3 24.2 %copy-start.1 = (s32[3,64]{1,0:T(4,128)S(1)}, s32[3,64]{1,0:T(4,128)}, u32[]{:S(2)}) copy-start(s32[3,64]{1,0:T(4,128)} %param.9) | copy-start | bytes 2308
  7.9 12.9 %collective-permute-start = (bf16[384,1024]{1,0:T(8,128)(2,1)}, bf16[384,1024]{1,0:T(8,128)(2,1)}, u32[]{:S(2)}, u32[]{:S(2)}) collective-permute-start(bf16[384,1024]{1,0:T(8,128)(2,1)} %get-tuple-element.28), channel_id=1, source_target_pairs={{0,8},{8,16},{16,24},{1,9},{9,17},{17,25},{2,10},{10,18},{18,26},{... | collective-permute-start | bytes 2359304 | tf_op jit(solution)/shard_map/ppermute | solution.py:366
  11.6 17.2 %collective-permute-start.1 = (bf16[384,1024]{1,0:T(8,128)(2,1)}, bf16[384,1024]{1,0:T(8,128)(2,1)}, u32[]{:S(2)}, u32[]{:S(2)}) collective-permute-start(bf16[384,1024]{1,0:T(8,128)(2,1)} %get-tuple-element.33), channel_id=1, source_target_pairs={{8,0},{16,8},{24,16},{9,1},{17,9},{25,17},{10,2},{18,10},{26,18},{... | collective-permute-start | bytes 2359304 | tf_op jit(solution)/shard_map/ppermute | solution.py:366
  13.6 39.7 %collective-permute-start.4 = (bf16[1024,384]{1,0:T(8,128)(2,1)}, bf16[1024,384]{1,0:T(8,128)(2,1)S(1)}, u32[]{:S(2)}, u32[]{:S(2)}) collective-permute-start(bf16[1024,384]{1,0:T(8,128)(2,1)} %get-tuple-element.37), channel_id=1, source_target_pairs={{0,1},{1,2},{2,3},{3,4},{4,5},{5,6},{6,7},{8,9},{9,10},{10,11},{11... | collective-permute-start | bytes 2359304 | tf_op jit(solution)/shard_map/ppermute | solution.py:366
  16.7 36.6 %collective-permute-start.5 = (bf16[1024,384]{1,0:T(8,128)(2,1)}, bf16[1024,384]{1,0:T(8,128)(2,1)}, u32[]{:S(2)}, u32[]{:S(2)}) collective-permute-start(bf16[1024,384]{1,0:T(8,128)(2,1)} %get-tuple-element.38), channel_id=1, source_target_pairs={{1,0},{2,1},{3,2},{4,3},{5,4},{6,5},{7,6},{9,8},{10,9},{11,10},{12... | collective-permute-start | bytes 2359304 | tf_op jit(solution)/shard_map/ppermute | solution.py:366
  20.9 26.3 %collective-permute-start.2 = (bf16[512,384]{1,0:T(8,128)(2,1)}, bf16[512,384]{1,0:T(8,128)(2,1)}, u32[]{:S(2)}, u32[]{:S(2)}) collective-permute-start(bf16[512,384]{1,0:T(8,128)(2,1)} %get-tuple-element.34), channel_id=1, source_target_pairs={{0,2},{1,1},{2,10},{3,9},{4,18},{5,17},{6,26},{7,25},{8,4},{9,3},{... | collective-permute-start | bytes 1179656 | tf_op jit(solution)/shard_map/ppermute | solution.py:429
  22.8 24.4 %collective-permute-start.3 = (bf16[512,384]{1,0:T(8,128)(2,1)}, bf16[512,384]{1,0:T(8,128)(2,1)}, u32[]{:S(2)}, u32[]{:S(2)}) collective-permute-start(bf16[512,384]{1,0:T(8,128)(2,1)} %get-tuple-element.36), channel_id=1, source_target_pairs={{0,0},{2,8},{4,16},{6,24},{8,2},{9,1},{10,10},{11,9},{12,18},{13,1... | collective-permute-start | bytes 1179656 | tf_op jit(solution)/shard_map/ppermute | solution.py:430
  53.3 8.8 %copy-start = (bf16[1024,384]{1,0:T(8,128)(2,1)}, bf16[1024,384]{1,0:T(8,128)(2,1)S(1)}, u32[]{:S(2)}) copy-start(bf16[1024,384]{1,0:T(8,128)(2,1)S(1)} %collective-permute-done.4.left_ref) | copy-start | bytes 2359300
  53.3 40.8 %collective-permute-start.6 = (bf16[512,384]{1,0:T(8,128)(2,1)}, bf16[512,384]{1,0:T(8,128)(2,1)}, u32[]{:S(2)}, u32[]{:S(2)}) collective-permute-start(bf16[512,384]{1,0:T(8,128)(2,1)} %get-tuple-element.41), channel_id=1, source_target_pairs={{0,1},{1,2},{2,3},{3,4},{4,5},{5,6},{6,7},{8,9},{9,10},{10,11},{11... | collective-permute-start | bytes 1179656 | tf_op jit(solution)/shard_map/ppermute | solution.py:366
  60.2 33.9 %collective-permute-start.7 = (bf16[512,384]{1,0:T(8,128)(2,1)}, bf16[512,384]{1,0:T(8,128)(2,1)}, u32[]{:S(2)}, u32[]{:S(2)}) collective-permute-start(bf16[512,384]{1,0:T(8,128)(2,1)} %get-tuple-element.42), channel_id=1, source_target_pairs={{1,0},{2,1},{3,2},{4,3},{5,4},{6,5},{7,6},{9,8},{10,9},{11,10},{12... | collective-permute-start | bytes 1179656 | tf_op jit(solution)/shard_map/ppermute | solution.py:366
  74.5 26.6 %collective-permute-start.8 = (bf16[384,1024]{1,0:T(8,128)(2,1)}, bf16[384,1024]{1,0:T(8,128)(2,1)}, u32[]{:S(2)}, u32[]{:S(2)}) collective-permute-start(bf16[384,1024]{1,0:T(8,128)(2,1)} %get-tuple-element.47), channel_id=1, source_target_pairs={{0,8},{8,16},{16,24},{1,9},{9,17},{17,25},{2,10},{10,18},{18,26},{... | collective-permute-start | bytes 2359304 | tf_op jit(solution)/shard_map/ppermute | solution.py:366
  92.0 13.6 %collective-permute-start.9 = (bf16[384,1024]{1,0:T(8,128)(2,1)}, bf16[384,1024]{1,0:T(8,128)(2,1)}, u32[]{:S(2)}, u32[]{:S(2)}) collective-permute-start(bf16[384,1024]{1,0:T(8,128)(2,1)} %get-tuple-element.48), channel_id=1, source_target_pairs={{8,0},{16,8},{24,16},{9,1},{17,9},{25,17},{10,2},{18,10},{26,18},{... | collective-permute-start | bytes 2359304 | tf_op jit(solution)/shard_map/ppermute | solution.py:366

commit v3 on v1

--- a/solution.py
+++ b/solution.py
@@ -160,7 +160,7 @@
 
 
 def columns_operator(
-    covariance, left, right, stencil, where, unit, steps, nlon, count, block_at, held=None, work=1
+    covariance, halos, stencil, where, unit, steps, nlon, count, block_at, held=None, ends=False, work=1
 ):
     rows, cols = covariance.shape
     lats = cols // nlon
@@ -169,12 +169,14 @@
     span = 2 * steps * nlon
     pairs = lats // 2
 
-    def kernel(where_ref, stencil_ref, p_ref, left_ref, right_ref, *rest):
+    def kernel(where_ref, stencil_ref, p_ref, *rest):
+        halo_refs, rest = rest[: 2 * len(halos)], rest[2 * len(halos) :]
         outs, (data_ref, b_high, b_low) = rest[:-3], rest[-3:]
         if held is not None:
             outs = outs[1:]
         t_ref = outs[0]
         i = pl.program_id(0)
+        col_odd, row_odd = where_ref[2] != 0, where_ref[3] != 0
 
         @pl.when(i == 0)
         def _():
@@ -189,8 +191,20 @@
                         b_high[at, a * nlon : (a + 1) * nlon] = high
                         b_low[at, a * nlon : (a + 1) * nlon] = low
 
-        data_ref[:size, :wide] = left_ref[...]
-        data_ref[:size, wide + cols :] = right_ref[...]
+        for k in range(len(halos)):
+            even_ref, odd_ref = halo_refs[2 * k : 2 * k + 2]
+            chosen = i >= 0 if len(halos) == 1 else i == k
+
+            @pl.when(jnp.logical_and(chosen, col_odd))
+            def _(even_ref=even_ref, odd_ref=odd_ref):
+                data_ref[:size, :wide] = even_ref[...]
+                data_ref[:size, wide + cols :] = odd_ref[...]
+
+            @pl.when(jnp.logical_and(chosen, jnp.logical_not(col_odd)))
+            def _(even_ref=even_ref, odd_ref=odd_ref):
+                data_ref[:size, :wide] = odd_ref[...]
+                data_ref[:size, wide + cols :] = even_ref[...]
+
         data_ref[:size, wide : wide + cols], data_ref[size:, wide : wide + cols] = split(p_ref[...])
         for q in range(pairs):
             window = slice((2 * q + 1) * nlon, (2 * q + 1) * nlon + span)
@@ -203,33 +217,34 @@
                 far_values = data_ref[:size, far].astype(F32) + data_ref[size:, far].astype(F32)
                 value = total[:, a * nlon : (a + 1) * nlon] + weight * far_values
                 t_ref[:, (2 * q + a) * nlon : (2 * q + a + 1) * nlon] = value.astype(BF16)
-        if held is None:
-
-            @pl.when(i == 0)
-            def _():
-                outs[1][...] = t_ref[:wide, :]
-
-            @pl.when(i == count - 1)
-            def _():
-                outs[2][...] = t_ref[size - wide :, :]
-
+        if ends:
+            for odd in range(2):
+                is_odd = row_odd if odd else jnp.logical_not(row_odd)
+
+                @pl.when(jnp.logical_and(i == 0, is_odd))
+                def _(odd=odd):
+                    outs[2 - odd][...] = t_ref[:wide, :]
+
+                @pl.when(jnp.logical_and(i == count - 1, is_odd))
+                def _(odd=odd):
+                    outs[1 + odd][...] = t_ref[size - wide :, :]
+
+    halo_at = (lambda i, at: (i, 0)) if len(halos) == 1 else (lambda i, at: (0, 0))
     in_specs = [
         pl.BlockSpec(stencil.shape, lambda i, at: (0, 0, 0)),
         pl.BlockSpec((size, cols), lambda i, at: (block_at(i, at), 0)),
-        pl.BlockSpec((size, wide), lambda i, at: (i, 0)),
-        pl.BlockSpec((size, wide), lambda i, at: (i, 0)),
-    ]
+    ] + [pl.BlockSpec((size, wide), halo_at)] * (2 * len(halos))
     out_specs = [pl.BlockSpec((size, cols), lambda i, at: (block_at(i, at), 0))]
     out_shape = [jax.ShapeDtypeStruct((rows, cols), BF16)]
-    operands = [where, stencil, covariance, left, right]
+    operands = [where, stencil, covariance] + [array for pair in halos for array in pair]
     aliases = {}
-    if held is None:
+    if ends:
         out_specs += [pl.BlockSpec((wide, cols), lambda i, at: (0, 0))] * 2
         out_shape += [jax.ShapeDtypeStruct((wide, cols), BF16)] * 2
-    else:
+    if held is not None:
         in_specs.append(pl.BlockSpec(memory_space=pl.ANY))
+        aliases = {len(operands): 0}
         operands.append(held)
-        aliases = {5: 0}
     return pl.pallas_call(
         kernel,
         grid_spec=pltpu.PrefetchScalarGridSpec(
@@ -238,7 +253,7 @@
             in_specs=in_specs,
             out_specs=out_specs,
             scratch_shapes=[pltpu.VMEM((2 * size, cols + 2 * wide), BF16)]
-            + [pltpu.VMEM((pairs * span, size), BF16)] * 2,
+            + [pltpu.VMEM((pairs * span, 2 * nlon), BF16)] * 2,
         ),
         out_shape=out_shape,
         input_output_aliases=aliases,
@@ -248,22 +263,27 @@
     )(*operands)
 
 
-def rows_operator(values, top, bottom, stencil, steps, nlon, out_dtype, noise=None, diagonal=None):
+def rows_operator(values, even, odd, stencil, where, steps, nlon, out_dtype, blocks=None, noise=None):
     rows, cols = values.shape
     lat_rows = rows // nlon
     wide = steps * nlon
     size = 2 * nlon
     span = 2 * steps * nlon
     pairs = lat_rows // 2
-    ahead = min((steps + 1) // 2, pairs - 1)
+    group = 2 if pairs % 2 == 0 else 1
+    ahead = (steps + 1) // 2
     exact = values.dtype == BF16
+    makes = blocks is None
     chunk = min(cols, 256)
 
-    def kernel(stencil_ref, x_ref, top_ref, bottom_ref, *rest):
-        extra, rest = (rest[:2], rest[2:]) if noise is not None else ((), rest)
-        out_ref, a_ref, high_ref, sem = rest[:4]
-        raw_ref, low_ref = (None, None) if exact else rest[4:]
-        p = pl.program_id(0)
+    def kernel(where_ref, stencil_ref, x_ref, even_ref, odd_ref, *rest):
+        if makes:
+            out_ref, a_ref = rest[:2]
+        else:
+            a_ref, noise_ref, out_ref = rest[:3]
+        high_ref, sem = rest[2 if makes else 3 :][:2]
+        raw_ref, low_ref = (None, None) if exact else rest[-2:]
+        step = pl.program_id(0)
 
         def load(q):
             here = pl.ds(pl.multiple_of(q * size, size), size)
@@ -278,11 +298,14 @@
                 here = pl.ds(pl.multiple_of(q * size, size), size)
                 high_ref[there, :], low_ref[there, :] = split(raw_ref[here, :])
 
-        @pl.when(p == 0)
+        @pl.when(step == 0)
         def _():
+            is_odd = where_ref[3]
+            at_even = pl.ds(pl.multiple_of((1 - is_odd) * (wide + rows), nlon), wide)
+            at_odd = pl.ds(pl.multiple_of(is_odd * (wide + rows), nlon), wide)
             halos = [
-                pltpu.make_async_copy(top_ref, high_ref.at[:wide, :], sem.at[pairs]),
-                pltpu.make_async_copy(bottom_ref, high_ref.at[wide + rows :, :], sem.at[pairs + 1]),
+                pltpu.make_async_copy(even_ref, high_ref.at[at_even, :], sem.at[pairs]),
+                pltpu.make_async_copy(odd_ref, high_ref.at[at_odd, :], sem.at[pairs + 1]),
             ]
             for halo in halos:
                 halo.start()
@@ -293,38 +316,44 @@
                 low_ref[wide + rows :, :] = jnp.zeros((wide, cols), BF16)
             for halo in halos:
                 halo.wait()
-            for q in range(ahead):
+            for q in range(min(ahead, pairs)):
                 ready(q)
 
-        @pl.when(p + ahead < pairs)
-        def _():
-            ready(p + ahead)
-
-        row = lambda d, a: stencil_ref[d + steps, pl.ds(2 * p + a, 1), :]
-        for a in range(2):
-            for k in range(2 * steps):
-                high, low = split(circulant(row(k - (steps - 1) - a, a)))
-                a_ref[a * nlon : (a + 1) * nlon, k * nlon : (k + 1) * nlon] = high
-                a_ref[size + a * nlon : size + (a + 1) * nlon, k * nlon : (k + 1) * nlon] = low
-        unit = lambda k: pl.multiple_of((2 * p + k) * nlon, nlon)
-        for lane in range(0, cols, chunk):
-            lanes = slice(lane, lane + chunk)
-            window = high_ref[pl.ds(unit(1), span), lanes]
-            both = product(a_ref[...], window)
-            total = both[:size] + both[size:]
-            if not exact:
-                total += product(a_ref[:size, :], low_ref[pl.ds(unit(1), span), lanes])
-            for a, k, d in ((0, 0, -steps), (1, 2 * steps + 1, steps)):
-                far = high_ref[pl.ds(unit(k), nlon), lanes].astype(F32)
+        for j in range(group):
+            q = step * group + j + ahead
+
+            @pl.when(q < pairs)
+            def _(q=q):
+                ready(q)
+
+        row = lambda j, d, a: stencil_ref[d + steps, pl.ds(2 * (step * group + j) + a, 1), :]
+        if makes:
+            for j in range(group):
+                for a in range(2):
+                    for k in range(2 * steps):
+                        high, low = split(circulant(row(j, k - (steps - 1) - a, a)))
+                        top = 2 * j * size + a * nlon
+                        a_ref[top : top + nlon, k * nlon : (k + 1) * nlon] = high
+                        a_ref[top + size : top + size + nlon, k * nlon : (k + 1) * nlon] = low
+        for j in range(group):
+            unit = lambda k: pl.multiple_of((2 * (step * group + j) + k) * nlon, nlon)
+            weights = [jnp.sum(row(j, d, a), axis=1, keepdims=True) for a, d in ((0, -steps), (1, steps))]
+            top = 2 * j * size
+            for lane in range(0, cols, chunk):
+                lanes = slice(lane, lane + chunk)
+                both = product(a_ref[top : top + 2 * size, :], high_ref[pl.ds(unit(1), span), lanes])
+                total = both[:size] + both[size:]
                 if not exact:
-                    far += low_ref[pl.ds(unit(k), nlon), lanes].astype(F32)
-                weight = jnp.sum(row(d, a), axis=1, keepdims=True)
-                value = total[a * nlon : (a + 1) * nlon, :] + weight * far
-                out_ref[a * nlon : (a + 1) * nlon, lanes] = value.astype(out_dtype)
+                    total += product(a_ref[top : top + size, :], low_ref[pl.ds(unit(1), span), lanes])
+                for a, k in ((0, 0), (1, 2 * steps + 1)):
+                    far = high_ref[pl.ds(unit(k), nlon), lanes].astype(F32)
+                    if not exact:
+                        far += low_ref[pl.ds(unit(k), nlon), lanes].astype(F32)
+                    value = total[a * nlon : (a + 1) * nlon, :] + weights[a] * far
+                    out_ref[j * size + a * nlon : j * size + (a + 1) * nlon, lanes] = value.astype(out_dtype)
         if noise is not None:
-            diagonal_ref, noise_ref = extra
-            for a in range(2):
-                lat = 2 * p + a - diagonal_ref[0]
+            for a in range(2 * group):
+                lat = 2 * group * step + a - where_ref[4]
 
                 @pl.when(jnp.logical_and(lat >= 0, lat < cols // nlon))
                 def _(a=a, lat=lat):
@@ -332,28 +361,31 @@
                     eye = lax.broadcasted_iota(jnp.int32, (nlon, nlon), 0) == lax.broadcasted_iota(
                         jnp.int32, (nlon, nlon), 1
                     )
-                    added = jnp.where(eye, noise_ref[pl.ds(2 * p + a, 1), :], 0.0)
+                    added = jnp.where(eye, noise_ref[pl.ds(2 * group * step + a, 1), :], 0.0)
                     out_ref[a * nlon : (a + 1) * nlon, lanes] += added
 
-    in_specs = [
-        pl.BlockSpec(stencil.shape, lambda g: (0, 0, 0)),
-        pl.BlockSpec(memory_space=pl.ANY),
-        pl.BlockSpec(memory_space=pl.ANY),
-        pl.BlockSpec(memory_space=pl.ANY),
-    ]
-    operands = [stencil, values, top, bottom]
-    if noise is not None:
-        in_specs += [pl.BlockSpec(memory_space=pltpu.SMEM), pl.BlockSpec(noise.shape, lambda g: (0, 0))]
-        operands += [diagonal, noise]
+    in_specs = [pl.BlockSpec(stencil.shape, lambda g, at: (0, 0, 0))] + [pl.BlockSpec(memory_space=pl.ANY)] * 3
+    operands = [where, stencil, values, even, odd]
+    out_specs = [pl.BlockSpec((group * size, cols), lambda g, at: (g, 0))]
+    out_shape = [jax.ShapeDtypeStruct((rows, cols), out_dtype)]
+    blocks_spec = pl.BlockSpec((2 * group * size, span), lambda g, at: (g, 0))
+    if makes:
+        out_specs.append(blocks_spec)
+        out_shape.append(jax.ShapeDtypeStruct((2 * rows, span), BF16))
+    else:
+        in_specs += [blocks_spec, pl.BlockSpec(noise.shape, lambda g, at: (0, 0))]
+        operands += [blocks, noise]
     return pl.pallas_call(
         kernel,
-        grid=(pairs,),
-        in_specs=in_specs,
-        out_specs=pl.BlockSpec((size, cols), lambda g: (g, 0)),
-        out_shape=jax.ShapeDtypeStruct((rows, cols), out_dtype),
-        scratch_shapes=[pltpu.VMEM((2 * size, span), BF16)]
-        + [pltpu.VMEM((rows + 2 * wide, cols), BF16), pltpu.SemaphoreType.DMA((pairs + 2,))]
-        + ([] if exact else [pltpu.VMEM((rows, cols), F32), pltpu.VMEM((rows + 2 * wide, cols), BF16)]),
+        grid_spec=pltpu.PrefetchScalarGridSpec(
+            num_scalar_prefetch=1,
+            grid=(pairs // group,),
+            in_specs=in_specs,
+            out_specs=out_specs,
+            scratch_shapes=[pltpu.VMEM((rows + 2 * wide, cols), BF16), pltpu.SemaphoreType.DMA((pairs + 2,))]
+            + ([] if exact else [pltpu.VMEM((rows, cols), F32), pltpu.VMEM((rows + 2 * wide, cols), BF16)]),
+        ),
+        out_shape=out_shape,
         compiler_params=params(),
         cost_estimate=cost(1),
         name="rows_operator",
@@ -379,14 +411,22 @@
     return join(before), join(after)
 
 
-def mirror_pairs(n_row, n_col, side):
+def exchanged(block, axis, odd):
+    pairs = []
+    for i in range(odd, lax.axis_size(axis) - 1, 2):
+        pairs += [(i, i + 1), (i + 1, i)]
+    return lax.ppermute(block, axis, pairs)
+
+
+def mirrored(block, odd):
+    n_row, n_col = lax.axis_size("row"), lax.axis_size("col")
     pairs = []
     for a in range(n_row):
         for b in range(n_col):
-            to = 2 * a + (1 - b % 2) + side
+            to = 2 * a + (1 - b % 2) + (1 if (b + odd) % 2 else -1)
             if 0 <= to < n_col:
                 pairs.append((a * n_col + b, (b // 2) * n_col + to))
-    return pairs
+    return lax.ppermute(block, ("row", "col"), pairs)
 
 
 def body(covariance, noise_var, wind_table, diffusivity, wind_index):
@@ -394,69 +434,66 @@
     lat_rows, nlon = noise_var.shape
     steps, nlat = wind_index.shape
     lats = cols_dev // nlon
-    n_row, n_col = lax.axis_size("row"), lax.axis_size("col")
     row_id, col_id = lax.axis_index("row"), lax.axis_index("col")
     own = lat_rows // 4
-    mirrored = lat_rows == 2 * lats and own % 2 == 0 and own >= steps and own <= lats - steps
-
-    if not mirrored:
+    fits = lat_rows == 2 * lats and own % 2 == 0 and own >= steps and own <= lats - steps
+    if not fits or lax.axis_size("col") != 2 * lax.axis_size("row"):
         return plain_body(covariance, noise_var, wind_table, diffusivity, wind_index)
 
     near = lat_rows // 2 - own
     middle = lat_rows // 2
-    parity = col_id % 2
-    by_parity = lambda even, odd: jnp.where(parity == 0, even, odd).astype(jnp.int32)
-    mirror_at = by_parity(middle - own, middle).reshape(1)
-    direct_at = by_parity(middle, middle - own).reshape(1)
-    base = (1 - parity) * lats
-    sources = nlon * jnp.stack([mirror_at[0], base + lats - steps, base, by_parity(lats - own, 0)]).astype(jnp.int32)
     outer, inner, wide = near * nlon, own * nlon, steps * nlon
-    ends = (0, cols_dev - wide)
+    pick = lambda parity, even, odd: even + parity * (odd - even)
+    col_odd, row_odd = col_id % 2, row_id % 2
+    mirror_at, direct_at = pick(col_odd, middle - own, middle), pick(col_odd, middle, middle - own)
+    diagonal = col_id * lats - row_id * lat_rows
+    where = jnp.stack([mirror_at // own, direct_at // own, col_odd, row_odd, diagonal]).astype(jnp.int32)
+    sources = jnp.stack(
+        [
+            mirror_at * nlon,
+            pick(col_odd, lats, lats - steps) * nlon,
+            pick(col_odd, 2 * lats - steps, 0) * nlon,
+            pick(col_odd, lats - own, 0) * nlon,
+            pick(col_odd, cols_dev - wide, 0),
+            pick(col_odd, 0, cols_dev - wide),
+            pick(row_odd, rows_dev - wide, 0),
+            pick(row_odd, 0, rows_dev - wide),
+        ]
+    ).astype(jnp.int32)
     pieces = [
-        (row, outer, lane, wide, k, there, 0)
+        (row, outer, (4 + k,), wide, k, there, 0)
         for row, there in ((0, 0), (rows_dev - outer, outer))
-        for k, lane in enumerate(ends)
+        for k in range(2)
     ]
-    pieces += [(row, wide, 0, cols_dev, k + 2, 0, 0) for k, row in enumerate((0, rows_dev - wide))]
-    pieces += [((k + 1,), wide, (3,), inner, k + 4, 0, nlon) for k in range(2)]
-    pieces += [((0,), inner, lane, wide, k + 6, 0, 0) for k, lane in enumerate(ends)]
-    first, last, top, bottom, left_m, right_m, first_inner, last_inner = packed(covariance, sources, pieces)
-    left = shifted(last, "col", 1)
-    right = shifted(first, "col", -1)
-    p_top = shifted(bottom, "row", 1)
-    p_bottom = shifted(top, "row", -1)
-    left_m, right_m, first_inner, wind_index, p_top = lax.optimization_barrier(
-        (left_m, right_m, first_inner, wind_index, p_top)
-    )
-    left_m = lax.ppermute(left_m, ("row", "col"), mirror_pairs(n_row, n_col, 1))
-    right_m = lax.ppermute(right_m, ("row", "col"), mirror_pairs(n_row, n_col, -1))
-    right_inner = shifted(first_inner, "col", -1)
+    pieces += [((6 + k,), wide, 0, cols_dev, k + 2, 0, 0) for k in range(2)]
+    pieces += [((1 + k,), wide, (3,), inner, k + 4, 0, nlon) for k in range(2)]
+    pieces += [((0,), inner, (4 + k,), wide, k + 6, 0, 0) for k in range(2)]
+    sent = packed(covariance, sources, pieces)
+    outers, ends, mirrors, inners = [list(sent[k : k + 2]) for k in range(0, 8, 2)]
+    outers = [exchanged(piece, "col", k) for k, piece in enumerate(outers)]
+    ends = [exchanged(piece, "row", k) for k, piece in enumerate(ends)]
+    mirrors[0], mirrors[1], wind_index, ends[0] = lax.optimization_barrier(
+        (mirrors[0], mirrors[1], wind_index, ends[0])
+    )
+    mirrors = [mirrored(piece, k) for k, piece in enumerate(mirrors)]
 
     row_s, col_s = stencil_rows(
         wind_table, diffusivity, wind_index, row_id * lat_rows, col_id * lats, lat_rows, lats, nlon
     )
-
-    operator_times_prior = rows_operator(covariance, p_top, p_bottom, row_s, steps, nlon, BF16)
-    operator_times_prior, left, right, last_inner = lax.optimization_barrier(
-        (operator_times_prior, left, right, last_inner)
-    )
-    left_inner = shifted(last_inner, "col", 1)
-    mirror, t_first, t_last = columns_operator(
-        covariance, left, right, col_s, mirror_at, near, steps, nlon, 2, lambda i, at: i * (lat_rows // near - 1)
-    )
-    t_top = shifted(t_last, "row", 1)
-    t_first, left_m = lax.optimization_barrier((t_first, left_m))
-    t_bottom = shifted(t_first, "row", -1)
-    inner_at = lambda i, at: at[0] // own + i
+    operator_times_prior, blocks = rows_operator(covariance, *ends, row_s, where, steps, nlon, BF16)
+    operator_times_prior, outers, inners = lax.optimization_barrier((operator_times_prior, outers, inners))
+    inners = [exchanged(piece, "col", k) for k, piece in enumerate(inners)]
+    mirror, *ends = columns_operator(
+        covariance, [outers], col_s, where, near, steps, nlon, 2, lambda i, at: i * (lat_rows // near - 1),
+        None, True,
+    )
+    ends = [exchanged(piece, "row", k) for k, piece in enumerate(ends)]
     (mirror,) = columns_operator(
-        covariance, left_m, right_m, col_s, mirror_at, own, steps, nlon, 1, inner_at, mirror
-    )
-    (mirror,) = columns_operator(
-        covariance, left_inner, right_inner, col_s, direct_at, own, steps, nlon, 1, inner_at, mirror, 10 ** 13
-    )
-    diagonal = (col_id * lats - row_id * lat_rows).astype(jnp.int32).reshape(1)
-    predicted_spread_matrix = rows_operator(
-        mirror, t_top, t_bottom, row_s, steps, nlon, F32, noise_var, diagonal
+        covariance, [mirrors, inners], col_s, where, own, steps, nlon, 2, lambda i, at: at[i], mirror, False,
+        10 ** 13,
+    )
+    (predicted_spread_matrix,) = rows_operator(
+        mirror, *ends, row_s, where, steps, nlon, F32, blocks, noise_var
     )
     return (predicted_spread_matrix, operator_times_prior)
 
@@ -468,21 +505,19 @@
     lats = cols_dev // nlon
     row_id, col_id = lax.axis_index("row"), lax.axis_index("col")
     sent = covariance.astype(BF16)
-    left, right = gathered(sent, sent, "col", 1, nlon, steps, lats)
-    p_top, p_bottom = gathered(sent, sent, "row", 0, nlon, steps, lat_rows)
+    sides = gathered(sent, sent, "col", 1, nlon, steps, lats)
+    ends = gathered(sent, sent, "row", 0, nlon, steps, lat_rows)
     row_s, col_s = stencil_rows(
         wind_table, diffusivity, wind_index, row_id * lat_rows, col_id * lats, lat_rows, lats, nlon
     )
-    operator_times_prior = rows_operator(covariance, p_top, p_bottom, row_s, steps, nlon, BF16)
-    unused = jnp.zeros((1,), jnp.int32)
-    held = jnp.zeros((rows_dev, cols_dev), BF16)
+    where = jnp.stack([0, 0, 1, 1, col_id * lats - row_id * lat_rows]).astype(jnp.int32)
+    operator_times_prior, blocks = rows_operator(covariance, *ends, row_s, where, steps, nlon, BF16)
     (mirror,) = columns_operator(
-        covariance, left, right, col_s, unused, 2, steps, nlon, lat_rows // 2, lambda i, at: i, held
-    )
-    t_top, t_bottom = gathered(mirror, mirror, "row", 0, nlon, steps, lat_rows)
-    diagonal = (col_id * lats - row_id * lat_rows).astype(jnp.int32).reshape(1)
-    predicted_spread_matrix = rows_operator(
-        mirror, t_top, t_bottom, row_s, steps, nlon, F32, noise_var, diagonal
+        covariance, [sides], col_s, where, 2, steps, nlon, lat_rows // 2, lambda i, at: i
+    )
+    ends = gathered(mirror, mirror, "row", 0, nlon, steps, lat_rows)
+    (predicted_spread_matrix,) = rows_operator(
+        mirror, *ends, row_s, where, steps, nlon, F32, blocks, noise_var
     )
     return (predicted_spread_matrix, operator_times_prior)
 

time: 109 us -> 96.7 us (0.89)
  the two profiles are of different devices: /device:TPU:1 before, /device:TPU:5 now
where the time goes in v3:
time: 96.7 us; the launch traced here: 95.9 us
  Pallas kernels  65.4 us (68%)
  starting transfers between devices  21.9 us (23%)
  local copies, waits for them, and re-layouts  4.28 us (4%)
  waiting for transfers between devices  3.33 us (3%)
  between operations  1.03 us (1%)
    pallas_call x2, Pallas kernels, rows_operator(): pl.pallas_call(kernel, grid_spec=pltpu.PrefetchScalarGridSpec(num_scalar_...  31 us
    pallas_call x2, Pallas kernels, columns_operator(): pl.pallas_call(kernel, grid_spec=pltpu.PrefetchScalarGridSpec(num_scalar_...  26.1 us
    ppermute x8, starting transfers between devices, exchanged(): return lax.ppermute(block, axis, pairs)  16.5 us
    pallas_call x1, Pallas kernels, packed(): pl.pallas_call(kernel, in_specs=[pl.BlockSpec(memory_space=pltpu.SMEM), p...  6.53 us
    ppermute x2, starting transfers between devices, mirrored(): return lax.ppermute(block, ('row', 'col'), pairs)  5.4 us
    ppermute x8, waiting for transfers between devices, exchanged(): return lax.ppermute(block, axis, pairs)  3.32 us
  transfers between devices with their start and end apart: 10, of which 1 were waited for; matrix products, arithmetic and copies ran while one was open for 3% of the time, Pallas kernels for 47%

profile of v3, /device:TPU:5, one launch (start us, length us, event | category | flops | bytes accessed | tf_op | source)
XLA Modules:
  0.0 95.9 jit_solution(3393626903072584985)
XLA Ops:
  0.6 0.0 copy-start.2
  0.6 0.0 copy-start.1
  0.7 0.6 stack.59.where_ref
  1.3 6.5 %packed.1 = (bf16[1024,384]{1,0:T(8,128)(2,1)}, bf16[1024,384]{1,0:T(8,128)(2,1)}, bf16[384,1024]{1,0:T(8,128)(2,1)}, bf16[384,1024]{1,0:T(8,128)(2,1)}, bf16[51...) custom-call(s32[8]{0:T(128)} %stack.59.where_ref, ...), custom_call_target="tpu_custom_call" | custom-call | flops 1 | bytes 1 | tf_op jit(solution)/shard_map/packed/pallas_call | solution.py:148
  7.8 0.7 collective-permute-start
  8.5 3.0 %collective-permute-start.3 = (bf16[384,1024]{1,0:T(8,128)(2,1)}, bf16[384,1024]{1,0:T(8,128)(2,1)}, u32[]{:S(2)}, u32[]{:S(2)}) collective-permute-start(bf16[384,1024]{1,0:T(8,128)(2,1)} %get-tuple-element.35), channel_id=1, source_target_pairs={{8,16},{16,8},{9,17},{17,9},{10,18},{18,10},{11,19},{19,11},{12,20... | collective-permute-start | bytes 2359304 | tf_op jit(solution)/shard_map/ppermute | solution.py:418
  11.6 0.3 collective-permute-start.4
  11.9 4.2 %collective-permute-start.5 = (bf16[1024,384]{1,0:T(8,128)(2,1)}, bf16[1024,384]{1,0:T(8,128)(2,1)}, u32[]{:S(2)}, u32[]{:S(2)}) collective-permute-start(bf16[1024,384]{1,0:T(8,128)(2,1)} %get-tuple-element.38), channel_id=1, source_target_pairs={{1,2},{2,1},{3,4},{4,3},{5,6},{6,5},{9,10},{10,9},{11,12},{12,11},... | collective-permute-start | bytes 2359304 | tf_op jit(solution)/shard_map/ppermute | solution.py:418
  16.1 0.0 copy-done.2
  16.1 0.1 copy.9
  16.1 0.6 reshape.9.table_ref
  16.7 0.6 stack.50.where_ref
  17.3 0.0 collective-permute-done.even_ref
  17.3 0.0 copy-start
  17.3 2.1 %collective-permute-start.1 = (bf16[512,384]{1,0:T(8,128)(2,1)}, bf16[512,384]{1,0:T(8,128)(2,1)}, u32[]{:S(2)}, u32[]{:S(2)}) collective-permute-start(bf16[512,384]{1,0:T(8,128)(2,1)} %get-tuple-element.32), channel_id=1, source_target_pairs={{0,0},{1,1},{2,8},{3,9},{4,16},{5,17},{6,24},{7,25},{8,2},{9,3},{1... | collective-permute-start | bytes 1179656 | tf_op jit(solution)/shard_map/ppermute | solution.py:429
  19.5 3.3 %collective-permute-start.2 = (bf16[512,384]{1,0:T(8,128)(2,1)}, bf16[512,384]{1,0:T(8,128)(2,1)}, u32[]{:S(2)}, u32[]{:S(2)}) collective-permute-start(bf16[512,384]{1,0:T(8,128)(2,1)} %get-tuple-element.33), channel_id=1, source_target_pairs={{0,2},{2,10},{4,18},{6,26},{8,4},{9,1},{10,12},{11,9},{12,20},{13,... | collective-permute-start | bytes 1179656 | tf_op jit(solution)/shard_map/ppermute | solution.py:429
  22.8 0.0 copy-done.1
  22.8 0.1 pad_dynamic-slice_fusion
  22.8 0.1 pad_dynamic-slice_fusion.1
  22.9 0.7 broadcast_in_dim.5.col_ref
  23.6 0.7 broadcast_in_dim.4.row_ref
  24.3 1.7 %stencil_rows.1 = (f32[7,16,128]{2,1,0:T(8,128)}, f32[7,8,128]{2,1,0:T(8,128)}) custom-call(f32[32]{0:T(128)} %reshape.9.table_ref, f32[16]{0:T(128)} %diffuse_ref.1, s32[3,22,128]{2,1,0:T(8,128)} %broadcast_in_dim.4.row_ref, s32[3,14,128]{2,1,0:T(8,128)} %broadcast_in_dim.5.col_ref), custom_call_target="tpu_custom_call" | custom-call | flops 1 | bytes 1 | tf_op jit(solution)/shard_map/stencil_rows/pallas_call | solution.py:98
  26.0 0.0 collective-permute-done.3.odd_ref
  26.0 0.0 copy-done
  26.0 17.6 %rows_operator.2 = (bf16[2048,1024]{1,0:T(8,128)(2,1)}, bf16[4096,768]{1,0:T(8,128)(2,1)}) custom-call(s32[5]{0:T(128)} %stack.50.where_ref, f32[7,16,128]{2,1,0:T(8,128)} %get-tuple-element.30.stencil_ref, f32[2048,1024]{1,0:T(8,128)} %p_ref.5, bf16[384,1024]{1,0:T(8,128)(2,1)} %copy-done, bf16[384,1024]{1,0:T(8,128)(2,1)} %collective-permute-done.3.odd_ref), custom_call_target="tpu_custom_call" | custom-call | flops 1 | bytes 1 | tf_op jit(solution)/shard_map/rows_operator/pallas_call | solution.py:378
  43.7 3.3 %collective-permute-done.4.rest_0_ = bf16[1024,384]{1,0:T(8,128)(2,1)} collective-permute-done((bf16[1024,384]{1,0:T(8,128)(2,1)}, bf16[1024,384]{1,0:T(8,128)(2,1)}, u32[]{:S(2)}, u32[]{:S(2)}) %collective-permute-start.4) | collective-permute-done | bytes 786464 | tf_op jit(solution)/shard_map/ppermute | solution.py:418
  47.0 0.0 collective-permute-done.5.rest_1_
  47.0 0.0 collective-permute-start.6
  47.0 4.7 %collective-permute-start.7 = (bf16[512,384]{1,0:T(8,128)(2,1)}, bf16[512,384]{1,0:T(8,128)(2,1)S(1)}, u32[]{:S(2)}, u32[]{:S(2)}) collective-permute-start(bf16[512,384]{1,0:T(8,128)(2,1)} %get-tuple-element.42), channel_id=1, source_target_pairs={{1,2},{2,1},{3,4},{4,3},{5,6},{6,5},{9,10},{10,9},{11,12},{12,11},... | collective-permute-start | bytes 1179656 | tf_op jit(solution)/shard_map/ppermute | solution.py:418
  51.7 13.2 %columns_operator.2 = (bf16[2048,1024]{1,0:T(8,128)(2,1)}, bf16[384,1024]{1,0:T(8,128)(2,1)}, bf16[384,1024]{1,0:T(8,128)(2,1)}) custom-call(s32[5]{0:T(128)} %stack.50.where_ref, f32[7,8,128]{2,1,0:T(8,128)} %get-tuple-element.31.stencil_ref, f32[2048,1024]{1,0:T(8,128)} %p_ref.5, bf16[1024,384]{1,0:T(8,128)(2,1)} %collective-permute-done.4.rest_0_, ...), custom_call_target="tpu_custom_call" | custom-call | flops 1 | bytes 1 | tf_op jit(solution)/shard_map/columns_operator/pallas_call | solution.py:248
  64.9 0.0 collective-permute-start.8
  64.9 0.0 collective-permute-done.1.rest_0_
  64.9 3.7 %collective-permute-start.9 = (bf16[384,1024]{1,0:T(8,128)(2,1)}, bf16[384,1024]{1,0:T(8,128)(2,1)}, u32[]{:S(2)}, u32[]{:S(2)}) collective-permute-start(bf16[384,1024]{1,0:T(8,128)(2,1)} %get-tuple-element.47), channel_id=1, source_target_pairs={{8,16},{16,8},{9,17},{17,9},{10,18},{18,10},{11,19},{19,11},{12,20... | collective-permute-start | bytes 2359304 | tf_op jit(solution)/shard_map/ppermute | solution.py:418
  68.6 0.0 collective-permute-done.2.rest_1_
  68.6 0.0 collective-permute-done.6.rest_2_
  68.6 0.0 copy-start.3
  68.6 0.0 collective-permute-done.7.rest_3_
  68.6 0.0 copy-start.4
  68.6 0.7 copy-done.3
  69.3 0.2 copy-done.4
  69.5 12.9 %columns_operator.3.x_ref = bf16[2048,1024]{1,0:T(8,128)(2,1)} custom-call(s32[5]{0:T(128)} %stack.50.where_ref, f32[7,8,128]{2,1,0:T(8,128)} %get-tuple-element.31.stencil_ref, f32[2048,1024]{1,0:T(8,128)} %p_ref.5, bf16[512,384]{1,0:T(8,128)(2,1)} %collective-permute-done.1.rest_0_, ...), custom_call_target="tpu_custom_call", output_to_operand_aliasing={{}: (7, {})} | custom-call | flops 9999999827968 | bytes 9999999827968 | tf_op jit(solution)/shard_map/columns_operator/pallas_call | solution.py:248
  82.4 0.0 collective-permute-done.8.even_ref
  82.4 0.0 collective-permute-done.9.odd_ref
  82.4 13.4 %rows_operator.3 = f32[2048,1024]{1,0:T(8,128)} custom-call(s32[5]{0:T(128)} %stack.50.where_ref, f32[7,16,128]{2,1,0:T(8,128)} %get-tuple-element.30.stencil_ref, bf16[2048,1024]{1,0:T(8,128)(2,1)} %columns_operator.3.x_ref, bf16[384,1024]{1,0:T(8,128)(2,1)} %collective-permute-done.8.even_ref, bf16[384,1024]{1,0:T(8,128)(2,1)} %collective-permute-done.9.odd_ref, ...), custom_call_target="tpu_custom_call" | custom-call | flops 1 | bytes 1 | tf_op jit(solution)/shard_map/rows_operator/pallas_call | solution.py:378
Async XLA Ops:
  0.6 15.4 %copy-start.2 = (f32[16,2]{0,1:T(2,128)S(1)}, f32[16,2]{0,1:T(2,128)}, u32[]{:S(2)}) copy-start(f32[16,2]{0,1:T(2,128)} %param.7) | copy-start | bytes 388
  0.6 22.1 %copy-start.1 = (s32[3,64]{1,0:T(4,128)S(1)}, s32[3,64]{1,0:T(4,128)}, u32[]{:S(2)}) copy-start(s32[3,64]{1,0:T(4,128)} %param.9) | copy-start | bytes 2308
  7.8 9.5 %collective-permute-start = (bf16[384,1024]{1,0:T(8,128)(2,1)}, bf16[384,1024]{1,0:T(8,128)(2,1)S(1)}, u32[]{:S(2)}, u32[]{:S(2)}) collective-permute-start(bf16[384,1024]{1,0:T(8,128)(2,1)} %get-tuple-element.28), channel_id=1, source_target_pairs={{0,8},{8,0},{16,24},{24,16},{1,9},{9,1},{17,25},{25,17},{2,10},{10... | collective-permute-start | bytes 2359304 | tf_op jit(solution)/shard_map/ppermute | solution.py:418
  8.5 17.5 %collective-permute-start.3 = (bf16[384,1024]{1,0:T(8,128)(2,1)}, bf16[384,1024]{1,0:T(8,128)(2,1)}, u32[]{:S(2)}, u32[]{:S(2)}) collective-permute-start(bf16[384,1024]{1,0:T(8,128)(2,1)} %get-tuple-element.35), channel_id=1, source_target_pairs={{8,16},{16,8},{9,17},{17,9},{10,18},{18,10},{11,19},{19,11},{12,20... | collective-permute-start | bytes 2359304 | tf_op jit(solution)/shard_map/ppermute | solution.py:418
  11.6 35.4 %collective-permute-start.4 = (bf16[1024,384]{1,0:T(8,128)(2,1)}, bf16[1024,384]{1,0:T(8,128)(2,1)}, u32[]{:S(2)}, u32[]{:S(2)}) collective-permute-start(bf16[1024,384]{1,0:T(8,128)(2,1)} %get-tuple-element.37), channel_id=1, source_target_pairs={{0,1},{1,0},{2,3},{3,2},{4,5},{5,4},{6,7},{7,6},{8,9},{9,8},{10,11... | collective-permute-start | bytes 2359304 | tf_op jit(solution)/shard_map/ppermute | solution.py:418
  11.9 35.1 %collective-permute-start.5 = (bf16[1024,384]{1,0:T(8,128)(2,1)}, bf16[1024,384]{1,0:T(8,128)(2,1)}, u32[]{:S(2)}, u32[]{:S(2)}) collective-permute-start(bf16[1024,384]{1,0:T(8,128)(2,1)} %get-tuple-element.38), channel_id=1, source_target_pairs={{1,2},{2,1},{3,4},{4,3},{5,6},{6,5},{9,10},{10,9},{11,12},{12,11},... | collective-permute-start | bytes 2359304 | tf_op jit(solution)/shard_map/ppermute | solution.py:418
  17.3 8.7 %copy-start = (bf16[384,1024]{1,0:T(8,128)(2,1)}, bf16[384,1024]{1,0:T(8,128)(2,1)S(1)}, u32[]{:S(2)}) copy-start(bf16[384,1024]{1,0:T(8,128)(2,1)S(1)} %collective-permute-done.even_ref) | copy-start | bytes 2359300
  17.3 47.6 %collective-permute-start.1 = (bf16[512,384]{1,0:T(8,128)(2,1)}, bf16[512,384]{1,0:T(8,128)(2,1)}, u32[]{:S(2)}, u32[]{:S(2)}) collective-permute-start(bf16[512,384]{1,0:T(8,128)(2,1)} %get-tuple-element.32), channel_id=1, source_target_pairs={{0,0},{1,1},{2,8},{3,9},{4,16},{5,17},{6,24},{7,25},{8,2},{9,3},{1... | collective-permute-start | bytes 1179656 | tf_op jit(solution)/shard_map/ppermute | solution.py:429
  19.5 49.1 %collective-permute-start.2 = (bf16[512,384]{1,0:T(8,128)(2,1)}, bf16[512,384]{1,0:T(8,128)(2,1)}, u32[]{:S(2)}, u32[]{:S(2)}) collective-permute-start(bf16[512,384]{1,0:T(8,128)(2,1)} %get-tuple-element.33), channel_id=1, source_target_pairs={{0,2},{2,10},{4,18},{6,26},{8,4},{9,1},{10,12},{11,9},{12,20},{13,... | collective-permute-start | bytes 1179656 | tf_op jit(solution)/shard_map/ppermute | solution.py:429
  47.0 21.6 %collective-permute-start.6 = (bf16[512,384]{1,0:T(8,128)(2,1)}, bf16[512,384]{1,0:T(8,128)(2,1)S(1)}, u32[]{:S(2)}, u32[]{:S(2)}) collective-permute-start(bf16[512,384]{1,0:T(8,128)(2,1)} %get-tuple-element.41), channel_id=1, source_target_pairs={{0,1},{1,0},{2,3},{3,2},{4,5},{5,4},{6,7},{7,6},{8,9},{9,8},{10,11... | collective-permute-start | bytes 1179656 | tf_op jit(solution)/shard_map/ppermute | solution.py:418
  47.0 21.6 %collective-permute-start.7 = (bf16[512,384]{1,0:T(8,128)(2,1)}, bf16[512,384]{1,0:T(8,128)(2,1)S(1)}, u32[]{:S(2)}, u32[]{:S(2)}) collective-permute-start(bf16[512,384]{1,0:T(8,128)(2,1)} %get-tuple-element.42), channel_id=1, source_target_pairs={{1,2},{2,1},{3,4},{4,3},{5,6},{6,5},{9,10},{10,9},{11,12},{12,11},... | collective-permute-start | bytes 1179656 | tf_op jit(solution)/shard_map/ppermute | solution.py:418
  64.9 17.5 %collective-permute-start.8 = (bf16[384,1024]{1,0:T(8,128)(2,1)}, bf16[384,1024]{1,0:T(8,128)(2,1)}, u32[]{:S(2)}, u32[]{:S(2)}) collective-permute-start(bf16[384,1024]{1,0:T(8,128)(2,1)} %get-tuple-element.46), channel_id=1, source_target_pairs={{0,8},{8,0},{16,24},{24,16},{1,9},{9,1},{17,25},{25,17},{2,10},{10... | collective-permute-start | bytes 2359304 | tf_op jit(solution)/shard_map/ppermute | solution.py:418
  64.9 17.5 %collective-permute-start.9 = (bf16[384,1024]{1,0:T(8,128)(2,1)}, bf16[384,1024]{1,0:T(8,128)(2,1)}, u32[]{:S(2)}, u32[]{:S(2)}) collective-permute-start(bf16[384,1024]{1,0:T(8,128)(2,1)} %get-tuple-element.47), channel_id=1, source_target_pairs={{8,16},{16,8},{9,17},{17,9},{10,18},{18,10},{11,19},{19,11},{12,20... | collective-permute-start | bytes 2359304 | tf_op jit(solution)/shard_map/ppermute | solution.py:418
  68.6 0.8 copy-start.3
  68.6 0.9 copy-start.4

commit v4 on v3

--- a/solution.py
+++ b/solution.py
@@ -35,9 +35,8 @@
 
 
 def circulant(row):
-    size, group = row.shape[1], 8
-    first = pltpu.roll(jnp.broadcast_to(row, (group, size)), 0, 1, stride=1, stride_axis=0)
-    return jnp.concatenate([first] + [pltpu.roll(first, at, 1) for at in range(group, size, group)], axis=0)
+    size = row.shape[1]
+    return pltpu.roll(jnp.broadcast_to(row, (size, size)), 0, 1, stride=1, stride_axis=0)
 
 
 def product(left, right):
@@ -68,43 +67,51 @@
     return rows
 
 
-def stencil_rows(wind_table, diffusivity, wind_index, row_lat, col_lat, lat_rows, lats, nlon):
-    steps = wind_index.shape[0]
-    table = wind_table.shape[0]
-    padded = jnp.pad(wind_index, ((0, 0), (steps, steps)), constant_values=-1)
-
-    def local(first, count):
-        part = lax.dynamic_slice_in_dim(padded, first, count + 2 * steps, 1)
-        return jnp.broadcast_to(part[:, :, None], part.shape + (nlon,))
-
-    def kernel(table_ref, diffuse_ref, row_ref, col_ref, row_out, col_out):
-        for ref, out, size, turned in ((row_ref, row_out, lat_rows, False), (col_ref, col_out, lats, True)):
+def stencils(wind_table, diffusivity, wind_index, where, lat_rows, lats, nlon):
+    steps, nlat = wind_index.shape
+    sizes = (lat_rows, lats)
+    span = 2 * steps * nlon
+    pairs = lats // 2
+
+    def kernel(table_ref, diffuse_ref, index_ref, where_ref, row_out, col_out, high_out, low_out, *scratch):
+        for side, out in enumerate((row_out, col_out)):
+            looked_up = scratch[side]
             terms = []
             for step_no in range(steps):
-                index = ref[step_no]
-                zonal = merid = diffuse = jnp.zeros(index.shape, F32)
-                for entry in range(table):
-                    here = index == entry
-                    zonal = jnp.where(here, table_ref[2 * entry], zonal)
-                    merid = jnp.where(here, table_ref[2 * entry + 1], merid)
-                    diffuse = jnp.where(here, diffuse_ref[entry], diffuse)
+                for i in range(sizes[side] + 2 * steps):
+                    lat = where_ref[5 + side] + i - steps
+                    inside = jnp.logical_and(lat >= 0, lat < nlat)
+                    entry = index_ref[step_no, jnp.clip(lat, 0, nlat - 1)]
+                    values = (table_ref[entry, 0], table_ref[entry, 1], diffuse_ref[entry], inside.astype(F32))
+                    for k, value in enumerate(values):
+                        looked_up[k, i : i + 1, :] = jnp.full((1, nlon), value, F32)
+                here = looked_up[3] > 0.5
                 c, e, w, n, s = [
-                    jnp.where(index >= 0, term, 0.0) for term in stencil_terms(zonal, merid, diffuse)
+                    jnp.where(here, term, 0.0)
+                    for term in stencil_terms(looked_up[0], looked_up[1], looked_up[2])
                 ]
-                terms.append((c, w, e, n, s) if turned else (c, e, w, n, s))
-            for d, value in composed(terms, size, nlon).items():
+                terms.append((c, w, e, n, s) if side else (c, e, w, n, s))
+            for d, value in composed(terms, sizes[side], nlon).items():
                 out[d + steps] = value
+        for q in range(pairs):
+            for a in range(2):
+                for k in range(2 * steps):
+                    d = k - (steps - 1) - a
+                    high, low = split(circulant(col_out[d + steps, 2 * q + a : 2 * q + a + 1, :]))
+                    at = pl.ds(q * span + k * nlon, nlon)
+                    high_out[at, a * nlon : (a + 1) * nlon] = high
+                    low_out[at, a * nlon : (a + 1) * nlon] = low
 
     return pl.pallas_call(
         kernel,
-        in_specs=[pl.BlockSpec(memory_space=pltpu.SMEM)] * 2 + [pl.BlockSpec(memory_space=pltpu.VMEM)] * 2,
-        out_shape=[
-            jax.ShapeDtypeStruct((2 * steps + 1, size, nlon), F32) for size in (lat_rows, lats)
-        ],
+        in_specs=[pl.BlockSpec(memory_space=pltpu.SMEM)] * 4,
+        out_shape=[jax.ShapeDtypeStruct((2 * steps + 1, size, nlon), F32) for size in sizes]
+        + [jax.ShapeDtypeStruct((pairs * span, 2 * nlon), BF16)] * 2,
+        scratch_shapes=[pltpu.VMEM((4, size + 2 * steps, nlon), F32) for size in sizes],
         compiler_params=params(),
         cost_estimate=cost(1),
-        name="stencil_rows",
-    )(wind_table.reshape(-1), diffusivity, local(row_lat, lat_rows), local(col_lat, lats))
+        name="stencils",
+    )(wind_table, diffusivity, wind_index, where)
 
 
 def packed(covariance, where, pieces):
@@ -160,7 +167,7 @@
 
 
 def columns_operator(
-    covariance, halos, stencil, where, unit, steps, nlon, count, block_at, held=None, ends=False, work=1
+    covariance, halos, stencil, blocks, where, unit, steps, nlon, count, block_at, held=None, ends=False, work=1
 ):
     rows, cols = covariance.shape
     lats = cols // nlon
@@ -171,7 +178,7 @@
 
     def kernel(where_ref, stencil_ref, p_ref, *rest):
         halo_refs, rest = rest[: 2 * len(halos)], rest[2 * len(halos) :]
-        outs, (data_ref, b_high, b_low) = rest[:-3], rest[-3:]
+        (b_high, b_low), outs, data_ref = rest[:2], rest[2:-1], rest[-1]
         if held is not None:
             outs = outs[1:]
         t_ref = outs[0]
@@ -182,14 +189,6 @@
         def _():
             data_ref[size:, :wide] = jnp.zeros((size, wide), BF16)
             data_ref[size:, wide + cols :] = jnp.zeros((size, wide), BF16)
-            for q in range(pairs):
-                for a in range(2):
-                    for k in range(2 * steps):
-                        d = k - (steps - 1) - a
-                        high, low = split(circulant(stencil_ref[d + steps, 2 * q + a : 2 * q + a + 1, :]))
-                        at = pl.ds(q * span + k * nlon, nlon)
-                        b_high[at, a * nlon : (a + 1) * nlon] = high
-                        b_low[at, a * nlon : (a + 1) * nlon] = low
 
         for k in range(len(halos)):
             even_ref, odd_ref = halo_refs[2 * k : 2 * k + 2]
@@ -233,10 +232,12 @@
     in_specs = [
         pl.BlockSpec(stencil.shape, lambda i, at: (0, 0, 0)),
         pl.BlockSpec((size, cols), lambda i, at: (block_at(i, at), 0)),
-    ] + [pl.BlockSpec((size, wide), halo_at)] * (2 * len(halos))
+    ]
+    in_specs += [pl.BlockSpec((size, wide), halo_at)] * (2 * len(halos))
+    in_specs += [pl.BlockSpec(block.shape, lambda i, at: (0, 0)) for block in blocks]
     out_specs = [pl.BlockSpec((size, cols), lambda i, at: (block_at(i, at), 0))]
     out_shape = [jax.ShapeDtypeStruct((rows, cols), BF16)]
-    operands = [where, stencil, covariance] + [array for pair in halos for array in pair]
+    operands = [where, stencil, covariance] + [array for pair in halos for array in pair] + list(blocks)
     aliases = {}
     if ends:
         out_specs += [pl.BlockSpec((wide, cols), lambda i, at: (0, 0))] * 2
@@ -252,8 +253,7 @@
             grid=(count,),
             in_specs=in_specs,
             out_specs=out_specs,
-            scratch_shapes=[pltpu.VMEM((2 * size, cols + 2 * wide), BF16)]
-            + [pltpu.VMEM((pairs * span, 2 * nlon), BF16)] * 2,
+            scratch_shapes=[pltpu.VMEM((2 * size, cols + 2 * wide), BF16)],
         ),
         out_shape=out_shape,
         input_output_aliases=aliases,
@@ -447,9 +447,15 @@
     col_odd, row_odd = col_id % 2, row_id % 2
     mirror_at, direct_at = pick(col_odd, middle - own, middle), pick(col_odd, middle, middle - own)
     diagonal = col_id * lats - row_id * lat_rows
-    where = jnp.stack([mirror_at // own, direct_at // own, col_odd, row_odd, diagonal]).astype(jnp.int32)
-    sources = jnp.stack(
+    where = jnp.stack(
         [
+            mirror_at // own,
+            direct_at // own,
+            col_odd,
+            row_odd,
+            diagonal,
+            row_id * lat_rows,
+            col_id * lats,
             mirror_at * nlon,
             pick(col_odd, lats, lats - steps) * nlon,
             pick(col_odd, 2 * lats - steps, 0) * nlon,
@@ -461,14 +467,14 @@
         ]
     ).astype(jnp.int32)
     pieces = [
-        (row, outer, (4 + k,), wide, k, there, 0)
+        (row, outer, (11 + k,), wide, k, there, 0)
         for row, there in ((0, 0), (rows_dev - outer, outer))
         for k in range(2)
     ]
-    pieces += [((6 + k,), wide, 0, cols_dev, k + 2, 0, 0) for k in range(2)]
-    pieces += [((1 + k,), wide, (3,), inner, k + 4, 0, nlon) for k in range(2)]
-    pieces += [((0,), inner, (4 + k,), wide, k + 6, 0, 0) for k in range(2)]
-    sent = packed(covariance, sources, pieces)
+    pieces += [((13 + k,), wide, 0, cols_dev, k + 2, 0, 0) for k in range(2)]
+    pieces += [((8 + k,), wide, (10,), inner, k + 4, 0, nlon) for k in range(2)]
+    pieces += [((7,), inner, (11 + k,), wide, k + 6, 0, 0) for k in range(2)]
+    sent = packed(covariance, where, pieces)
     outers, ends, mirrors, inners = [list(sent[k : k + 2]) for k in range(0, 8, 2)]
     outers = [exchanged(piece, "col", k) for k, piece in enumerate(outers)]
     ends = [exchanged(piece, "row", k) for k, piece in enumerate(ends)]
@@ -477,19 +483,17 @@
     )
     mirrors = [mirrored(piece, k) for k, piece in enumerate(mirrors)]
 
-    row_s, col_s = stencil_rows(
-        wind_table, diffusivity, wind_index, row_id * lat_rows, col_id * lats, lat_rows, lats, nlon
-    )
+    row_s, col_s, *col_blocks = stencils(wind_table, diffusivity, wind_index, where, lat_rows, lats, nlon)
     operator_times_prior, blocks = rows_operator(covariance, *ends, row_s, where, steps, nlon, BF16)
     operator_times_prior, outers, inners = lax.optimization_barrier((operator_times_prior, outers, inners))
     inners = [exchanged(piece, "col", k) for k, piece in enumerate(inners)]
     mirror, *ends = columns_operator(
-        covariance, [outers], col_s, where, near, steps, nlon, 2, lambda i, at: i * (lat_rows // near - 1),
+        covariance, [outers], col_s, col_blocks, where, near, steps, nlon, 2, lambda i, at: i * (lat_rows // near - 1),
         None, True,
     )
     ends = [exchanged(piece, "row", k) for k, piece in enumerate(ends)]
     (mirror,) = columns_operator(
-        covariance, [mirrors, inners], col_s, where, own, steps, nlon, 2, lambda i, at: at[i], mirror, False,
+        covariance, [mirrors, inners], col_s, col_blocks, where, own, steps, nlon, 2, lambda i, at: at[i], mirror, False,
         10 ** 13,
     )
     (predicted_spread_matrix,) = rows_operator(
@@ -507,13 +511,12 @@
     sent = covariance.astype(BF16)
     sides = gathered(sent, sent, "col", 1, nlon, steps, lats)
     ends = gathered(sent, sent, "row", 0, nlon, steps, lat_rows)
-    row_s, col_s = stencil_rows(
-        wind_table, diffusivity, wind_index, row_id * lat_rows, col_id * lats, lat_rows, lats, nlon
-    )
-    where = jnp.stack([0, 0, 1, 1, col_id * lats - row_id * lat_rows]).astype(jnp.int32)
+    firsts = (row_id * lat_rows, col_id * lats)
+    where = jnp.stack([0, 0, 1, 1, firsts[1] - firsts[0], *firsts]).astype(jnp.int32)
+    row_s, col_s, *col_blocks = stencils(wind_table, diffusivity, wind_index, where, lat_rows, lats, nlon)
     operator_times_prior, blocks = rows_operator(covariance, *ends, row_s, where, steps, nlon, BF16)
     (mirror,) = columns_operator(
-        covariance, [sides], col_s, where, 2, steps, nlon, lat_rows // 2, lambda i, at: i
+        covariance, [sides], col_s, col_blocks, where, 2, steps, nlon, lat_rows // 2, lambda i, at: i
     )
     ends = gathered(mirror, mirror, "row", 0, nlon, steps, lat_rows)
     (predicted_spread_matrix,) = rows_operator(

time: 96.7 us -> 92.9 us (0.961)
  Pallas kernels: 65.4 us -> 62.1 us
  local copies, waits for them, and re-layouts: 4.28 us -> 2.21 us
  waiting for transfers between devices: 3.33 us -> 4.55 us
    pallas_call x2, Pallas kernels: 26.1 us -> 21.3 us  [columns_operator(): pl.pallas_call(kernel, grid_spec=pltpu.PrefetchScalarGridSpec(num_scalar_...]
    pallas_call x1, Pallas kernels: 1.74 us -> 4.04 us  [stencils(): pl.pallas_call(kernel, in_specs=[pl.BlockSpec(memory_space=pltpu.SMEM)] *...]
    broadcast_in_dim x2 -> x0, local copies, waits for them, and re-layouts: 1.37 us -> none  [local(): return jnp.broadcast_to(part[:, :, None], part.shape + (nlon,))]
    ppermute x8, waiting for transfers between devices: 3.32 us -> 4.55 us  [exchanged(): return lax.ppermute(block, axis, pairs)]
  transfers between devices with their start and end apart: 10 -> 10, of which waited for: 1 -> 2; matrix products, arithmetic and copies ran while one was open for 3% -> 1% of each run, Pallas kernels for 47% -> 46%
where the time goes in v4:
time: 92.9 us; the launch traced here: 91.7 us
  Pallas kernels  62.1 us (67%)
  starting transfers between devices  21.9 us (24%)
  waiting for transfers between devices  4.55 us (5%)
  local copies, waits for them, and re-layouts  2.21 us (2%)
  between operations  0.96 us (1%)
    pallas_call x2, Pallas kernels, rows_operator(): pl.pallas_call(kernel, grid_spec=pltpu.PrefetchScalarGridSpec(num_scalar_...  30.1 us
    pallas_call x2, Pallas kernels, columns_operator(): pl.pallas_call(kernel, grid_spec=pltpu.PrefetchScalarGridSpec(num_scalar_...  21.3 us
    ppermute x8, starting transfers between devices, exchanged(): return lax.ppermute(block, axis, pairs)  16.5 us
    pallas_call x1, Pallas kernels, packed(): pl.pallas_call(kernel, in_specs=[pl.BlockSpec(memory_space=pltpu.SMEM), p...  6.64 us
    ppermute x2, starting transfers between devices, mirrored(): return lax.ppermute(block, ('row', 'col'), pairs)  5.41 us
    ppermute x8, waiting for transfers between devices, exchanged(): return lax.ppermute(block, axis, pairs)  4.55 us
    pallas_call x1, Pallas kernels, stencils(): pl.pallas_call(kernel, in_specs=[pl.BlockSpec(memory_space=pltpu.SMEM)] *...  4.04 us
  transfers between devices with their start and end apart: 10, of which 2 were waited for; matrix products, arithmetic and copies ran while one was open for 1% of the time, Pallas kernels for 46%

profile of v4, /device:TPU:5, one launch (start us, length us, event | category | flops | bytes accessed | tf_op | source)
XLA Modules:
  0.0 91.7 jit_solution(6831879730066711528)
XLA Ops:
  0.7 0.6 stack.63.where_ref
  1.3 0.0 copy-start.1
  1.3 6.6 %packed.1 = (bf16[1024,384]{1,0:T(8,128)(2,1)}, bf16[1024,384]{1,0:T(8,128)(2,1)}, bf16[384,1024]{1,0:T(8,128)(2,1)}, bf16[384,1024]{1,0:T(8,128)(2,1)}, bf16[51...) custom-call(s32[15]{0:T(128)} %stack.63.where_ref, ...), custom_call_target="tpu_custom_call" | custom-call | flops 1 | bytes 1 | tf_op jit(solution)/shard_map/packed/pallas_call | solution.py:155
  8.0 0.7 collective-permute-start
  8.7 3.0 %collective-permute-start.3 = (bf16[384,1024]{1,0:T(8,128)(2,1)}, bf16[384,1024]{1,0:T(8,128)(2,1)}, u32[]{:S(2)}, u32[]{:S(2)}) collective-permute-start(bf16[384,1024]{1,0:T(8,128)(2,1)} %get-tuple-element.37), channel_id=1, source_target_pairs={{8,16},{16,8},{9,17},{17,9},{10,18},{18,10},{11,19},{19,11},{12,20... | collective-permute-start | bytes 2359304 | tf_op jit(solution)/shard_map/ppermute | solution.py:418
  11.7 0.3 collective-permute-start.4
  12.0 4.2 %collective-permute-start.5 = (bf16[1024,384]{1,0:T(8,128)(2,1)}, bf16[1024,384]{1,0:T(8,128)(2,1)}, u32[]{:S(2)}, u32[]{:S(2)}) collective-permute-start(bf16[1024,384]{1,0:T(8,128)(2,1)} %get-tuple-element.40), channel_id=1, source_target_pairs={{1,2},{2,1},{3,4},{4,3},{5,6},{6,5},{9,10},{10,9},{11,12},{12,11},... | collective-permute-start | bytes 2359304 | tf_op jit(solution)/shard_map/ppermute | solution.py:418
  16.2 0.0 copy-done.1
  16.2 0.7 copy.8.table_ref
  16.9 0.0 collective-permute-done.even_ref
  16.9 0.0 copy-start
  16.9 2.1 %collective-permute-start.1 = (bf16[512,384]{1,0:T(8,128)(2,1)}, bf16[512,384]{1,0:T(8,128)(2,1)}, u32[]{:S(2)}, u32[]{:S(2)}) collective-permute-start(bf16[512,384]{1,0:T(8,128)(2,1)} %get-tuple-element.34), channel_id=1, source_target_pairs={{0,0},{1,1},{2,8},{3,9},{4,16},{5,17},{6,24},{7,25},{8,2},{9,3},{1... | collective-permute-start | bytes 1179656 | tf_op jit(solution)/shard_map/ppermute | solution.py:429
  19.0 3.3 %collective-permute-start.2 = (bf16[512,384]{1,0:T(8,128)(2,1)}, bf16[512,384]{1,0:T(8,128)(2,1)}, u32[]{:S(2)}, u32[]{:S(2)}) collective-permute-start(bf16[512,384]{1,0:T(8,128)(2,1)} %get-tuple-element.35), channel_id=1, source_target_pairs={{0,2},{2,10},{4,18},{6,26},{8,4},{9,1},{10,12},{11,9},{12,20},{13,... | collective-permute-start | bytes 1179656 | tf_op jit(solution)/shard_map/ppermute | solution.py:429
  22.3 4.0 %stencils.1 = (f32[7,16,128]{2,1,0:T(8,128)}, f32[7,8,128]{2,1,0:T(8,128)}, bf16[3072,256]{1,0:T(8,128)(2,1)}, bf16[3072,256]{1,0:T(8,128)(2,1)}) custom-call(f32[16,2]{1,0:T(8,128)} %copy.8.table_ref, f32[16]{0:T(128)} %diffuse_ref.1, s32[3,64]{1,0:T(4,128)} %index_ref, s32[15]{0:T(128)} %stack.63.where_ref), custom_call_target="tpu_custom_call" | custom-call | flops 1 | bytes 1 | tf_op jit(solution)/shard_map/stencils/pallas_call | solution.py:105
  26.4 0.0 collective-permute-done.3.odd_ref
  26.4 0.0 copy-done
  26.4 16.7 %rows_operator.2 = (bf16[2048,1024]{1,0:T(8,128)(2,1)}, bf16[4096,768]{1,0:T(8,128)(2,1)}) custom-call(s32[15]{0:T(128)} %stack.63.where_ref, f32[7,16,128]{2,1,0:T(8,128)} %get-tuple-element.32.stencil_ref, f32[2048,1024]{1,0:T(8,128)} %p_ref.5, bf16[384,1024]{1,0:T(8,128)(2,1)} %copy-done, bf16[384,1024]{1,0:T(8,128)(2,1)} %collective-permute-done.3.odd_ref), custom_call_target="tpu_custom_call" | custom-call | flops 1 | bytes 1 | tf_op jit(solution)/shard_map/rows_operator/pallas_call | solution.py:378
  43.1 4.1 %collective-permute-done.4.rest_0_ = bf16[1024,384]{1,0:T(8,128)(2,1)} collective-permute-done((bf16[1024,384]{1,0:T(8,128)(2,1)}, bf16[1024,384]{1,0:T(8,128)(2,1)}, u32[]{:S(2)}, u32[]{:S(2)}) %collective-permute-start.4) | collective-permute-done | bytes 786464 | tf_op jit(solution)/shard_map/ppermute | solution.py:418
  47.2 0.0 collective-permute-done.5.rest_1_
  47.2 0.0 collective-permute-start.6
  47.2 4.7 %collective-permute-start.7 = (bf16[512,384]{1,0:T(8,128)(2,1)}, bf16[512,384]{1,0:T(8,128)(2,1)S(1)}, u32[]{:S(2)}, u32[]{:S(2)}) collective-permute-start(bf16[512,384]{1,0:T(8,128)(2,1)} %get-tuple-element.44), channel_id=1, source_target_pairs={{1,2},{2,1},{3,4},{4,3},{5,6},{6,5},{9,10},{10,9},{11,12},{12,11},... | collective-permute-start | bytes 1179656 | tf_op jit(solution)/shard_map/ppermute | solution.py:418
  51.9 10.9 %columns_operator.2 = (bf16[2048,1024]{1,0:T(8,128)(2,1)}, bf16[384,1024]{1,0:T(8,128)(2,1)}, bf16[384,1024]{1,0:T(8,128)(2,1)}) custom-call(s32[15]{0:T(128)} %stack.63.where_ref, f32[7,8,128]{2,1,0:T(8,128)} %get-tuple-element.33.stencil_ref, f32[2048,1024]{1,0:T(8,128)} %p_ref.5, bf16[1024,384]{1,0:T(8,128)(2,1)} %collective-permute-done.4.rest_0_, ...), custom_call_target="tpu_custom_call" | custom-call | flops 1 | bytes 1 | tf_op jit(solution)/shard_map/columns_operator/pallas_call | solution.py:249
  62.7 0.0 collective-permute-start.8
  62.8 0.0 collective-permute-done.1.rest_0_
  62.8 3.7 %collective-permute-start.9 = (bf16[384,1024]{1,0:T(8,128)(2,1)}, bf16[384,1024]{1,0:T(8,128)(2,1)}, u32[]{:S(2)}, u32[]{:S(2)}) collective-permute-start(bf16[384,1024]{1,0:T(8,128)(2,1)} %get-tuple-element.51), channel_id=1, source_target_pairs={{8,16},{16,8},{9,17},{17,9},{10,18},{18,10},{11,19},{19,11},{12,20... | collective-permute-start | bytes 2359304 | tf_op jit(solution)/shard_map/ppermute | solution.py:418
  66.4 0.0 collective-permute-done.2.rest_1_
  66.4 0.4 collective-permute-done.6.rest_2_
  66.9 0.0 copy-start.2
  66.9 0.0 collective-permute-done.7.rest_3_
  66.9 0.0 copy-start.3
  66.9 0.7 copy-done.2
  67.6 0.1 copy-done.3
  67.8 10.4 %columns_operator.3.x_ref = bf16[2048,1024]{1,0:T(8,128)(2,1)} custom-call(s32[15]{0:T(128)} %stack.63.where_ref, f32[7,8,128]{2,1,0:T(8,128)} %get-tuple-element.33.stencil_ref, f32[2048,1024]{1,0:T(8,128)} %p_ref.5, bf16[512,384]{1,0:T(8,128)(2,1)} %collective-permute-done.1.rest_0_, ...), custom_call_target="tpu_custom_call", output_to_operand_aliasing={{}: (9, {})} | custom-call | flops 9999999827968 | bytes 9999999827968 | tf_op jit(solution)/shard_map/columns_operator/pallas_call | solution.py:249
  78.2 0.0 collective-permute-done.8.even_ref
  78.2 0.0 collective-permute-done.9.odd_ref
  78.2 13.4 %rows_operator.3 = f32[2048,1024]{1,0:T(8,128)} custom-call(s32[15]{0:T(128)} %stack.63.where_ref, f32[7,16,128]{2,1,0:T(8,128)} %get-tuple-element.32.stencil_ref, bf16[2048,1024]{1,0:T(8,128)(2,1)} %columns_operator.3.x_ref, bf16[384,1024]{1,0:T(8,128)(2,1)} %collective-permute-done.8.even_ref, bf16[384,1024]{1,0:T(8,128)(2,1)} %collective-permute-done.9.odd_ref, ...), custom_call_target="tpu_custom_call" | custom-call | flops 1 | bytes 1 | tf_op jit(solution)/shard_map/rows_operator/pallas_call | solution.py:378
Async XLA Ops:
  1.3 14.9 %copy-start.1 = (f32[16,2]{0,1:T(2,128)S(1)}, f32[16,2]{0,1:T(2,128)}, u32[]{:S(2)}) copy-start(f32[16,2]{0,1:T(2,128)} %param.7) | copy-start | bytes 388
  8.0 8.9 %collective-permute-start = (bf16[384,1024]{1,0:T(8,128)(2,1)}, bf16[384,1024]{1,0:T(8,128)(2,1)S(1)}, u32[]{:S(2)}, u32[]{:S(2)}) collective-permute-start(bf16[384,1024]{1,0:T(8,128)(2,1)} %get-tuple-element.30), channel_id=1, source_target_pairs={{0,8},{8,0},{16,24},{24,16},{1,9},{9,1},{17,25},{25,17},{2,10},{10... | collective-permute-start | bytes 2359304 | tf_op jit(solution)/shard_map/ppermute | solution.py:418
  8.7 17.6 %collective-permute-start.3 = (bf16[384,1024]{1,0:T(8,128)(2,1)}, bf16[384,1024]{1,0:T(8,128)(2,1)}, u32[]{:S(2)}, u32[]{:S(2)}) collective-permute-start(bf16[384,1024]{1,0:T(8,128)(2,1)} %get-tuple-element.37), channel_id=1, source_target_pairs={{8,16},{16,8},{9,17},{17,9},{10,18},{18,10},{11,19},{19,11},{12,20... | collective-permute-start | bytes 2359304 | tf_op jit(solution)/shard_map/ppermute | solution.py:418
  11.7 35.4 %collective-permute-start.4 = (bf16[1024,384]{1,0:T(8,128)(2,1)}, bf16[1024,384]{1,0:T(8,128)(2,1)}, u32[]{:S(2)}, u32[]{:S(2)}) collective-permute-start(bf16[1024,384]{1,0:T(8,128)(2,1)} %get-tuple-element.39), channel_id=1, source_target_pairs={{0,1},{1,0},{2,3},{3,2},{4,5},{5,4},{6,7},{7,6},{8,9},{9,8},{10,11... | collective-permute-start | bytes 2359304 | tf_op jit(solution)/shard_map/ppermute | solution.py:418
  12.0 35.2 %collective-permute-start.5 = (bf16[1024,384]{1,0:T(8,128)(2,1)}, bf16[1024,384]{1,0:T(8,128)(2,1)}, u32[]{:S(2)}, u32[]{:S(2)}) collective-permute-start(bf16[1024,384]{1,0:T(8,128)(2,1)} %get-tuple-element.40), channel_id=1, source_target_pairs={{1,2},{2,1},{3,4},{4,3},{5,6},{6,5},{9,10},{10,9},{11,12},{12,11},... | collective-permute-start | bytes 2359304 | tf_op jit(solution)/shard_map/ppermute | solution.py:418
  16.9 9.5 %copy-start = (bf16[384,1024]{1,0:T(8,128)(2,1)}, bf16[384,1024]{1,0:T(8,128)(2,1)S(1)}, u32[]{:S(2)}) copy-start(bf16[384,1024]{1,0:T(8,128)(2,1)S(1)} %collective-permute-done.even_ref) | copy-start | bytes 2359300
  16.9 45.9 %collective-permute-start.1 = (bf16[512,384]{1,0:T(8,128)(2,1)}, bf16[512,384]{1,0:T(8,128)(2,1)}, u32[]{:S(2)}, u32[]{:S(2)}) collective-permute-start(bf16[512,384]{1,0:T(8,128)(2,1)} %get-tuple-element.34), channel_id=1, source_target_pairs={{0,0},{1,1},{2,8},{3,9},{4,16},{5,17},{6,24},{7,25},{8,2},{9,3},{1... | collective-permute-start | bytes 1179656 | tf_op jit(solution)/shard_map/ppermute | solution.py:429
  19.0 47.4 %collective-permute-start.2 = (bf16[512,384]{1,0:T(8,128)(2,1)}, bf16[512,384]{1,0:T(8,128)(2,1)}, u32[]{:S(2)}, u32[]{:S(2)}) collective-permute-start(bf16[512,384]{1,0:T(8,128)(2,1)} %get-tuple-element.35), channel_id=1, source_target_pairs={{0,2},{2,10},{4,18},{6,26},{8,4},{9,1},{10,12},{11,9},{12,20},{13,... | collective-permute-start | bytes 1179656 | tf_op jit(solution)/shard_map/ppermute | solution.py:429
  47.2 19.7 %collective-permute-start.6 = (bf16[512,384]{1,0:T(8,128)(2,1)}, bf16[512,384]{1,0:T(8,128)(2,1)S(1)}, u32[]{:S(2)}, u32[]{:S(2)}) collective-permute-start(bf16[512,384]{1,0:T(8,128)(2,1)} %get-tuple-element.43), channel_id=1, source_target_pairs={{0,1},{1,0},{2,3},{3,2},{4,5},{5,4},{6,7},{7,6},{8,9},{9,8},{10,11... | collective-permute-start | bytes 1179656 | tf_op jit(solution)/shard_map/ppermute | solution.py:418
  47.2 19.7 %collective-permute-start.7 = (bf16[512,384]{1,0:T(8,128)(2,1)}, bf16[512,384]{1,0:T(8,128)(2,1)S(1)}, u32[]{:S(2)}, u32[]{:S(2)}) collective-permute-start(bf16[512,384]{1,0:T(8,128)(2,1)} %get-tuple-element.44), channel_id=1, source_target_pairs={{1,2},{2,1},{3,4},{4,3},{5,6},{6,5},{9,10},{10,9},{11,12},{12,11},... | collective-permute-start | bytes 1179656 | tf_op jit(solution)/shard_map/ppermute | solution.py:418
  62.7 15.4 %collective-permute-start.8 = (bf16[384,1024]{1,0:T(8,128)(2,1)}, bf16[384,1024]{1,0:T(8,128)(2,1)}, u32[]{:S(2)}, u32[]{:S(2)}) collective-permute-start(bf16[384,1024]{1,0:T(8,128)(2,1)} %get-tuple-element.50), channel_id=1, source_target_pairs={{0,8},{8,0},{16,24},{24,16},{1,9},{9,1},{17,25},{25,17},{2,10},{10... | collective-permute-start | bytes 2359304 | tf_op jit(solution)/shard_map/ppermute | solution.py:418
  62.8 15.4 %collective-permute-start.9 = (bf16[384,1024]{1,0:T(8,128)(2,1)}, bf16[384,1024]{1,0:T(8,128)(2,1)}, u32[]{:S(2)}, u32[]{:S(2)}) collective-permute-start(bf16[384,1024]{1,0:T(8,128)(2,1)} %get-tuple-element.51), channel_id=1, source_target_pairs={{8,16},{16,8},{9,17},{17,9},{10,18},{18,10},{11,19},{19,11},{12,20... | collective-permute-start | bytes 2359304 | tf_op jit(solution)/shard_map/ppermute | solution.py:418
  66.9 0.7 copy-start.2
  66.9 0.9 copy-start.3

commit v5 on v4

--- a/solution.py
+++ b/solution.py
@@ -67,13 +67,32 @@
     return rows
 
 
+def swept(planes, weights):
+    for step_no, (c, e, w, n, s) in enumerate(weights):
+        fresh = []
+        for i in range(1, len(planes) - 1):
+            at, u = i + step_no, planes[i]
+            nlon = u.shape[1]
+            fresh.append(
+                c(at) * u
+                + e(at) * pltpu.roll(u, nlon - 1, 1)
+                + w(at) * pltpu.roll(u, 1, 1)
+                + n(at) * planes[i + 1]
+                + s(at) * planes[i - 1]
+            )
+        planes = fresh
+    return planes
+
+
 def stencils(wind_table, diffusivity, wind_index, where, lat_rows, lats, nlon):
     steps, nlat = wind_index.shape
     sizes = (lat_rows, lats)
     span = 2 * steps * nlon
     pairs = lats // 2
 
-    def kernel(table_ref, diffuse_ref, index_ref, where_ref, row_out, col_out, high_out, low_out, *scratch):
+    def kernel(
+        table_ref, diffuse_ref, index_ref, where_ref, row_out, col_out, high_out, low_out, step_out, *scratch
+    ):
         for side, out in enumerate((row_out, col_out)):
             looked_up = scratch[side]
             terms = []
@@ -91,6 +110,9 @@
                     for term in stencil_terms(looked_up[0], looked_up[1], looked_up[2])
                 ]
                 terms.append((c, w, e, n, s) if side else (c, e, w, n, s))
+                if side:
+                    for member, value in enumerate((c, e, w, n, s)):
+                        step_out[5 * step_no + member] = value
             for d, value in composed(terms, sizes[side], nlon).items():
                 out[d + steps] = value
         for q in range(pairs):
@@ -106,7 +128,8 @@
         kernel,
         in_specs=[pl.BlockSpec(memory_space=pltpu.SMEM)] * 4,
         out_shape=[jax.ShapeDtypeStruct((2 * steps + 1, size, nlon), F32) for size in sizes]
-        + [jax.ShapeDtypeStruct((pairs * span, 2 * nlon), BF16)] * 2,
+        + [jax.ShapeDtypeStruct((pairs * span, 2 * nlon), BF16)] * 2
+        + [jax.ShapeDtypeStruct((5 * steps, lats + 2 * steps, nlon), F32)],
         scratch_shapes=[pltpu.VMEM((4, size + 2 * steps, nlon), F32) for size in sizes],
         compiler_params=params(),
         cost_estimate=cost(1),
@@ -175,10 +198,12 @@
     size = unit * nlon
     span = 2 * steps * nlon
     pairs = lats // 2
+    part = nlon // 2
+    upper = size - part * (3 * size // (8 * part))
 
     def kernel(where_ref, stencil_ref, p_ref, *rest):
         halo_refs, rest = rest[: 2 * len(halos)], rest[2 * len(halos) :]
-        (b_high, b_low), outs, data_ref = rest[:2], rest[2:-1], rest[-1]
+        (b_high, b_low, step_ref), outs, data_ref = rest[:3], rest[3:-1], rest[-1]
         if held is not None:
             outs = outs[1:]
         t_ref = outs[0]
@@ -204,18 +229,41 @@
                 data_ref[:size, :wide] = odd_ref[...]
                 data_ref[:size, wide + cols :] = even_ref[...]
 
-        data_ref[:size, wide : wide + cols], data_ref[size:, wide : wide + cols] = split(p_ref[...])
-        for q in range(pairs):
-            window = slice((2 * q + 1) * nlon, (2 * q + 1) * nlon + span)
-            of = pl.ds(q * span, span)
-            both = product(data_ref[:, window], b_high[of, :])
-            total = both[:size] + both[size:] + product(data_ref[:size, window], b_low[of, :])
-            for a, k, d in ((0, 2 * q, -steps), (1, 2 * q + 2 * steps + 1, steps)):
-                far = slice(k * nlon, (k + 1) * nlon)
-                weight = jnp.sum(stencil_ref[d + steps, 2 * q + a : 2 * q + a + 1, :], axis=1, keepdims=True)
-                far_values = data_ref[:size, far].astype(F32) + data_ref[size:, far].astype(F32)
-                value = total[:, a * nlon : (a + 1) * nlon] + weight * far_values
-                t_ref[:, (2 * q + a) * nlon : (2 * q + a + 1) * nlon] = value.astype(BF16)
+        data_ref[:upper, wide : wide + cols], data_ref[size : size + upper, wide : wide + cols] = split(
+            p_ref[:upper, :]
+        )
+        weights = [
+            [
+                lambda at, k=5 * step_no + member: step_ref[k, at : at + 1, :]
+                for member in range(5)
+            ]
+            for step_no in range(steps)
+        ]
+        starts = list(range(upper, size, part))
+        for q in range(max(pairs, len(starts))):
+            if q < pairs:
+                window = slice((2 * q + 1) * nlon, (2 * q + 1) * nlon + span)
+                of = pl.ds(q * span, span)
+                total = product(data_ref[:upper, window], b_high[of, :])
+                total += product(data_ref[size : size + upper, window], b_high[of, :])
+                total += product(data_ref[:upper, window], b_low[of, :])
+                for a, k, d in ((0, 2 * q, -steps), (1, 2 * q + 2 * steps + 1, steps)):
+                    far = slice(k * nlon, (k + 1) * nlon)
+                    row = stencil_ref[d + steps, 2 * q + a : 2 * q + a + 1, :]
+                    weight = jnp.sum(row, axis=1, keepdims=True)
+                    far_values = data_ref[:upper, far].astype(F32) + data_ref[size : size + upper, far].astype(F32)
+                    value = total[:, a * nlon : (a + 1) * nlon] + weight * far_values
+                    t_ref[:upper, (2 * q + a) * nlon : (2 * q + a + 1) * nlon] = value.astype(BF16)
+            if q < len(starts):
+                rows_at = slice(starts[q], starts[q] + part)
+                planes = []
+                for k in range(lats + 2 * steps):
+                    if steps <= k < steps + lats:
+                        planes.append(p_ref[rows_at, (k - steps) * nlon : (k - steps + 1) * nlon])
+                    else:
+                        planes.append(data_ref[rows_at, k * nlon : (k + 1) * nlon].astype(F32))
+                for k, plane in enumerate(swept(planes, weights)):
+                    t_ref[rows_at, k * nlon : (k + 1) * nlon] = plane.astype(BF16)
         if ends:
             for odd in range(2):
                 is_odd = row_odd if odd else jnp.logical_not(row_odd)
@@ -234,7 +282,7 @@
         pl.BlockSpec((size, cols), lambda i, at: (block_at(i, at), 0)),
     ]
     in_specs += [pl.BlockSpec((size, wide), halo_at)] * (2 * len(halos))
-    in_specs += [pl.BlockSpec(block.shape, lambda i, at: (0, 0)) for block in blocks]
+    in_specs += [pl.BlockSpec(block.shape, lambda i, at, n=block.ndim: (0,) * n) for block in blocks]
     out_specs = [pl.BlockSpec((size, cols), lambda i, at: (block_at(i, at), 0))]
     out_shape = [jax.ShapeDtypeStruct((rows, cols), BF16)]
     operands = [where, stencil, covariance] + [array for pair in halos for array in pair] + list(blocks)
@@ -472,12 +520,15 @@
         for k in range(2)
     ]
     pieces += [((13 + k,), wide, 0, cols_dev, k + 2, 0, 0) for k in range(2)]
-    pieces += [((8 + k,), wide, (10,), inner, k + 4, 0, nlon) for k in range(2)]
-    pieces += [((7,), inner, (11 + k,), wide, k + 6, 0, 0) for k in range(2)]
+    others = [((8 + k,), wide, (10,), inner, k, 0, nlon) for k in range(2)]
+    others += [((7,), inner, (11 + k,), wide, k + 2, 0, 0) for k in range(2)]
     sent = packed(covariance, where, pieces)
-    outers, ends, mirrors, inners = [list(sent[k : k + 2]) for k in range(0, 8, 2)]
+    outers, ends = list(sent[:2]), list(sent[2:])
     outers = [exchanged(piece, "col", k) for k, piece in enumerate(outers)]
     ends = [exchanged(piece, "row", k) for k, piece in enumerate(ends)]
+    late, ends[0] = lax.optimization_barrier((where, ends[0]))
+    sent = packed(covariance, late, others)
+    mirrors, inners = list(sent[:2]), list(sent[2:])
     mirrors[0], mirrors[1], wind_index, ends[0] = lax.optimization_barrier(
         (mirrors[0], mirrors[1], wind_index, ends[0])
     )

time: 92.9 us -> 89.6 us (0.964)
  waiting for transfers between devices: 4.55 us -> 1.65 us
  starting transfers between devices: 21.9 us -> 22.9 us
    pallas_call x2, Pallas kernels: 21.3 us -> 18.3 us  [columns_operator(): pl.pallas_call(kernel, grid_spec=pltpu.PrefetchScalarGridSpec(num_scalar_...]
    ppermute x8, waiting for transfers between devices: 4.55 us -> 1.64 us  [exchanged(): return lax.ppermute(block, axis, pairs)]
    pallas_call x1 -> x2, Pallas kernels: 6.64 us -> 8.74 us  [packed(): pl.pallas_call(kernel, in_specs=[pl.BlockSpec(memory_space=pltpu.SMEM), p...]
  transfers between devices with their start and end apart: 10 -> 10, of which waited for: 2 -> 2; matrix products, arithmetic and copies ran while one was open for 1% -> 1% of each run, Pallas kernels for 46% -> 48%
where the time goes in v5:
time: 89.6 us; the launch traced here: 88.1 us
  Pallas kernels  61.2 us (68%)
  starting transfers between devices  22.9 us (26%)
  waiting for transfers between devices  1.65 us (2%)
  local copies, waits for them, and re-layouts  1.38 us (2%)
  between operations  0.97 us (1%)
    pallas_call x2, Pallas kernels, rows_operator(): pl.pallas_call(kernel, grid_spec=pltpu.PrefetchScalarGridSpec(num_scalar_...  30.1 us
    pallas_call x2, Pallas kernels, columns_operator(): pl.pallas_call(kernel, grid_spec=pltpu.PrefetchScalarGridSpec(num_scalar_...  18.3 us
    ppermute x8, starting transfers between devices, exchanged(): return lax.ppermute(block, axis, pairs)  17.5 us
    pallas_call x2, Pallas kernels, packed(): pl.pallas_call(kernel, in_specs=[pl.BlockSpec(memory_space=pltpu.SMEM), p...  8.74 us
    ppermute x2, starting transfers between devices, mirrored(): return lax.ppermute(block, ('row', 'col'), pairs)  5.42 us
    pallas_call x1, Pallas kernels, stencils(): pl.pallas_call(kernel, in_specs=[pl.BlockSpec(memory_space=pltpu.SMEM)] *...  4.06 us
  transfers between devices with their start and end apart: 10, of which 2 were waited for; matrix products, arithmetic and copies ran while one was open for 1% of the time, Pallas kernels for 48%

profile of v5, /device:TPU:5, one launch (start us, length us, event | category | flops | bytes accessed | tf_op | source)
XLA Modules:
  0.0 88.1 jit_solution(6275731388597665690)
XLA Ops:
  0.7 0.7 stack.63.where_ref
  1.4 0.0 copy-start.1
  1.4 5.4 %packed.2 = (bf16[1024,384]{1,0:T(8,128)(2,1)}, bf16[1024,384]{1,0:T(8,128)(2,1)}, bf16[384,1024]{1,0:T(8,128)(2,1)}, bf16[384,1024]{1,0:T(8,128)(2,1)}) custom-call(s32[15]{0:T(128)} %stack.63.where_ref, f32[2048,1024]{1,0:T(8,128)} %p_ref.7), custom_call_target="tpu_custom_call" | custom-call | flops 1 | bytes 1 | tf_op jit(solution)/shard_map/packed/pallas_call | solution.py:178
  6.7 0.7 collective-permute-start
  7.5 3.0 %collective-permute-start.3 = (bf16[384,1024]{1,0:T(8,128)(2,1)}, bf16[384,1024]{1,0:T(8,128)(2,1)}, u32[]{:S(2)}, u32[]{:S(2)}) collective-permute-start(bf16[384,1024]{1,0:T(8,128)(2,1)} %get-tuple-element.42), channel_id=1, source_target_pairs={{8,16},{16,8},{9,17},{17,9},{10,18},{18,10},{11,19},{19,11},{12,20... | collective-permute-start | bytes 2359304 | tf_op jit(solution)/shard_map/ppermute | solution.py:466
  10.5 0.3 collective-permute-start.4
  10.8 4.2 %collective-permute-start.5 = (bf16[1024,384]{1,0:T(8,128)(2,1)}, bf16[1024,384]{1,0:T(8,128)(2,1)}, u32[]{:S(2)}, u32[]{:S(2)}) collective-permute-start(bf16[1024,384]{1,0:T(8,128)(2,1)} %get-tuple-element.45), channel_id=1, source_target_pairs={{1,2},{2,1},{3,4},{4,3},{5,6},{6,5},{9,10},{10,9},{11,12},{12,11},... | collective-permute-start | bytes 2359304 | tf_op jit(solution)/shard_map/ppermute | solution.py:466
  15.0 0.0 copy-done.1
  15.0 0.7 copy.8.table_ref
  15.7 0.0 collective-permute-done.even_ref
  15.7 3.4 %packed.3 = (bf16[512,384]{1,0:T(8,128)(2,1)}, bf16[512,384]{1,0:T(8,128)(2,1)}, bf16[512,384]{1,0:T(8,128)(2,1)}, bf16[512,384]{1,0:T(8,128)(2,1)}) custom-call(s32[15]{0:T(128)} %stack.63.where_ref, f32[2048,1024]{1,0:T(8,128)} %p_ref.7), custom_call_target="tpu_custom_call" | custom-call | flops 1 | bytes 1 | tf_op jit(solution)/shard_map/packed/pallas_call | solution.py:178
  19.1 2.1 %collective-permute-start.1 = (bf16[512,384]{1,0:T(8,128)(2,1)}, bf16[512,384]{1,0:T(8,128)(2,1)}, u32[]{:S(2)}, u32[]{:S(2)}) collective-permute-start(bf16[512,384]{1,0:T(8,128)(2,1)} %get-tuple-element.39), channel_id=1, source_target_pairs={{0,0},{1,1},{2,8},{3,9},{4,16},{5,17},{6,24},{7,25},{8,2},{9,3},{1... | collective-permute-start | bytes 1179656 | tf_op jit(solution)/shard_map/ppermute | solution.py:477
  21.2 3.3 %collective-permute-start.2 = (bf16[512,384]{1,0:T(8,128)(2,1)}, bf16[512,384]{1,0:T(8,128)(2,1)}, u32[]{:S(2)}, u32[]{:S(2)}) collective-permute-start(bf16[512,384]{1,0:T(8,128)(2,1)} %get-tuple-element.40), channel_id=1, source_target_pairs={{0,2},{2,10},{4,18},{6,26},{8,4},{9,1},{10,12},{11,9},{12,20},{13,... | collective-permute-start | bytes 1179656 | tf_op jit(solution)/shard_map/ppermute | solution.py:477
  24.5 4.1 %stencils.1 = (f32[7,16,128]{2,1,0:T(8,128)}, f32[7,8,128]{2,1,0:T(8,128)}, bf16[3072,256]{1,0:T(8,128)(2,1)}, bf16[3072,256]{1,0:T(8,128)(2,1)}, f32[15,14,128]{2,1,0:T(8,128)}) custom-call(f32[16,2]{1,0:T(8,128)} %copy.8.table_ref, f32[16]{0:T(128)} %diffuse_ref.1, s32[3,64]{1,0:T(4,128)} %index_ref, s32[15]{0:T(128)} %stack.63.where_ref), custom_call_target="tpu_custom_call" | custom-call | flops 1 | bytes 1 | tf_op jit(solution)/shard_map/stencils/pallas_call | solution.py:127
  28.6 0.0 collective-permute-done.3.odd_ref
  28.6 16.7 %rows_operator.2 = (bf16[2048,1024]{1,0:T(8,128)(2,1)}, bf16[4096,768]{1,0:T(8,128)(2,1)}) custom-call(s32[15]{0:T(128)} %stack.63.where_ref, f32[7,16,128]{2,1,0:T(8,128)} %get-tuple-element.37.stencil_ref, f32[2048,1024]{1,0:T(8,128)} %p_ref.7, bf16[384,1024]{1,0:T(8,128)(2,1)} %collective-permute-done.even_ref, ...), custom_call_target="tpu_custom_call" | custom-call | flops 1 | bytes 1 | tf_op jit(solution)/shard_map/rows_operator/pallas_call | solution.py:426
  45.3 0.6 collective-permute-done.4.rest_0_
  45.9 0.0 copy-start
  45.9 0.0 collective-permute-done.5.rest_1_
  45.9 0.6 collective-permute-start.6
  46.4 4.3 %collective-permute-start.7 = (bf16[512,384]{1,0:T(8,128)(2,1)}, bf16[512,384]{1,0:T(8,128)(2,1)}, u32[]{:S(2)}, u32[]{:S(2)}) collective-permute-start(bf16[512,384]{1,0:T(8,128)(2,1)} %get-tuple-element.49), channel_id=1, source_target_pairs={{1,2},{2,1},{3,4},{4,3},{5,6},{6,5},{9,10},{10,9},{11,12},{12,11},... | collective-permute-start | bytes 1179656 | tf_op jit(solution)/shard_map/ppermute | solution.py:466
  50.7 0.0 copy-done
  50.7 9.4 %columns_operator.2 = (bf16[2048,1024]{1,0:T(8,128)(2,1)}, bf16[384,1024]{1,0:T(8,128)(2,1)}, bf16[384,1024]{1,0:T(8,128)(2,1)}) custom-call(s32[15]{0:T(128)} %stack.63.where_ref, f32[7,8,128]{2,1,0:T(8,128)} %get-tuple-element.38.stencil_ref, f32[2048,1024]{1,0:T(8,128)} %p_ref.7, bf16[1024,384]{1,0:T(8,128)(2,1)} %copy-done, ...), custom_call_target="tpu_custom_call" | custom-call | flops 1 | bytes 1 | tf_op jit(solution)/shard_map/columns_operator/pallas_call | solution.py:297
  60.2 0.0 collective-permute-start.8
  60.2 0.0 collective-permute-done.1.rest_0_
  60.2 4.4 %collective-permute-start.9 = (bf16[384,1024]{1,0:T(8,128)(2,1)}, bf16[384,1024]{1,0:T(8,128)(2,1)}, u32[]{:S(2)}, u32[]{:S(2)}) collective-permute-start(bf16[384,1024]{1,0:T(8,128)(2,1)} %get-tuple-element.57), channel_id=1, source_target_pairs={{8,16},{16,8},{9,17},{17,9},{10,18},{18,10},{11,19},{19,11},{12,20... | collective-permute-start | bytes 2359304 | tf_op jit(solution)/shard_map/ppermute | solution.py:466
  64.6 0.0 collective-permute-done.2.rest_1_
  64.6 1.0 %collective-permute-done.6.rest_2_ = bf16[512,384]{1,0:T(8,128)(2,1)} collective-permute-done((bf16[512,384]{1,0:T(8,128)(2,1)}, bf16[512,384]{1,0:T(8,128)(2,1)}, u32[]{:S(2)}, u32[]{:S(2)}) %collective-permute-start.6) | collective-permute-done | bytes 393248 | tf_op jit(solution)/shard_map/ppermute | solution.py:466
  65.7 0.0 collective-permute-done.7.rest_3_
  65.7 8.9 %columns_operator.3.x_ref = bf16[2048,1024]{1,0:T(8,128)(2,1)} custom-call(s32[15]{0:T(128)} %stack.63.where_ref, f32[7,8,128]{2,1,0:T(8,128)} %get-tuple-element.38.stencil_ref, f32[2048,1024]{1,0:T(8,128)} %p_ref.7, bf16[512,384]{1,0:T(8,128)(2,1)} %collective-permute-done.1.rest_0_, ...), custom_call_target="tpu_custom_call", output_to_operand_aliasing={{}: (10, {})} | custom-call | flops 9999999827968 | bytes 9999999827968 | tf_op jit(solution)/shard_map/columns_operator/pallas_call | solution.py:297
  74.6 0.0 collective-permute-done.8.even_ref
  74.6 0.0 collective-permute-done.9.odd_ref
  74.6 13.4 %rows_operator.3 = f32[2048,1024]{1,0:T(8,128)} custom-call(s32[15]{0:T(128)} %stack.63.where_ref, f32[7,16,128]{2,1,0:T(8,128)} %get-tuple-element.37.stencil_ref, bf16[2048,1024]{1,0:T(8,128)(2,1)} %columns_operator.3.x_ref, bf16[384,1024]{1,0:T(8,128)(2,1)} %collective-permute-done.8.even_ref, bf16[384,1024]{1,0:T(8,128)(2,1)} %collective-permute-done.9.odd_ref, ...), custom_call_target="tpu_custom_call" | custom-call | flops 1 | bytes 1 | tf_op jit(solution)/shard_map/rows_operator/pallas_call | solution.py:426
Async XLA Ops:
  1.4 13.6 %copy-start.1 = (f32[16,2]{0,1:T(2,128)S(1)}, f32[16,2]{0,1:T(2,128)}, u32[]{:S(2)}) copy-start(f32[16,2]{0,1:T(2,128)} %param.7) | copy-start | bytes 388
  6.7 8.9 %collective-permute-start = (bf16[384,1024]{1,0:T(8,128)(2,1)}, bf16[384,1024]{1,0:T(8,128)(2,1)}, u32[]{:S(2)}, u32[]{:S(2)}) collective-permute-start(bf16[384,1024]{1,0:T(8,128)(2,1)} %get-tuple-element.31), channel_id=1, source_target_pairs={{0,8},{8,0},{16,24},{24,16},{1,9},{9,1},{17,25},{25,17},{2,10},{10... | collective-permute-start | bytes 2359304 | tf_op jit(solution)/shard_map/ppermute | solution.py:466
  7.5 21.1 %collective-permute-start.3 = (bf16[384,1024]{1,0:T(8,128)(2,1)}, bf16[384,1024]{1,0:T(8,128)(2,1)}, u32[]{:S(2)}, u32[]{:S(2)}) collective-permute-start(bf16[384,1024]{1,0:T(8,128)(2,1)} %get-tuple-element.42), channel_id=1, source_target_pairs={{8,16},{16,8},{9,17},{17,9},{10,18},{18,10},{11,19},{19,11},{12,20... | collective-permute-start | bytes 2359304 | tf_op jit(solution)/shard_map/ppermute | solution.py:466
  10.5 35.3 %collective-permute-start.4 = (bf16[1024,384]{1,0:T(8,128)(2,1)}, bf16[1024,384]{1,0:T(8,128)(2,1)S(1)}, u32[]{:S(2)}, u32[]{:S(2)}) collective-permute-start(bf16[1024,384]{1,0:T(8,128)(2,1)} %get-tuple-element.44), channel_id=1, source_target_pairs={{0,1},{1,0},{2,3},{3,2},{4,5},{5,4},{6,7},{7,6},{8,9},{9,8},{10,11... | collective-permute-start | bytes 2359304 | tf_op jit(solution)/shard_map/ppermute | solution.py:466
  10.8 35.1 %collective-permute-start.5 = (bf16[1024,384]{1,0:T(8,128)(2,1)}, bf16[1024,384]{1,0:T(8,128)(2,1)}, u32[]{:S(2)}, u32[]{:S(2)}) collective-permute-start(bf16[1024,384]{1,0:T(8,128)(2,1)} %get-tuple-element.45), channel_id=1, source_target_pairs={{1,2},{2,1},{3,4},{4,3},{5,6},{6,5},{9,10},{10,9},{11,12},{12,11},... | collective-permute-start | bytes 2359304 | tf_op jit(solution)/shard_map/ppermute | solution.py:466
  19.1 41.1 %collective-permute-start.1 = (bf16[512,384]{1,0:T(8,128)(2,1)}, bf16[512,384]{1,0:T(8,128)(2,1)}, u32[]{:S(2)}, u32[]{:S(2)}) collective-permute-start(bf16[512,384]{1,0:T(8,128)(2,1)} %get-tuple-element.39), channel_id=1, source_target_pairs={{0,0},{1,1},{2,8},{3,9},{4,16},{5,17},{6,24},{7,25},{8,2},{9,3},{1... | collective-permute-start | bytes 1179656 | tf_op jit(solution)/shard_map/ppermute | solution.py:477
  21.2 43.4 %collective-permute-start.2 = (bf16[512,384]{1,0:T(8,128)(2,1)}, bf16[512,384]{1,0:T(8,128)(2,1)}, u32[]{:S(2)}, u32[]{:S(2)}) collective-permute-start(bf16[512,384]{1,0:T(8,128)(2,1)} %get-tuple-element.40), channel_id=1, source_target_pairs={{0,2},{2,10},{4,18},{6,26},{8,4},{9,1},{10,12},{11,9},{12,20},{13,... | collective-permute-start | bytes 1179656 | tf_op jit(solution)/shard_map/ppermute | solution.py:477
  45.9 4.9 %copy-start = (bf16[1024,384]{1,0:T(8,128)(2,1)}, bf16[1024,384]{1,0:T(8,128)(2,1)S(1)}, u32[]{:S(2)}) copy-start(bf16[1024,384]{1,0:T(8,128)(2,1)S(1)} %collective-permute-done.4.rest_0_) | copy-start | bytes 2359300
  45.9 19.8 %collective-permute-start.6 = (bf16[512,384]{1,0:T(8,128)(2,1)}, bf16[512,384]{1,0:T(8,128)(2,1)}, u32[]{:S(2)}, u32[]{:S(2)}) collective-permute-start(bf16[512,384]{1,0:T(8,128)(2,1)} %get-tuple-element.48), channel_id=1, source_target_pairs={{0,1},{1,0},{2,3},{3,2},{4,5},{5,4},{6,7},{7,6},{8,9},{9,8},{10,11... | collective-permute-start | bytes 1179656 | tf_op jit(solution)/shard_map/ppermute | solution.py:466
  46.4 19.2 %collective-permute-start.7 = (bf16[512,384]{1,0:T(8,128)(2,1)}, bf16[512,384]{1,0:T(8,128)(2,1)}, u32[]{:S(2)}, u32[]{:S(2)}) collective-permute-start(bf16[512,384]{1,0:T(8,128)(2,1)} %get-tuple-element.49), channel_id=1, source_target_pairs={{1,2},{2,1},{3,4},{4,3},{5,6},{6,5},{9,10},{10,9},{11,12},{12,11},... | collective-permute-start | bytes 1179656 | tf_op jit(solution)/shard_map/ppermute | solution.py:466
  60.2 14.4 %collective-permute-start.8 = (bf16[384,1024]{1,0:T(8,128)(2,1)}, bf16[384,1024]{1,0:T(8,128)(2,1)}, u32[]{:S(2)}, u32[]{:S(2)}) collective-permute-start(bf16[384,1024]{1,0:T(8,128)(2,1)} %get-tuple-element.56), channel_id=1, source_target_pairs={{0,8},{8,0},{16,24},{24,16},{1,9},{9,1},{17,25},{25,17},{2,10},{10... | collective-permute-start | bytes 2359304 | tf_op jit(solution)/shard_map/ppermute | solution.py:466
  60.2 14.4 %collective-permute-start.9 = (bf16[384,1024]{1,0:T(8,128)(2,1)}, bf16[384,1024]{1,0:T(8,128)(2,1)}, u32[]{:S(2)}, u32[]{:S(2)}) collective-permute-start(bf16[384,1024]{1,0:T(8,128)(2,1)} %get-tuple-element.57), channel_id=1, source_target_pairs={{8,16},{16,8},{9,17},{17,9},{10,18},{18,10},{11,19},{19,11},{12,20... | collective-permute-start | bytes 2359304 | tf_op jit(solution)/shard_map/ppermute | solution.py:466

commit v6 on v5

--- a/solution.py
+++ b/solution.py
@@ -84,15 +84,79 @@
     return planes
 
 
-def stencils(wind_table, diffusivity, wind_index, where, lat_rows, lats, nlon):
+def packing(pieces):
+    def placed(piece):
+        _, size, _, width, _, _, turn = piece
+        return (width, size) if turn else (size, width)
+
+    shapes = {}
+    for piece in pieces:
+        shape, out = placed(piece), piece[4]
+        shapes[out] = (max(piece[5] + shape[0], shapes.get(out, (0,))[0]), shape[1])
+    count = len(pieces)
+    scratch = [pltpu.VMEM(piece[1:4:2], F32) for piece in pieces]
+    scratch += [pltpu.VMEM(placed(piece), BF16) for piece in pieces]
+    scratch += [pltpu.SemaphoreType.DMA((count,)), pltpu.SemaphoreType.DMA((count,))]
+
+    def start(where_ref, p_ref, refs):
+        first = lambda at: pl.multiple_of(where_ref[at[0]], 128) if isinstance(at, tuple) else at
+        loads = []
+        for k, (row, size, col, width, _, _, _) in enumerate(pieces):
+            source = p_ref.at[pl.ds(first(row), size), pl.ds(first(col), width)]
+            loads.append(pltpu.make_async_copy(source, refs[k], refs[2 * count].at[k]))
+            loads[-1].start()
+        return loads
+
+    def finish(loads, results, refs):
+        stores = []
+        for k, piece in enumerate(pieces):
+            loads[k].wait()
+            got, made, turn, shape = refs[k], refs[count + k], piece[6], placed(piece)
+            if turn:
+                for a in range(0, shape[0], turn):
+                    for b in range(0, shape[1], turn):
+                        made[a : a + turn, b : b + turn] = got[b : b + turn, a : a + turn].T.astype(BF16)
+            else:
+                made[...] = got[...].astype(BF16)
+            target = results[piece[4]].at[pl.ds(piece[5], shape[0]), :]
+            stores.append(pltpu.make_async_copy(made, target, refs[2 * count + 1].at[k]))
+            stores[-1].start()
+        for copy in stores:
+            copy.wait()
+
+    return [jax.ShapeDtypeStruct(shapes[k], BF16) for k in range(len(shapes))], scratch, start, finish
+
+
+def packed(covariance, where, pieces):
+    out_shape, scratch, start, finish = packing(pieces)
+
+    def kernel(where_ref, p_ref, *refs):
+        results, refs = refs[: len(out_shape)], refs[len(out_shape) :]
+        finish(start(where_ref, p_ref, refs), results, refs)
+
+    return pl.pallas_call(
+        kernel,
+        in_specs=[pl.BlockSpec(memory_space=pltpu.SMEM), pl.BlockSpec(memory_space=pl.ANY)],
+        out_specs=[pl.BlockSpec(memory_space=pl.ANY)] * len(out_shape),
+        out_shape=out_shape,
+        scratch_shapes=scratch,
+        compiler_params=params(),
+        cost_estimate=cost(1),
+        name="packed",
+    )(where, covariance)
+
+
+def stencils(wind_table, diffusivity, wind_index, where, lat_rows, lats, nlon, covariance, pieces):
     steps, nlat = wind_index.shape
     sizes = (lat_rows, lats)
     span = 2 * steps * nlon
     pairs = lats // 2
-
-    def kernel(
-        table_ref, diffuse_ref, index_ref, where_ref, row_out, col_out, high_out, low_out, step_out, *scratch
-    ):
+    packs, pack_scratch, start, finish = packing(pieces)
+
+    def kernel(table_ref, diffuse_ref, index_ref, where_ref, p_ref, *refs):
+        row_out, col_out, high_out, low_out, step_out = refs[:5]
+        results, scratch, refs = refs[5 : 5 + len(packs)], refs[5 + len(packs) :][:2], refs[7 + len(packs) :]
+        loads = start(where_ref, p_ref, refs)
         for side, out in enumerate((row_out, col_out)):
             looked_up = scratch[side]
             terms = []
@@ -101,7 +165,7 @@
                     lat = where_ref[5 + side] + i - steps
                     inside = jnp.logical_and(lat >= 0, lat < nlat)
                     entry = index_ref[step_no, jnp.clip(lat, 0, nlat - 1)]
-                    values = (table_ref[entry, 0], table_ref[entry, 1], diffuse_ref[entry], inside.astype(F32))
+                    values = (table_ref[0, entry], table_ref[1, entry], diffuse_ref[entry], inside.astype(F32))
                     for k, value in enumerate(values):
                         looked_up[k, i : i + 1, :] = jnp.full((1, nlon), value, F32)
                 here = looked_up[3] > 0.5
@@ -123,70 +187,22 @@
                     at = pl.ds(q * span + k * nlon, nlon)
                     high_out[at, a * nlon : (a + 1) * nlon] = high
                     low_out[at, a * nlon : (a + 1) * nlon] = low
+        finish(loads, results, refs)
 
     return pl.pallas_call(
         kernel,
-        in_specs=[pl.BlockSpec(memory_space=pltpu.SMEM)] * 4,
+        in_specs=[pl.BlockSpec(memory_space=pltpu.SMEM)] * 4 + [pl.BlockSpec(memory_space=pl.ANY)],
+        out_specs=[pl.BlockSpec(memory_space=pltpu.VMEM)] * 5 + [pl.BlockSpec(memory_space=pl.ANY)] * len(packs),
         out_shape=[jax.ShapeDtypeStruct((2 * steps + 1, size, nlon), F32) for size in sizes]
         + [jax.ShapeDtypeStruct((pairs * span, 2 * nlon), BF16)] * 2
-        + [jax.ShapeDtypeStruct((5 * steps, lats + 2 * steps, nlon), F32)],
-        scratch_shapes=[pltpu.VMEM((4, size + 2 * steps, nlon), F32) for size in sizes],
+        + [jax.ShapeDtypeStruct((5 * steps, lats + 2 * steps, nlon), F32)]
+        + packs,
+        scratch_shapes=[pltpu.VMEM((4, size + 2 * steps, nlon), F32) for size in sizes]
+        + pack_scratch,
         compiler_params=params(),
         cost_estimate=cost(1),
         name="stencils",
-    )(wind_table, diffusivity, wind_index, where)
-
-
-def packed(covariance, where, pieces):
-    outs = 1 + max(piece[4] for piece in pieces)
-
-    def placed(piece):
-        _, size, _, width, _, _, turn = piece
-        return (width, size) if turn else (size, width)
-
-    out_shapes = [None] * outs
-    for piece in pieces:
-        shape = placed(piece)
-        out_shapes[piece[4]] = (max(piece[5] + shape[0], (out_shapes[piece[4]] or (0,))[0]), shape[1])
-
-    def kernel(where_ref, p_ref, *refs):
-        count = len(pieces)
-        results, got, made = refs[:outs], refs[outs : outs + count], refs[outs + count : outs + 2 * count]
-        in_sem, out_sem = refs[outs + 2 * count :]
-        start = lambda at: pl.multiple_of(where_ref[at[0]], 128) if isinstance(at, tuple) else at
-        loads = []
-        for k, (row, size, col, width, _, _, _) in enumerate(pieces):
-            source = p_ref.at[pl.ds(start(row), size), pl.ds(start(col), width)]
-            loads.append(pltpu.make_async_copy(source, got[k], in_sem.at[k]))
-            loads[-1].start()
-        stores = []
-        for k, piece in enumerate(pieces):
-            loads[k].wait()
-            turn, shape = piece[6], placed(piece)
-            if turn:
-                for a in range(0, shape[0], turn):
-                    for b in range(0, shape[1], turn):
-                        made[k][a : a + turn, b : b + turn] = got[k][b : b + turn, a : a + turn].T.astype(BF16)
-            else:
-                made[k][...] = got[k][...].astype(BF16)
-            target = results[piece[4]].at[pl.ds(piece[5], shape[0]), :]
-            stores.append(pltpu.make_async_copy(made[k], target, out_sem.at[k]))
-            stores[-1].start()
-        for copy in stores:
-            copy.wait()
-
-    return pl.pallas_call(
-        kernel,
-        in_specs=[pl.BlockSpec(memory_space=pltpu.SMEM), pl.BlockSpec(memory_space=pl.ANY)],
-        out_specs=[pl.BlockSpec(memory_space=pl.ANY)] * outs,
-        out_shape=[jax.ShapeDtypeStruct(shape, BF16) for shape in out_shapes],
-        scratch_shapes=[pltpu.VMEM(piece[1:4:2], F32) for piece in pieces]
-        + [pltpu.VMEM(placed(piece), BF16) for piece in pieces]
-        + [pltpu.SemaphoreType.DMA((len(pieces),)), pltpu.SemaphoreType.DMA((len(pieces),))],
-        compiler_params=params(),
-        cost_estimate=cost(1),
-        name="packed",
-    )(where, covariance)
+    )(wind_table.T, diffusivity, wind_index, where, covariance)
 
 
 def columns_operator(
@@ -515,29 +531,28 @@
         ]
     ).astype(jnp.int32)
     pieces = [
-        (row, outer, (11 + k,), wide, k, there, 0)
-        for row, there in ((0, 0), (rows_dev - outer, outer))
+        (row, size, (11 + k,), wide, k, there, 0)
+        for row, size, there in ((0, outer, 0), (rows_dev - outer, outer, outer), (0, 16, 2 * outer))
         for k in range(2)
     ]
-    pieces += [((13 + k,), wide, 0, cols_dev, k + 2, 0, 0) for k in range(2)]
-    others = [((8 + k,), wide, (10,), inner, k, 0, nlon) for k in range(2)]
-    others += [((7,), inner, (11 + k,), wide, k + 2, 0, 0) for k in range(2)]
-    sent = packed(covariance, where, pieces)
-    outers, ends = list(sent[:2]), list(sent[2:])
+    others = [((13 + k,), wide, 0, cols_dev, k, 0, 0) for k in range(2)]
+    others += [((8 + k,), wide, (10,), inner, k + 2, 0, nlon) for k in range(2)]
+    others += [((7,), inner, (11 + k,), wide, k + 4, 0, 0) for k in range(2)]
+    outers = packed(covariance, where, pieces)
     outers = [exchanged(piece, "col", k) for k, piece in enumerate(outers)]
+    row_s, col_s, *rest = stencils(
+        wind_table, diffusivity, wind_index, where, lat_rows, lats, nlon, covariance, others
+    )
+    col_blocks, ends, mirrors, inners = rest[:3], rest[3:5], rest[5:7], rest[7:9]
     ends = [exchanged(piece, "row", k) for k, piece in enumerate(ends)]
-    late, ends[0] = lax.optimization_barrier((where, ends[0]))
-    sent = packed(covariance, late, others)
-    mirrors, inners = list(sent[:2]), list(sent[2:])
-    mirrors[0], mirrors[1], wind_index, ends[0] = lax.optimization_barrier(
-        (mirrors[0], mirrors[1], wind_index, ends[0])
-    )
     mirrors = [mirrored(piece, k) for k, piece in enumerate(mirrors)]
 
-    row_s, col_s, *col_blocks = stencils(wind_table, diffusivity, wind_index, where, lat_rows, lats, nlon)
     operator_times_prior, blocks = rows_operator(covariance, *ends, row_s, where, steps, nlon, BF16)
-    operator_times_prior, outers, inners = lax.optimization_barrier((operator_times_prior, outers, inners))
-    inners = [exchanged(piece, "col", k) for k, piece in enumerate(inners)]
+    inners[0] = exchanged(inners[0], "col", 0)
+    operator_times_prior, outers, inners[1] = lax.optimization_barrier(
+        (operator_times_prior, outers, inners[1])
+    )
+    inners[1] = exchanged(inners[1], "col", 1)
     mirror, *ends = columns_operator(
         covariance, [outers], col_s, col_blocks, where, near, steps, nlon, 2, lambda i, at: i * (lat_rows // near - 1),
         None, True,
@@ -564,7 +579,9 @@
     ends = gathered(sent, sent, "row", 0, nlon, steps, lat_rows)
     firsts = (row_id * lat_rows, col_id * lats)
     where = jnp.stack([0, 0, 1, 1, firsts[1] - firsts[0], *firsts]).astype(jnp.int32)
-    row_s, col_s, *col_blocks = stencils(wind_table, diffusivity, wind_index, where, lat_rows, lats, nlon)
+    row_s, col_s, *col_blocks = stencils(
+        wind_table, diffusivity, wind_index, where, lat_rows, lats, nlon, covariance, []
+    )
     operator_times_prior, blocks = rows_operator(covariance, *ends, row_s, where, steps, nlon, BF16)
     (mirror,) = columns_operator(
         covariance, [sides], col_s, col_blocks, where, 2, steps, nlon, lat_rows // 2, lambda i, at: i

time: 89.6 us -> 98.2 us (1.096)
  the two profiles are of different devices: /device:TPU:5 before, /device:TPU:21 now
where the time goes in v6:
time: 98.2 us; the launch traced here: 97.6 us
  Pallas kernels  60.1 us (61%)
  starting transfers between devices  25.5 us (26%)
  waiting for transfers between devices  10.2 us (10%)
  between operations  1.01 us (1%)
    pallas_call x2, Pallas kernels, rows_operator(): pl.pallas_call(kernel, grid_spec=pltpu.PrefetchScalarGridSpec(num_scalar_...  30.1 us
    ppermute x8, starting transfers between devices, exchanged(): return lax.ppermute(block, axis, pairs)  19.8 us
    pallas_call x2, Pallas kernels, columns_operator(): pl.pallas_call(kernel, grid_spec=pltpu.PrefetchScalarGridSpec(num_scalar_...  18.2 us
    ppermute x8, waiting for transfers between devices, exchanged(): return lax.ppermute(block, axis, pairs)  10.2 us
    pallas_call x1, Pallas kernels, stencils(): pl.pallas_call(kernel, in_specs=[pl.BlockSpec(memory_space=pltpu.SMEM)] *...  8.47 us
    ppermute x2, starting transfers between devices, mirrored(): return lax.ppermute(block, ('row', 'col'), pairs)  5.78 us
    pallas_call x1, Pallas kernels, packed(): pl.pallas_call(kernel, in_specs=[pl.BlockSpec(memory_space=pltpu.SMEM), p...  3.44 us
  transfers between devices with their start and end apart: 10, of which 2 were waited for; matrix products, arithmetic and copies ran while one was open for 0% of the time, Pallas kernels for 44%

profile of v6, /device:TPU:21, one launch (start us, length us, event | category | flops | bytes accessed | tf_op | source)
XLA Modules:
  0.0 97.6 jit_solution(10426521034935162224)
XLA Ops:
  0.7 0.7 stack.63.where_ref
  1.4 3.4 %packed.1 = (bf16[1040,384]{1,0:T(8,128)(2,1)}, bf16[1040,384]{1,0:T(8,128)(2,1)}) custom-call(s32[15]{0:T(128)} %stack.63.where_ref, f32[2048,1024]{1,0:T(8,128)} %p_ref.7), custom_call_target="tpu_custom_call" | custom-call | flops 1 | bytes 1 | tf_op jit(solution)/shard_map/packed/pallas_call | solution.py:137
  4.8 0.3 collective-permute-start.5
  5.1 4.2 %collective-permute-start.6 = (bf16[1040,384]{1,0:T(8,128)(2,1)}, bf16[1040,384]{1,0:T(8,128)(2,1)}, u32[]{:S(2)}, u32[]{:S(2)}) collective-permute-start(bf16[1040,384]{1,0:T(8,128)(2,1)} %get-tuple-element.33), channel_id=1, source_target_pairs={{1,2},{2,1},{3,4},{4,3},{5,6},{6,5},{9,10},{10,9},{11,12},{12,11},... | collective-permute-start | bytes 2396168 | tf_op jit(solution)/shard_map/ppermute | solution.py:482
  9.3 8.5 %stencils.1 = (f32[7,16,128]{2,1,0:T(8,128)}, f32[7,8,128]{2,1,0:T(8,128)}, bf16[3072,256]{1,0:T(8,128)(2,1)}, bf16[3072,256]{1,0:T(8,128)(2,1)}, f32[15,14,128]...) custom-call(f32[2,16]{1,0:T(2,128)} %bitcast.16, ...), custom_call_target="tpu_custom_call" | custom-call | flops 1 | bytes 1 | tf_op jit(solution)/shard_map/stencils/pallas_call | solution.py:192
  17.8 1.3 %collective-permute-start.3 = (bf16[384,1024]{1,0:T(8,128)(2,1)}, bf16[384,1024]{1,0:T(8,128)(2,1)}, u32[]{:S(2)}, u32[]{:S(2)}) collective-permute-start(bf16[384,1024]{1,0:T(8,128)(2,1)} %get-tuple-element.29), channel_id=1, source_target_pairs={{0,8},{8,0},{16,24},{24,16},{1,9},{9,1},{17,25},{25,17},{2,10},{10... | collective-permute-start | bytes 2359304 | tf_op jit(solution)/shard_map/ppermute | solution.py:482
  19.1 3.0 %collective-permute-start.4 = (bf16[384,1024]{1,0:T(8,128)(2,1)}, bf16[384,1024]{1,0:T(8,128)(2,1)}, u32[]{:S(2)}, u32[]{:S(2)}) collective-permute-start(bf16[384,1024]{1,0:T(8,128)(2,1)} %get-tuple-element.30), channel_id=1, source_target_pairs={{8,16},{16,8},{9,17},{17,9},{10,18},{18,10},{11,19},{19,11},{12,20... | collective-permute-start | bytes 2359304 | tf_op jit(solution)/shard_map/ppermute | solution.py:482
  22.1 2.4 %collective-permute-start = (bf16[512,384]{1,0:T(8,128)(2,1)}, bf16[512,384]{1,0:T(8,128)(2,1)}, u32[]{:S(2)}, u32[]{:S(2)}) collective-permute-start(bf16[512,384]{1,0:T(8,128)(2,1)} %get-tuple-element.26), channel_id=1, source_target_pairs={{0,0},{1,1},{2,8},{3,9},{4,16},{5,17},{6,24},{7,25},{8,2},{9,3},{1... | collective-permute-start | bytes 1179656 | tf_op jit(solution)/shard_map/ppermute | solution.py:493
  24.5 0.0 collective-permute-done.3.even_ref
  24.5 3.4 %collective-permute-start.1 = (bf16[512,384]{1,0:T(8,128)(2,1)}, bf16[512,384]{1,0:T(8,128)(2,1)}, u32[]{:S(2)}, u32[]{:S(2)}) collective-permute-start(bf16[512,384]{1,0:T(8,128)(2,1)} %get-tuple-element.27), channel_id=1, source_target_pairs={{0,2},{2,10},{4,18},{6,26},{8,4},{9,1},{10,12},{11,9},{12,20},{13,... | collective-permute-start | bytes 1179656 | tf_op jit(solution)/shard_map/ppermute | solution.py:493
  27.9 7.5 %collective-permute-done.4.odd_ref = bf16[384,1024]{1,0:T(8,128)(2,1)} collective-permute-done((bf16[384,1024]{1,0:T(8,128)(2,1)}, bf16[384,1024]{1,0:T(8,128)(2,1)}, u32[]{:S(2)}, u32[]{:S(2)}) %collective-permute-start.4) | collective-permute-done | bytes 786464 | tf_op jit(solution)/shard_map/ppermute | solution.py:482
  35.4 0.9 collective-permute-start.2
  36.3 16.7 %rows_operator.2 = (bf16[2048,1024]{1,0:T(8,128)(2,1)}, bf16[4096,768]{1,0:T(8,128)(2,1)}) custom-call(s32[15]{0:T(128)} %stack.63.where_ref, f32[7,16,128]{2,1,0:T(8,128)} %get-tuple-element.24.stencil_ref, f32[2048,1024]{1,0:T(8,128)} %p_ref.7, bf16[384,1024]{1,0:T(8,128)(2,1)} %collective-permute-done.3.even_ref, ...), custom_call_target="tpu_custom_call" | custom-call | flops 1 | bytes 1 | tf_op jit(solution)/shard_map/rows_operator/pallas_call | solution.py:442
  53.1 0.0 collective-permute-done.5.rest_0_
  53.1 0.0 copy-start
  53.1 0.0 collective-permute-done.6.rest_1_
  53.1 8.0 %collective-permute-start.7 = (bf16[512,384]{1,0:T(8,128)(2,1)}, bf16[512,384]{1,0:T(8,128)(2,1)}, u32[]{:S(2)}, u32[]{:S(2)}) collective-permute-start(bf16[512,384]{1,0:T(8,128)(2,1)} %get-tuple-element.35), channel_id=1, source_target_pairs={{1,2},{2,1},{3,4},{4,3},{5,6},{6,5},{9,10},{10,9},{11,12},{12,11},... | collective-permute-start | bytes 1179656 | tf_op jit(solution)/shard_map/ppermute | solution.py:482
  61.1 0.0 copy-done
  61.1 9.3 %columns_operator.2 = (bf16[2048,1024]{1,0:T(8,128)(2,1)}, bf16[384,1024]{1,0:T(8,128)(2,1)}, bf16[384,1024]{1,0:T(8,128)(2,1)}) custom-call(s32[15]{0:T(128)} %stack.63.where_ref, f32[7,8,128]{2,1,0:T(8,128)} %get-tuple-element.25.stencil_ref, f32[2048,1024]{1,0:T(8,128)} %p_ref.7, bf16[1040,384]{1,0:T(8,128)(2,1)} %copy-done, ...), custom_call_target="tpu_custom_call" | custom-call | flops 1 | bytes 1 | tf_op jit(solution)/shard_map/columns_operator/pallas_call | solution.py:313
  70.4 0.0 collective-permute-start.8
  70.4 0.0 collective-permute-done.rest_0_
  70.4 2.1 %collective-permute-start.9 = (bf16[384,1024]{1,0:T(8,128)(2,1)}, bf16[384,1024]{1,0:T(8,128)(2,1)}, u32[]{:S(2)}, u32[]{:S(2)}) collective-permute-start(bf16[384,1024]{1,0:T(8,128)(2,1)} %get-tuple-element.43), channel_id=1, source_target_pairs={{8,16},{16,8},{9,17},{17,9},{10,18},{18,10},{11,19},{19,11},{12,20... | collective-permute-start | bytes 2359304 | tf_op jit(solution)/shard_map/ppermute | solution.py:482
  72.5 0.0 collective-permute-done.1.rest_1_
  72.5 0.0 collective-permute-done.2.rest_2_
  72.5 0.0 collective-permute-done.7.rest_3_
  72.5 8.9 %columns_operator.3.x_ref = bf16[2048,1024]{1,0:T(8,128)(2,1)} custom-call(s32[15]{0:T(128)} %stack.63.where_ref, f32[7,8,128]{2,1,0:T(8,128)} %get-tuple-element.25.stencil_ref, f32[2048,1024]{1,0:T(8,128)} %p_ref.7, bf16[512,384]{1,0:T(8,128)(2,1)} %collective-permute-done.rest_0_, ...), custom_call_target="tpu_custom_call", output_to_operand_aliasing={{}: (10, {})} | custom-call | flops 9999999827968 | bytes 9999999827968 | tf_op jit(solution)/shard_map/columns_operator/pallas_call | solution.py:313
  81.4 0.0 collective-permute-done.8.even_ref
  81.4 2.6 %collective-permute-done.9.odd_ref = bf16[384,1024]{1,0:T(8,128)(2,1)} collective-permute-done((bf16[384,1024]{1,0:T(8,128)(2,1)}, bf16[384,1024]{1,0:T(8,128)(2,1)}, u32[]{:S(2)}, u32[]{:S(2)}) %collective-permute-start.9) | collective-permute-done | bytes 786464 | tf_op jit(solution)/shard_map/ppermute | solution.py:482
  84.0 13.4 %rows_operator.3 = f32[2048,1024]{1,0:T(8,128)} custom-call(s32[15]{0:T(128)} %stack.63.where_ref, f32[7,16,128]{2,1,0:T(8,128)} %get-tuple-element.24.stencil_ref, bf16[2048,1024]{1,0:T(8,128)(2,1)} %columns_operator.3.x_ref, bf16[384,1024]{1,0:T(8,128)(2,1)} %collective-permute-done.8.even_ref, bf16[384,1024]{1,0:T(8,128)(2,1)} %collective-permute-done.9.odd_ref, ...), custom_call_target="tpu_custom_call" | custom-call | flops 1 | bytes 1 | tf_op jit(solution)/shard_map/rows_operator/pallas_call | solution.py:442
Async XLA Ops:
  4.8 48.2 %collective-permute-start.5 = (bf16[1040,384]{1,0:T(8,128)(2,1)}, bf16[1040,384]{1,0:T(8,128)(2,1)S(1)}, u32[]{:S(2)}, u32[]{:S(2)}) collective-permute-start(bf16[1040,384]{1,0:T(8,128)(2,1)} %get-tuple-element.32), channel_id=1, source_target_pairs={{0,1},{1,0},{2,3},{3,2},{4,5},{5,4},{6,7},{7,6},{8,9},{9,8},{10,11... | collective-permute-start | bytes 2396168 | tf_op jit(solution)/shard_map/ppermute | solution.py:482
  5.1 48.0 %collective-permute-start.6 = (bf16[1040,384]{1,0:T(8,128)(2,1)}, bf16[1040,384]{1,0:T(8,128)(2,1)}, u32[]{:S(2)}, u32[]{:S(2)}) collective-permute-start(bf16[1040,384]{1,0:T(8,128)(2,1)} %get-tuple-element.33), channel_id=1, source_target_pairs={{1,2},{2,1},{3,4},{4,3},{5,6},{6,5},{9,10},{10,9},{11,12},{12,11},... | collective-permute-start | bytes 2396168 | tf_op jit(solution)/shard_map/ppermute | solution.py:482
  17.8 6.8 %collective-permute-start.3 = (bf16[384,1024]{1,0:T(8,128)(2,1)}, bf16[384,1024]{1,0:T(8,128)(2,1)}, u32[]{:S(2)}, u32[]{:S(2)}) collective-permute-start(bf16[384,1024]{1,0:T(8,128)(2,1)} %get-tuple-element.29), channel_id=1, source_target_pairs={{0,8},{8,0},{16,24},{24,16},{1,9},{9,1},{17,25},{25,17},{2,10},{10... | collective-permute-start | bytes 2359304 | tf_op jit(solution)/shard_map/ppermute | solution.py:482
  19.1 16.4 %collective-permute-start.4 = (bf16[384,1024]{1,0:T(8,128)(2,1)}, bf16[384,1024]{1,0:T(8,128)(2,1)}, u32[]{:S(2)}, u32[]{:S(2)}) collective-permute-start(bf16[384,1024]{1,0:T(8,128)(2,1)} %get-tuple-element.30), channel_id=1, source_target_pairs={{8,16},{16,8},{9,17},{17,9},{10,18},{18,10},{11,19},{19,11},{12,20... | collective-permute-start | bytes 2359304 | tf_op jit(solution)/shard_map/ppermute | solution.py:482
  22.1 48.3 %collective-permute-start = (bf16[512,384]{1,0:T(8,128)(2,1)}, bf16[512,384]{1,0:T(8,128)(2,1)}, u32[]{:S(2)}, u32[]{:S(2)}) collective-permute-start(bf16[512,384]{1,0:T(8,128)(2,1)} %get-tuple-element.26), channel_id=1, source_target_pairs={{0,0},{1,1},{2,8},{3,9},{4,16},{5,17},{6,24},{7,25},{8,2},{9,3},{1... | collective-permute-start | bytes 1179656 | tf_op jit(solution)/shard_map/ppermute | solution.py:493
  24.5 48.0 %collective-permute-start.1 = (bf16[512,384]{1,0:T(8,128)(2,1)}, bf16[512,384]{1,0:T(8,128)(2,1)}, u32[]{:S(2)}, u32[]{:S(2)}) collective-permute-start(bf16[512,384]{1,0:T(8,128)(2,1)} %get-tuple-element.27), channel_id=1, source_target_pairs={{0,2},{2,10},{4,18},{6,26},{8,4},{9,1},{10,12},{11,9},{12,20},{13,... | collective-permute-start | bytes 1179656 | tf_op jit(solution)/shard_map/ppermute | solution.py:493
  35.4 37.1 %collective-permute-start.2 = (bf16[512,384]{1,0:T(8,128)(2,1)}, bf16[512,384]{1,0:T(8,128)(2,1)}, u32[]{:S(2)}, u32[]{:S(2)}) collective-permute-start(bf16[512,384]{1,0:T(8,128)(2,1)} %get-tuple-element.28), channel_id=1, source_target_pairs={{0,1},{1,0},{2,3},{3,2},{4,5},{5,4},{6,7},{7,6},{8,9},{9,8},{10,11... | collective-permute-start | bytes 1179656 | tf_op jit(solution)/shard_map/ppermute | solution.py:482
  53.1 8.0 %copy-start = (bf16[1040,384]{1,0:T(8,128)(2,1)}, bf16[1040,384]{1,0:T(8,128)(2,1)S(1)}, u32[]{:S(2)}) copy-start(bf16[1040,384]{1,0:T(8,128)(2,1)S(1)} %collective-permute-done.5.rest_0_) | copy-start | bytes 2396164
  53.1 19.4 %collective-permute-start.7 = (bf16[512,384]{1,0:T(8,128)(2,1)}, bf16[512,384]{1,0:T(8,128)(2,1)}, u32[]{:S(2)}, u32[]{:S(2)}) collective-permute-start(bf16[512,384]{1,0:T(8,128)(2,1)} %get-tuple-element.35), channel_id=1, source_target_pairs={{1,2},{2,1},{3,4},{4,3},{5,6},{6,5},{9,10},{10,9},{11,12},{12,11},... | collective-permute-start | bytes 1179656 | tf_op jit(solution)/shard_map/ppermute | solution.py:482
  70.4 11.1 %collective-permute-start.8 = (bf16[384,1024]{1,0:T(8,128)(2,1)}, bf16[384,1024]{1,0:T(8,128)(2,1)}, u32[]{:S(2)}, u32[]{:S(2)}) collective-permute-start(bf16[384,1024]{1,0:T(8,128)(2,1)} %get-tuple-element.42), channel_id=1, source_target_pairs={{0,8},{8,0},{16,24},{24,16},{1,9},{9,1},{17,25},{25,17},{2,10},{10... | collective-permute-start | bytes 2359304 | tf_op jit(solution)/shard_map/ppermute | solution.py:482
  70.4 13.6 %collective-permute-start.9 = (bf16[384,1024]{1,0:T(8,128)(2,1)}, bf16[384,1024]{1,0:T(8,128)(2,1)}, u32[]{:S(2)}, u32[]{:S(2)}) collective-permute-start(bf16[384,1024]{1,0:T(8,128)(2,1)} %get-tuple-element.43), channel_id=1, source_target_pairs={{8,16},{16,8},{9,17},{17,9},{10,18},{18,10},{11,19},{19,11},{12,20... | collective-permute-start | bytes 2359304 | tf_op jit(solution)/shard_map/ppermute | solution.py:482

commit v7 on v6

--- a/solution.py
+++ b/solution.py
@@ -531,20 +531,22 @@
         ]
     ).astype(jnp.int32)
     pieces = [
-        (row, size, (11 + k,), wide, k, there, 0)
-        for row, size, there in ((0, outer, 0), (rows_dev - outer, outer, outer), (0, 16, 2 * outer))
+        (row, outer, (11 + k,), wide, k, there, 0)
+        for row, there in ((0, 0), (rows_dev - outer, outer))
         for k in range(2)
     ]
-    others = [((13 + k,), wide, 0, cols_dev, k, 0, 0) for k in range(2)]
-    others += [((8 + k,), wide, (10,), inner, k + 2, 0, nlon) for k in range(2)]
-    others += [((7,), inner, (11 + k,), wide, k + 4, 0, 0) for k in range(2)]
-    outers = packed(covariance, where, pieces)
+    pieces += [((13 + k,), wide, 0, cols_dev, k + 2, 0, 0) for k in range(2)]
+    others = [((8 + k,), wide, (10,), inner, k, 0, nlon) for k in range(2)]
+    others += [((7,), inner, (11 + k,), wide, k + 2, 0, 0) for k in range(2)]
+    sent = packed(covariance, where, pieces)
+    outers, ends = list(sent[:2]), list(sent[2:])
     outers = [exchanged(piece, "col", k) for k, piece in enumerate(outers)]
+    ends = [exchanged(piece, "row", k) for k, piece in enumerate(ends)]
+    wind_index, ends[0] = lax.optimization_barrier((wind_index, ends[0]))
     row_s, col_s, *rest = stencils(
         wind_table, diffusivity, wind_index, where, lat_rows, lats, nlon, covariance, others
     )
-    col_blocks, ends, mirrors, inners = rest[:3], rest[3:5], rest[5:7], rest[7:9]
-    ends = [exchanged(piece, "row", k) for k, piece in enumerate(ends)]
+    col_blocks, mirrors, inners = rest[:3], rest[3:5], rest[5:7]
     mirrors = [mirrored(piece, k) for k, piece in enumerate(mirrors)]
 
     operator_times_prior, blocks = rows_operator(covariance, *ends, row_s, where, steps, nlon, BF16)

time: 98.2 us -> 89.4 us (0.910)
  the two profiles are of different devices: /device:TPU:21 before, /device:TPU:19 now
where the time goes in v7:
time: 89.4 us; the launch traced here: 88.7 us
  Pallas kernels  60.4 us (68%)
  starting transfers between devices  22.3 us (25%)
  waiting for transfers between devices  4.47 us (5%)
  between operations  0.96 us (1%)
    pallas_call x2, Pallas kernels, rows_operator(): pl.pallas_call(kernel, grid_spec=pltpu.PrefetchScalarGridSpec(num_scalar_...  30.1 us
    pallas_call x2, Pallas kernels, columns_operator(): pl.pallas_call(kernel, grid_spec=pltpu.PrefetchScalarGridSpec(num_scalar_...  18.4 us
    ppermute x8, starting transfers between devices, exchanged(): return lax.ppermute(block, axis, pairs)  16.3 us
    pallas_call x1, Pallas kernels, stencils(): pl.pallas_call(kernel, in_specs=[pl.BlockSpec(memory_space=pltpu.SMEM)] *...  6.7 us
    ppermute x2, starting transfers between devices, mirrored(): return lax.ppermute(block, ('row', 'col'), pairs)  6 us
    pallas_call x1, Pallas kernels, packed(): pl.pallas_call(kernel, in_specs=[pl.BlockSpec(memory_space=pltpu.SMEM), p...  5.23 us
    ppermute x8, waiting for transfers between devices, exchanged(): return lax.ppermute(block, axis, pairs)  4.46 us
  transfers between devices with their start and end apart: 10, of which 1 were waited for; matrix products, arithmetic and copies ran while one was open for 0% of the time, Pallas kernels for 47%

profile of v7, /device:TPU:19, one launch (start us, length us, event | category | flops | bytes accessed | tf_op | source)
XLA Modules:
  0.0 88.7 jit_solution(12336132535717162060)
XLA Ops:
  0.7 0.7 stack.63.where_ref
  1.4 5.2 %packed.1 = (bf16[1024,384]{1,0:T(8,128)(2,1)}, bf16[1024,384]{1,0:T(8,128)(2,1)}, bf16[384,1024]{1,0:T(8,128)(2,1)}, bf16[384,1024]{1,0:T(8,128)(2,1)}) custom-call(s32[15]{0:T(128)} %stack.63.where_ref, f32[2048,1024]{1,0:T(8,128)} %p_ref.7), custom_call_target="tpu_custom_call" | custom-call | flops 1 | bytes 1 | tf_op jit(solution)/shard_map/packed/pallas_call | solution.py:137
  6.6 0.7 collective-permute-start
  7.4 1.6 %collective-permute-start.4 = (bf16[384,1024]{1,0:T(8,128)(2,1)}, bf16[384,1024]{1,0:T(8,128)(2,1)}, u32[]{:S(2)}, u32[]{:S(2)}) collective-permute-start(bf16[384,1024]{1,0:T(8,128)(2,1)} %get-tuple-element.34), channel_id=1, source_target_pairs={{8,16},{16,8},{9,17},{17,9},{10,18},{18,10},{11,19},{19,11},{12,20... | collective-permute-start | bytes 2359304 | tf_op jit(solution)/shard_map/ppermute | solution.py:482
  8.9 1.2 %collective-permute-start.5 = (bf16[1024,384]{1,0:T(8,128)(2,1)}, bf16[1024,384]{1,0:T(8,128)(2,1)S(1)}, u32[]{:S(2)}, u32[]{:S(2)}) collective-permute-start(bf16[1024,384]{1,0:T(8,128)(2,1)} %get-tuple-element.36), channel_id=1, source_target_pairs={{0,1},{1,0},{2,3},{3,2},{4,5},{5,4},{6,7},{7,6},{8,9},{9,8},{10,11... | collective-permute-start | bytes 2359304 | tf_op jit(solution)/shard_map/ppermute | solution.py:482
  10.2 2.0 %collective-permute-start.6 = (bf16[1024,384]{1,0:T(8,128)(2,1)}, bf16[1024,384]{1,0:T(8,128)(2,1)}, u32[]{:S(2)}, u32[]{:S(2)}) collective-permute-start(bf16[1024,384]{1,0:T(8,128)(2,1)} %get-tuple-element.37), channel_id=1, source_target_pairs={{1,2},{2,1},{3,4},{4,3},{5,6},{6,5},{9,10},{10,9},{11,12},{12,11},... | collective-permute-start | bytes 2359304 | tf_op jit(solution)/shard_map/ppermute | solution.py:482
  12.2 0.0 collective-permute-done.even_ref
  12.2 6.7 %stencils.1 = (f32[7,16,128]{2,1,0:T(8,128)}, f32[7,8,128]{2,1,0:T(8,128)}, bf16[3072,256]{1,0:T(8,128)(2,1)}, bf16[3072,256]{1,0:T(8,128)(2,1)}, f32[15,14,128]...) custom-call(f32[2,16]{1,0:T(2,128)} %bitcast.16, ...), custom_call_target="tpu_custom_call" | custom-call | flops 1 | bytes 1 | tf_op jit(solution)/shard_map/stencils/pallas_call | solution.py:192
  18.9 4.7 %collective-permute-start.1 = (bf16[512,384]{1,0:T(8,128)(2,1)}, bf16[512,384]{1,0:T(8,128)(2,1)}, u32[]{:S(2)}, u32[]{:S(2)}) collective-permute-start(bf16[512,384]{1,0:T(8,128)(2,1)} %get-tuple-element.30), channel_id=1, source_target_pairs={{0,0},{1,1},{2,8},{3,9},{4,16},{5,17},{6,24},{7,25},{8,2},{9,3},{1... | collective-permute-start | bytes 1179656 | tf_op jit(solution)/shard_map/ppermute | solution.py:493
  23.6 1.3 %collective-permute-start.2 = (bf16[512,384]{1,0:T(8,128)(2,1)}, bf16[512,384]{1,0:T(8,128)(2,1)}, u32[]{:S(2)}, u32[]{:S(2)}) collective-permute-start(bf16[512,384]{1,0:T(8,128)(2,1)} %get-tuple-element.31), channel_id=1, source_target_pairs={{0,2},{2,10},{4,18},{6,26},{8,4},{9,1},{10,12},{11,9},{12,20},{13,... | collective-permute-start | bytes 1179656 | tf_op jit(solution)/shard_map/ppermute | solution.py:493
  24.9 0.0 collective-permute-done.4.odd_ref
  24.9 4.4 %collective-permute-start.3 = (bf16[512,384]{1,0:T(8,128)(2,1)}, bf16[512,384]{1,0:T(8,128)(2,1)}, u32[]{:S(2)}, u32[]{:S(2)}) collective-permute-start(bf16[512,384]{1,0:T(8,128)(2,1)} %get-tuple-element.32), channel_id=1, source_target_pairs={{0,1},{1,0},{2,3},{3,2},{4,5},{5,4},{6,7},{7,6},{8,9},{9,8},{10,11... | collective-permute-start | bytes 1179656 | tf_op jit(solution)/shard_map/ppermute | solution.py:482
  29.4 16.7 %rows_operator.2 = (bf16[2048,1024]{1,0:T(8,128)(2,1)}, bf16[4096,768]{1,0:T(8,128)(2,1)}) custom-call(s32[15]{0:T(128)} %stack.63.where_ref, f32[7,16,128]{2,1,0:T(8,128)} %get-tuple-element.28.stencil_ref, f32[2048,1024]{1,0:T(8,128)} %p_ref.7, bf16[384,1024]{1,0:T(8,128)(2,1)} %collective-permute-done.even_ref, ...), custom_call_target="tpu_custom_call" | custom-call | flops 1 | bytes 1 | tf_op jit(solution)/shard_map/rows_operator/pallas_call | solution.py:442
  46.1 0.0 collective-permute-done.5.rest_0_
  46.1 0.0 copy-start
  46.1 0.0 collective-permute-done.6.rest_1_
  46.1 1.9 %collective-permute-start.7 = (bf16[512,384]{1,0:T(8,128)(2,1)}, bf16[512,384]{1,0:T(8,128)(2,1)}, u32[]{:S(2)}, u32[]{:S(2)}) collective-permute-start(bf16[512,384]{1,0:T(8,128)(2,1)} %get-tuple-element.39), channel_id=1, source_target_pairs={{1,2},{2,1},{3,4},{4,3},{5,6},{6,5},{9,10},{10,9},{11,12},{12,11},... | collective-permute-start | bytes 1179656 | tf_op jit(solution)/shard_map/ppermute | solution.py:482
  48.0 0.0 copy-done
  48.0 9.4 %columns_operator.2 = (bf16[2048,1024]{1,0:T(8,128)(2,1)}, bf16[384,1024]{1,0:T(8,128)(2,1)}, bf16[384,1024]{1,0:T(8,128)(2,1)}) custom-call(s32[15]{0:T(128)} %stack.63.where_ref, f32[7,8,128]{2,1,0:T(8,128)} %get-tuple-element.29.stencil_ref, f32[2048,1024]{1,0:T(8,128)} %p_ref.7, bf16[1024,384]{1,0:T(8,128)(2,1)} %copy-done, ...), custom_call_target="tpu_custom_call" | custom-call | flops 1 | bytes 1 | tf_op jit(solution)/shard_map/columns_operator/pallas_call | solution.py:313
  57.5 2.8 %collective-permute-start.8 = (bf16[384,1024]{1,0:T(8,128)(2,1)}, bf16[384,1024]{1,0:T(8,128)(2,1)}, u32[]{:S(2)}, u32[]{:S(2)}) collective-permute-start(bf16[384,1024]{1,0:T(8,128)(2,1)} %get-tuple-element.46), channel_id=1, source_target_pairs={{0,8},{8,0},{16,24},{24,16},{1,9},{9,1},{17,25},{25,17},{2,10},{10... | collective-permute-start | bytes 2359304 | tf_op jit(solution)/shard_map/ppermute | solution.py:482
  60.3 0.0 collective-permute-done.1.rest_0_
  60.3 1.5 %collective-permute-start.9 = (bf16[384,1024]{1,0:T(8,128)(2,1)}, bf16[384,1024]{1,0:T(8,128)(2,1)}, u32[]{:S(2)}, u32[]{:S(2)}) collective-permute-start(bf16[384,1024]{1,0:T(8,128)(2,1)} %get-tuple-element.47), channel_id=1, source_target_pairs={{8,16},{16,8},{9,17},{17,9},{10,18},{18,10},{11,19},{19,11},{12,20... | collective-permute-start | bytes 2359304 | tf_op jit(solution)/shard_map/ppermute | solution.py:482
  61.8 0.0 collective-permute-done.2.rest_1_
  61.8 0.0 collective-permute-done.3.rest_2_
  61.8 4.4 %collective-permute-done.7.rest_3_ = bf16[512,384]{1,0:T(8,128)(2,1)} collective-permute-done((bf16[512,384]{1,0:T(8,128)(2,1)}, bf16[512,384]{1,0:T(8,128)(2,1)}, u32[]{:S(2)}, u32[]{:S(2)}) %collective-permute-start.7) | collective-permute-done | bytes 393248 | tf_op jit(solution)/shard_map/ppermute | solution.py:482
  66.3 8.9 %columns_operator.3.x_ref = bf16[2048,1024]{1,0:T(8,128)(2,1)} custom-call(s32[15]{0:T(128)} %stack.63.where_ref, f32[7,8,128]{2,1,0:T(8,128)} %get-tuple-element.29.stencil_ref, f32[2048,1024]{1,0:T(8,128)} %p_ref.7, bf16[512,384]{1,0:T(8,128)(2,1)} %collective-permute-done.1.rest_0_, ...), custom_call_target="tpu_custom_call", output_to_operand_aliasing={{}: (10, {})} | custom-call | flops 9999999827968 | bytes 9999999827968 | tf_op jit(solution)/shard_map/columns_operator/pallas_call | solution.py:313
  75.2 0.0 collective-permute-done.8.even_ref
  75.2 0.0 collective-permute-done.9.odd_ref
  75.2 13.4 %rows_operator.3 = f32[2048,1024]{1,0:T(8,128)} custom-call(s32[15]{0:T(128)} %stack.63.where_ref, f32[7,16,128]{2,1,0:T(8,128)} %get-tuple-element.28.stencil_ref, bf16[2048,1024]{1,0:T(8,128)(2,1)} %columns_operator.3.x_ref, bf16[384,1024]{1,0:T(8,128)(2,1)} %collective-permute-done.8.even_ref, bf16[384,1024]{1,0:T(8,128)(2,1)} %collective-permute-done.9.odd_ref, ...), custom_call_target="tpu_custom_call" | custom-call | flops 1 | bytes 1 | tf_op jit(solution)/shard_map/rows_operator/pallas_call | solution.py:442
Async XLA Ops:
  6.6 5.6 %collective-permute-start = (bf16[384,1024]{1,0:T(8,128)(2,1)}, bf16[384,1024]{1,0:T(8,128)(2,1)}, u32[]{:S(2)}, u32[]{:S(2)}) collective-permute-start(bf16[384,1024]{1,0:T(8,128)(2,1)} %get-tuple-element.26), channel_id=1, source_target_pairs={{0,8},{8,0},{16,24},{24,16},{1,9},{9,1},{17,25},{25,17},{2,10},{10... | collective-permute-start | bytes 2359304 | tf_op jit(solution)/shard_map/ppermute | solution.py:482
  7.4 17.6 %collective-permute-start.4 = (bf16[384,1024]{1,0:T(8,128)(2,1)}, bf16[384,1024]{1,0:T(8,128)(2,1)}, u32[]{:S(2)}, u32[]{:S(2)}) collective-permute-start(bf16[384,1024]{1,0:T(8,128)(2,1)} %get-tuple-element.34), channel_id=1, source_target_pairs={{8,16},{16,8},{9,17},{17,9},{10,18},{18,10},{11,19},{19,11},{12,20... | collective-permute-start | bytes 2359304 | tf_op jit(solution)/shard_map/ppermute | solution.py:482
  8.9 37.2 %collective-permute-start.5 = (bf16[1024,384]{1,0:T(8,128)(2,1)}, bf16[1024,384]{1,0:T(8,128)(2,1)S(1)}, u32[]{:S(2)}, u32[]{:S(2)}) collective-permute-start(bf16[1024,384]{1,0:T(8,128)(2,1)} %get-tuple-element.36), channel_id=1, source_target_pairs={{0,1},{1,0},{2,3},{3,2},{4,5},{5,4},{6,7},{7,6},{8,9},{9,8},{10,11... | collective-permute-start | bytes 2359304 | tf_op jit(solution)/shard_map/ppermute | solution.py:482
  10.2 35.9 %collective-permute-start.6 = (bf16[1024,384]{1,0:T(8,128)(2,1)}, bf16[1024,384]{1,0:T(8,128)(2,1)}, u32[]{:S(2)}, u32[]{:S(2)}) collective-permute-start(bf16[1024,384]{1,0:T(8,128)(2,1)} %get-tuple-element.37), channel_id=1, source_target_pairs={{1,2},{2,1},{3,4},{4,3},{5,6},{6,5},{9,10},{10,9},{11,12},{12,11},... | collective-permute-start | bytes 2359304 | tf_op jit(solution)/shard_map/ppermute | solution.py:482
  18.9 41.4 %collective-permute-start.1 = (bf16[512,384]{1,0:T(8,128)(2,1)}, bf16[512,384]{1,0:T(8,128)(2,1)}, u32[]{:S(2)}, u32[]{:S(2)}) collective-permute-start(bf16[512,384]{1,0:T(8,128)(2,1)} %get-tuple-element.30), channel_id=1, source_target_pairs={{0,0},{1,1},{2,8},{3,9},{4,16},{5,17},{6,24},{7,25},{8,2},{9,3},{1... | collective-permute-start | bytes 1179656 | tf_op jit(solution)/shard_map/ppermute | solution.py:493
  23.6 38.2 %collective-permute-start.2 = (bf16[512,384]{1,0:T(8,128)(2,1)}, bf16[512,384]{1,0:T(8,128)(2,1)}, u32[]{:S(2)}, u32[]{:S(2)}) collective-permute-start(bf16[512,384]{1,0:T(8,128)(2,1)} %get-tuple-element.31), channel_id=1, source_target_pairs={{0,2},{2,10},{4,18},{6,26},{8,4},{9,1},{10,12},{11,9},{12,20},{13,... | collective-permute-start | bytes 1179656 | tf_op jit(solution)/shard_map/ppermute | solution.py:493
  24.9 36.9 %collective-permute-start.3 = (bf16[512,384]{1,0:T(8,128)(2,1)}, bf16[512,384]{1,0:T(8,128)(2,1)}, u32[]{:S(2)}, u32[]{:S(2)}) collective-permute-start(bf16[512,384]{1,0:T(8,128)(2,1)} %get-tuple-element.32), channel_id=1, source_target_pairs={{0,1},{1,0},{2,3},{3,2},{4,5},{5,4},{6,7},{7,6},{8,9},{9,8},{10,11... | collective-permute-start | bytes 1179656 | tf_op jit(solution)/shard_map/ppermute | solution.py:482
  46.1 2.0 %copy-start = (bf16[1024,384]{1,0:T(8,128)(2,1)}, bf16[1024,384]{1,0:T(8,128)(2,1)S(1)}, u32[]{:S(2)}) copy-start(bf16[1024,384]{1,0:T(8,128)(2,1)S(1)} %collective-permute-done.5.rest_0_) | copy-start | bytes 2359300
  46.1 20.2 %collective-permute-start.7 = (bf16[512,384]{1,0:T(8,128)(2,1)}, bf16[512,384]{1,0:T(8,128)(2,1)}, u32[]{:S(2)}, u32[]{:S(2)}) collective-permute-start(bf16[512,384]{1,0:T(8,128)(2,1)} %get-tuple-element.39), channel_id=1, source_target_pairs={{1,2},{2,1},{3,4},{4,3},{5,6},{6,5},{9,10},{10,9},{11,12},{12,11},... | collective-permute-start | bytes 1179656 | tf_op jit(solution)/shard_map/ppermute | solution.py:482
  57.5 17.7 %collective-permute-start.8 = (bf16[384,1024]{1,0:T(8,128)(2,1)}, bf16[384,1024]{1,0:T(8,128)(2,1)}, u32[]{:S(2)}, u32[]{:S(2)}) collective-permute-start(bf16[384,1024]{1,0:T(8,128)(2,1)} %get-tuple-element.46), channel_id=1, source_target_pairs={{0,8},{8,0},{16,24},{24,16},{1,9},{9,1},{17,25},{25,17},{2,10},{10... | collective-permute-start | bytes 2359304 | tf_op jit(solution)/shard_map/ppermute | solution.py:482
  60.3 14.9 %collective-permute-start.9 = (bf16[384,1024]{1,0:T(8,128)(2,1)}, bf16[384,1024]{1,0:T(8,128)(2,1)}, u32[]{:S(2)}, u32[]{:S(2)}) collective-permute-start(bf16[384,1024]{1,0:T(8,128)(2,1)} %get-tuple-element.47), channel_id=1, source_target_pairs={{8,16},{16,8},{9,17},{17,9},{10,18},{18,10},{11,19},{19,11},{12,20... | collective-permute-start | bytes 2359304 | tf_op jit(solution)/shard_map/ppermute | solution.py:482

commit v8 on v7

--- a/solution.py
+++ b/solution.py
@@ -99,7 +99,7 @@
     scratch += [pltpu.SemaphoreType.DMA((count,)), pltpu.SemaphoreType.DMA((count,))]
 
     def start(where_ref, p_ref, refs):
-        first = lambda at: pl.multiple_of(where_ref[at[0]], 128) if isinstance(at, tuple) else at
+        first = lambda at: pl.multiple_of(where_ref[at[0]] + sum(at[1:]), 128) if isinstance(at, tuple) else at
         loads = []
         for k, (row, size, col, width, _, _, _) in enumerate(pieces):
             source = p_ref.at[pl.ds(first(row), size), pl.ds(first(col), width)]
@@ -530,19 +530,17 @@
             pick(row_odd, 0, rows_dev - wide),
         ]
     ).astype(jnp.int32)
-    pieces = [
-        (row, outer, (11 + k,), wide, k, there, 0)
-        for row, there in ((0, 0), (rows_dev - outer, outer))
-        for k in range(2)
-    ]
-    pieces += [((13 + k,), wide, 0, cols_dev, k + 2, 0, 0) for k in range(2)]
+    half = outer // 2
+    spans = [(0, half, 0), (half, half, half)]
+    spans += [(rows_dev - outer, half, outer), (rows_dev - half, half, outer + half), (0, 16, 2 * outer)]
+    pieces = [(row, size, (11 + k,), wide, k, there, 0) for row, size, there in spans for k in range(2)]
+    pieces += [((13 + k, j * nlon), nlon, 0, cols_dev, k + 2, j * nlon, 0) for k in range(2) for j in range(steps)]
     others = [((8 + k,), wide, (10,), inner, k, 0, nlon) for k in range(2)]
     others += [((7,), inner, (11 + k,), wide, k + 2, 0, 0) for k in range(2)]
     sent = packed(covariance, where, pieces)
     outers, ends = list(sent[:2]), list(sent[2:])
     outers = [exchanged(piece, "col", k) for k, piece in enumerate(outers)]
     ends = [exchanged(piece, "row", k) for k, piece in enumerate(ends)]
-    wind_index, ends[0] = lax.optimization_barrier((wind_index, ends[0]))
     row_s, col_s, *rest = stencils(
         wind_table, diffusivity, wind_index, where, lat_rows, lats, nlon, covariance, others
     )

time: 89.4 us -> 87.4 us (0.978)
  the two profiles are of different devices: /device:TPU:19 before, /device:TPU:5 now
where the time goes in v8:
time: 87.4 us; the launch traced here: 86.7 us
  Pallas kernels  60.1 us (69%)
  starting transfers between devices  24 us (27%)
  between operations  1.02 us (1%)
  waiting for transfers between devices  0.9 us (1%)
    pallas_call x2, Pallas kernels, rows_operator(): pl.pallas_call(kernel, grid_spec=pltpu.PrefetchScalarGridSpec(num_scalar_...  30.1 us
    ppermute x8, starting transfers between devices, exchanged(): return lax.ppermute(block, axis, pairs)  19.1 us
    pallas_call x2, Pallas kernels, columns_operator(): pl.pallas_call(kernel, grid_spec=pltpu.PrefetchScalarGridSpec(num_scalar_...  18.2 us
    pallas_call x1, Pallas kernels, stencils(): pl.pallas_call(kernel, in_specs=[pl.BlockSpec(memory_space=pltpu.SMEM)] *...  6.72 us
    pallas_call x1, Pallas kernels, packed(): pl.pallas_call(kernel, in_specs=[pl.BlockSpec(memory_space=pltpu.SMEM), p...  5.16 us
    ppermute x2, starting transfers between devices, mirrored(): return lax.ppermute(block, ('row', 'col'), pairs)  4.92 us
  transfers between devices with their start and end apart: 10, of which 1 were waited for; matrix products, arithmetic and copies ran while one was open for 0% of the time, Pallas kernels for 48%

profile of v8, /device:TPU:5, one launch (start us, length us, event | category | flops | bytes accessed | tf_op | source)
XLA Modules:
  0.0 86.7 jit_solution(2759918768678955200)
XLA Ops:
  0.7 0.7 stack.63.where_ref
  1.4 5.2 %packed.1 = (bf16[1040,384]{1,0:T(8,128)(2,1)}, bf16[1040,384]{1,0:T(8,128)(2,1)}, bf16[384,1024]{1,0:T(8,128)(2,1)}, bf16[384,1024]{1,0:T(8,128)(2,1)}) custom-call(s32[15]{0:T(128)} %stack.63.where_ref, f32[2048,1024]{1,0:T(8,128)} %p_ref.7), custom_call_target="tpu_custom_call" | custom-call | flops 1 | bytes 1 | tf_op jit(solution)/shard_map/packed/pallas_call | solution.py:137
  6.6 0.1 collective-permute-start.5
  6.6 4.4 %collective-permute-start.6 = (bf16[1040,384]{1,0:T(8,128)(2,1)}, bf16[1040,384]{1,0:T(8,128)(2,1)}, u32[]{:S(2)}, u32[]{:S(2)}) collective-permute-start(bf16[1040,384]{1,0:T(8,128)(2,1)} %get-tuple-element.33), channel_id=1, source_target_pairs={{1,2},{2,1},{3,4},{4,3},{5,6},{6,5},{9,10},{10,9},{11,12},{12,11},... | collective-permute-start | bytes 2396168 | tf_op jit(solution)/shard_map/ppermute | solution.py:482
  11.0 1.3 %collective-permute-start.3 = (bf16[384,1024]{1,0:T(8,128)(2,1)}, bf16[384,1024]{1,0:T(8,128)(2,1)}, u32[]{:S(2)}, u32[]{:S(2)}) collective-permute-start(bf16[384,1024]{1,0:T(8,128)(2,1)} %get-tuple-element.29), channel_id=1, source_target_pairs={{0,8},{8,0},{16,24},{24,16},{1,9},{9,1},{17,25},{25,17},{2,10},{10... | collective-permute-start | bytes 2359304 | tf_op jit(solution)/shard_map/ppermute | solution.py:482
  12.3 3.0 %collective-permute-start.4 = (bf16[384,1024]{1,0:T(8,128)(2,1)}, bf16[384,1024]{1,0:T(8,128)(2,1)}, u32[]{:S(2)}, u32[]{:S(2)}) collective-permute-start(bf16[384,1024]{1,0:T(8,128)(2,1)} %get-tuple-element.30), channel_id=1, source_target_pairs={{8,16},{16,8},{9,17},{17,9},{10,18},{18,10},{11,19},{19,11},{12,20... | collective-permute-start | bytes 2359304 | tf_op jit(solution)/shard_map/ppermute | solution.py:482
  15.3 6.7 %stencils.1 = (f32[7,16,128]{2,1,0:T(8,128)}, f32[7,8,128]{2,1,0:T(8,128)}, bf16[3072,256]{1,0:T(8,128)(2,1)}, bf16[3072,256]{1,0:T(8,128)(2,1)}, f32[15,14,128]...) custom-call(f32[2,16]{1,0:T(2,128)} %bitcast.16, ...), custom_call_target="tpu_custom_call" | custom-call | flops 1 | bytes 1 | tf_op jit(solution)/shard_map/stencils/pallas_call | solution.py:192
  22.1 1.9 %collective-permute-start = (bf16[512,384]{1,0:T(8,128)(2,1)}, bf16[512,384]{1,0:T(8,128)(2,1)}, u32[]{:S(2)}, u32[]{:S(2)}) collective-permute-start(bf16[512,384]{1,0:T(8,128)(2,1)} %get-tuple-element.26), channel_id=1, source_target_pairs={{0,0},{1,1},{2,8},{3,9},{4,16},{5,17},{6,24},{7,25},{8,2},{9,3},{1... | collective-permute-start | bytes 1179656 | tf_op jit(solution)/shard_map/ppermute | solution.py:493
  24.0 0.0 collective-permute-done.3.even_ref
  24.0 3.0 %collective-permute-start.1 = (bf16[512,384]{1,0:T(8,128)(2,1)}, bf16[512,384]{1,0:T(8,128)(2,1)}, u32[]{:S(2)}, u32[]{:S(2)}) collective-permute-start(bf16[512,384]{1,0:T(8,128)(2,1)} %get-tuple-element.27), channel_id=1, source_target_pairs={{0,2},{2,10},{4,18},{6,26},{8,4},{9,1},{10,12},{11,9},{12,20},{13,... | collective-permute-start | bytes 1179656 | tf_op jit(solution)/shard_map/ppermute | solution.py:493
  27.0 0.0 collective-permute-done.4.odd_ref
  27.0 1.0 %collective-permute-start.2 = (bf16[512,384]{1,0:T(8,128)(2,1)}, bf16[512,384]{1,0:T(8,128)(2,1)}, u32[]{:S(2)}, u32[]{:S(2)}) collective-permute-start(bf16[512,384]{1,0:T(8,128)(2,1)} %get-tuple-element.28), channel_id=1, source_target_pairs={{0,1},{1,0},{2,3},{3,2},{4,5},{5,4},{6,7},{7,6},{8,9},{9,8},{10,11... | collective-permute-start | bytes 1179656 | tf_op jit(solution)/shard_map/ppermute | solution.py:482
  28.0 16.7 %rows_operator.2 = (bf16[2048,1024]{1,0:T(8,128)(2,1)}, bf16[4096,768]{1,0:T(8,128)(2,1)}) custom-call(s32[15]{0:T(128)} %stack.63.where_ref, f32[7,16,128]{2,1,0:T(8,128)} %get-tuple-element.24.stencil_ref, f32[2048,1024]{1,0:T(8,128)} %p_ref.7, bf16[384,1024]{1,0:T(8,128)(2,1)} %collective-permute-done.3.even_ref, ...), custom_call_target="tpu_custom_call" | custom-call | flops 1 | bytes 1 | tf_op jit(solution)/shard_map/rows_operator/pallas_call | solution.py:442
  44.7 0.0 collective-permute-done.5.rest_0_
  44.7 0.0 copy-start
  44.7 0.0 collective-permute-done.6.rest_1_
  44.7 5.0 %collective-permute-start.7 = (bf16[512,384]{1,0:T(8,128)(2,1)}, bf16[512,384]{1,0:T(8,128)(2,1)}, u32[]{:S(2)}, u32[]{:S(2)}) collective-permute-start(bf16[512,384]{1,0:T(8,128)(2,1)} %get-tuple-element.35), channel_id=1, source_target_pairs={{1,2},{2,1},{3,4},{4,3},{5,6},{6,5},{9,10},{10,9},{11,12},{12,11},... | collective-permute-start | bytes 1179656 | tf_op jit(solution)/shard_map/ppermute | solution.py:482
  49.7 0.0 copy-done
  49.7 9.3 %columns_operator.2 = (bf16[2048,1024]{1,0:T(8,128)(2,1)}, bf16[384,1024]{1,0:T(8,128)(2,1)}, bf16[384,1024]{1,0:T(8,128)(2,1)}) custom-call(s32[15]{0:T(128)} %stack.63.where_ref, f32[7,8,128]{2,1,0:T(8,128)} %get-tuple-element.25.stencil_ref, f32[2048,1024]{1,0:T(8,128)} %p_ref.7, bf16[1040,384]{1,0:T(8,128)(2,1)} %copy-done, ...), custom_call_target="tpu_custom_call" | custom-call | flops 1 | bytes 1 | tf_op jit(solution)/shard_map/columns_operator/pallas_call | solution.py:313
  59.0 0.0 collective-permute-start.8
  59.0 0.0 collective-permute-done.rest_0_
  59.0 4.4 %collective-permute-start.9 = (bf16[384,1024]{1,0:T(8,128)(2,1)}, bf16[384,1024]{1,0:T(8,128)(2,1)}, u32[]{:S(2)}, u32[]{:S(2)}) collective-permute-start(bf16[384,1024]{1,0:T(8,128)(2,1)} %get-tuple-element.43), channel_id=1, source_target_pairs={{8,16},{16,8},{9,17},{17,9},{10,18},{18,10},{11,19},{19,11},{12,20... | collective-permute-start | bytes 2359304 | tf_op jit(solution)/shard_map/ppermute | solution.py:482
  63.4 0.0 collective-permute-done.1.rest_1_
  63.4 0.0 collective-permute-done.2.rest_2_
  63.4 0.0 collective-permute-done.7.rest_3_
  63.4 8.9 %columns_operator.3.x_ref = bf16[2048,1024]{1,0:T(8,128)(2,1)} custom-call(s32[15]{0:T(128)} %stack.63.where_ref, f32[7,8,128]{2,1,0:T(8,128)} %get-tuple-element.25.stencil_ref, f32[2048,1024]{1,0:T(8,128)} %p_ref.7, bf16[512,384]{1,0:T(8,128)(2,1)} %collective-permute-done.rest_0_, ...), custom_call_target="tpu_custom_call", output_to_operand_aliasing={{}: (10, {})} | custom-call | flops 9999999827968 | bytes 9999999827968 | tf_op jit(solution)/shard_map/columns_operator/pallas_call | solution.py:313
  72.3 0.0 collective-permute-done.8.even_ref
  72.3 0.9 %collective-permute-done.9.odd_ref = bf16[384,1024]{1,0:T(8,128)(2,1)} collective-permute-done((bf16[384,1024]{1,0:T(8,128)(2,1)}, bf16[384,1024]{1,0:T(8,128)(2,1)}, u32[]{:S(2)}, u32[]{:S(2)}) %collective-permute-start.9) | collective-permute-done | bytes 786464 | tf_op jit(solution)/shard_map/ppermute | solution.py:482
  73.2 13.4 %rows_operator.3 = f32[2048,1024]{1,0:T(8,128)} custom-call(s32[15]{0:T(128)} %stack.63.where_ref, f32[7,16,128]{2,1,0:T(8,128)} %get-tuple-element.24.stencil_ref, bf16[2048,1024]{1,0:T(8,128)(2,1)} %columns_operator.3.x_ref, bf16[384,1024]{1,0:T(8,128)(2,1)} %collective-permute-done.8.even_ref, bf16[384,1024]{1,0:T(8,128)(2,1)} %collective-permute-done.9.odd_ref, ...), custom_call_target="tpu_custom_call" | custom-call | flops 1 | bytes 1 | tf_op jit(solution)/shard_map/rows_operator/pallas_call | solution.py:442
Async XLA Ops:
  6.6 38.1 %collective-permute-start.5 = (bf16[1040,384]{1,0:T(8,128)(2,1)}, bf16[1040,384]{1,0:T(8,128)(2,1)S(1)}, u32[]{:S(2)}, u32[]{:S(2)}) collective-permute-start(bf16[1040,384]{1,0:T(8,128)(2,1)} %get-tuple-element.32), channel_id=1, source_target_pairs={{0,1},{1,0},{2,3},{3,2},{4,5},{5,4},{6,7},{7,6},{8,9},{9,8},{10,11... | collective-permute-start | bytes 2396168 | tf_op jit(solution)/shard_map/ppermute | solution.py:482
  6.6 38.1 %collective-permute-start.6 = (bf16[1040,384]{1,0:T(8,128)(2,1)}, bf16[1040,384]{1,0:T(8,128)(2,1)}, u32[]{:S(2)}, u32[]{:S(2)}) collective-permute-start(bf16[1040,384]{1,0:T(8,128)(2,1)} %get-tuple-element.33), channel_id=1, source_target_pairs={{1,2},{2,1},{3,4},{4,3},{5,6},{6,5},{9,10},{10,9},{11,12},{12,11},... | collective-permute-start | bytes 2396168 | tf_op jit(solution)/shard_map/ppermute | solution.py:482
  11.0 13.0 %collective-permute-start.3 = (bf16[384,1024]{1,0:T(8,128)(2,1)}, bf16[384,1024]{1,0:T(8,128)(2,1)}, u32[]{:S(2)}, u32[]{:S(2)}) collective-permute-start(bf16[384,1024]{1,0:T(8,128)(2,1)} %get-tuple-element.29), channel_id=1, source_target_pairs={{0,8},{8,0},{16,24},{24,16},{1,9},{9,1},{17,25},{25,17},{2,10},{10... | collective-permute-start | bytes 2359304 | tf_op jit(solution)/shard_map/ppermute | solution.py:482
  12.3 14.7 %collective-permute-start.4 = (bf16[384,1024]{1,0:T(8,128)(2,1)}, bf16[384,1024]{1,0:T(8,128)(2,1)}, u32[]{:S(2)}, u32[]{:S(2)}) collective-permute-start(bf16[384,1024]{1,0:T(8,128)(2,1)} %get-tuple-element.30), channel_id=1, source_target_pairs={{8,16},{16,8},{9,17},{17,9},{10,18},{18,10},{11,19},{19,11},{12,20... | collective-permute-start | bytes 2359304 | tf_op jit(solution)/shard_map/ppermute | solution.py:482
  22.1 36.9 %collective-permute-start = (bf16[512,384]{1,0:T(8,128)(2,1)}, bf16[512,384]{1,0:T(8,128)(2,1)}, u32[]{:S(2)}, u32[]{:S(2)}) collective-permute-start(bf16[512,384]{1,0:T(8,128)(2,1)} %get-tuple-element.26), channel_id=1, source_target_pairs={{0,0},{1,1},{2,8},{3,9},{4,16},{5,17},{6,24},{7,25},{8,2},{9,3},{1... | collective-permute-start | bytes 1179656 | tf_op jit(solution)/shard_map/ppermute | solution.py:493
  24.0 39.4 %collective-permute-start.1 = (bf16[512,384]{1,0:T(8,128)(2,1)}, bf16[512,384]{1,0:T(8,128)(2,1)}, u32[]{:S(2)}, u32[]{:S(2)}) collective-permute-start(bf16[512,384]{1,0:T(8,128)(2,1)} %get-tuple-element.27), channel_id=1, source_target_pairs={{0,2},{2,10},{4,18},{6,26},{8,4},{9,1},{10,12},{11,9},{12,20},{13,... | collective-permute-start | bytes 1179656 | tf_op jit(solution)/shard_map/ppermute | solution.py:493
  27.0 36.4 %collective-permute-start.2 = (bf16[512,384]{1,0:T(8,128)(2,1)}, bf16[512,384]{1,0:T(8,128)(2,1)}, u32[]{:S(2)}, u32[]{:S(2)}) collective-permute-start(bf16[512,384]{1,0:T(8,128)(2,1)} %get-tuple-element.28), channel_id=1, source_target_pairs={{0,1},{1,0},{2,3},{3,2},{4,5},{5,4},{6,7},{7,6},{8,9},{9,8},{10,11... | collective-permute-start | bytes 1179656 | tf_op jit(solution)/shard_map/ppermute | solution.py:482
  44.7 5.0 %copy-start = (bf16[1040,384]{1,0:T(8,128)(2,1)}, bf16[1040,384]{1,0:T(8,128)(2,1)S(1)}, u32[]{:S(2)}) copy-start(bf16[1040,384]{1,0:T(8,128)(2,1)S(1)} %collective-permute-done.5.rest_0_) | copy-start | bytes 2396164
  44.7 18.7 %collective-permute-start.7 = (bf16[512,384]{1,0:T(8,128)(2,1)}, bf16[512,384]{1,0:T(8,128)(2,1)}, u32[]{:S(2)}, u32[]{:S(2)}) collective-permute-start(bf16[512,384]{1,0:T(8,128)(2,1)} %get-tuple-element.35), channel_id=1, source_target_pairs={{1,2},{2,1},{3,4},{4,3},{5,6},{6,5},{9,10},{10,9},{11,12},{12,11},... | collective-permute-start | bytes 1179656 | tf_op jit(solution)/shard_map/ppermute | solution.py:482
  59.0 13.3 %collective-permute-start.8 = (bf16[384,1024]{1,0:T(8,128)(2,1)}, bf16[384,1024]{1,0:T(8,128)(2,1)}, u32[]{:S(2)}, u32[]{:S(2)}) collective-permute-start(bf16[384,1024]{1,0:T(8,128)(2,1)} %get-tuple-element.42), channel_id=1, source_target_pairs={{0,8},{8,0},{16,24},{24,16},{1,9},{9,1},{17,25},{25,17},{2,10},{10... | collective-permute-start | bytes 2359304 | tf_op jit(solution)/shard_map/ppermute | solution.py:482
  59.0 14.2 %collective-permute-start.9 = (bf16[384,1024]{1,0:T(8,128)(2,1)}, bf16[384,1024]{1,0:T(8,128)(2,1)}, u32[]{:S(2)}, u32[]{:S(2)}) collective-permute-start(bf16[384,1024]{1,0:T(8,128)(2,1)} %get-tuple-element.43), channel_id=1, source_target_pairs={{8,16},{16,8},{9,17},{17,9},{10,18},{18,10},{11,19},{19,11},{12,20... | collective-permute-start | bytes 2359304 | tf_op jit(solution)/shard_map/ppermute | solution.py:482

commit v9 on v8

--- a/solution.py
+++ b/solution.py
@@ -214,7 +214,7 @@
     size = unit * nlon
     span = 2 * steps * nlon
     pairs = lats // 2
-    part = nlon // 2
+    part = 16
     upper = size - part * (3 * size // (8 * part))
 
     def kernel(where_ref, stencil_ref, p_ref, *rest):
@@ -256,22 +256,12 @@
             for step_no in range(steps)
         ]
         starts = list(range(upper, size, part))
-        for q in range(max(pairs, len(starts))):
-            if q < pairs:
-                window = slice((2 * q + 1) * nlon, (2 * q + 1) * nlon + span)
-                of = pl.ds(q * span, span)
-                total = product(data_ref[:upper, window], b_high[of, :])
-                total += product(data_ref[size : size + upper, window], b_high[of, :])
-                total += product(data_ref[:upper, window], b_low[of, :])
-                for a, k, d in ((0, 2 * q, -steps), (1, 2 * q + 2 * steps + 1, steps)):
-                    far = slice(k * nlon, (k + 1) * nlon)
-                    row = stencil_ref[d + steps, 2 * q + a : 2 * q + a + 1, :]
-                    weight = jnp.sum(row, axis=1, keepdims=True)
-                    far_values = data_ref[:upper, far].astype(F32) + data_ref[size : size + upper, far].astype(F32)
-                    value = total[:, a * nlon : (a + 1) * nlon] + weight * far_values
-                    t_ref[:upper, (2 * q + a) * nlon : (2 * q + a + 1) * nlon] = value.astype(BF16)
-            if q < len(starts):
-                rows_at = slice(starts[q], starts[q] + part)
+        share = -(-len(starts) // (3 * pairs))
+
+        def some_by_steps():
+            for _ in range(min(share, len(starts))):
+                start = starts.pop(0)
+                rows_at = slice(start, start + part)
                 planes = []
                 for k in range(lats + 2 * steps):
                     if steps <= k < steps + lats:
@@ -280,6 +270,23 @@
                         planes.append(data_ref[rows_at, k * nlon : (k + 1) * nlon].astype(F32))
                 for k, plane in enumerate(swept(planes, weights)):
                     t_ref[rows_at, k * nlon : (k + 1) * nlon] = plane.astype(BF16)
+
+        for q in range(pairs):
+            window = slice((2 * q + 1) * nlon, (2 * q + 1) * nlon + span)
+            of = pl.ds(q * span, span)
+            total = product(data_ref[:upper, window], b_high[of, :])
+            some_by_steps()
+            total += product(data_ref[size : size + upper, window], b_high[of, :])
+            some_by_steps()
+            total += product(data_ref[:upper, window], b_low[of, :])
+            some_by_steps()
+            for a, k, d in ((0, 2 * q, -steps), (1, 2 * q + 2 * steps + 1, steps)):
+                far = slice(k * nlon, (k + 1) * nlon)
+                row = stencil_ref[d + steps, 2 * q + a : 2 * q + a + 1, :]
+                weight = jnp.sum(row, axis=1, keepdims=True)
+                far_values = data_ref[:upper, far].astype(F32) + data_ref[size : size + upper, far].astype(F32)
+                value = total[:, a * nlon : (a + 1) * nlon] + weight * far_values
+                t_ref[:upper, (2 * q + a) * nlon : (2 * q + a + 1) * nlon] = value.astype(BF16)
         if ends:
             for odd in range(2):
                 is_odd = row_odd if odd else jnp.logical_not(row_odd)

time: 87.4 us -> 89.1 us (1.019)
  Pallas kernels: 60.1 us -> 62.7 us
    pallas_call x2, Pallas kernels: 18.2 us -> 20.7 us  [columns_operator(): pl.pallas_call(kernel, grid_spec=pltpu.PrefetchScalarGridSpec(num_scalar_...]
  transfers between devices with their start and end apart: 10 -> 10, of which waited for: 1 -> 0; matrix products, arithmetic and copies ran while one was open for 0% -> 0% of each run, Pallas kernels for 48% -> 50%
where the time goes in v9:
time: 89.1 us; the launch traced here: 88.4 us
  Pallas kernels  62.7 us (70%)
  starting transfers between devices  24 us (27%)
  between operations  1.02 us (1%)
    pallas_call x2, Pallas kernels, rows_operator(): pl.pallas_call(kernel, grid_spec=pltpu.PrefetchScalarGridSpec(num_scalar_...  30.1 us
    pallas_call x2, Pallas kernels, columns_operator(): pl.pallas_call(kernel, grid_spec=pltpu.PrefetchScalarGridSpec(num_scalar_...  20.7 us
    ppermute x8, starting transfers between devices, exchanged(): return lax.ppermute(block, axis, pairs)  19.1 us
    pallas_call x1, Pallas kernels, stencils(): pl.pallas_call(kernel, in_specs=[pl.BlockSpec(memory_space=pltpu.SMEM)] *...  6.72 us
    pallas_call x1, Pallas kernels, packed(): pl.pallas_call(kernel, in_specs=[pl.BlockSpec(memory_space=pltpu.SMEM), p...  5.16 us
    ppermute x2, starting transfers between devices, mirrored(): return lax.ppermute(block, ('row', 'col'), pairs)  4.92 us
  transfers between devices with their start and end apart: 10, of which 0 were waited for; matrix products, arithmetic and copies ran while one was open for 0% of the time, Pallas kernels for 50%

profile of v9, /device:TPU:5, one launch (start us, length us, event | category | flops | bytes accessed | tf_op | source)
XLA Modules:
  0.0 88.4 jit_solution(494093119085658475)
XLA Ops:
  0.7 0.7 stack.63.where_ref
  1.4 5.2 %packed.1 = (bf16[1040,384]{1,0:T(8,128)(2,1)}, bf16[1040,384]{1,0:T(8,128)(2,1)}, bf16[384,1024]{1,0:T(8,128)(2,1)}, bf16[384,1024]{1,0:T(8,128)(2,1)}) custom-call(s32[15]{0:T(128)} %stack.63.where_ref, f32[2048,1024]{1,0:T(8,128)} %p_ref.7), custom_call_target="tpu_custom_call" | custom-call | flops 1 | bytes 1 | tf_op jit(solution)/shard_map/packed/pallas_call | solution.py:137
  6.6 0.1 collective-permute-start.5
  6.6 4.4 %collective-permute-start.6 = (bf16[1040,384]{1,0:T(8,128)(2,1)}, bf16[1040,384]{1,0:T(8,128)(2,1)}, u32[]{:S(2)}, u32[]{:S(2)}) collective-permute-start(bf16[1040,384]{1,0:T(8,128)(2,1)} %get-tuple-element.33), channel_id=1, source_target_pairs={{1,2},{2,1},{3,4},{4,3},{5,6},{6,5},{9,10},{10,9},{11,12},{12,11},... | collective-permute-start | bytes 2396168 | tf_op jit(solution)/shard_map/ppermute | solution.py:489
  11.0 1.3 %collective-permute-start.3 = (bf16[384,1024]{1,0:T(8,128)(2,1)}, bf16[384,1024]{1,0:T(8,128)(2,1)}, u32[]{:S(2)}, u32[]{:S(2)}) collective-permute-start(bf16[384,1024]{1,0:T(8,128)(2,1)} %get-tuple-element.29), channel_id=1, source_target_pairs={{0,8},{8,0},{16,24},{24,16},{1,9},{9,1},{17,25},{25,17},{2,10},{10... | collective-permute-start | bytes 2359304 | tf_op jit(solution)/shard_map/ppermute | solution.py:489
  12.3 3.0 %collective-permute-start.4 = (bf16[384,1024]{1,0:T(8,128)(2,1)}, bf16[384,1024]{1,0:T(8,128)(2,1)}, u32[]{:S(2)}, u32[]{:S(2)}) collective-permute-start(bf16[384,1024]{1,0:T(8,128)(2,1)} %get-tuple-element.30), channel_id=1, source_target_pairs={{8,16},{16,8},{9,17},{17,9},{10,18},{18,10},{11,19},{19,11},{12,20... | collective-permute-start | bytes 2359304 | tf_op jit(solution)/shard_map/ppermute | solution.py:489
  15.3 6.7 %stencils.1 = (f32[7,16,128]{2,1,0:T(8,128)}, f32[7,8,128]{2,1,0:T(8,128)}, bf16[3072,256]{1,0:T(8,128)(2,1)}, bf16[3072,256]{1,0:T(8,128)(2,1)}, f32[15,14,128]...) custom-call(f32[2,16]{1,0:T(2,128)} %bitcast.16, ...), custom_call_target="tpu_custom_call" | custom-call | flops 1 | bytes 1 | tf_op jit(solution)/shard_map/stencils/pallas_call | solution.py:192
  22.1 1.9 %collective-permute-start = (bf16[512,384]{1,0:T(8,128)(2,1)}, bf16[512,384]{1,0:T(8,128)(2,1)}, u32[]{:S(2)}, u32[]{:S(2)}) collective-permute-start(bf16[512,384]{1,0:T(8,128)(2,1)} %get-tuple-element.26), channel_id=1, source_target_pairs={{0,0},{1,1},{2,8},{3,9},{4,16},{5,17},{6,24},{7,25},{8,2},{9,3},{1... | collective-permute-start | bytes 1179656 | tf_op jit(solution)/shard_map/ppermute | solution.py:500
  24.0 0.0 collective-permute-done.3.even_ref
  24.0 3.0 %collective-permute-start.1 = (bf16[512,384]{1,0:T(8,128)(2,1)}, bf16[512,384]{1,0:T(8,128)(2,1)}, u32[]{:S(2)}, u32[]{:S(2)}) collective-permute-start(bf16[512,384]{1,0:T(8,128)(2,1)} %get-tuple-element.27), channel_id=1, source_target_pairs={{0,2},{2,10},{4,18},{6,26},{8,4},{9,1},{10,12},{11,9},{12,20},{13,... | collective-permute-start | bytes 1179656 | tf_op jit(solution)/shard_map/ppermute | solution.py:500
  27.0 0.0 collective-permute-done.4.odd_ref
  27.0 1.0 %collective-permute-start.2 = (bf16[512,384]{1,0:T(8,128)(2,1)}, bf16[512,384]{1,0:T(8,128)(2,1)}, u32[]{:S(2)}, u32[]{:S(2)}) collective-permute-start(bf16[512,384]{1,0:T(8,128)(2,1)} %get-tuple-element.28), channel_id=1, source_target_pairs={{0,1},{1,0},{2,3},{3,2},{4,5},{5,4},{6,7},{7,6},{8,9},{9,8},{10,11... | collective-permute-start | bytes 1179656 | tf_op jit(solution)/shard_map/ppermute | solution.py:489
  28.0 16.7 %rows_operator.2 = (bf16[2048,1024]{1,0:T(8,128)(2,1)}, bf16[4096,768]{1,0:T(8,128)(2,1)}) custom-call(s32[15]{0:T(128)} %stack.63.where_ref, f32[7,16,128]{2,1,0:T(8,128)} %get-tuple-element.24.stencil_ref, f32[2048,1024]{1,0:T(8,128)} %p_ref.7, bf16[384,1024]{1,0:T(8,128)(2,1)} %collective-permute-done.3.even_ref, ...), custom_call_target="tpu_custom_call" | custom-call | flops 1 | bytes 1 | tf_op jit(solution)/shard_map/rows_operator/pallas_call | solution.py:449
  44.7 0.0 collective-permute-done.5.rest_0_
  44.7 0.0 copy-start
  44.7 0.0 collective-permute-done.6.rest_1_
  44.7 5.0 %collective-permute-start.7 = (bf16[512,384]{1,0:T(8,128)(2,1)}, bf16[512,384]{1,0:T(8,128)(2,1)}, u32[]{:S(2)}, u32[]{:S(2)}) collective-permute-start(bf16[512,384]{1,0:T(8,128)(2,1)} %get-tuple-element.35), channel_id=1, source_target_pairs={{1,2},{2,1},{3,4},{4,3},{5,6},{6,5},{9,10},{10,9},{11,12},{12,11},... | collective-permute-start | bytes 1179656 | tf_op jit(solution)/shard_map/ppermute | solution.py:489
  49.7 0.0 copy-done
  49.7 10.5 %columns_operator.2 = (bf16[2048,1024]{1,0:T(8,128)(2,1)}, bf16[384,1024]{1,0:T(8,128)(2,1)}, bf16[384,1024]{1,0:T(8,128)(2,1)}) custom-call(s32[15]{0:T(128)} %stack.63.where_ref, f32[7,8,128]{2,1,0:T(8,128)} %get-tuple-element.25.stencil_ref, f32[2048,1024]{1,0:T(8,128)} %p_ref.7, bf16[1040,384]{1,0:T(8,128)(2,1)} %copy-done, ...), custom_call_target="tpu_custom_call" | custom-call | flops 1 | bytes 1 | tf_op jit(solution)/shard_map/columns_operator/pallas_call | solution.py:320
  60.2 0.0 collective-permute-start.8
  60.2 0.0 collective-permute-done.rest_0_
  60.3 4.4 %collective-permute-start.9 = (bf16[384,1024]{1,0:T(8,128)(2,1)}, bf16[384,1024]{1,0:T(8,128)(2,1)}, u32[]{:S(2)}, u32[]{:S(2)}) collective-permute-start(bf16[384,1024]{1,0:T(8,128)(2,1)} %get-tuple-element.43), channel_id=1, source_target_pairs={{8,16},{16,8},{9,17},{17,9},{10,18},{18,10},{11,19},{19,11},{12,20... | collective-permute-start | bytes 2359304 | tf_op jit(solution)/shard_map/ppermute | solution.py:489
  64.6 0.0 collective-permute-done.1.rest_1_
  64.6 0.0 collective-permute-done.2.rest_2_
  64.7 0.0 collective-permute-done.7.rest_3_
  64.7 10.2 %columns_operator.3.x_ref = bf16[2048,1024]{1,0:T(8,128)(2,1)} custom-call(s32[15]{0:T(128)} %stack.63.where_ref, f32[7,8,128]{2,1,0:T(8,128)} %get-tuple-element.25.stencil_ref, f32[2048,1024]{1,0:T(8,128)} %p_ref.7, bf16[512,384]{1,0:T(8,128)(2,1)} %collective-permute-done.rest_0_, ...), custom_call_target="tpu_custom_call", output_to_operand_aliasing={{}: (10, {})} | custom-call | flops 9999999827968 | bytes 9999999827968 | tf_op jit(solution)/shard_map/columns_operator/pallas_call | solution.py:320
  74.9 0.0 collective-permute-done.8.even_ref
  74.9 0.0 collective-permute-done.9.odd_ref
  74.9 13.4 %rows_operator.3 = f32[2048,1024]{1,0:T(8,128)} custom-call(s32[15]{0:T(128)} %stack.63.where_ref, f32[7,16,128]{2,1,0:T(8,128)} %get-tuple-element.24.stencil_ref, bf16[2048,1024]{1,0:T(8,128)(2,1)} %columns_operator.3.x_ref, bf16[384,1024]{1,0:T(8,128)(2,1)} %collective-permute-done.8.even_ref, bf16[384,1024]{1,0:T(8,128)(2,1)} %collective-permute-done.9.odd_ref, ...), custom_call_target="tpu_custom_call" | custom-call | flops 1 | bytes 1 | tf_op jit(solution)/shard_map/rows_operator/pallas_call | solution.py:449
Async XLA Ops:
  6.6 38.1 %collective-permute-start.5 = (bf16[1040,384]{1,0:T(8,128)(2,1)}, bf16[1040,384]{1,0:T(8,128)(2,1)S(1)}, u32[]{:S(2)}, u32[]{:S(2)}) collective-permute-start(bf16[1040,384]{1,0:T(8,128)(2,1)} %get-tuple-element.32), channel_id=1, source_target_pairs={{0,1},{1,0},{2,3},{3,2},{4,5},{5,4},{6,7},{7,6},{8,9},{9,8},{10,11... | collective-permute-start | bytes 2396168 | tf_op jit(solution)/shard_map/ppermute | solution.py:489
  6.6 38.1 %collective-permute-start.6 = (bf16[1040,384]{1,0:T(8,128)(2,1)}, bf16[1040,384]{1,0:T(8,128)(2,1)}, u32[]{:S(2)}, u32[]{:S(2)}) collective-permute-start(bf16[1040,384]{1,0:T(8,128)(2,1)} %get-tuple-element.33), channel_id=1, source_target_pairs={{1,2},{2,1},{3,4},{4,3},{5,6},{6,5},{9,10},{10,9},{11,12},{12,11},... | collective-permute-start | bytes 2396168 | tf_op jit(solution)/shard_map/ppermute | solution.py:489
  11.0 13.0 %collective-permute-start.3 = (bf16[384,1024]{1,0:T(8,128)(2,1)}, bf16[384,1024]{1,0:T(8,128)(2,1)}, u32[]{:S(2)}, u32[]{:S(2)}) collective-permute-start(bf16[384,1024]{1,0:T(8,128)(2,1)} %get-tuple-element.29), channel_id=1, source_target_pairs={{0,8},{8,0},{16,24},{24,16},{1,9},{9,1},{17,25},{25,17},{2,10},{10... | collective-permute-start | bytes 2359304 | tf_op jit(solution)/shard_map/ppermute | solution.py:489
  12.3 14.7 %collective-permute-start.4 = (bf16[384,1024]{1,0:T(8,128)(2,1)}, bf16[384,1024]{1,0:T(8,128)(2,1)}, u32[]{:S(2)}, u32[]{:S(2)}) collective-permute-start(bf16[384,1024]{1,0:T(8,128)(2,1)} %get-tuple-element.30), channel_id=1, source_target_pairs={{8,16},{16,8},{9,17},{17,9},{10,18},{18,10},{11,19},{19,11},{12,20... | collective-permute-start | bytes 2359304 | tf_op jit(solution)/shard_map/ppermute | solution.py:489
  22.1 38.2 %collective-permute-start = (bf16[512,384]{1,0:T(8,128)(2,1)}, bf16[512,384]{1,0:T(8,128)(2,1)}, u32[]{:S(2)}, u32[]{:S(2)}) collective-permute-start(bf16[512,384]{1,0:T(8,128)(2,1)} %get-tuple-element.26), channel_id=1, source_target_pairs={{0,0},{1,1},{2,8},{3,9},{4,16},{5,17},{6,24},{7,25},{8,2},{9,3},{1... | collective-permute-start | bytes 1179656 | tf_op jit(solution)/shard_map/ppermute | solution.py:500
  24.0 40.6 %collective-permute-start.1 = (bf16[512,384]{1,0:T(8,128)(2,1)}, bf16[512,384]{1,0:T(8,128)(2,1)}, u32[]{:S(2)}, u32[]{:S(2)}) collective-permute-start(bf16[512,384]{1,0:T(8,128)(2,1)} %get-tuple-element.27), channel_id=1, source_target_pairs={{0,2},{2,10},{4,18},{6,26},{8,4},{9,1},{10,12},{11,9},{12,20},{13,... | collective-permute-start | bytes 1179656 | tf_op jit(solution)/shard_map/ppermute | solution.py:500
  27.0 37.6 %collective-permute-start.2 = (bf16[512,384]{1,0:T(8,128)(2,1)}, bf16[512,384]{1,0:T(8,128)(2,1)}, u32[]{:S(2)}, u32[]{:S(2)}) collective-permute-start(bf16[512,384]{1,0:T(8,128)(2,1)} %get-tuple-element.28), channel_id=1, source_target_pairs={{0,1},{1,0},{2,3},{3,2},{4,5},{5,4},{6,7},{7,6},{8,9},{9,8},{10,11... | collective-permute-start | bytes 1179656 | tf_op jit(solution)/shard_map/ppermute | solution.py:489
  44.7 5.0 %copy-start = (bf16[1040,384]{1,0:T(8,128)(2,1)}, bf16[1040,384]{1,0:T(8,128)(2,1)S(1)}, u32[]{:S(2)}) copy-start(bf16[1040,384]{1,0:T(8,128)(2,1)S(1)} %collective-permute-done.5.rest_0_) | copy-start | bytes 2396164
  44.7 19.9 %collective-permute-start.7 = (bf16[512,384]{1,0:T(8,128)(2,1)}, bf16[512,384]{1,0:T(8,128)(2,1)}, u32[]{:S(2)}, u32[]{:S(2)}) collective-permute-start(bf16[512,384]{1,0:T(8,128)(2,1)} %get-tuple-element.35), channel_id=1, source_target_pairs={{1,2},{2,1},{3,4},{4,3},{5,6},{6,5},{9,10},{10,9},{11,12},{12,11},... | collective-permute-start | bytes 1179656 | tf_op jit(solution)/shard_map/ppermute | solution.py:489
  60.2 14.6 %collective-permute-start.8 = (bf16[384,1024]{1,0:T(8,128)(2,1)}, bf16[384,1024]{1,0:T(8,128)(2,1)}, u32[]{:S(2)}, u32[]{:S(2)}) collective-permute-start(bf16[384,1024]{1,0:T(8,128)(2,1)} %get-tuple-element.42), channel_id=1, source_target_pairs={{0,8},{8,0},{16,24},{24,16},{1,9},{9,1},{17,25},{25,17},{2,10},{10... | collective-permute-start | bytes 2359304 | tf_op jit(solution)/shard_map/ppermute | solution.py:489
  60.3 14.6 %collective-permute-start.9 = (bf16[384,1024]{1,0:T(8,128)(2,1)}, bf16[384,1024]{1,0:T(8,128)(2,1)}, u32[]{:S(2)}, u32[]{:S(2)}) collective-permute-start(bf16[384,1024]{1,0:T(8,128)(2,1)} %get-tuple-element.43), channel_id=1, source_target_pairs={{8,16},{16,8},{9,17},{17,9},{10,18},{18,10},{11,19},{19,11},{12,20... | collective-permute-start | bytes 2359304 | tf_op jit(solution)/shard_map/ppermute | solution.py:489

commit v10 on v8

--- a/solution.py
+++ b/solution.py
@@ -218,7 +218,10 @@
     upper = size - part * (3 * size // (8 * part))
 
     def kernel(where_ref, stencil_ref, p_ref, *rest):
-        halo_refs, rest = rest[: 2 * len(halos)], rest[2 * len(halos) :]
+        halo_groups = []
+        for group in halos:
+            halo_groups.append(rest[: len(group)])
+            rest = rest[len(group) :]
         (b_high, b_low, step_ref), outs, data_ref = rest[:3], rest[3:-1], rest[-1]
         if held is not None:
             outs = outs[1:]
@@ -231,19 +234,23 @@
             data_ref[size:, :wide] = jnp.zeros((size, wide), BF16)
             data_ref[size:, wide + cols :] = jnp.zeros((size, wide), BF16)
 
-        for k in range(len(halos)):
-            even_ref, odd_ref = halo_refs[2 * k : 2 * k + 2]
+        for k, refs in enumerate(halo_groups):
             chosen = i >= 0 if len(halos) == 1 else i == k
-
-            @pl.when(jnp.logical_and(chosen, col_odd))
-            def _(even_ref=even_ref, odd_ref=odd_ref):
-                data_ref[:size, :wide] = even_ref[...]
-                data_ref[:size, wide + cols :] = odd_ref[...]
-
-            @pl.when(jnp.logical_and(chosen, jnp.logical_not(col_odd)))
-            def _(even_ref=even_ref, odd_ref=odd_ref):
-                data_ref[:size, :wide] = odd_ref[...]
-                data_ref[:size, wide + cols :] = even_ref[...]
+            for odd in range(2):
+                here = jnp.logical_and(chosen, col_odd if odd else jnp.logical_not(col_odd))
+                even_at, odd_at = (0, wide + cols) if odd else (wide + cols, 0)
+
+                @pl.when(here)
+                def _(refs=refs, odd_at=odd_at):
+                    data_ref[:size, odd_at : odd_at + wide] = refs[1][...]
+
+                for ref, use in ((refs[0], None),) if len(refs) == 2 else ((refs[0], 0), (refs[2], 1)):
+                    if use is not None:
+                        here_too = jnp.logical_and(here, where_ref[15] == use)
+
+                    @pl.when(here if use is None else here_too)
+                    def _(ref=ref, even_at=even_at):
+                        data_ref[:size, even_at : even_at + wide] = ref[...]
 
         data_ref[:upper, wide : wide + cols], data_ref[size : size + upper, wide : wide + cols] = split(
             p_ref[:upper, :]
@@ -297,11 +304,11 @@
         pl.BlockSpec(stencil.shape, lambda i, at: (0, 0, 0)),
         pl.BlockSpec((size, cols), lambda i, at: (block_at(i, at), 0)),
     ]
-    in_specs += [pl.BlockSpec((size, wide), halo_at)] * (2 * len(halos))
+    in_specs += [pl.BlockSpec((size, wide), halo_at)] * sum(len(group) for group in halos)
     in_specs += [pl.BlockSpec(block.shape, lambda i, at, n=block.ndim: (0,) * n) for block in blocks]
     out_specs = [pl.BlockSpec((size, cols), lambda i, at: (block_at(i, at), 0))]
     out_shape = [jax.ShapeDtypeStruct((rows, cols), BF16)]
-    operands = [where, stencil, covariance] + [array for pair in halos for array in pair] + list(blocks)
+    operands = [where, stencil, covariance] + [array for group in halos for array in group] + list(blocks)
     aliases = {}
     if ends:
         out_specs += [pl.BlockSpec((wide, cols), lambda i, at: (0, 0))] * 2
@@ -338,7 +345,7 @@
     ahead = (steps + 1) // 2
     exact = values.dtype == BF16
     makes = blocks is None
-    chunk = min(cols, 256)
+    chunk = cols if exact else min(cols, 512)
 
     def kernel(where_ref, stencil_ref, x_ref, even_ref, odd_ref, *rest):
         if makes:
@@ -488,8 +495,9 @@
     for a in range(n_row):
         for b in range(n_col):
             to = 2 * a + (1 - b % 2) + (1 if (b + odd) % 2 else -1)
-            if 0 <= to < n_col:
-                pairs.append((a * n_col + b, (b // 2) * n_col + to))
+            here, there = a * n_col + b, (b // 2) * n_col + to
+            if 0 <= to < n_col and here != there:
+                pairs.append((here, there))
     return lax.ppermute(block, ("row", "col"), pairs)
 
 
@@ -528,6 +536,7 @@
             pick(col_odd, 0, cols_dev - wide),
             pick(row_odd, rows_dev - wide, 0),
             pick(row_odd, 0, rows_dev - wide),
+            col_id // 2 == row_id,
         ]
     ).astype(jnp.int32)
     half = outer // 2
@@ -545,7 +554,7 @@
         wind_table, diffusivity, wind_index, where, lat_rows, lats, nlon, covariance, others
     )
     col_blocks, mirrors, inners = rest[:3], rest[3:5], rest[5:7]
-    mirrors = [mirrored(piece, k) for k, piece in enumerate(mirrors)]
+    mirrors = [mirrored(piece, k) for k, piece in enumerate(mirrors)] + [mirrors[0]]
 
     operator_times_prior, blocks = rows_operator(covariance, *ends, row_s, where, steps, nlon, BF16)
     inners[0] = exchanged(inners[0], "col", 0)

time: 87.4 us -> 87.4 us (level); the launches traced: 86.7 us -> 85.8 us
  starting transfers between devices: 24 us -> 21.4 us
  waiting for transfers between devices: 0.9 us -> 2.36 us
    ppermute x8, starting transfers between devices: 19.1 us -> 17.6 us  [exchanged(): return lax.ppermute(block, axis, pairs)]
    ppermute x8, waiting for transfers between devices: 0.89 us -> 2.35 us  [exchanged(): return lax.ppermute(block, axis, pairs)]
    ppermute x2, starting transfers between devices: 4.92 us -> 3.83 us  [mirrored(): return lax.ppermute(block, ('row', 'col'), pairs)]
  transfers between devices with their start and end apart: 10 -> 10, of which waited for: 1 -> 2; matrix products, arithmetic and copies ran while one was open for 0% -> 0% of each run, Pallas kernels for 48% -> 49%
where the time goes in v10:
time: 87.4 us; the launch traced here: 85.8 us
  Pallas kernels  60.3 us (69%)
  starting transfers between devices  21.4 us (24%)
  waiting for transfers between devices  2.36 us (3%)
  between operations  1.01 us (1%)
    pallas_call x2, Pallas kernels, rows_operator(): pl.pallas_call(kernel, grid_spec=pltpu.PrefetchScalarGridSpec(num_scalar_...  30.1 us
    pallas_call x2, Pallas kernels, columns_operator(): pl.pallas_call(kernel, grid_spec=pltpu.PrefetchScalarGridSpec(num_scalar_...  18.3 us
    ppermute x8, starting transfers between devices, exchanged(): return lax.ppermute(block, axis, pairs)  17.6 us
    pallas_call x1, Pallas kernels, stencils(): pl.pallas_call(kernel, in_specs=[pl.BlockSpec(memory_space=pltpu.SMEM)] *...  6.72 us
    pallas_call x1, Pallas kernels, packed(): pl.pallas_call(kernel, in_specs=[pl.BlockSpec(memory_space=pltpu.SMEM), p...  5.16 us
    ppermute x2, starting transfers between devices, mirrored(): return lax.ppermute(block, ('row', 'col'), pairs)  3.83 us
    ppermute x8, waiting for transfers between devices, exchanged(): return lax.ppermute(block, axis, pairs)  2.35 us
  transfers between devices with their start and end apart: 10, of which 2 were waited for; matrix products, arithmetic and copies ran while one was open for 0% of the time, Pallas kernels for 49%

profile of v10, /device:TPU:5, one launch (start us, length us, event | category | flops | bytes accessed | tf_op | source)
XLA Modules:
  0.0 85.8 jit_solution(416276224052075808)
XLA Ops:
  0.7 0.7 stack.71.where_ref
  1.4 5.2 %packed.1 = (bf16[1040,384]{1,0:T(8,128)(2,1)}, bf16[1040,384]{1,0:T(8,128)(2,1)}, bf16[384,1024]{1,0:T(8,128)(2,1)}, bf16[384,1024]{1,0:T(8,128)(2,1)}) custom-call(s32[16]{0:T(128)} %stack.71.where_ref, f32[2048,1024]{1,0:T(8,128)} %p_ref.7), custom_call_target="tpu_custom_call" | custom-call | flops 1 | bytes 1 | tf_op jit(solution)/shard_map/packed/pallas_call | solution.py:137
  6.6 0.1 collective-permute-start.5
  6.6 4.4 %collective-permute-start.6 = (bf16[1040,384]{1,0:T(8,128)(2,1)}, bf16[1040,384]{1,0:T(8,128)(2,1)}, u32[]{:S(2)}, u32[]{:S(2)}) collective-permute-start(bf16[1040,384]{1,0:T(8,128)(2,1)} %get-tuple-element.33), channel_id=1, source_target_pairs={{1,2},{2,1},{3,4},{4,3},{5,6},{6,5},{9,10},{10,9},{11,12},{12,11},... | collective-permute-start | bytes 2396168 | tf_op jit(solution)/shard_map/ppermute | solution.py:489
  11.0 1.3 %collective-permute-start.3 = (bf16[384,1024]{1,0:T(8,128)(2,1)}, bf16[384,1024]{1,0:T(8,128)(2,1)}, u32[]{:S(2)}, u32[]{:S(2)}) collective-permute-start(bf16[384,1024]{1,0:T(8,128)(2,1)} %get-tuple-element.29), channel_id=1, source_target_pairs={{0,8},{8,0},{16,24},{24,16},{1,9},{9,1},{17,25},{25,17},{2,10},{10... | collective-permute-start | bytes 2359304 | tf_op jit(solution)/shard_map/ppermute | solution.py:489
  12.3 3.0 %collective-permute-start.4 = (bf16[384,1024]{1,0:T(8,128)(2,1)}, bf16[384,1024]{1,0:T(8,128)(2,1)}, u32[]{:S(2)}, u32[]{:S(2)}) collective-permute-start(bf16[384,1024]{1,0:T(8,128)(2,1)} %get-tuple-element.30), channel_id=1, source_target_pairs={{8,16},{16,8},{9,17},{17,9},{10,18},{18,10},{11,19},{19,11},{12,20... | collective-permute-start | bytes 2359304 | tf_op jit(solution)/shard_map/ppermute | solution.py:489
  15.3 6.7 %stencils.1 = (f32[7,16,128]{2,1,0:T(8,128)}, f32[7,8,128]{2,1,0:T(8,128)}, bf16[3072,256]{1,0:T(8,128)(2,1)}, bf16[3072,256]{1,0:T(8,128)(2,1)}, f32[15,14,128]...) custom-call(f32[2,16]{1,0:T(2,128)} %bitcast.17, ...), custom_call_target="tpu_custom_call" | custom-call | flops 1 | bytes 1 | tf_op jit(solution)/shard_map/stencils/pallas_call | solution.py:192
  22.1 1.9 %collective-permute-start.1 = (bf16[512,384]{1,0:T(8,128)(2,1)}, bf16[512,384]{1,0:T(8,128)(2,1)}, u32[]{:S(2)}, u32[]{:S(2)}) collective-permute-start(bf16[512,384]{1,0:T(8,128)(2,1)} %get-tuple-element.27), channel_id=1, source_target_pairs={{0,2},{2,10},{4,18},{6,26},{8,4},{9,1},{10,12},{11,9},{12,20},{13,... | collective-permute-start | bytes 1179656 | tf_op jit(solution)/shard_map/ppermute | solution.py:501
  24.0 0.0 collective-permute-done.3.even_ref
  24.0 0.6 collective-permute-start.2
  24.6 1.6 %collective-permute-done.4.odd_ref = bf16[384,1024]{1,0:T(8,128)(2,1)} collective-permute-done((bf16[384,1024]{1,0:T(8,128)(2,1)}, bf16[384,1024]{1,0:T(8,128)(2,1)}, u32[]{:S(2)}, u32[]{:S(2)}) %collective-permute-start.4) | collective-permute-done | bytes 786464 | tf_op jit(solution)/shard_map/ppermute | solution.py:489
  26.2 1.9 %collective-permute-start = (bf16[512,384]{1,0:T(8,128)(2,1)}, bf16[512,384]{1,0:T(8,128)(2,1)}, u32[]{:S(2)}, u32[]{:S(2)}) collective-permute-start(bf16[512,384]{1,0:T(8,128)(2,1)} %get-tuple-element.26.rest_2_), channel_id=1, source_target_pairs={{2,8},{3,9},{4,16},{5,17},{6,24},{7,25},{8,2},{9,3},{12,18},{13,19... | collective-permute-start | bytes 1179656 | tf_op jit(solution)/shard_map/ppermute | solution.py:501
  28.1 16.7 %rows_operator.2 = (bf16[2048,1024]{1,0:T(8,128)(2,1)}, bf16[4096,768]{1,0:T(8,128)(2,1)}) custom-call(s32[16]{0:T(128)} %stack.71.where_ref, f32[7,16,128]{2,1,0:T(8,128)} %get-tuple-element.24.stencil_ref, f32[2048,1024]{1,0:T(8,128)} %p_ref.7, bf16[384,1024]{1,0:T(8,128)(2,1)} %collective-permute-done.3.even_ref, ...), custom_call_target="tpu_custom_call" | custom-call | flops 1 | bytes 1 | tf_op jit(solution)/shard_map/rows_operator/pallas_call | solution.py:449
  44.9 0.0 collective-permute-done.5.rest_0_
  44.9 0.0 copy-start
  44.9 0.0 collective-permute-done.6.rest_1_
  44.9 1.9 %collective-permute-start.7 = (bf16[512,384]{1,0:T(8,128)(2,1)}, bf16[512,384]{1,0:T(8,128)(2,1)}, u32[]{:S(2)}, u32[]{:S(2)}) collective-permute-start(bf16[512,384]{1,0:T(8,128)(2,1)} %get-tuple-element.35), channel_id=1, source_target_pairs={{1,2},{2,1},{3,4},{4,3},{5,6},{6,5},{9,10},{10,9},{11,12},{12,11},... | collective-permute-start | bytes 1179656 | tf_op jit(solution)/shard_map/ppermute | solution.py:489
  46.8 0.0 copy-done
  46.8 9.3 %columns_operator.2 = (bf16[2048,1024]{1,0:T(8,128)(2,1)}, bf16[384,1024]{1,0:T(8,128)(2,1)}, bf16[384,1024]{1,0:T(8,128)(2,1)}) custom-call(s32[16]{0:T(128)} %stack.71.where_ref, f32[7,8,128]{2,1,0:T(8,128)} %get-tuple-element.25.stencil_ref, f32[2048,1024]{1,0:T(8,128)} %p_ref.7, bf16[1040,384]{1,0:T(8,128)(2,1)} %copy-done, ...), custom_call_target="tpu_custom_call" | custom-call | flops 1 | bytes 1 | tf_op jit(solution)/shard_map/columns_operator/pallas_call | solution.py:320
  56.1 1.9 %collective-permute-start.8 = (bf16[384,1024]{1,0:T(8,128)(2,1)}, bf16[384,1024]{1,0:T(8,128)(2,1)}, u32[]{:S(2)}, u32[]{:S(2)}) collective-permute-start(bf16[384,1024]{1,0:T(8,128)(2,1)} %get-tuple-element.42), channel_id=1, source_target_pairs={{0,8},{8,0},{16,24},{24,16},{1,9},{9,1},{17,25},{25,17},{2,10},{10... | collective-permute-start | bytes 2359304 | tf_op jit(solution)/shard_map/ppermute | solution.py:489
  58.0 0.0 collective-permute-done.1.rest_1_
  58.0 4.4 %collective-permute-start.9 = (bf16[384,1024]{1,0:T(8,128)(2,1)}, bf16[384,1024]{1,0:T(8,128)(2,1)}, u32[]{:S(2)}, u32[]{:S(2)}) collective-permute-start(bf16[384,1024]{1,0:T(8,128)(2,1)} %get-tuple-element.43), channel_id=1, source_target_pairs={{8,16},{16,8},{9,17},{17,9},{10,18},{18,10},{11,19},{19,11},{12,20... | collective-permute-start | bytes 2359304 | tf_op jit(solution)/shard_map/ppermute | solution.py:489
  62.4 0.0 collective-permute-done.2.rest_3_
  62.5 0.0 collective-permute-done.rest_0_
  62.5 0.0 collective-permute-done.7.rest_4_
  62.5 9.1 %columns_operator.3.x_ref = bf16[2048,1024]{1,0:T(8,128)(2,1)} custom-call(s32[16]{0:T(128)} %stack.71.where_ref, f32[7,8,128]{2,1,0:T(8,128)} %get-tuple-element.25.stencil_ref, f32[2048,1024]{1,0:T(8,128)} %p_ref.7, bf16[512,384]{1,0:T(8,128)(2,1)} %collective-permute-done.rest_0_, ...), custom_call_target="tpu_custom_call", output_to_operand_aliasing={{}: (11, {})} | custom-call | flops 9999999827968 | bytes 9999999827968 | tf_op jit(solution)/shard_map/columns_operator/pallas_call | solution.py:320
  71.5 0.0 collective-permute-done.8.even_ref
  71.5 0.7 collective-permute-done.9.odd_ref
  72.2 13.4 %rows_operator.3 = f32[2048,1024]{1,0:T(8,128)} custom-call(s32[16]{0:T(128)} %stack.71.where_ref, f32[7,16,128]{2,1,0:T(8,128)} %get-tuple-element.24.stencil_ref, bf16[2048,1024]{1,0:T(8,128)(2,1)} %columns_operator.3.x_ref, bf16[384,1024]{1,0:T(8,128)(2,1)} %collective-permute-done.8.even_ref, bf16[384,1024]{1,0:T(8,128)(2,1)} %collective-permute-done.9.odd_ref, ...), custom_call_target="tpu_custom_call" | custom-call | flops 1 | bytes 1 | tf_op jit(solution)/shard_map/rows_operator/pallas_call | solution.py:449
Async XLA Ops:
  6.6 38.3 %collective-permute-start.5 = (bf16[1040,384]{1,0:T(8,128)(2,1)}, bf16[1040,384]{1,0:T(8,128)(2,1)S(1)}, u32[]{:S(2)}, u32[]{:S(2)}) collective-permute-start(bf16[1040,384]{1,0:T(8,128)(2,1)} %get-tuple-element.32), channel_id=1, source_target_pairs={{0,1},{1,0},{2,3},{3,2},{4,5},{5,4},{6,7},{7,6},{8,9},{9,8},{10,11... | collective-permute-start | bytes 2396168 | tf_op jit(solution)/shard_map/ppermute | solution.py:489
  6.6 38.2 %collective-permute-start.6 = (bf16[1040,384]{1,0:T(8,128)(2,1)}, bf16[1040,384]{1,0:T(8,128)(2,1)}, u32[]{:S(2)}, u32[]{:S(2)}) collective-permute-start(bf16[1040,384]{1,0:T(8,128)(2,1)} %get-tuple-element.33), channel_id=1, source_target_pairs={{1,2},{2,1},{3,4},{4,3},{5,6},{6,5},{9,10},{10,9},{11,12},{12,11},... | collective-permute-start | bytes 2396168 | tf_op jit(solution)/shard_map/ppermute | solution.py:489
  11.0 13.0 %collective-permute-start.3 = (bf16[384,1024]{1,0:T(8,128)(2,1)}, bf16[384,1024]{1,0:T(8,128)(2,1)}, u32[]{:S(2)}, u32[]{:S(2)}) collective-permute-start(bf16[384,1024]{1,0:T(8,128)(2,1)} %get-tuple-element.29), channel_id=1, source_target_pairs={{0,8},{8,0},{16,24},{24,16},{1,9},{9,1},{17,25},{25,17},{2,10},{10... | collective-permute-start | bytes 2359304 | tf_op jit(solution)/shard_map/ppermute | solution.py:489
  12.3 13.9 %collective-permute-start.4 = (bf16[384,1024]{1,0:T(8,128)(2,1)}, bf16[384,1024]{1,0:T(8,128)(2,1)}, u32[]{:S(2)}, u32[]{:S(2)}) collective-permute-start(bf16[384,1024]{1,0:T(8,128)(2,1)} %get-tuple-element.30), channel_id=1, source_target_pairs={{8,16},{16,8},{9,17},{17,9},{10,18},{18,10},{11,19},{19,11},{12,20... | collective-permute-start | bytes 2359304 | tf_op jit(solution)/shard_map/ppermute | solution.py:489
  22.1 36.0 %collective-permute-start.1 = (bf16[512,384]{1,0:T(8,128)(2,1)}, bf16[512,384]{1,0:T(8,128)(2,1)}, u32[]{:S(2)}, u32[]{:S(2)}) collective-permute-start(bf16[512,384]{1,0:T(8,128)(2,1)} %get-tuple-element.27), channel_id=1, source_target_pairs={{0,2},{2,10},{4,18},{6,26},{8,4},{9,1},{10,12},{11,9},{12,20},{13,... | collective-permute-start | bytes 1179656 | tf_op jit(solution)/shard_map/ppermute | solution.py:501
  24.0 38.4 %collective-permute-start.2 = (bf16[512,384]{1,0:T(8,128)(2,1)}, bf16[512,384]{1,0:T(8,128)(2,1)}, u32[]{:S(2)}, u32[]{:S(2)}) collective-permute-start(bf16[512,384]{1,0:T(8,128)(2,1)} %get-tuple-element.28), channel_id=1, source_target_pairs={{0,1},{1,0},{2,3},{3,2},{4,5},{5,4},{6,7},{7,6},{8,9},{9,8},{10,11... | collective-permute-start | bytes 1179656 | tf_op jit(solution)/shard_map/ppermute | solution.py:489
  26.2 36.2 %collective-permute-start = (bf16[512,384]{1,0:T(8,128)(2,1)}, bf16[512,384]{1,0:T(8,128)(2,1)}, u32[]{:S(2)}, u32[]{:S(2)}) collective-permute-start(bf16[512,384]{1,0:T(8,128)(2,1)} %get-tuple-element.26.rest_2_), channel_id=1, source_target_pairs={{2,8},{3,9},{4,16},{5,17},{6,24},{7,25},{8,2},{9,3},{12,18},{13,19... | collective-permute-start | bytes 1179656 | tf_op jit(solution)/shard_map/ppermute | solution.py:501
  44.9 2.0 %copy-start = (bf16[1040,384]{1,0:T(8,128)(2,1)}, bf16[1040,384]{1,0:T(8,128)(2,1)S(1)}, u32[]{:S(2)}) copy-start(bf16[1040,384]{1,0:T(8,128)(2,1)S(1)} %collective-permute-done.5.rest_0_) | copy-start | bytes 2396164
  44.9 17.6 %collective-permute-start.7 = (bf16[512,384]{1,0:T(8,128)(2,1)}, bf16[512,384]{1,0:T(8,128)(2,1)}, u32[]{:S(2)}, u32[]{:S(2)}) collective-permute-start(bf16[512,384]{1,0:T(8,128)(2,1)} %get-tuple-element.35), channel_id=1, source_target_pairs={{1,2},{2,1},{3,4},{4,3},{5,6},{6,5},{9,10},{10,9},{11,12},{12,11},... | collective-permute-start | bytes 1179656 | tf_op jit(solution)/shard_map/ppermute | solution.py:489
  56.1 15.4 %collective-permute-start.8 = (bf16[384,1024]{1,0:T(8,128)(2,1)}, bf16[384,1024]{1,0:T(8,128)(2,1)}, u32[]{:S(2)}, u32[]{:S(2)}) collective-permute-start(bf16[384,1024]{1,0:T(8,128)(2,1)} %get-tuple-element.42), channel_id=1, source_target_pairs={{0,8},{8,0},{16,24},{24,16},{1,9},{9,1},{17,25},{25,17},{2,10},{10... | collective-permute-start | bytes 2359304 | tf_op jit(solution)/shard_map/ppermute | solution.py:489
  58.0 14.2 %collective-permute-start.9 = (bf16[384,1024]{1,0:T(8,128)(2,1)}, bf16[384,1024]{1,0:T(8,128)(2,1)}, u32[]{:S(2)}, u32[]{:S(2)}) collective-permute-start(bf16[384,1024]{1,0:T(8,128)(2,1)} %get-tuple-element.43), channel_id=1, source_target_pairs={{8,16},{16,8},{9,17},{17,9},{10,18},{18,10},{11,19},{19,11},{12,20... | collective-permute-start | bytes 2359304 | tf_op jit(solution)/shard_map/ppermute | solution.py:489

commit v11 on v10

--- a/solution.py
+++ b/solution.py
@@ -164,14 +164,17 @@
                 for i in range(sizes[side] + 2 * steps):
                     lat = where_ref[5 + side] + i - steps
                     inside = jnp.logical_and(lat >= 0, lat < nlat)
-                    entry = index_ref[step_no, jnp.clip(lat, 0, nlat - 1)]
-                    values = (table_ref[0, entry], table_ref[1, entry], diffuse_ref[entry], inside.astype(F32))
-                    for k, value in enumerate(values):
-                        looked_up[k, i : i + 1, :] = jnp.full((1, nlon), value, F32)
-                here = looked_up[3] > 0.5
+                    entry = jnp.where(inside, index_ref[step_no, jnp.clip(lat, 0, nlat - 1)], -1)
+                    looked_up[i : i + 1, :] = jnp.full((1, nlon), entry, jnp.int32)
+                index = looked_up[...]
+                zonal = merid = diffuse = jnp.zeros(index.shape, F32)
+                for entry in range(wind_table.shape[0]):
+                    here = index == entry
+                    zonal = jnp.where(here, table_ref[0, entry], zonal)
+                    merid = jnp.where(here, table_ref[1, entry], merid)
+                    diffuse = jnp.where(here, diffuse_ref[entry], diffuse)
                 c, e, w, n, s = [
-                    jnp.where(here, term, 0.0)
-                    for term in stencil_terms(looked_up[0], looked_up[1], looked_up[2])
+                    jnp.where(index >= 0, term, 0.0) for term in stencil_terms(zonal, merid, diffuse)
                 ]
                 terms.append((c, w, e, n, s) if side else (c, e, w, n, s))
                 if side:
@@ -197,7 +200,7 @@
         + [jax.ShapeDtypeStruct((pairs * span, 2 * nlon), BF16)] * 2
         + [jax.ShapeDtypeStruct((5 * steps, lats + 2 * steps, nlon), F32)]
         + packs,
-        scratch_shapes=[pltpu.VMEM((4, size + 2 * steps, nlon), F32) for size in sizes]
+        scratch_shapes=[pltpu.VMEM((size + 2 * steps, nlon), jnp.int32) for size in sizes]
         + pack_scratch,
         compiler_params=params(),
         cost_estimate=cost(1),
@@ -543,11 +546,12 @@
     spans = [(0, half, 0), (half, half, half)]
     spans += [(rows_dev - outer, half, outer), (rows_dev - half, half, outer + half), (0, 16, 2 * outer)]
     pieces = [(row, size, (11 + k,), wide, k, there, 0) for row, size, there in spans for k in range(2)]
-    pieces += [((13 + k, j * nlon), nlon, 0, cols_dev, k + 2, j * nlon, 0) for k in range(2) for j in range(steps)]
+    end_pieces = [((13 + k, j * nlon), nlon, 0, cols_dev, k, j * nlon, 0) for k in range(2) for j in range(steps)]
     others = [((8 + k,), wide, (10,), inner, k, 0, nlon) for k in range(2)]
     others += [((7,), inner, (11 + k,), wide, k + 2, 0, 0) for k in range(2)]
-    sent = packed(covariance, where, pieces)
-    outers, ends = list(sent[:2]), list(sent[2:])
+    outers = list(packed(covariance, where, pieces))
+    later, outers[0] = lax.optimization_barrier((where, outers[0]))
+    ends = packed(covariance, later, end_pieces)
     outers = [exchanged(piece, "col", k) for k, piece in enumerate(outers)]
     ends = [exchanged(piece, "row", k) for k, piece in enumerate(ends)]
     row_s, col_s, *rest = stencils(

time: 87.4 us -> 87.8 us (level); the launches traced: 85.8 us -> 87.1 us
  Pallas kernels: 60.3 us -> 61.6 us
    pallas_call x1 -> x2, Pallas kernels: 5.16 us -> 6.72 us  [packed(): pl.pallas_call(kernel, in_specs=[pl.BlockSpec(memory_space=pltpu.SMEM), p...]
  transfers between devices with their start and end apart: 10 -> 10, of which waited for: 2 -> 2; matrix products, arithmetic and copies ran while one was open for 0% -> 0% of each run, Pallas kernels for 49% -> 52%
where the time goes in v11:
time: 87.8 us; the launch traced here: 87.1 us
  Pallas kernels  61.6 us (70%)
  starting transfers between devices  21.3 us (24%)
  waiting for transfers between devices  2.55 us (3%)
  between operations  1.02 us (1%)
    pallas_call x2, Pallas kernels, rows_operator(): pl.pallas_call(kernel, grid_spec=pltpu.PrefetchScalarGridSpec(num_scalar_...  30.1 us
    pallas_call x2, Pallas kernels, columns_operator(): pl.pallas_call(kernel, grid_spec=pltpu.PrefetchScalarGridSpec(num_scalar_...  18.3 us
    ppermute x8, starting transfers between devices, exchanged(): return lax.ppermute(block, axis, pairs)  17.4 us
    pallas_call x2, Pallas kernels, packed(): pl.pallas_call(kernel, in_specs=[pl.BlockSpec(memory_space=pltpu.SMEM), p...  6.72 us
    pallas_call x1, Pallas kernels, stencils(): pl.pallas_call(kernel, in_specs=[pl.BlockSpec(memory_space=pltpu.SMEM)] *...  6.48 us
    ppermute x2, starting transfers between devices, mirrored(): return lax.ppermute(block, ('row', 'col'), pairs)  3.83 us
    ppermute x8, waiting for transfers between devices, exchanged(): return lax.ppermute(block, axis, pairs)  2.55 us
  transfers between devices with their start and end apart: 10, of which 2 were waited for; matrix products, arithmetic and copies ran while one was open for 0% of the time, Pallas kernels for 52%

profile of v11, /device:TPU:5, one launch (start us, length us, event | category | flops | bytes accessed | tf_op | source)
XLA Modules:
  0.0 87.1 jit_solution(14560633590746128696)
XLA Ops:
  0.7 0.6 stack.71.where_ref
  1.3 3.4 %packed.2 = (bf16[1040,384]{1,0:T(8,128)(2,1)}, bf16[1040,384]{1,0:T(8,128)(2,1)}) custom-call(s32[16]{0:T(128)} %stack.71.where_ref, f32[2048,1024]{1,0:T(8,128)} %p_ref.9), custom_call_target="tpu_custom_call" | custom-call | flops 1 | bytes 1 | tf_op jit(solution)/shard_map/packed/pallas_call | solution.py:137
  4.7 0.1 collective-permute-start.5
  4.8 4.4 %collective-permute-start.6 = (bf16[1040,384]{1,0:T(8,128)(2,1)}, bf16[1040,384]{1,0:T(8,128)(2,1)}, u32[]{:S(2)}, u32[]{:S(2)}) collective-permute-start(bf16[1040,384]{1,0:T(8,128)(2,1)} %get-tuple-element.37), channel_id=1, source_target_pairs={{1,2},{2,1},{3,4},{4,3},{5,6},{6,5},{9,10},{10,9},{11,12},{12,11},... | collective-permute-start | bytes 2396168 | tf_op jit(solution)/shard_map/ppermute | solution.py:492
  9.2 3.3 %packed.3 = (bf16[384,1024]{1,0:T(8,128)(2,1)}, bf16[384,1024]{1,0:T(8,128)(2,1)}) custom-call(s32[16]{0:T(128)} %stack.71.where_ref, f32[2048,1024]{1,0:T(8,128)} %p_ref.9), custom_call_target="tpu_custom_call" | custom-call | flops 1 | bytes 1 | tf_op jit(solution)/shard_map/packed/pallas_call | solution.py:137
  12.5 1.3 %collective-permute-start.3 = (bf16[384,1024]{1,0:T(8,128)(2,1)}, bf16[384,1024]{1,0:T(8,128)(2,1)}, u32[]{:S(2)}, u32[]{:S(2)}) collective-permute-start(bf16[384,1024]{1,0:T(8,128)(2,1)} %get-tuple-element.33), channel_id=1, source_target_pairs={{0,8},{8,0},{16,24},{24,16},{1,9},{9,1},{17,25},{25,17},{2,10},{10... | collective-permute-start | bytes 2359304 | tf_op jit(solution)/shard_map/ppermute | solution.py:492
  13.8 3.0 %collective-permute-start.4 = (bf16[384,1024]{1,0:T(8,128)(2,1)}, bf16[384,1024]{1,0:T(8,128)(2,1)}, u32[]{:S(2)}, u32[]{:S(2)}) collective-permute-start(bf16[384,1024]{1,0:T(8,128)(2,1)} %get-tuple-element.34), channel_id=1, source_target_pairs={{8,16},{16,8},{9,17},{17,9},{10,18},{18,10},{11,19},{19,11},{12,20... | collective-permute-start | bytes 2359304 | tf_op jit(solution)/shard_map/ppermute | solution.py:492
  16.9 6.5 %stencils.1 = (f32[7,16,128]{2,1,0:T(8,128)}, f32[7,8,128]{2,1,0:T(8,128)}, bf16[3072,256]{1,0:T(8,128)(2,1)}, bf16[3072,256]{1,0:T(8,128)(2,1)}, f32[15,14,128]...) custom-call(f32[2,16]{1,0:T(2,128)} %bitcast.17, ...), custom_call_target="tpu_custom_call" | custom-call | flops 1 | bytes 1 | tf_op jit(solution)/shard_map/stencils/pallas_call | solution.py:195
  23.4 1.9 %collective-permute-start.1 = (bf16[512,384]{1,0:T(8,128)(2,1)}, bf16[512,384]{1,0:T(8,128)(2,1)}, u32[]{:S(2)}, u32[]{:S(2)}) collective-permute-start(bf16[512,384]{1,0:T(8,128)(2,1)} %get-tuple-element.29), channel_id=1, source_target_pairs={{0,2},{2,10},{4,18},{6,26},{8,4},{9,1},{10,12},{11,9},{12,20},{13,... | collective-permute-start | bytes 1179656 | tf_op jit(solution)/shard_map/ppermute | solution.py:504
  25.3 0.0 collective-permute-done.3.even_ref
  25.3 0.6 collective-permute-start.2
  25.9 1.8 %collective-permute-done.4.odd_ref = bf16[384,1024]{1,0:T(8,128)(2,1)} collective-permute-done((bf16[384,1024]{1,0:T(8,128)(2,1)}, bf16[384,1024]{1,0:T(8,128)(2,1)}, u32[]{:S(2)}, u32[]{:S(2)}) %collective-permute-start.4) | collective-permute-done | bytes 786464 | tf_op jit(solution)/shard_map/ppermute | solution.py:492
  27.7 1.9 %collective-permute-start = (bf16[512,384]{1,0:T(8,128)(2,1)}, bf16[512,384]{1,0:T(8,128)(2,1)}, u32[]{:S(2)}, u32[]{:S(2)}) collective-permute-start(bf16[512,384]{1,0:T(8,128)(2,1)} %get-tuple-element.28.rest_2_), channel_id=1, source_target_pairs={{2,8},{3,9},{4,16},{5,17},{6,24},{7,25},{8,2},{9,3},{12,18},{13,19... | collective-permute-start | bytes 1179656 | tf_op jit(solution)/shard_map/ppermute | solution.py:504
  29.7 16.7 %rows_operator.2 = (bf16[2048,1024]{1,0:T(8,128)(2,1)}, bf16[4096,768]{1,0:T(8,128)(2,1)}) custom-call(s32[16]{0:T(128)} %stack.71.where_ref, f32[7,16,128]{2,1,0:T(8,128)} %get-tuple-element.26.stencil_ref, f32[2048,1024]{1,0:T(8,128)} %p_ref.9, bf16[384,1024]{1,0:T(8,128)(2,1)} %collective-permute-done.3.even_ref, ...), custom_call_target="tpu_custom_call" | custom-call | flops 1 | bytes 1 | tf_op jit(solution)/shard_map/rows_operator/pallas_call | solution.py:452
  46.4 0.0 collective-permute-done.5.rest_0_
  46.4 0.0 copy-start
  46.4 0.0 collective-permute-done.6.rest_1_
  46.4 1.9 %collective-permute-start.7 = (bf16[512,384]{1,0:T(8,128)(2,1)}, bf16[512,384]{1,0:T(8,128)(2,1)}, u32[]{:S(2)}, u32[]{:S(2)}) collective-permute-start(bf16[512,384]{1,0:T(8,128)(2,1)} %get-tuple-element.39), channel_id=1, source_target_pairs={{1,2},{2,1},{3,4},{4,3},{5,6},{6,5},{9,10},{10,9},{11,12},{12,11},... | collective-permute-start | bytes 1179656 | tf_op jit(solution)/shard_map/ppermute | solution.py:492
  48.3 0.0 copy-done
  48.3 9.3 %columns_operator.2 = (bf16[2048,1024]{1,0:T(8,128)(2,1)}, bf16[384,1024]{1,0:T(8,128)(2,1)}, bf16[384,1024]{1,0:T(8,128)(2,1)}) custom-call(s32[16]{0:T(128)} %stack.71.where_ref, f32[7,8,128]{2,1,0:T(8,128)} %get-tuple-element.27.stencil_ref, f32[2048,1024]{1,0:T(8,128)} %p_ref.9, bf16[1040,384]{1,0:T(8,128)(2,1)} %copy-done, ...), custom_call_target="tpu_custom_call" | custom-call | flops 1 | bytes 1 | tf_op jit(solution)/shard_map/columns_operator/pallas_call | solution.py:323
  57.6 0.9 %collective-permute-start.8 = (bf16[384,1024]{1,0:T(8,128)(2,1)}, bf16[384,1024]{1,0:T(8,128)(2,1)}, u32[]{:S(2)}, u32[]{:S(2)}) collective-permute-start(bf16[384,1024]{1,0:T(8,128)(2,1)} %get-tuple-element.46), channel_id=1, source_target_pairs={{0,8},{8,0},{16,24},{24,16},{1,9},{9,1},{17,25},{25,17},{2,10},{10... | collective-permute-start | bytes 2359304 | tf_op jit(solution)/shard_map/ppermute | solution.py:492
  58.5 0.0 collective-permute-done.1.rest_1_
  58.6 5.2 %collective-permute-start.9 = (bf16[384,1024]{1,0:T(8,128)(2,1)}, bf16[384,1024]{1,0:T(8,128)(2,1)}, u32[]{:S(2)}, u32[]{:S(2)}) collective-permute-start(bf16[384,1024]{1,0:T(8,128)(2,1)} %get-tuple-element.47), channel_id=1, source_target_pairs={{8,16},{16,8},{9,17},{17,9},{10,18},{18,10},{11,19},{19,11},{12,20... | collective-permute-start | bytes 2359304 | tf_op jit(solution)/shard_map/ppermute | solution.py:492
  63.8 0.0 collective-permute-done.2.rest_3_
  63.8 0.0 collective-permute-done.rest_0_
  63.8 0.0 collective-permute-done.7.rest_4_
  63.8 9.1 %columns_operator.3.x_ref = bf16[2048,1024]{1,0:T(8,128)(2,1)} custom-call(s32[16]{0:T(128)} %stack.71.where_ref, f32[7,8,128]{2,1,0:T(8,128)} %get-tuple-element.27.stencil_ref, f32[2048,1024]{1,0:T(8,128)} %p_ref.9, bf16[512,384]{1,0:T(8,128)(2,1)} %collective-permute-done.rest_0_, ...), custom_call_target="tpu_custom_call", output_to_operand_aliasing={{}: (11, {})} | custom-call | flops 9999999827968 | bytes 9999999827968 | tf_op jit(solution)/shard_map/columns_operator/pallas_call | solution.py:323
  72.9 0.0 collective-permute-done.8.even_ref
  72.9 0.7 collective-permute-done.9.odd_ref
  73.6 13.4 %rows_operator.3 = f32[2048,1024]{1,0:T(8,128)} custom-call(s32[16]{0:T(128)} %stack.71.where_ref, f32[7,16,128]{2,1,0:T(8,128)} %get-tuple-element.26.stencil_ref, bf16[2048,1024]{1,0:T(8,128)(2,1)} %columns_operator.3.x_ref, bf16[384,1024]{1,0:T(8,128)(2,1)} %collective-permute-done.8.even_ref, bf16[384,1024]{1,0:T(8,128)(2,1)} %collective-permute-done.9.odd_ref, ...), custom_call_target="tpu_custom_call" | custom-call | flops 1 | bytes 1 | tf_op jit(solution)/shard_map/rows_operator/pallas_call | solution.py:452
Async XLA Ops:
  4.7 41.6 %collective-permute-start.5 = (bf16[1040,384]{1,0:T(8,128)(2,1)}, bf16[1040,384]{1,0:T(8,128)(2,1)S(1)}, u32[]{:S(2)}, u32[]{:S(2)}) collective-permute-start(bf16[1040,384]{1,0:T(8,128)(2,1)} %get-tuple-element.36), channel_id=1, source_target_pairs={{0,1},{1,0},{2,3},{3,2},{4,5},{5,4},{6,7},{7,6},{8,9},{9,8},{10,11... | collective-permute-start | bytes 2396168 | tf_op jit(solution)/shard_map/ppermute | solution.py:492
  4.8 41.6 %collective-permute-start.6 = (bf16[1040,384]{1,0:T(8,128)(2,1)}, bf16[1040,384]{1,0:T(8,128)(2,1)}, u32[]{:S(2)}, u32[]{:S(2)}) collective-permute-start(bf16[1040,384]{1,0:T(8,128)(2,1)} %get-tuple-element.37), channel_id=1, source_target_pairs={{1,2},{2,1},{3,4},{4,3},{5,6},{6,5},{9,10},{10,9},{11,12},{12,11},... | collective-permute-start | bytes 2396168 | tf_op jit(solution)/shard_map/ppermute | solution.py:492
  12.5 12.8 %collective-permute-start.3 = (bf16[384,1024]{1,0:T(8,128)(2,1)}, bf16[384,1024]{1,0:T(8,128)(2,1)}, u32[]{:S(2)}, u32[]{:S(2)}) collective-permute-start(bf16[384,1024]{1,0:T(8,128)(2,1)} %get-tuple-element.33), channel_id=1, source_target_pairs={{0,8},{8,0},{16,24},{24,16},{1,9},{9,1},{17,25},{25,17},{2,10},{10... | collective-permute-start | bytes 2359304 | tf_op jit(solution)/shard_map/ppermute | solution.py:492
  13.8 13.9 %collective-permute-start.4 = (bf16[384,1024]{1,0:T(8,128)(2,1)}, bf16[384,1024]{1,0:T(8,128)(2,1)}, u32[]{:S(2)}, u32[]{:S(2)}) collective-permute-start(bf16[384,1024]{1,0:T(8,128)(2,1)} %get-tuple-element.34), channel_id=1, source_target_pairs={{8,16},{16,8},{9,17},{17,9},{10,18},{18,10},{11,19},{19,11},{12,20... | collective-permute-start | bytes 2359304 | tf_op jit(solution)/shard_map/ppermute | solution.py:492
  23.4 35.2 %collective-permute-start.1 = (bf16[512,384]{1,0:T(8,128)(2,1)}, bf16[512,384]{1,0:T(8,128)(2,1)}, u32[]{:S(2)}, u32[]{:S(2)}) collective-permute-start(bf16[512,384]{1,0:T(8,128)(2,1)} %get-tuple-element.29), channel_id=1, source_target_pairs={{0,2},{2,10},{4,18},{6,26},{8,4},{9,1},{10,12},{11,9},{12,20},{13,... | collective-permute-start | bytes 1179656 | tf_op jit(solution)/shard_map/ppermute | solution.py:504
  25.3 38.5 %collective-permute-start.2 = (bf16[512,384]{1,0:T(8,128)(2,1)}, bf16[512,384]{1,0:T(8,128)(2,1)}, u32[]{:S(2)}, u32[]{:S(2)}) collective-permute-start(bf16[512,384]{1,0:T(8,128)(2,1)} %get-tuple-element.30), channel_id=1, source_target_pairs={{0,1},{1,0},{2,3},{3,2},{4,5},{5,4},{6,7},{7,6},{8,9},{9,8},{10,11... | collective-permute-start | bytes 1179656 | tf_op jit(solution)/shard_map/ppermute | solution.py:492
  27.7 36.0 %collective-permute-start = (bf16[512,384]{1,0:T(8,128)(2,1)}, bf16[512,384]{1,0:T(8,128)(2,1)}, u32[]{:S(2)}, u32[]{:S(2)}) collective-permute-start(bf16[512,384]{1,0:T(8,128)(2,1)} %get-tuple-element.28.rest_2_), channel_id=1, source_target_pairs={{2,8},{3,9},{4,16},{5,17},{6,24},{7,25},{8,2},{9,3},{12,18},{13,19... | collective-permute-start | bytes 1179656 | tf_op jit(solution)/shard_map/ppermute | solution.py:504
  46.4 2.0 %copy-start = (bf16[1040,384]{1,0:T(8,128)(2,1)}, bf16[1040,384]{1,0:T(8,128)(2,1)S(1)}, u32[]{:S(2)}) copy-start(bf16[1040,384]{1,0:T(8,128)(2,1)S(1)} %collective-permute-done.5.rest_0_) | copy-start | bytes 2396164
  46.4 17.4 %collective-permute-start.7 = (bf16[512,384]{1,0:T(8,128)(2,1)}, bf16[512,384]{1,0:T(8,128)(2,1)}, u32[]{:S(2)}, u32[]{:S(2)}) collective-permute-start(bf16[512,384]{1,0:T(8,128)(2,1)} %get-tuple-element.39), channel_id=1, source_target_pairs={{1,2},{2,1},{3,4},{4,3},{5,6},{6,5},{9,10},{10,9},{11,12},{12,11},... | collective-permute-start | bytes 1179656 | tf_op jit(solution)/shard_map/ppermute | solution.py:492
  57.6 15.3 %collective-permute-start.8 = (bf16[384,1024]{1,0:T(8,128)(2,1)}, bf16[384,1024]{1,0:T(8,128)(2,1)}, u32[]{:S(2)}, u32[]{:S(2)}) collective-permute-start(bf16[384,1024]{1,0:T(8,128)(2,1)} %get-tuple-element.46), channel_id=1, source_target_pairs={{0,8},{8,0},{16,24},{24,16},{1,9},{9,1},{17,25},{25,17},{2,10},{10... | collective-permute-start | bytes 2359304 | tf_op jit(solution)/shard_map/ppermute | solution.py:492
  58.6 15.0 %collective-permute-start.9 = (bf16[384,1024]{1,0:T(8,128)(2,1)}, bf16[384,1024]{1,0:T(8,128)(2,1)}, u32[]{:S(2)}, u32[]{:S(2)}) collective-permute-start(bf16[384,1024]{1,0:T(8,128)(2,1)} %get-tuple-element.47), channel_id=1, source_target_pairs={{8,16},{16,8},{9,17},{17,9},{10,18},{18,10},{11,19},{19,11},{12,20... | collective-permute-start | bytes 2359304 | tf_op jit(solution)/shard_map/ppermute | solution.py:492

commit v12 on v11

--- a/solution.py
+++ b/solution.py
@@ -302,16 +302,18 @@
                 def _(odd=odd):
                     outs[1 + odd][...] = t_ref[size - wide :, :]
 
-    halo_at = (lambda i, at: (i, 0)) if len(halos) == 1 else (lambda i, at: (0, 0))
+    members = [member if isinstance(member, tuple) else (member, 0) for group in halos for member in group]
     in_specs = [
         pl.BlockSpec(stencil.shape, lambda i, at: (0, 0, 0)),
         pl.BlockSpec((size, cols), lambda i, at: (block_at(i, at), 0)),
     ]
-    in_specs += [pl.BlockSpec((size, wide), halo_at)] * sum(len(group) for group in halos)
+    for _, block in members:
+        halo_at = (lambda i, at: (i, 0)) if len(halos) == 1 else (lambda i, at, block=block: (block, 0))
+        in_specs.append(pl.BlockSpec((size, wide), halo_at))
     in_specs += [pl.BlockSpec(block.shape, lambda i, at, n=block.ndim: (0,) * n) for block in blocks]
     out_specs = [pl.BlockSpec((size, cols), lambda i, at: (block_at(i, at), 0))]
     out_shape = [jax.ShapeDtypeStruct((rows, cols), BF16)]
-    operands = [where, stencil, covariance] + [array for group in halos for array in group] + list(blocks)
+    operands = [where, stencil, covariance] + [array for array, _ in members] + list(blocks)
     aliases = {}
     if ends:
         out_specs += [pl.BlockSpec((wide, cols), lambda i, at: (0, 0))] * 2
@@ -544,11 +546,12 @@
     ).astype(jnp.int32)
     half = outer // 2
     spans = [(0, half, 0), (half, half, half)]
-    spans += [(rows_dev - outer, half, outer), (rows_dev - half, half, outer + half), (0, 16, 2 * outer)]
+    spans += [(rows_dev - outer, half, outer), (rows_dev - half, half, outer + half)]
     pieces = [(row, size, (11 + k,), wide, k, there, 0) for row, size, there in spans for k in range(2)]
+    pieces += [((7,), inner, (11,), wide, 0, 2 * outer, 0), (0, 16, (12,), wide, 1, 2 * outer, 0)]
     end_pieces = [((13 + k, j * nlon), nlon, 0, cols_dev, k, j * nlon, 0) for k in range(2) for j in range(steps)]
     others = [((8 + k,), wide, (10,), inner, k, 0, nlon) for k in range(2)]
-    others += [((7,), inner, (11 + k,), wide, k + 2, 0, 0) for k in range(2)]
+    others += [((7,), inner, (12,), wide, 2, 0, 0)]
     outers = list(packed(covariance, where, pieces))
     later, outers[0] = lax.optimization_barrier((where, outers[0]))
     ends = packed(covariance, later, end_pieces)
@@ -557,22 +560,19 @@
     row_s, col_s, *rest = stencils(
         wind_table, diffusivity, wind_index, where, lat_rows, lats, nlon, covariance, others
     )
-    col_blocks, mirrors, inners = rest[:3], rest[3:5], rest[5:7]
+    col_blocks, mirrors, inner_odd = rest[:3], rest[3:5], rest[5]
     mirrors = [mirrored(piece, k) for k, piece in enumerate(mirrors)] + [mirrors[0]]
 
     operator_times_prior, blocks = rows_operator(covariance, *ends, row_s, where, steps, nlon, BF16)
-    inners[0] = exchanged(inners[0], "col", 0)
-    operator_times_prior, outers, inners[1] = lax.optimization_barrier(
-        (operator_times_prior, outers, inners[1])
-    )
-    inners[1] = exchanged(inners[1], "col", 1)
+    operator_times_prior, outers, inner_odd = lax.optimization_barrier((operator_times_prior, outers, inner_odd))
+    inner_odd = exchanged(inner_odd, "col", 1)
     mirror, *ends = columns_operator(
         covariance, [outers], col_s, col_blocks, where, near, steps, nlon, 2, lambda i, at: i * (lat_rows // near - 1),
         None, True,
     )
     ends = [exchanged(piece, "row", k) for k, piece in enumerate(ends)]
     (mirror,) = columns_operator(
-        covariance, [mirrors, inners], col_s, col_blocks, where, own, steps, nlon, 2, lambda i, at: at[i], mirror, False,
+        covariance, [mirrors, [(outers[0], 2 * near // own), inner_odd]], col_s, col_blocks, where, own, steps, nlon, 2, lambda i, at: at[i], mirror, False,
         10 ** 13,
     )
     (predicted_spread_matrix,) = rows_operator(

time: 87.8 us -> 91.7 us (1.044)
  waiting for transfers between devices: 2.55 us -> 6.54 us
    ppermute x8 -> x7, waiting for transfers between devices: 2.55 us -> 6.53 us  [exchanged(): return lax.ppermute(block, axis, pairs)]
    ppermute x8 -> x7, starting transfers between devices: 17.4 us -> 16.9 us  [exchanged(): return lax.ppermute(block, axis, pairs)]
  transfers between devices with their start and end apart: 10 -> 9, of which waited for: 2 -> 3; matrix products, arithmetic and copies ran while one was open for 0% -> 0% of each run, Pallas kernels for 52% -> 49%
where the time goes in v12:
time: 91.7 us; the launch traced here: 91.2 us
  Pallas kernels  62.2 us (68%)
  starting transfers between devices  20.8 us (23%)
  waiting for transfers between devices  6.54 us (7%)
  between operations  1.01 us (1%)
    pallas_call x2, Pallas kernels, rows_operator(): pl.pallas_call(kernel, grid_spec=pltpu.PrefetchScalarGridSpec(num_scalar_...  30.1 us
    pallas_call x2, Pallas kernels, columns_operator(): pl.pallas_call(kernel, grid_spec=pltpu.PrefetchScalarGridSpec(num_scalar_...  18.4 us
    ppermute x7, starting transfers between devices, exchanged(): return lax.ppermute(block, axis, pairs)  16.9 us
    pallas_call x2, Pallas kernels, packed(): pl.pallas_call(kernel, in_specs=[pl.BlockSpec(memory_space=pltpu.SMEM), p...  7.35 us
    ppermute x7, waiting for transfers between devices, exchanged(): return lax.ppermute(block, axis, pairs)  6.53 us
    pallas_call x1, Pallas kernels, stencils(): pl.pallas_call(kernel, in_specs=[pl.BlockSpec(memory_space=pltpu.SMEM)] *...  6.31 us
    ppermute x2, starting transfers between devices, mirrored(): return lax.ppermute(block, ('row', 'col'), pairs)  3.84 us
  transfers between devices with their start and end apart: 9, of which 3 were waited for; matrix products, arithmetic and copies ran while one was open for 0% of the time, Pallas kernels for 49%

profile of v12, /device:TPU:5, one launch (start us, length us, event | category | flops | bytes accessed | tf_op | source)
XLA Modules:
  0.0 91.2 jit_solution(6360152338839550455)
XLA Ops:
  0.7 0.7 stack.71.where_ref
  1.4 4.0 %packed.2 = (bf16[1536,384]{1,0:T(8,128)(2,1)}, bf16[1040,384]{1,0:T(8,128)(2,1)}) custom-call(s32[16]{0:T(128)} %stack.71.where_ref, f32[2048,1024]{1,0:T(8,128)} %p_ref.9), custom_call_target="tpu_custom_call" | custom-call | flops 1 | bytes 1 | tf_op jit(solution)/shard_map/packed/pallas_call | solution.py:137
  5.4 0.1 collective-permute-start.4
  5.5 4.4 %collective-permute-start.5 = (bf16[1040,384]{1,0:T(8,128)(2,1)}, bf16[1040,384]{1,0:T(8,128)(2,1)S(1)}, u32[]{:S(2)}, u32[]{:S(2)}) collective-permute-start(bf16[1040,384]{1,0:T(8,128)(2,1)} %get-tuple-element.35), channel_id=1, source_target_pairs={{1,2},{2,1},{3,4},{4,3},{5,6},{6,5},{9,10},{10,9},{11,12},{12,11},... | collective-permute-start | bytes 2396168 | tf_op jit(solution)/shard_map/ppermute | solution.py:494
  9.9 3.3 %packed.3 = (bf16[384,1024]{1,0:T(8,128)(2,1)}, bf16[384,1024]{1,0:T(8,128)(2,1)}) custom-call(s32[16]{0:T(128)} %stack.71.where_ref, f32[2048,1024]{1,0:T(8,128)} %p_ref.9), custom_call_target="tpu_custom_call" | custom-call | flops 1 | bytes 1 | tf_op jit(solution)/shard_map/packed/pallas_call | solution.py:137
  13.2 1.3 %collective-permute-start.2 = (bf16[384,1024]{1,0:T(8,128)(2,1)}, bf16[384,1024]{1,0:T(8,128)(2,1)}, u32[]{:S(2)}, u32[]{:S(2)}) collective-permute-start(bf16[384,1024]{1,0:T(8,128)(2,1)} %get-tuple-element.31), channel_id=1, source_target_pairs={{0,8},{8,0},{16,24},{24,16},{1,9},{9,1},{17,25},{25,17},{2,10},{10... | collective-permute-start | bytes 2359304 | tf_op jit(solution)/shard_map/ppermute | solution.py:494
  14.5 3.0 %collective-permute-start.3 = (bf16[384,1024]{1,0:T(8,128)(2,1)}, bf16[384,1024]{1,0:T(8,128)(2,1)}, u32[]{:S(2)}, u32[]{:S(2)}) collective-permute-start(bf16[384,1024]{1,0:T(8,128)(2,1)} %get-tuple-element.32), channel_id=1, source_target_pairs={{8,16},{16,8},{9,17},{17,9},{10,18},{18,10},{11,19},{19,11},{12,20... | collective-permute-start | bytes 2359304 | tf_op jit(solution)/shard_map/ppermute | solution.py:494
  17.5 6.3 %stencils.1 = (f32[7,16,128]{2,1,0:T(8,128)}, f32[7,8,128]{2,1,0:T(8,128)}, bf16[3072,256]{1,0:T(8,128)(2,1)}, bf16[3072,256]{1,0:T(8,128)(2,1)}, f32[15,14,128]...) custom-call(f32[2,16]{1,0:T(2,128)} %bitcast.17, f32[16]{0:T(128)} %diffuse_ref.1, ...), custom_call_target="tpu_custom_call" | custom-call | flops 1 | bytes 1 | tf_op jit(solution)/shard_map/stencils/pallas_call | solution.py:195
  23.9 1.9 %collective-permute-start.1 = (bf16[512,384]{1,0:T(8,128)(2,1)}, bf16[512,384]{1,0:T(8,128)(2,1)}, u32[]{:S(2)}, u32[]{:S(2)}) collective-permute-start(bf16[512,384]{1,0:T(8,128)(2,1)} %get-tuple-element.28), channel_id=1, source_target_pairs={{0,2},{2,10},{4,18},{6,26},{8,4},{9,1},{10,12},{11,9},{12,20},{13,... | collective-permute-start | bytes 1179656 | tf_op jit(solution)/shard_map/ppermute | solution.py:506
  25.8 0.0 collective-permute-done.2.even_ref
  25.8 1.9 %collective-permute-start = (bf16[512,384]{1,0:T(8,128)(2,1)}, bf16[512,384]{1,0:T(8,128)(2,1)}, u32[]{:S(2)}, u32[]{:S(2)}) collective-permute-start(bf16[512,384]{1,0:T(8,128)(2,1)} %get-tuple-element.27.rest_2_), channel_id=1, source_target_pairs={{2,8},{3,9},{4,16},{5,17},{6,24},{7,25},{8,2},{9,3},{12,18},{13,19... | collective-permute-start | bytes 1179656 | tf_op jit(solution)/shard_map/ppermute | solution.py:506
  27.7 0.7 collective-permute-done.3.odd_ref
  28.4 16.7 %rows_operator.2 = (bf16[2048,1024]{1,0:T(8,128)(2,1)}, bf16[4096,768]{1,0:T(8,128)(2,1)}) custom-call(s32[16]{0:T(128)} %stack.71.where_ref, f32[7,16,128]{2,1,0:T(8,128)} %get-tuple-element.25.stencil_ref, f32[2048,1024]{1,0:T(8,128)} %p_ref.9, bf16[384,1024]{1,0:T(8,128)(2,1)} %collective-permute-done.2.even_ref, ...), custom_call_target="tpu_custom_call" | custom-call | flops 1 | bytes 1 | tf_op jit(solution)/shard_map/rows_operator/pallas_call | solution.py:454
  45.1 0.0 collective-permute-done.5.rest_1_
  45.1 0.0 copy-start
  45.1 4.6 %collective-permute-done.4.rest_0_.rest_3_ = bf16[1536,384]{1,0:T(8,128)(2,1)} collective-permute-done((bf16[1536,384]{1,0:T(8,128)(2,1)}, bf16[1536,384]{1,0:T(8,128)(2,1)}, u32[]{:S(2)}, u32[]{:S(2)}) %collective-permute-start.4) | collective-permute-done | bytes 1179680 | tf_op jit(solution)/shard_map/ppermute | solution.py:494
  49.7 3.1 %collective-permute-start.6 = (bf16[512,384]{1,0:T(8,128)(2,1)}, bf16[512,384]{1,0:T(8,128)(2,1)}, u32[]{:S(2)}, u32[]{:S(2)}) collective-permute-start(bf16[512,384]{1,0:T(8,128)(2,1)} %get-tuple-element.38), channel_id=1, source_target_pairs={{1,2},{2,1},{3,4},{4,3},{5,6},{6,5},{9,10},{10,9},{11,12},{12,11},... | collective-permute-start | bytes 1179656 | tf_op jit(solution)/shard_map/ppermute | solution.py:494
  52.9 0.0 copy-done
  52.9 9.3 %columns_operator.2 = (bf16[2048,1024]{1,0:T(8,128)(2,1)}, bf16[384,1024]{1,0:T(8,128)(2,1)}, bf16[384,1024]{1,0:T(8,128)(2,1)}) custom-call(s32[16]{0:T(128)} %stack.71.where_ref, f32[7,8,128]{2,1,0:T(8,128)} %get-tuple-element.26.stencil_ref, f32[2048,1024]{1,0:T(8,128)} %p_ref.9, bf16[1536,384]{1,0:T(8,128)(2,1)} %collective-permute-done.4.rest_0_.rest_3_, ...), custom_call_target="tpu_custom_call" | custom-call | flops 1 | bytes 1 | tf_op jit(solution)/shard_map/columns_operator/pallas_call | solution.py:325
  62.2 1.8 %collective-permute-start.7 = (bf16[384,1024]{1,0:T(8,128)(2,1)}, bf16[384,1024]{1,0:T(8,128)(2,1)}, u32[]{:S(2)}, u32[]{:S(2)}) collective-permute-start(bf16[384,1024]{1,0:T(8,128)(2,1)} %get-tuple-element.44), channel_id=1, source_target_pairs={{0,8},{8,0},{16,24},{24,16},{1,9},{9,1},{17,25},{25,17},{2,10},{10... | collective-permute-start | bytes 2359304 | tf_op jit(solution)/shard_map/ppermute | solution.py:494
  64.0 3.2 %collective-permute-start.8 = (bf16[384,1024]{1,0:T(8,128)(2,1)}, bf16[384,1024]{1,0:T(8,128)(2,1)}, u32[]{:S(2)}, u32[]{:S(2)}) collective-permute-start(bf16[384,1024]{1,0:T(8,128)(2,1)} %get-tuple-element.45), channel_id=1, source_target_pairs={{8,16},{16,8},{9,17},{17,9},{10,18},{18,10},{11,19},{19,11},{12,20... | collective-permute-start | bytes 2359304 | tf_op jit(solution)/shard_map/ppermute | solution.py:494
  67.2 0.0 collective-permute-done.1.rest_1_
  67.2 0.0 collective-permute-done.rest_0_
  67.2 0.0 collective-permute-done.6.rest_4_
  67.3 9.1 %columns_operator.3.x_ref = bf16[2048,1024]{1,0:T(8,128)(2,1)} custom-call(s32[16]{0:T(128)} %stack.71.where_ref, f32[7,8,128]{2,1,0:T(8,128)} %get-tuple-element.26.stencil_ref, f32[2048,1024]{1,0:T(8,128)} %p_ref.9, bf16[512,384]{1,0:T(8,128)(2,1)} %collective-permute-done.rest_0_, ...), custom_call_target="tpu_custom_call", output_to_operand_aliasing={{}: (11, {})} | custom-call | flops 9999999827968 | bytes 9999999827968 | tf_op jit(solution)/shard_map/columns_operator/pallas_call | solution.py:325
  76.4 0.0 collective-permute-done.7.even_ref
  76.4 1.2 %collective-permute-done.8.odd_ref = bf16[384,1024]{1,0:T(8,128)(2,1)} collective-permute-done((bf16[384,1024]{1,0:T(8,128)(2,1)}, bf16[384,1024]{1,0:T(8,128)(2,1)}, u32[]{:S(2)}, u32[]{:S(2)}) %collective-permute-start.8) | collective-permute-done | bytes 786464 | tf_op jit(solution)/shard_map/ppermute | solution.py:494
  77.6 13.4 %rows_operator.3 = f32[2048,1024]{1,0:T(8,128)} custom-call(s32[16]{0:T(128)} %stack.71.where_ref, f32[7,16,128]{2,1,0:T(8,128)} %get-tuple-element.25.stencil_ref, bf16[2048,1024]{1,0:T(8,128)(2,1)} %columns_operator.3.x_ref, bf16[384,1024]{1,0:T(8,128)(2,1)} %collective-permute-done.7.even_ref, bf16[384,1024]{1,0:T(8,128)(2,1)} %collective-permute-done.8.odd_ref, ...), custom_call_target="tpu_custom_call" | custom-call | flops 1 | bytes 1 | tf_op jit(solution)/shard_map/rows_operator/pallas_call | solution.py:454
Async XLA Ops:
  5.4 44.3 %collective-permute-start.4 = (bf16[1536,384]{1,0:T(8,128)(2,1)}, bf16[1536,384]{1,0:T(8,128)(2,1)}, u32[]{:S(2)}, u32[]{:S(2)}) collective-permute-start(bf16[1536,384]{1,0:T(8,128)(2,1)} %get-tuple-element.34), channel_id=1, source_target_pairs={{0,1},{1,0},{2,3},{3,2},{4,5},{5,4},{6,7},{7,6},{8,9},{9,8},{10,11... | collective-permute-start | bytes 3538952 | tf_op jit(solution)/shard_map/ppermute | solution.py:494
  5.5 39.6 %collective-permute-start.5 = (bf16[1040,384]{1,0:T(8,128)(2,1)}, bf16[1040,384]{1,0:T(8,128)(2,1)S(1)}, u32[]{:S(2)}, u32[]{:S(2)}) collective-permute-start(bf16[1040,384]{1,0:T(8,128)(2,1)} %get-tuple-element.35), channel_id=1, source_target_pairs={{1,2},{2,1},{3,4},{4,3},{5,6},{6,5},{9,10},{10,9},{11,12},{12,11},... | collective-permute-start | bytes 2396168 | tf_op jit(solution)/shard_map/ppermute | solution.py:494
  13.2 12.6 %collective-permute-start.2 = (bf16[384,1024]{1,0:T(8,128)(2,1)}, bf16[384,1024]{1,0:T(8,128)(2,1)}, u32[]{:S(2)}, u32[]{:S(2)}) collective-permute-start(bf16[384,1024]{1,0:T(8,128)(2,1)} %get-tuple-element.31), channel_id=1, source_target_pairs={{0,8},{8,0},{16,24},{24,16},{1,9},{9,1},{17,25},{25,17},{2,10},{10... | collective-permute-start | bytes 2359304 | tf_op jit(solution)/shard_map/ppermute | solution.py:494
  14.5 13.9 %collective-permute-start.3 = (bf16[384,1024]{1,0:T(8,128)(2,1)}, bf16[384,1024]{1,0:T(8,128)(2,1)}, u32[]{:S(2)}, u32[]{:S(2)}) collective-permute-start(bf16[384,1024]{1,0:T(8,128)(2,1)} %get-tuple-element.32), channel_id=1, source_target_pairs={{8,16},{16,8},{9,17},{17,9},{10,18},{18,10},{11,19},{19,11},{12,20... | collective-permute-start | bytes 2359304 | tf_op jit(solution)/shard_map/ppermute | solution.py:494
  23.9 43.4 %collective-permute-start.1 = (bf16[512,384]{1,0:T(8,128)(2,1)}, bf16[512,384]{1,0:T(8,128)(2,1)}, u32[]{:S(2)}, u32[]{:S(2)}) collective-permute-start(bf16[512,384]{1,0:T(8,128)(2,1)} %get-tuple-element.28), channel_id=1, source_target_pairs={{0,2},{2,10},{4,18},{6,26},{8,4},{9,1},{10,12},{11,9},{12,20},{13,... | collective-permute-start | bytes 1179656 | tf_op jit(solution)/shard_map/ppermute | solution.py:506
  25.8 41.4 %collective-permute-start = (bf16[512,384]{1,0:T(8,128)(2,1)}, bf16[512,384]{1,0:T(8,128)(2,1)}, u32[]{:S(2)}, u32[]{:S(2)}) collective-permute-start(bf16[512,384]{1,0:T(8,128)(2,1)} %get-tuple-element.27.rest_2_), channel_id=1, source_target_pairs={{2,8},{3,9},{4,16},{5,17},{6,24},{7,25},{8,2},{9,3},{12,18},{13,19... | collective-permute-start | bytes 1179656 | tf_op jit(solution)/shard_map/ppermute | solution.py:506
  45.1 7.8 %copy-start = (bf16[1040,384]{1,0:T(8,128)(2,1)}, bf16[1040,384]{1,0:T(8,128)(2,1)S(1)}, u32[]{:S(2)}) copy-start(bf16[1040,384]{1,0:T(8,128)(2,1)S(1)} %collective-permute-done.5.rest_1_) | copy-start | bytes 2396164
  49.7 17.5 %collective-permute-start.6 = (bf16[512,384]{1,0:T(8,128)(2,1)}, bf16[512,384]{1,0:T(8,128)(2,1)}, u32[]{:S(2)}, u32[]{:S(2)}) collective-permute-start(bf16[512,384]{1,0:T(8,128)(2,1)} %get-tuple-element.38), channel_id=1, source_target_pairs={{1,2},{2,1},{3,4},{4,3},{5,6},{6,5},{9,10},{10,9},{11,12},{12,11},... | collective-permute-start | bytes 1179656 | tf_op jit(solution)/shard_map/ppermute | solution.py:494
  62.2 14.2 %collective-permute-start.7 = (bf16[384,1024]{1,0:T(8,128)(2,1)}, bf16[384,1024]{1,0:T(8,128)(2,1)}, u32[]{:S(2)}, u32[]{:S(2)}) collective-permute-start(bf16[384,1024]{1,0:T(8,128)(2,1)} %get-tuple-element.44), channel_id=1, source_target_pairs={{0,8},{8,0},{16,24},{24,16},{1,9},{9,1},{17,25},{25,17},{2,10},{10... | collective-permute-start | bytes 2359304 | tf_op jit(solution)/shard_map/ppermute | solution.py:494
  64.0 13.6 %collective-permute-start.8 = (bf16[384,1024]{1,0:T(8,128)(2,1)}, bf16[384,1024]{1,0:T(8,128)(2,1)}, u32[]{:S(2)}, u32[]{:S(2)}) collective-permute-start(bf16[384,1024]{1,0:T(8,128)(2,1)} %get-tuple-element.45), channel_id=1, source_target_pairs={{8,16},{16,8},{9,17},{17,9},{10,18},{18,10},{11,19},{19,11},{12,20... | collective-permute-start | bytes 2359304 | tf_op jit(solution)/shard_map/ppermute | solution.py:494

commit v13 on v11

--- a/solution.py
+++ b/solution.py
@@ -561,11 +561,8 @@
     mirrors = [mirrored(piece, k) for k, piece in enumerate(mirrors)] + [mirrors[0]]
 
     operator_times_prior, blocks = rows_operator(covariance, *ends, row_s, where, steps, nlon, BF16)
-    inners[0] = exchanged(inners[0], "col", 0)
-    operator_times_prior, outers, inners[1] = lax.optimization_barrier(
-        (operator_times_prior, outers, inners[1])
-    )
-    inners[1] = exchanged(inners[1], "col", 1)
+    operator_times_prior, outers, inners = lax.optimization_barrier((operator_times_prior, outers, inners))
+    inners = [exchanged(piece, "col", k) for k, piece in enumerate(inners)]
     mirror, *ends = columns_operator(
         covariance, [outers], col_s, col_blocks, where, near, steps, nlon, 2, lambda i, at: i * (lat_rows // near - 1),
         None, True,

time: 87.8 us -> 89.4 us (1.018)
  the two profiles are of different devices: /device:TPU:5 before, /device:TPU:15 now
where the time goes in v13:
time: 89.4 us; the launch traced here: 88.9 us
  Pallas kernels  61.6 us (69%)
  starting transfers between devices  19.6 us (22%)
  waiting for transfers between devices  6.03 us (7%)
  between operations  1 us (1%)
    pallas_call x2, Pallas kernels, rows_operator(): pl.pallas_call(kernel, grid_spec=pltpu.PrefetchScalarGridSpec(num_scalar_...  30.1 us
    pallas_call x2, Pallas kernels, columns_operator(): pl.pallas_call(kernel, grid_spec=pltpu.PrefetchScalarGridSpec(num_scalar_...  18.3 us
    ppermute x8, starting transfers between devices, exchanged(): return lax.ppermute(block, axis, pairs)  11.9 us
    ppermute x2, starting transfers between devices, mirrored(): return lax.ppermute(block, ('row', 'col'), pairs)  7.71 us
    pallas_call x2, Pallas kernels, packed(): pl.pallas_call(kernel, in_specs=[pl.BlockSpec(memory_space=pltpu.SMEM), p...  6.72 us
    pallas_call x1, Pallas kernels, stencils(): pl.pallas_call(kernel, in_specs=[pl.BlockSpec(memory_space=pltpu.SMEM)] *...  6.47 us
    ppermute x8, waiting for transfers between devices, exchanged(): return lax.ppermute(block, axis, pairs)  6.02 us
  transfers between devices with their start and end apart: 10, of which 1 were waited for; matrix products, arithmetic and copies ran while one was open for 0% of the time, Pallas kernels for 50%

profile of v13, /device:TPU:15, one launch (start us, length us, event | category | flops | bytes accessed | tf_op | source)
XLA Modules:
  0.0 88.9 jit_solution(17241815853296731399)
XLA Ops:
  0.7 0.6 stack.71.where_ref
  1.3 3.4 %packed.2 = (bf16[1040,384]{1,0:T(8,128)(2,1)}, bf16[1040,384]{1,0:T(8,128)(2,1)}) custom-call(s32[16]{0:T(128)} %stack.71.where_ref, f32[2048,1024]{1,0:T(8,128)} %p_ref.9), custom_call_target="tpu_custom_call" | custom-call | flops 1 | bytes 1 | tf_op jit(solution)/shard_map/packed/pallas_call | solution.py:137
  4.7 0.3 collective-permute-start.4
  5.0 4.2 %collective-permute-start.5 = (bf16[1040,384]{1,0:T(8,128)(2,1)}, bf16[1040,384]{1,0:T(8,128)(2,1)}, u32[]{:S(2)}, u32[]{:S(2)}) collective-permute-start(bf16[1040,384]{1,0:T(8,128)(2,1)} %get-tuple-element.37), channel_id=1, source_target_pairs={{1,2},{2,1},{3,4},{4,3},{5,6},{6,5},{9,10},{10,9},{11,12},{12,11},... | collective-permute-start | bytes 2396168 | tf_op jit(solution)/shard_map/ppermute | solution.py:492
  9.2 3.3 %packed.3 = (bf16[384,1024]{1,0:T(8,128)(2,1)}, bf16[384,1024]{1,0:T(8,128)(2,1)}) custom-call(s32[16]{0:T(128)} %stack.71.where_ref, f32[2048,1024]{1,0:T(8,128)} %p_ref.9), custom_call_target="tpu_custom_call" | custom-call | flops 1 | bytes 1 | tf_op jit(solution)/shard_map/packed/pallas_call | solution.py:137
  12.5 1.3 %collective-permute-start.2 = (bf16[384,1024]{1,0:T(8,128)(2,1)}, bf16[384,1024]{1,0:T(8,128)(2,1)}, u32[]{:S(2)}, u32[]{:S(2)}) collective-permute-start(bf16[384,1024]{1,0:T(8,128)(2,1)} %get-tuple-element.33), channel_id=1, source_target_pairs={{0,8},{8,0},{16,24},{24,16},{1,9},{9,1},{17,25},{25,17},{2,10},{10... | collective-permute-start | bytes 2359304 | tf_op jit(solution)/shard_map/ppermute | solution.py:492
  13.8 1.6 %collective-permute-start.3 = (bf16[384,1024]{1,0:T(8,128)(2,1)}, bf16[384,1024]{1,0:T(8,128)(2,1)}, u32[]{:S(2)}, u32[]{:S(2)}) collective-permute-start(bf16[384,1024]{1,0:T(8,128)(2,1)} %get-tuple-element.34), channel_id=1, source_target_pairs={{8,16},{16,8},{9,17},{17,9},{10,18},{18,10},{11,19},{19,11},{12,20... | collective-permute-start | bytes 2359304 | tf_op jit(solution)/shard_map/ppermute | solution.py:492
  15.4 6.5 %stencils.1 = (f32[7,16,128]{2,1,0:T(8,128)}, f32[7,8,128]{2,1,0:T(8,128)}, bf16[3072,256]{1,0:T(8,128)(2,1)}, bf16[3072,256]{1,0:T(8,128)(2,1)}, f32[15,14,128]...) custom-call(f32[2,16]{1,0:T(2,128)} %bitcast.17, ...), custom_call_target="tpu_custom_call" | custom-call | flops 1 | bytes 1 | tf_op jit(solution)/shard_map/stencils/pallas_call | solution.py:195
  21.9 4.6 %collective-permute-start.1 = (bf16[512,384]{1,0:T(8,128)(2,1)}, bf16[512,384]{1,0:T(8,128)(2,1)}, u32[]{:S(2)}, u32[]{:S(2)}) collective-permute-start(bf16[512,384]{1,0:T(8,128)(2,1)} %get-tuple-element.30), channel_id=1, source_target_pairs={{0,2},{2,10},{4,18},{6,26},{8,4},{9,1},{10,12},{11,9},{12,20},{13,... | collective-permute-start | bytes 1179656 | tf_op jit(solution)/shard_map/ppermute | solution.py:504
  26.5 0.0 collective-permute-done.2.even_ref
  26.6 3.1 %collective-permute-start = (bf16[512,384]{1,0:T(8,128)(2,1)}, bf16[512,384]{1,0:T(8,128)(2,1)}, u32[]{:S(2)}, u32[]{:S(2)}) collective-permute-start(bf16[512,384]{1,0:T(8,128)(2,1)} %get-tuple-element.29.rest_2_), channel_id=1, source_target_pairs={{2,8},{3,9},{4,16},{5,17},{6,24},{7,25},{8,2},{9,3},{12,18},{13,19... | collective-permute-start | bytes 1179656 | tf_op jit(solution)/shard_map/ppermute | solution.py:504
  29.6 0.0 collective-permute-done.3.odd_ref
  29.7 16.7 %rows_operator.2 = (bf16[2048,1024]{1,0:T(8,128)(2,1)}, bf16[4096,768]{1,0:T(8,128)(2,1)}) custom-call(s32[16]{0:T(128)} %stack.71.where_ref, f32[7,16,128]{2,1,0:T(8,128)} %get-tuple-element.27.stencil_ref, f32[2048,1024]{1,0:T(8,128)} %p_ref.9, bf16[384,1024]{1,0:T(8,128)(2,1)} %collective-permute-done.2.even_ref, ...), custom_call_target="tpu_custom_call" | custom-call | flops 1 | bytes 1 | tf_op jit(solution)/shard_map/rows_operator/pallas_call | solution.py:452
  46.4 0.0 collective-permute-done.4.rest_0_
  46.4 0.0 copy-start
  46.4 0.0 collective-permute-done.5.rest_1_
  46.4 0.1 collective-permute-start.6
  46.5 2.8 %collective-permute-start.7 = (bf16[512,384]{1,0:T(8,128)(2,1)}, bf16[512,384]{1,0:T(8,128)(2,1)}, u32[]{:S(2)}, u32[]{:S(2)}) collective-permute-start(bf16[512,384]{1,0:T(8,128)(2,1)} %get-tuple-element.41), channel_id=1, source_target_pairs={{1,2},{2,1},{3,4},{4,3},{5,6},{6,5},{9,10},{10,9},{11,12},{12,11},... | collective-permute-start | bytes 1179656 | tf_op jit(solution)/shard_map/ppermute | solution.py:492
  49.3 0.0 copy-done
  49.3 9.3 %columns_operator.2 = (bf16[2048,1024]{1,0:T(8,128)(2,1)}, bf16[384,1024]{1,0:T(8,128)(2,1)}, bf16[384,1024]{1,0:T(8,128)(2,1)}) custom-call(s32[16]{0:T(128)} %stack.71.where_ref, f32[7,8,128]{2,1,0:T(8,128)} %get-tuple-element.28.stencil_ref, f32[2048,1024]{1,0:T(8,128)} %p_ref.9, bf16[1040,384]{1,0:T(8,128)(2,1)} %copy-done, ...), custom_call_target="tpu_custom_call" | custom-call | flops 1 | bytes 1 | tf_op jit(solution)/shard_map/columns_operator/pallas_call | solution.py:323
  58.6 0.0 collective-permute-start.8
  58.6 0.0 collective-permute-done.1.rest_1_
  58.7 1.6 %collective-permute-start.9 = (bf16[384,1024]{1,0:T(8,128)(2,1)}, bf16[384,1024]{1,0:T(8,128)(2,1)}, u32[]{:S(2)}, u32[]{:S(2)}) collective-permute-start(bf16[384,1024]{1,0:T(8,128)(2,1)} %get-tuple-element.49), channel_id=1, source_target_pairs={{8,16},{16,8},{9,17},{17,9},{10,18},{18,10},{11,19},{19,11},{12,20... | collective-permute-start | bytes 2359304 | tf_op jit(solution)/shard_map/ppermute | solution.py:492
  60.3 0.0 collective-permute-done.rest_0_
  60.3 6.0 %collective-permute-done.6.rest_3_ = bf16[512,384]{1,0:T(8,128)(2,1)} collective-permute-done((bf16[512,384]{1,0:T(8,128)(2,1)}, bf16[512,384]{1,0:T(8,128)(2,1)}, u32[]{:S(2)}, u32[]{:S(2)}) %collective-permute-start.6) | collective-permute-done | bytes 393248 | tf_op jit(solution)/shard_map/ppermute | solution.py:492
  66.3 0.0 collective-permute-done.7.rest_4_
  66.3 9.1 %columns_operator.3.x_ref = bf16[2048,1024]{1,0:T(8,128)(2,1)} custom-call(s32[16]{0:T(128)} %stack.71.where_ref, f32[7,8,128]{2,1,0:T(8,128)} %get-tuple-element.28.stencil_ref, f32[2048,1024]{1,0:T(8,128)} %p_ref.9, bf16[512,384]{1,0:T(8,128)(2,1)} %collective-permute-done.rest_0_, ...), custom_call_target="tpu_custom_call", output_to_operand_aliasing={{}: (11, {})} | custom-call | flops 9999999827968 | bytes 9999999827968 | tf_op jit(solution)/shard_map/columns_operator/pallas_call | solution.py:323
  75.3 0.0 collective-permute-done.8.even_ref
  75.3 0.0 collective-permute-done.9.odd_ref
  75.3 13.4 %rows_operator.3 = f32[2048,1024]{1,0:T(8,128)} custom-call(s32[16]{0:T(128)} %stack.71.where_ref, f32[7,16,128]{2,1,0:T(8,128)} %get-tuple-element.27.stencil_ref, bf16[2048,1024]{1,0:T(8,128)(2,1)} %columns_operator.3.x_ref, bf16[384,1024]{1,0:T(8,128)(2,1)} %collective-permute-done.8.even_ref, bf16[384,1024]{1,0:T(8,128)(2,1)} %collective-permute-done.9.odd_ref, ...), custom_call_target="tpu_custom_call" | custom-call | flops 1 | bytes 1 | tf_op jit(solution)/shard_map/rows_operator/pallas_call | solution.py:452
Async XLA Ops:
  4.7 41.6 %collective-permute-start.4 = (bf16[1040,384]{1,0:T(8,128)(2,1)}, bf16[1040,384]{1,0:T(8,128)(2,1)S(1)}, u32[]{:S(2)}, u32[]{:S(2)}) collective-permute-start(bf16[1040,384]{1,0:T(8,128)(2,1)} %get-tuple-element.36), channel_id=1, source_target_pairs={{0,1},{1,0},{2,3},{3,2},{4,5},{5,4},{6,7},{7,6},{8,9},{9,8},{10,11... | collective-permute-start | bytes 2396168 | tf_op jit(solution)/shard_map/ppermute | solution.py:492
  5.0 41.4 %collective-permute-start.5 = (bf16[1040,384]{1,0:T(8,128)(2,1)}, bf16[1040,384]{1,0:T(8,128)(2,1)}, u32[]{:S(2)}, u32[]{:S(2)}) collective-permute-start(bf16[1040,384]{1,0:T(8,128)(2,1)} %get-tuple-element.37), channel_id=1, source_target_pairs={{1,2},{2,1},{3,4},{4,3},{5,6},{6,5},{9,10},{10,9},{11,12},{12,11},... | collective-permute-start | bytes 2396168 | tf_op jit(solution)/shard_map/ppermute | solution.py:492
  12.5 14.0 %collective-permute-start.2 = (bf16[384,1024]{1,0:T(8,128)(2,1)}, bf16[384,1024]{1,0:T(8,128)(2,1)}, u32[]{:S(2)}, u32[]{:S(2)}) collective-permute-start(bf16[384,1024]{1,0:T(8,128)(2,1)} %get-tuple-element.33), channel_id=1, source_target_pairs={{0,8},{8,0},{16,24},{24,16},{1,9},{9,1},{17,25},{25,17},{2,10},{10... | collective-permute-start | bytes 2359304 | tf_op jit(solution)/shard_map/ppermute | solution.py:492
  13.8 15.8 %collective-permute-start.3 = (bf16[384,1024]{1,0:T(8,128)(2,1)}, bf16[384,1024]{1,0:T(8,128)(2,1)}, u32[]{:S(2)}, u32[]{:S(2)}) collective-permute-start(bf16[384,1024]{1,0:T(8,128)(2,1)} %get-tuple-element.34), channel_id=1, source_target_pairs={{8,16},{16,8},{9,17},{17,9},{10,18},{18,10},{11,19},{19,11},{12,20... | collective-permute-start | bytes 2359304 | tf_op jit(solution)/shard_map/ppermute | solution.py:492
  21.9 36.7 %collective-permute-start.1 = (bf16[512,384]{1,0:T(8,128)(2,1)}, bf16[512,384]{1,0:T(8,128)(2,1)}, u32[]{:S(2)}, u32[]{:S(2)}) collective-permute-start(bf16[512,384]{1,0:T(8,128)(2,1)} %get-tuple-element.30), channel_id=1, source_target_pairs={{0,2},{2,10},{4,18},{6,26},{8,4},{9,1},{10,12},{11,9},{12,20},{13,... | collective-permute-start | bytes 1179656 | tf_op jit(solution)/shard_map/ppermute | solution.py:504
  26.6 33.7 %collective-permute-start = (bf16[512,384]{1,0:T(8,128)(2,1)}, bf16[512,384]{1,0:T(8,128)(2,1)}, u32[]{:S(2)}, u32[]{:S(2)}) collective-permute-start(bf16[512,384]{1,0:T(8,128)(2,1)} %get-tuple-element.29.rest_2_), channel_id=1, source_target_pairs={{2,8},{3,9},{4,16},{5,17},{6,24},{7,25},{8,2},{9,3},{12,18},{13,19... | collective-permute-start | bytes 1179656 | tf_op jit(solution)/shard_map/ppermute | solution.py:504
  46.4 3.0 %copy-start = (bf16[1040,384]{1,0:T(8,128)(2,1)}, bf16[1040,384]{1,0:T(8,128)(2,1)S(1)}, u32[]{:S(2)}) copy-start(bf16[1040,384]{1,0:T(8,128)(2,1)S(1)} %collective-permute-done.4.rest_0_) | copy-start | bytes 2396164
  46.4 19.9 %collective-permute-start.6 = (bf16[512,384]{1,0:T(8,128)(2,1)}, bf16[512,384]{1,0:T(8,128)(2,1)}, u32[]{:S(2)}, u32[]{:S(2)}) collective-permute-start(bf16[512,384]{1,0:T(8,128)(2,1)} %get-tuple-element.40), channel_id=1, source_target_pairs={{0,1},{1,0},{2,3},{3,2},{4,5},{5,4},{6,7},{7,6},{8,9},{9,8},{10,11... | collective-permute-start | bytes 1179656 | tf_op jit(solution)/shard_map/ppermute | solution.py:492
  46.5 19.8 %collective-permute-start.7 = (bf16[512,384]{1,0:T(8,128)(2,1)}, bf16[512,384]{1,0:T(8,128)(2,1)}, u32[]{:S(2)}, u32[]{:S(2)}) collective-permute-start(bf16[512,384]{1,0:T(8,128)(2,1)} %get-tuple-element.41), channel_id=1, source_target_pairs={{1,2},{2,1},{3,4},{4,3},{5,6},{6,5},{9,10},{10,9},{11,12},{12,11},... | collective-permute-start | bytes 1179656 | tf_op jit(solution)/shard_map/ppermute | solution.py:492
  58.6 16.7 %collective-permute-start.8 = (bf16[384,1024]{1,0:T(8,128)(2,1)}, bf16[384,1024]{1,0:T(8,128)(2,1)}, u32[]{:S(2)}, u32[]{:S(2)}) collective-permute-start(bf16[384,1024]{1,0:T(8,128)(2,1)} %get-tuple-element.48), channel_id=1, source_target_pairs={{0,8},{8,0},{16,24},{24,16},{1,9},{9,1},{17,25},{25,17},{2,10},{10... | collective-permute-start | bytes 2359304 | tf_op jit(solution)/shard_map/ppermute | solution.py:492
  58.7 16.7 %collective-permute-start.9 = (bf16[384,1024]{1,0:T(8,128)(2,1)}, bf16[384,1024]{1,0:T(8,128)(2,1)}, u32[]{:S(2)}, u32[]{:S(2)}) collective-permute-start(bf16[384,1024]{1,0:T(8,128)(2,1)} %get-tuple-element.49), channel_id=1, source_target_pairs={{8,16},{16,8},{9,17},{17,9},{10,18},{18,10},{11,19},{19,11},{12,20... | collective-permute-start | bytes 2359304 | tf_op jit(solution)/shard_map/ppermute | solution.py:492

commit v14 on v10

--- a/solution.py
+++ b/solution.py
@@ -215,7 +215,7 @@
     span = 2 * steps * nlon
     pairs = lats // 2
     part = nlon // 2
-    upper = size - part * (3 * size // (8 * part))
+    upper = size - part * (size // (2 * part))
 
     def kernel(where_ref, stencil_ref, p_ref, *rest):
         halo_groups = []

time: 87.4 us -> 88.1 us (level)
  Pallas kernels: 60.3 us -> 61.8 us
    pallas_call x2, Pallas kernels: 18.3 us -> 19.9 us  [columns_operator(): pl.pallas_call(kernel, grid_spec=pltpu.PrefetchScalarGridSpec(num_scalar_...]
  transfers between devices with their start and end apart: 10 -> 10, of which waited for: 2 -> 1; matrix products, arithmetic and copies ran while one was open for 0% -> 0% of each run, Pallas kernels for 49% -> 50%
where the time goes in v14:
time: 88.1 us; the launch traced here: 86.6 us
  Pallas kernels  61.8 us (70%)
  starting transfers between devices  21.4 us (24%)
  waiting for transfers between devices  1.67 us (2%)
  between operations  1.01 us (1%)
    pallas_call x2, Pallas kernels, rows_operator(): pl.pallas_call(kernel, grid_spec=pltpu.PrefetchScalarGridSpec(num_scalar_...  30.1 us
    pallas_call x2, Pallas kernels, columns_operator(): pl.pallas_call(kernel, grid_spec=pltpu.PrefetchScalarGridSpec(num_scalar_...  19.9 us
    ppermute x8, starting transfers between devices, exchanged(): return lax.ppermute(block, axis, pairs)  17.6 us
    pallas_call x1, Pallas kernels, stencils(): pl.pallas_call(kernel, in_specs=[pl.BlockSpec(memory_space=pltpu.SMEM)] *...  6.72 us
    pallas_call x1, Pallas kernels, packed(): pl.pallas_call(kernel, in_specs=[pl.BlockSpec(memory_space=pltpu.SMEM), p...  5.16 us
    ppermute x2, starting transfers between devices, mirrored(): return lax.ppermute(block, ('row', 'col'), pairs)  3.83 us
  transfers between devices with their start and end apart: 10, of which 1 were waited for; matrix products, arithmetic and copies ran while one was open for 0% of the time, Pallas kernels for 50%

profile of v14, /device:TPU:5, one launch (start us, length us, event | category | flops | bytes accessed | tf_op | source)
XLA Modules:
  0.0 86.6 jit_solution(17708426864625803424)
XLA Ops:
  0.7 0.7 stack.71.where_ref
  1.4 5.2 %packed.1 = (bf16[1040,384]{1,0:T(8,128)(2,1)}, bf16[1040,384]{1,0:T(8,128)(2,1)}, bf16[384,1024]{1,0:T(8,128)(2,1)}, bf16[384,1024]{1,0:T(8,128)(2,1)}) custom-call(s32[16]{0:T(128)} %stack.71.where_ref, f32[2048,1024]{1,0:T(8,128)} %p_ref.7), custom_call_target="tpu_custom_call" | custom-call | flops 1 | bytes 1 | tf_op jit(solution)/shard_map/packed/pallas_call | solution.py:137
  6.6 0.1 collective-permute-start.5
  6.6 4.4 %collective-permute-start.6 = (bf16[1040,384]{1,0:T(8,128)(2,1)}, bf16[1040,384]{1,0:T(8,128)(2,1)}, u32[]{:S(2)}, u32[]{:S(2)}) collective-permute-start(bf16[1040,384]{1,0:T(8,128)(2,1)} %get-tuple-element.33), channel_id=1, source_target_pairs={{1,2},{2,1},{3,4},{4,3},{5,6},{6,5},{9,10},{10,9},{11,12},{12,11},... | collective-permute-start | bytes 2396168 | tf_op jit(solution)/shard_map/ppermute | solution.py:489
  11.0 1.3 %collective-permute-start.3 = (bf16[384,1024]{1,0:T(8,128)(2,1)}, bf16[384,1024]{1,0:T(8,128)(2,1)}, u32[]{:S(2)}, u32[]{:S(2)}) collective-permute-start(bf16[384,1024]{1,0:T(8,128)(2,1)} %get-tuple-element.29), channel_id=1, source_target_pairs={{0,8},{8,0},{16,24},{24,16},{1,9},{9,1},{17,25},{25,17},{2,10},{10... | collective-permute-start | bytes 2359304 | tf_op jit(solution)/shard_map/ppermute | solution.py:489
  12.3 3.0 %collective-permute-start.4 = (bf16[384,1024]{1,0:T(8,128)(2,1)}, bf16[384,1024]{1,0:T(8,128)(2,1)}, u32[]{:S(2)}, u32[]{:S(2)}) collective-permute-start(bf16[384,1024]{1,0:T(8,128)(2,1)} %get-tuple-element.30), channel_id=1, source_target_pairs={{8,16},{16,8},{9,17},{17,9},{10,18},{18,10},{11,19},{19,11},{12,20... | collective-permute-start | bytes 2359304 | tf_op jit(solution)/shard_map/ppermute | solution.py:489
  15.3 6.7 %stencils.1 = (f32[7,16,128]{2,1,0:T(8,128)}, f32[7,8,128]{2,1,0:T(8,128)}, bf16[3072,256]{1,0:T(8,128)(2,1)}, bf16[3072,256]{1,0:T(8,128)(2,1)}, f32[15,14,128]...) custom-call(f32[2,16]{1,0:T(2,128)} %bitcast.17, ...), custom_call_target="tpu_custom_call" | custom-call | flops 1 | bytes 1 | tf_op jit(solution)/shard_map/stencils/pallas_call | solution.py:192
  22.1 1.9 %collective-permute-start.1 = (bf16[512,384]{1,0:T(8,128)(2,1)}, bf16[512,384]{1,0:T(8,128)(2,1)}, u32[]{:S(2)}, u32[]{:S(2)}) collective-permute-start(bf16[512,384]{1,0:T(8,128)(2,1)} %get-tuple-element.27), channel_id=1, source_target_pairs={{0,2},{2,10},{4,18},{6,26},{8,4},{9,1},{10,12},{11,9},{12,20},{13,... | collective-permute-start | bytes 1179656 | tf_op jit(solution)/shard_map/ppermute | solution.py:501
  24.0 0.0 collective-permute-done.3.even_ref
  24.0 0.6 collective-permute-start.2
  24.6 1.6 %collective-permute-done.4.odd_ref = bf16[384,1024]{1,0:T(8,128)(2,1)} collective-permute-done((bf16[384,1024]{1,0:T(8,128)(2,1)}, bf16[384,1024]{1,0:T(8,128)(2,1)}, u32[]{:S(2)}, u32[]{:S(2)}) %collective-permute-start.4) | collective-permute-done | bytes 786464 | tf_op jit(solution)/shard_map/ppermute | solution.py:489
  26.2 1.9 %collective-permute-start = (bf16[512,384]{1,0:T(8,128)(2,1)}, bf16[512,384]{1,0:T(8,128)(2,1)}, u32[]{:S(2)}, u32[]{:S(2)}) collective-permute-start(bf16[512,384]{1,0:T(8,128)(2,1)} %get-tuple-element.26.rest_2_), channel_id=1, source_target_pairs={{2,8},{3,9},{4,16},{5,17},{6,24},{7,25},{8,2},{9,3},{12,18},{13,19... | collective-permute-start | bytes 1179656 | tf_op jit(solution)/shard_map/ppermute | solution.py:501
  28.1 16.7 %rows_operator.2 = (bf16[2048,1024]{1,0:T(8,128)(2,1)}, bf16[4096,768]{1,0:T(8,128)(2,1)}) custom-call(s32[16]{0:T(128)} %stack.71.where_ref, f32[7,16,128]{2,1,0:T(8,128)} %get-tuple-element.24.stencil_ref, f32[2048,1024]{1,0:T(8,128)} %p_ref.7, bf16[384,1024]{1,0:T(8,128)(2,1)} %collective-permute-done.3.even_ref, ...), custom_call_target="tpu_custom_call" | custom-call | flops 1 | bytes 1 | tf_op jit(solution)/shard_map/rows_operator/pallas_call | solution.py:449
  44.9 0.0 collective-permute-done.5.rest_0_
  44.9 0.0 copy-start
  44.9 0.0 collective-permute-done.6.rest_1_
  44.9 1.9 %collective-permute-start.7 = (bf16[512,384]{1,0:T(8,128)(2,1)}, bf16[512,384]{1,0:T(8,128)(2,1)}, u32[]{:S(2)}, u32[]{:S(2)}) collective-permute-start(bf16[512,384]{1,0:T(8,128)(2,1)} %get-tuple-element.35), channel_id=1, source_target_pairs={{1,2},{2,1},{3,4},{4,3},{5,6},{6,5},{9,10},{10,9},{11,12},{12,11},... | collective-permute-start | bytes 1179656 | tf_op jit(solution)/shard_map/ppermute | solution.py:489
  46.8 0.0 copy-done
  46.8 10.0 %columns_operator.2 = (bf16[2048,1024]{1,0:T(8,128)(2,1)}, bf16[384,1024]{1,0:T(8,128)(2,1)}, bf16[384,1024]{1,0:T(8,128)(2,1)}) custom-call(s32[16]{0:T(128)} %stack.71.where_ref, f32[7,8,128]{2,1,0:T(8,128)} %get-tuple-element.25.stencil_ref, f32[2048,1024]{1,0:T(8,128)} %p_ref.7, bf16[1040,384]{1,0:T(8,128)(2,1)} %copy-done, ...), custom_call_target="tpu_custom_call" | custom-call | flops 1 | bytes 1 | tf_op jit(solution)/shard_map/columns_operator/pallas_call | solution.py:320
  56.9 1.9 %collective-permute-start.8 = (bf16[384,1024]{1,0:T(8,128)(2,1)}, bf16[384,1024]{1,0:T(8,128)(2,1)}, u32[]{:S(2)}, u32[]{:S(2)}) collective-permute-start(bf16[384,1024]{1,0:T(8,128)(2,1)} %get-tuple-element.42), channel_id=1, source_target_pairs={{0,8},{8,0},{16,24},{24,16},{1,9},{9,1},{17,25},{25,17},{2,10},{10... | collective-permute-start | bytes 2359304 | tf_op jit(solution)/shard_map/ppermute | solution.py:489
  58.8 0.0 collective-permute-done.1.rest_1_
  58.8 4.4 %collective-permute-start.9 = (bf16[384,1024]{1,0:T(8,128)(2,1)}, bf16[384,1024]{1,0:T(8,128)(2,1)}, u32[]{:S(2)}, u32[]{:S(2)}) collective-permute-start(bf16[384,1024]{1,0:T(8,128)(2,1)} %get-tuple-element.43), channel_id=1, source_target_pairs={{8,16},{16,8},{9,17},{17,9},{10,18},{18,10},{11,19},{19,11},{12,20... | collective-permute-start | bytes 2359304 | tf_op jit(solution)/shard_map/ppermute | solution.py:489
  63.2 0.0 collective-permute-done.2.rest_3_
  63.2 0.0 collective-permute-done.rest_0_
  63.2 0.0 collective-permute-done.7.rest_4_
  63.2 9.8 %columns_operator.3.x_ref = bf16[2048,1024]{1,0:T(8,128)(2,1)} custom-call(s32[16]{0:T(128)} %stack.71.where_ref, f32[7,8,128]{2,1,0:T(8,128)} %get-tuple-element.25.stencil_ref, f32[2048,1024]{1,0:T(8,128)} %p_ref.7, bf16[512,384]{1,0:T(8,128)(2,1)} %collective-permute-done.rest_0_, ...), custom_call_target="tpu_custom_call", output_to_operand_aliasing={{}: (11, {})} | custom-call | flops 9999999827968 | bytes 9999999827968 | tf_op jit(solution)/shard_map/columns_operator/pallas_call | solution.py:320
  73.1 0.0 collective-permute-done.8.even_ref
  73.1 0.0 collective-permute-done.9.odd_ref
  73.1 13.4 %rows_operator.3 = f32[2048,1024]{1,0:T(8,128)} custom-call(s32[16]{0:T(128)} %stack.71.where_ref, f32[7,16,128]{2,1,0:T(8,128)} %get-tuple-element.24.stencil_ref, bf16[2048,1024]{1,0:T(8,128)(2,1)} %columns_operator.3.x_ref, bf16[384,1024]{1,0:T(8,128)(2,1)} %collective-permute-done.8.even_ref, bf16[384,1024]{1,0:T(8,128)(2,1)} %collective-permute-done.9.odd_ref, ...), custom_call_target="tpu_custom_call" | custom-call | flops 1 | bytes 1 | tf_op jit(solution)/shard_map/rows_operator/pallas_call | solution.py:449
Async XLA Ops:
  6.6 38.3 %collective-permute-start.5 = (bf16[1040,384]{1,0:T(8,128)(2,1)}, bf16[1040,384]{1,0:T(8,128)(2,1)S(1)}, u32[]{:S(2)}, u32[]{:S(2)}) collective-permute-start(bf16[1040,384]{1,0:T(8,128)(2,1)} %get-tuple-element.32), channel_id=1, source_target_pairs={{0,1},{1,0},{2,3},{3,2},{4,5},{5,4},{6,7},{7,6},{8,9},{9,8},{10,11... | collective-permute-start | bytes 2396168 | tf_op jit(solution)/shard_map/ppermute | solution.py:489
  6.6 38.2 %collective-permute-start.6 = (bf16[1040,384]{1,0:T(8,128)(2,1)}, bf16[1040,384]{1,0:T(8,128)(2,1)}, u32[]{:S(2)}, u32[]{:S(2)}) collective-permute-start(bf16[1040,384]{1,0:T(8,128)(2,1)} %get-tuple-element.33), channel_id=1, source_target_pairs={{1,2},{2,1},{3,4},{4,3},{5,6},{6,5},{9,10},{10,9},{11,12},{12,11},... | collective-permute-start | bytes 2396168 | tf_op jit(solution)/shard_map/ppermute | solution.py:489
  11.0 13.0 %collective-permute-start.3 = (bf16[384,1024]{1,0:T(8,128)(2,1)}, bf16[384,1024]{1,0:T(8,128)(2,1)}, u32[]{:S(2)}, u32[]{:S(2)}) collective-permute-start(bf16[384,1024]{1,0:T(8,128)(2,1)} %get-tuple-element.29), channel_id=1, source_target_pairs={{0,8},{8,0},{16,24},{24,16},{1,9},{9,1},{17,25},{25,17},{2,10},{10... | collective-permute-start | bytes 2359304 | tf_op jit(solution)/shard_map/ppermute | solution.py:489
  12.3 13.9 %collective-permute-start.4 = (bf16[384,1024]{1,0:T(8,128)(2,1)}, bf16[384,1024]{1,0:T(8,128)(2,1)}, u32[]{:S(2)}, u32[]{:S(2)}) collective-permute-start(bf16[384,1024]{1,0:T(8,128)(2,1)} %get-tuple-element.30), channel_id=1, source_target_pairs={{8,16},{16,8},{9,17},{17,9},{10,18},{18,10},{11,19},{19,11},{12,20... | collective-permute-start | bytes 2359304 | tf_op jit(solution)/shard_map/ppermute | solution.py:489
  22.1 36.7 %collective-permute-start.1 = (bf16[512,384]{1,0:T(8,128)(2,1)}, bf16[512,384]{1,0:T(8,128)(2,1)}, u32[]{:S(2)}, u32[]{:S(2)}) collective-permute-start(bf16[512,384]{1,0:T(8,128)(2,1)} %get-tuple-element.27), channel_id=1, source_target_pairs={{0,2},{2,10},{4,18},{6,26},{8,4},{9,1},{10,12},{11,9},{12,20},{13,... | collective-permute-start | bytes 1179656 | tf_op jit(solution)/shard_map/ppermute | solution.py:501
  24.0 39.2 %collective-permute-start.2 = (bf16[512,384]{1,0:T(8,128)(2,1)}, bf16[512,384]{1,0:T(8,128)(2,1)}, u32[]{:S(2)}, u32[]{:S(2)}) collective-permute-start(bf16[512,384]{1,0:T(8,128)(2,1)} %get-tuple-element.28), channel_id=1, source_target_pairs={{0,1},{1,0},{2,3},{3,2},{4,5},{5,4},{6,7},{7,6},{8,9},{9,8},{10,11... | collective-permute-start | bytes 1179656 | tf_op jit(solution)/shard_map/ppermute | solution.py:489
  26.2 37.0 %collective-permute-start = (bf16[512,384]{1,0:T(8,128)(2,1)}, bf16[512,384]{1,0:T(8,128)(2,1)}, u32[]{:S(2)}, u32[]{:S(2)}) collective-permute-start(bf16[512,384]{1,0:T(8,128)(2,1)} %get-tuple-element.26.rest_2_), channel_id=1, source_target_pairs={{2,8},{3,9},{4,16},{5,17},{6,24},{7,25},{8,2},{9,3},{12,18},{13,19... | collective-permute-start | bytes 1179656 | tf_op jit(solution)/shard_map/ppermute | solution.py:501
  44.9 2.0 %copy-start = (bf16[1040,384]{1,0:T(8,128)(2,1)}, bf16[1040,384]{1,0:T(8,128)(2,1)S(1)}, u32[]{:S(2)}) copy-start(bf16[1040,384]{1,0:T(8,128)(2,1)S(1)} %collective-permute-done.5.rest_0_) | copy-start | bytes 2396164
  44.9 18.3 %collective-permute-start.7 = (bf16[512,384]{1,0:T(8,128)(2,1)}, bf16[512,384]{1,0:T(8,128)(2,1)}, u32[]{:S(2)}, u32[]{:S(2)}) collective-permute-start(bf16[512,384]{1,0:T(8,128)(2,1)} %get-tuple-element.35), channel_id=1, source_target_pairs={{1,2},{2,1},{3,4},{4,3},{5,6},{6,5},{9,10},{10,9},{11,12},{12,11},... | collective-permute-start | bytes 1179656 | tf_op jit(solution)/shard_map/ppermute | solution.py:489
  56.9 16.2 %collective-permute-start.8 = (bf16[384,1024]{1,0:T(8,128)(2,1)}, bf16[384,1024]{1,0:T(8,128)(2,1)}, u32[]{:S(2)}, u32[]{:S(2)}) collective-permute-start(bf16[384,1024]{1,0:T(8,128)(2,1)} %get-tuple-element.42), channel_id=1, source_target_pairs={{0,8},{8,0},{16,24},{24,16},{1,9},{9,1},{17,25},{25,17},{2,10},{10... | collective-permute-start | bytes 2359304 | tf_op jit(solution)/shard_map/ppermute | solution.py:489
  58.8 14.3 %collective-permute-start.9 = (bf16[384,1024]{1,0:T(8,128)(2,1)}, bf16[384,1024]{1,0:T(8,128)(2,1)}, u32[]{:S(2)}, u32[]{:S(2)}) collective-permute-start(bf16[384,1024]{1,0:T(8,128)(2,1)} %get-tuple-element.43), channel_id=1, source_target_pairs={{8,16},{16,8},{9,17},{17,9},{10,18},{18,10},{11,19},{19,11},{12,20... | collective-permute-start | bytes 2359304 | tf_op jit(solution)/shard_map/ppermute | solution.py:489

commit v15 on v14

--- a/solution.py
+++ b/solution.py
@@ -215,7 +215,7 @@
     span = 2 * steps * nlon
     pairs = lats // 2
     part = nlon // 2
-    upper = size - part * (size // (2 * part))
+    upper = size - part * (size // (4 * part))
 
     def kernel(where_ref, stencil_ref, p_ref, *rest):
         halo_groups = []

time: 88.1 us -> 87.6 us (level)
  Pallas kernels: 61.8 us -> 60.8 us
    pallas_call x2, Pallas kernels: 19.9 us -> 18.8 us  [columns_operator(): pl.pallas_call(kernel, grid_spec=pltpu.PrefetchScalarGridSpec(num_scalar_...]
  transfers between devices with their start and end apart: 10 -> 10, of which waited for: 1 -> 2; matrix products, arithmetic and copies ran while one was open for 0% -> 0% of each run, Pallas kernels for 50% -> 49%
where the time goes in v15:
time: 87.6 us; the launch traced here: 86 us
  Pallas kernels  60.8 us (69%)
  starting transfers between devices  21.4 us (24%)
  waiting for transfers between devices  2.12 us (2%)
  between operations  1.01 us (1%)
    pallas_call x2, Pallas kernels, rows_operator(): pl.pallas_call(kernel, grid_spec=pltpu.PrefetchScalarGridSpec(num_scalar_...  30.1 us
    pallas_call x2, Pallas kernels, columns_operator(): pl.pallas_call(kernel, grid_spec=pltpu.PrefetchScalarGridSpec(num_scalar_...  18.8 us
    ppermute x8, starting transfers between devices, exchanged(): return lax.ppermute(block, axis, pairs)  17.6 us
    pallas_call x1, Pallas kernels, stencils(): pl.pallas_call(kernel, in_specs=[pl.BlockSpec(memory_space=pltpu.SMEM)] *...  6.72 us
    pallas_call x1, Pallas kernels, packed(): pl.pallas_call(kernel, in_specs=[pl.BlockSpec(memory_space=pltpu.SMEM), p...  5.16 us
    ppermute x2, starting transfers between devices, mirrored(): return lax.ppermute(block, ('row', 'col'), pairs)  3.83 us
    ppermute x8, waiting for transfers between devices, exchanged(): return lax.ppermute(block, axis, pairs)  2.11 us
  transfers between devices with their start and end apart: 10, of which 2 were waited for; matrix products, arithmetic and copies ran while one was open for 0% of the time, Pallas kernels for 49%

profile of v15, /device:TPU:5, one launch (start us, length us, event | category | flops | bytes accessed | tf_op | source)
XLA Modules:
  0.0 86.0 jit_solution(3277726740257829347)
XLA Ops:
  0.7 0.7 stack.71.where_ref
  1.4 5.2 %packed.1 = (bf16[1040,384]{1,0:T(8,128)(2,1)}, bf16[1040,384]{1,0:T(8,128)(2,1)}, bf16[384,1024]{1,0:T(8,128)(2,1)}, bf16[384,1024]{1,0:T(8,128)(2,1)}) custom-call(s32[16]{0:T(128)} %stack.71.where_ref, f32[2048,1024]{1,0:T(8,128)} %p_ref.7), custom_call_target="tpu_custom_call" | custom-call | flops 1 | bytes 1 | tf_op jit(solution)/shard_map/packed/pallas_call | solution.py:137
  6.6 0.1 collective-permute-start.5
  6.6 4.4 %collective-permute-start.6 = (bf16[1040,384]{1,0:T(8,128)(2,1)}, bf16[1040,384]{1,0:T(8,128)(2,1)}, u32[]{:S(2)}, u32[]{:S(2)}) collective-permute-start(bf16[1040,384]{1,0:T(8,128)(2,1)} %get-tuple-element.33), channel_id=1, source_target_pairs={{1,2},{2,1},{3,4},{4,3},{5,6},{6,5},{9,10},{10,9},{11,12},{12,11},... | collective-permute-start | bytes 2396168 | tf_op jit(solution)/shard_map/ppermute | solution.py:489
  11.0 1.3 %collective-permute-start.3 = (bf16[384,1024]{1,0:T(8,128)(2,1)}, bf16[384,1024]{1,0:T(8,128)(2,1)}, u32[]{:S(2)}, u32[]{:S(2)}) collective-permute-start(bf16[384,1024]{1,0:T(8,128)(2,1)} %get-tuple-element.29), channel_id=1, source_target_pairs={{0,8},{8,0},{16,24},{24,16},{1,9},{9,1},{17,25},{25,17},{2,10},{10... | collective-permute-start | bytes 2359304 | tf_op jit(solution)/shard_map/ppermute | solution.py:489
  12.3 3.0 %collective-permute-start.4 = (bf16[384,1024]{1,0:T(8,128)(2,1)}, bf16[384,1024]{1,0:T(8,128)(2,1)}, u32[]{:S(2)}, u32[]{:S(2)}) collective-permute-start(bf16[384,1024]{1,0:T(8,128)(2,1)} %get-tuple-element.30), channel_id=1, source_target_pairs={{8,16},{16,8},{9,17},{17,9},{10,18},{18,10},{11,19},{19,11},{12,20... | collective-permute-start | bytes 2359304 | tf_op jit(solution)/shard_map/ppermute | solution.py:489
  15.3 6.7 %stencils.1 = (f32[7,16,128]{2,1,0:T(8,128)}, f32[7,8,128]{2,1,0:T(8,128)}, bf16[3072,256]{1,0:T(8,128)(2,1)}, bf16[3072,256]{1,0:T(8,128)(2,1)}, f32[15,14,128]...) custom-call(f32[2,16]{1,0:T(2,128)} %bitcast.17, ...), custom_call_target="tpu_custom_call" | custom-call | flops 1 | bytes 1 | tf_op jit(solution)/shard_map/stencils/pallas_call | solution.py:192
  22.1 1.9 %collective-permute-start.1 = (bf16[512,384]{1,0:T(8,128)(2,1)}, bf16[512,384]{1,0:T(8,128)(2,1)}, u32[]{:S(2)}, u32[]{:S(2)}) collective-permute-start(bf16[512,384]{1,0:T(8,128)(2,1)} %get-tuple-element.27), channel_id=1, source_target_pairs={{0,2},{2,10},{4,18},{6,26},{8,4},{9,1},{10,12},{11,9},{12,20},{13,... | collective-permute-start | bytes 1179656 | tf_op jit(solution)/shard_map/ppermute | solution.py:501
  24.0 0.0 collective-permute-done.3.even_ref
  24.0 0.6 collective-permute-start.2
  24.6 1.6 %collective-permute-done.4.odd_ref = bf16[384,1024]{1,0:T(8,128)(2,1)} collective-permute-done((bf16[384,1024]{1,0:T(8,128)(2,1)}, bf16[384,1024]{1,0:T(8,128)(2,1)}, u32[]{:S(2)}, u32[]{:S(2)}) %collective-permute-start.4) | collective-permute-done | bytes 786464 | tf_op jit(solution)/shard_map/ppermute | solution.py:489
  26.2 1.9 %collective-permute-start = (bf16[512,384]{1,0:T(8,128)(2,1)}, bf16[512,384]{1,0:T(8,128)(2,1)}, u32[]{:S(2)}, u32[]{:S(2)}) collective-permute-start(bf16[512,384]{1,0:T(8,128)(2,1)} %get-tuple-element.26.rest_2_), channel_id=1, source_target_pairs={{2,8},{3,9},{4,16},{5,17},{6,24},{7,25},{8,2},{9,3},{12,18},{13,19... | collective-permute-start | bytes 1179656 | tf_op jit(solution)/shard_map/ppermute | solution.py:501
  28.1 16.7 %rows_operator.2 = (bf16[2048,1024]{1,0:T(8,128)(2,1)}, bf16[4096,768]{1,0:T(8,128)(2,1)}) custom-call(s32[16]{0:T(128)} %stack.71.where_ref, f32[7,16,128]{2,1,0:T(8,128)} %get-tuple-element.24.stencil_ref, f32[2048,1024]{1,0:T(8,128)} %p_ref.7, bf16[384,1024]{1,0:T(8,128)(2,1)} %collective-permute-done.3.even_ref, ...), custom_call_target="tpu_custom_call" | custom-call | flops 1 | bytes 1 | tf_op jit(solution)/shard_map/rows_operator/pallas_call | solution.py:449
  44.9 0.0 collective-permute-done.5.rest_0_
  44.9 0.0 copy-start
  44.9 0.0 collective-permute-done.6.rest_1_
  44.9 1.9 %collective-permute-start.7 = (bf16[512,384]{1,0:T(8,128)(2,1)}, bf16[512,384]{1,0:T(8,128)(2,1)}, u32[]{:S(2)}, u32[]{:S(2)}) collective-permute-start(bf16[512,384]{1,0:T(8,128)(2,1)} %get-tuple-element.35), channel_id=1, source_target_pairs={{1,2},{2,1},{3,4},{4,3},{5,6},{6,5},{9,10},{10,9},{11,12},{12,11},... | collective-permute-start | bytes 1179656 | tf_op jit(solution)/shard_map/ppermute | solution.py:489
  46.8 0.0 copy-done
  46.8 9.5 %columns_operator.2 = (bf16[2048,1024]{1,0:T(8,128)(2,1)}, bf16[384,1024]{1,0:T(8,128)(2,1)}, bf16[384,1024]{1,0:T(8,128)(2,1)}) custom-call(s32[16]{0:T(128)} %stack.71.where_ref, f32[7,8,128]{2,1,0:T(8,128)} %get-tuple-element.25.stencil_ref, f32[2048,1024]{1,0:T(8,128)} %p_ref.7, bf16[1040,384]{1,0:T(8,128)(2,1)} %copy-done, ...), custom_call_target="tpu_custom_call" | custom-call | flops 1 | bytes 1 | tf_op jit(solution)/shard_map/columns_operator/pallas_call | solution.py:320
  56.4 1.9 %collective-permute-start.8 = (bf16[384,1024]{1,0:T(8,128)(2,1)}, bf16[384,1024]{1,0:T(8,128)(2,1)}, u32[]{:S(2)}, u32[]{:S(2)}) collective-permute-start(bf16[384,1024]{1,0:T(8,128)(2,1)} %get-tuple-element.42), channel_id=1, source_target_pairs={{0,8},{8,0},{16,24},{24,16},{1,9},{9,1},{17,25},{25,17},{2,10},{10... | collective-permute-start | bytes 2359304 | tf_op jit(solution)/shard_map/ppermute | solution.py:489
  58.3 0.0 collective-permute-done.1.rest_1_
  58.3 4.4 %collective-permute-start.9 = (bf16[384,1024]{1,0:T(8,128)(2,1)}, bf16[384,1024]{1,0:T(8,128)(2,1)}, u32[]{:S(2)}, u32[]{:S(2)}) collective-permute-start(bf16[384,1024]{1,0:T(8,128)(2,1)} %get-tuple-element.43), channel_id=1, source_target_pairs={{8,16},{16,8},{9,17},{17,9},{10,18},{18,10},{11,19},{19,11},{12,20... | collective-permute-start | bytes 2359304 | tf_op jit(solution)/shard_map/ppermute | solution.py:489
  62.7 0.0 collective-permute-done.2.rest_3_
  62.7 0.0 collective-permute-done.rest_0_
  62.7 0.0 collective-permute-done.7.rest_4_
  62.7 9.3 %columns_operator.3.x_ref = bf16[2048,1024]{1,0:T(8,128)(2,1)} custom-call(s32[16]{0:T(128)} %stack.71.where_ref, f32[7,8,128]{2,1,0:T(8,128)} %get-tuple-element.25.stencil_ref, f32[2048,1024]{1,0:T(8,128)} %p_ref.7, bf16[512,384]{1,0:T(8,128)(2,1)} %collective-permute-done.rest_0_, ...), custom_call_target="tpu_custom_call", output_to_operand_aliasing={{}: (11, {})} | custom-call | flops 9999999827968 | bytes 9999999827968 | tf_op jit(solution)/shard_map/columns_operator/pallas_call | solution.py:320
  72.0 0.0 collective-permute-done.8.even_ref
  72.0 0.5 collective-permute-done.9.odd_ref
  72.5 13.4 %rows_operator.3 = f32[2048,1024]{1,0:T(8,128)} custom-call(s32[16]{0:T(128)} %stack.71.where_ref, f32[7,16,128]{2,1,0:T(8,128)} %get-tuple-element.24.stencil_ref, bf16[2048,1024]{1,0:T(8,128)(2,1)} %columns_operator.3.x_ref, bf16[384,1024]{1,0:T(8,128)(2,1)} %collective-permute-done.8.even_ref, bf16[384,1024]{1,0:T(8,128)(2,1)} %collective-permute-done.9.odd_ref, ...), custom_call_target="tpu_custom_call" | custom-call | flops 1 | bytes 1 | tf_op jit(solution)/shard_map/rows_operator/pallas_call | solution.py:449
Async XLA Ops:
  6.6 38.3 %collective-permute-start.5 = (bf16[1040,384]{1,0:T(8,128)(2,1)}, bf16[1040,384]{1,0:T(8,128)(2,1)S(1)}, u32[]{:S(2)}, u32[]{:S(2)}) collective-permute-start(bf16[1040,384]{1,0:T(8,128)(2,1)} %get-tuple-element.32), channel_id=1, source_target_pairs={{0,1},{1,0},{2,3},{3,2},{4,5},{5,4},{6,7},{7,6},{8,9},{9,8},{10,11... | collective-permute-start | bytes 2396168 | tf_op jit(solution)/shard_map/ppermute | solution.py:489
  6.6 38.2 %collective-permute-start.6 = (bf16[1040,384]{1,0:T(8,128)(2,1)}, bf16[1040,384]{1,0:T(8,128)(2,1)}, u32[]{:S(2)}, u32[]{:S(2)}) collective-permute-start(bf16[1040,384]{1,0:T(8,128)(2,1)} %get-tuple-element.33), channel_id=1, source_target_pairs={{1,2},{2,1},{3,4},{4,3},{5,6},{6,5},{9,10},{10,9},{11,12},{12,11},... | collective-permute-start | bytes 2396168 | tf_op jit(solution)/shard_map/ppermute | solution.py:489
  11.0 13.0 %collective-permute-start.3 = (bf16[384,1024]{1,0:T(8,128)(2,1)}, bf16[384,1024]{1,0:T(8,128)(2,1)}, u32[]{:S(2)}, u32[]{:S(2)}) collective-permute-start(bf16[384,1024]{1,0:T(8,128)(2,1)} %get-tuple-element.29), channel_id=1, source_target_pairs={{0,8},{8,0},{16,24},{24,16},{1,9},{9,1},{17,25},{25,17},{2,10},{10... | collective-permute-start | bytes 2359304 | tf_op jit(solution)/shard_map/ppermute | solution.py:489
  12.3 13.9 %collective-permute-start.4 = (bf16[384,1024]{1,0:T(8,128)(2,1)}, bf16[384,1024]{1,0:T(8,128)(2,1)}, u32[]{:S(2)}, u32[]{:S(2)}) collective-permute-start(bf16[384,1024]{1,0:T(8,128)(2,1)} %get-tuple-element.30), channel_id=1, source_target_pairs={{8,16},{16,8},{9,17},{17,9},{10,18},{18,10},{11,19},{19,11},{12,20... | collective-permute-start | bytes 2359304 | tf_op jit(solution)/shard_map/ppermute | solution.py:489
  22.1 36.2 %collective-permute-start.1 = (bf16[512,384]{1,0:T(8,128)(2,1)}, bf16[512,384]{1,0:T(8,128)(2,1)}, u32[]{:S(2)}, u32[]{:S(2)}) collective-permute-start(bf16[512,384]{1,0:T(8,128)(2,1)} %get-tuple-element.27), channel_id=1, source_target_pairs={{0,2},{2,10},{4,18},{6,26},{8,4},{9,1},{10,12},{11,9},{12,20},{13,... | collective-permute-start | bytes 1179656 | tf_op jit(solution)/shard_map/ppermute | solution.py:501
  24.0 38.7 %collective-permute-start.2 = (bf16[512,384]{1,0:T(8,128)(2,1)}, bf16[512,384]{1,0:T(8,128)(2,1)}, u32[]{:S(2)}, u32[]{:S(2)}) collective-permute-start(bf16[512,384]{1,0:T(8,128)(2,1)} %get-tuple-element.28), channel_id=1, source_target_pairs={{0,1},{1,0},{2,3},{3,2},{4,5},{5,4},{6,7},{7,6},{8,9},{9,8},{10,11... | collective-permute-start | bytes 1179656 | tf_op jit(solution)/shard_map/ppermute | solution.py:489
  26.2 36.5 %collective-permute-start = (bf16[512,384]{1,0:T(8,128)(2,1)}, bf16[512,384]{1,0:T(8,128)(2,1)}, u32[]{:S(2)}, u32[]{:S(2)}) collective-permute-start(bf16[512,384]{1,0:T(8,128)(2,1)} %get-tuple-element.26.rest_2_), channel_id=1, source_target_pairs={{2,8},{3,9},{4,16},{5,17},{6,24},{7,25},{8,2},{9,3},{12,18},{13,19... | collective-permute-start | bytes 1179656 | tf_op jit(solution)/shard_map/ppermute | solution.py:501
  44.9 2.0 %copy-start = (bf16[1040,384]{1,0:T(8,128)(2,1)}, bf16[1040,384]{1,0:T(8,128)(2,1)S(1)}, u32[]{:S(2)}) copy-start(bf16[1040,384]{1,0:T(8,128)(2,1)S(1)} %collective-permute-done.5.rest_0_) | copy-start | bytes 2396164
  44.9 17.8 %collective-permute-start.7 = (bf16[512,384]{1,0:T(8,128)(2,1)}, bf16[512,384]{1,0:T(8,128)(2,1)}, u32[]{:S(2)}, u32[]{:S(2)}) collective-permute-start(bf16[512,384]{1,0:T(8,128)(2,1)} %get-tuple-element.35), channel_id=1, source_target_pairs={{1,2},{2,1},{3,4},{4,3},{5,6},{6,5},{9,10},{10,9},{11,12},{12,11},... | collective-permute-start | bytes 1179656 | tf_op jit(solution)/shard_map/ppermute | solution.py:489
  56.4 15.7 %collective-permute-start.8 = (bf16[384,1024]{1,0:T(8,128)(2,1)}, bf16[384,1024]{1,0:T(8,128)(2,1)}, u32[]{:S(2)}, u32[]{:S(2)}) collective-permute-start(bf16[384,1024]{1,0:T(8,128)(2,1)} %get-tuple-element.42), channel_id=1, source_target_pairs={{0,8},{8,0},{16,24},{24,16},{1,9},{9,1},{17,25},{25,17},{2,10},{10... | collective-permute-start | bytes 2359304 | tf_op jit(solution)/shard_map/ppermute | solution.py:489
  58.3 14.2 %collective-permute-start.9 = (bf16[384,1024]{1,0:T(8,128)(2,1)}, bf16[384,1024]{1,0:T(8,128)(2,1)}, u32[]{:S(2)}, u32[]{:S(2)}) collective-permute-start(bf16[384,1024]{1,0:T(8,128)(2,1)} %get-tuple-element.43), channel_id=1, source_target_pairs={{8,16},{16,8},{9,17},{17,9},{10,18},{18,10},{11,19},{19,11},{12,20... | collective-permute-start | bytes 2359304 | tf_op jit(solution)/shard_map/ppermute | solution.py:489

commit v16 on v8

--- a/solution.py
+++ b/solution.py
@@ -362,15 +362,18 @@
                 here = pl.ds(pl.multiple_of(q * size, size), size)
                 high_ref[there, :], low_ref[there, :] = split(raw_ref[here, :])
 
-        @pl.when(step == 0)
-        def _():
+        def ends():
             is_odd = where_ref[3]
             at_even = pl.ds(pl.multiple_of((1 - is_odd) * (wide + rows), nlon), wide)
             at_odd = pl.ds(pl.multiple_of(is_odd * (wide + rows), nlon), wide)
-            halos = [
+            return [
                 pltpu.make_async_copy(even_ref, high_ref.at[at_even, :], sem.at[pairs]),
                 pltpu.make_async_copy(odd_ref, high_ref.at[at_odd, :], sem.at[pairs + 1]),
             ]
+
+        @pl.when(step == 0)
+        def _():
+            halos = ends()
             for halo in halos:
                 halo.start()
             for q in range(pairs):
@@ -378,17 +381,6 @@
             if not exact:
                 low_ref[:wide, :] = jnp.zeros((wide, cols), BF16)
                 low_ref[wide + rows :, :] = jnp.zeros((wide, cols), BF16)
-            for halo in halos:
-                halo.wait()
-            for q in range(min(ahead, pairs)):
-                ready(q)
-
-        for j in range(group):
-            q = step * group + j + ahead
-
-            @pl.when(q < pairs)
-            def _(q=q):
-                ready(q)
 
         row = lambda j, d, a: stencil_ref[d + steps, pl.ds(2 * (step * group + j) + a, 1), :]
         if makes:
@@ -399,6 +391,20 @@
                         top = 2 * j * size + a * nlon
                         a_ref[top : top + nlon, k * nlon : (k + 1) * nlon] = high
                         a_ref[top + size : top + size + nlon, k * nlon : (k + 1) * nlon] = low
+        @pl.when(step == 0)
+        def _():
+            for halo in ends():
+                halo.wait()
+            for q in range(min(ahead, pairs)):
+                ready(q)
+
+        for j in range(group):
+            q = step * group + j + ahead
+
+            @pl.when(q < pairs)
+            def _(q=q):
+                ready(q)
+
         for j in range(group):
             unit = lambda k: pl.multiple_of((2 * (step * group + j) + k) * nlon, nlon)
             weights = [jnp.sum(row(j, d, a), axis=1, keepdims=True) for a, d in ((0, -steps), (1, steps))]

time: 87.4 us -> 88.9 us (1.017)
  Pallas kernels: 60.1 us -> 61.6 us
    pallas_call x2, Pallas kernels: 30.1 us -> 31.5 us  [rows_operator(): pl.pallas_call(kernel, grid_spec=pltpu.PrefetchScalarGridSpec(num_scalar_...]
  transfers between devices with their start and end apart: 10 -> 10, of which waited for: 1 -> 1; matrix products, arithmetic and copies ran while one was open for 0% -> 0% of each run, Pallas kernels for 48% -> 49%
where the time goes in v16:
time: 88.9 us; the launch traced here: 88.2 us
  Pallas kernels  61.6 us (69%)
  starting transfers between devices  24 us (27%)
  between operations  1.02 us (1%)
  waiting for transfers between devices  0.9 us (1%)
    pallas_call x2, Pallas kernels, rows_operator(): pl.pallas_call(kernel, grid_spec=pltpu.PrefetchScalarGridSpec(num_scalar_...  31.5 us
    ppermute x8, starting transfers between devices, exchanged(): return lax.ppermute(block, axis, pairs)  19.1 us
    pallas_call x2, Pallas kernels, columns_operator(): pl.pallas_call(kernel, grid_spec=pltpu.PrefetchScalarGridSpec(num_scalar_...  18.2 us
    pallas_call x1, Pallas kernels, stencils(): pl.pallas_call(kernel, in_specs=[pl.BlockSpec(memory_space=pltpu.SMEM)] *...  6.72 us
    pallas_call x1, Pallas kernels, packed(): pl.pallas_call(kernel, in_specs=[pl.BlockSpec(memory_space=pltpu.SMEM), p...  5.16 us
    ppermute x2, starting transfers between devices, mirrored(): return lax.ppermute(block, ('row', 'col'), pairs)  4.92 us
  transfers between devices with their start and end apart: 10, of which 1 were waited for; matrix products, arithmetic and copies ran while one was open for 0% of the time, Pallas kernels for 49%

profile of v16, /device:TPU:5, one launch (start us, length us, event | category | flops | bytes accessed | tf_op | source)
XLA Modules:
  0.0 88.2 jit_solution(10056504021824987266)
XLA Ops:
  0.7 0.7 stack.63.where_ref
  1.4 5.2 %packed.1 = (bf16[1040,384]{1,0:T(8,128)(2,1)}, bf16[1040,384]{1,0:T(8,128)(2,1)}, bf16[384,1024]{1,0:T(8,128)(2,1)}, bf16[384,1024]{1,0:T(8,128)(2,1)}) custom-call(s32[15]{0:T(128)} %stack.63.where_ref, f32[2048,1024]{1,0:T(8,128)} %p_ref.7), custom_call_target="tpu_custom_call" | custom-call | flops 1 | bytes 1 | tf_op jit(solution)/shard_map/packed/pallas_call | solution.py:137
  6.6 0.1 collective-permute-start.5
  6.6 4.4 %collective-permute-start.6 = (bf16[1040,384]{1,0:T(8,128)(2,1)}, bf16[1040,384]{1,0:T(8,128)(2,1)}, u32[]{:S(2)}, u32[]{:S(2)}) collective-permute-start(bf16[1040,384]{1,0:T(8,128)(2,1)} %get-tuple-element.33), channel_id=1, source_target_pairs={{1,2},{2,1},{3,4},{4,3},{5,6},{6,5},{9,10},{10,9},{11,12},{12,11},... | collective-permute-start | bytes 2396168 | tf_op jit(solution)/shard_map/ppermute | solution.py:488
  11.0 1.3 %collective-permute-start.3 = (bf16[384,1024]{1,0:T(8,128)(2,1)}, bf16[384,1024]{1,0:T(8,128)(2,1)}, u32[]{:S(2)}, u32[]{:S(2)}) collective-permute-start(bf16[384,1024]{1,0:T(8,128)(2,1)} %get-tuple-element.29), channel_id=1, source_target_pairs={{0,8},{8,0},{16,24},{24,16},{1,9},{9,1},{17,25},{25,17},{2,10},{10... | collective-permute-start | bytes 2359304 | tf_op jit(solution)/shard_map/ppermute | solution.py:488
  12.3 3.0 %collective-permute-start.4 = (bf16[384,1024]{1,0:T(8,128)(2,1)}, bf16[384,1024]{1,0:T(8,128)(2,1)}, u32[]{:S(2)}, u32[]{:S(2)}) collective-permute-start(bf16[384,1024]{1,0:T(8,128)(2,1)} %get-tuple-element.30), channel_id=1, source_target_pairs={{8,16},{16,8},{9,17},{17,9},{10,18},{18,10},{11,19},{19,11},{12,20... | collective-permute-start | bytes 2359304 | tf_op jit(solution)/shard_map/ppermute | solution.py:488
  15.3 6.7 %stencils.1 = (f32[7,16,128]{2,1,0:T(8,128)}, f32[7,8,128]{2,1,0:T(8,128)}, bf16[3072,256]{1,0:T(8,128)(2,1)}, bf16[3072,256]{1,0:T(8,128)(2,1)}, f32[15,14,128]...) custom-call(f32[2,16]{1,0:T(2,128)} %bitcast.16, ...), custom_call_target="tpu_custom_call" | custom-call | flops 1 | bytes 1 | tf_op jit(solution)/shard_map/stencils/pallas_call | solution.py:192
  22.1 1.9 %collective-permute-start = (bf16[512,384]{1,0:T(8,128)(2,1)}, bf16[512,384]{1,0:T(8,128)(2,1)}, u32[]{:S(2)}, u32[]{:S(2)}) collective-permute-start(bf16[512,384]{1,0:T(8,128)(2,1)} %get-tuple-element.26), channel_id=1, source_target_pairs={{0,0},{1,1},{2,8},{3,9},{4,16},{5,17},{6,24},{7,25},{8,2},{9,3},{1... | collective-permute-start | bytes 1179656 | tf_op jit(solution)/shard_map/ppermute | solution.py:499
  24.0 0.0 collective-permute-done.3.even_ref
  24.0 3.0 %collective-permute-start.1 = (bf16[512,384]{1,0:T(8,128)(2,1)}, bf16[512,384]{1,0:T(8,128)(2,1)}, u32[]{:S(2)}, u32[]{:S(2)}) collective-permute-start(bf16[512,384]{1,0:T(8,128)(2,1)} %get-tuple-element.27), channel_id=1, source_target_pairs={{0,2},{2,10},{4,18},{6,26},{8,4},{9,1},{10,12},{11,9},{12,20},{13,... | collective-permute-start | bytes 1179656 | tf_op jit(solution)/shard_map/ppermute | solution.py:499
  27.0 0.0 collective-permute-done.4.odd_ref
  27.0 1.0 %collective-permute-start.2 = (bf16[512,384]{1,0:T(8,128)(2,1)}, bf16[512,384]{1,0:T(8,128)(2,1)}, u32[]{:S(2)}, u32[]{:S(2)}) collective-permute-start(bf16[512,384]{1,0:T(8,128)(2,1)} %get-tuple-element.28), channel_id=1, source_target_pairs={{0,1},{1,0},{2,3},{3,2},{4,5},{5,4},{6,7},{7,6},{8,9},{9,8},{10,11... | collective-permute-start | bytes 1179656 | tf_op jit(solution)/shard_map/ppermute | solution.py:488
  28.0 18.2 %rows_operator.2 = (bf16[2048,1024]{1,0:T(8,128)(2,1)}, bf16[4096,768]{1,0:T(8,128)(2,1)}) custom-call(s32[15]{0:T(128)} %stack.63.where_ref, f32[7,16,128]{2,1,0:T(8,128)} %get-tuple-element.24.stencil_ref, f32[2048,1024]{1,0:T(8,128)} %p_ref.7, bf16[384,1024]{1,0:T(8,128)(2,1)} %collective-permute-done.3.even_ref, ...), custom_call_target="tpu_custom_call" | custom-call | flops 1 | bytes 1 | tf_op jit(solution)/shard_map/rows_operator/pallas_call | solution.py:448
  46.1 0.0 collective-permute-done.5.rest_0_
  46.2 0.0 copy-start
  46.2 0.0 collective-permute-done.6.rest_1_
  46.2 5.0 %collective-permute-start.7 = (bf16[512,384]{1,0:T(8,128)(2,1)}, bf16[512,384]{1,0:T(8,128)(2,1)}, u32[]{:S(2)}, u32[]{:S(2)}) collective-permute-start(bf16[512,384]{1,0:T(8,128)(2,1)} %get-tuple-element.35), channel_id=1, source_target_pairs={{1,2},{2,1},{3,4},{4,3},{5,6},{6,5},{9,10},{10,9},{11,12},{12,11},... | collective-permute-start | bytes 1179656 | tf_op jit(solution)/shard_map/ppermute | solution.py:488
  51.2 0.0 copy-done
  51.2 9.3 %columns_operator.2 = (bf16[2048,1024]{1,0:T(8,128)(2,1)}, bf16[384,1024]{1,0:T(8,128)(2,1)}, bf16[384,1024]{1,0:T(8,128)(2,1)}) custom-call(s32[15]{0:T(128)} %stack.63.where_ref, f32[7,8,128]{2,1,0:T(8,128)} %get-tuple-element.25.stencil_ref, f32[2048,1024]{1,0:T(8,128)} %p_ref.7, bf16[1040,384]{1,0:T(8,128)(2,1)} %copy-done, ...), custom_call_target="tpu_custom_call" | custom-call | flops 1 | bytes 1 | tf_op jit(solution)/shard_map/columns_operator/pallas_call | solution.py:313
  60.4 0.0 collective-permute-start.8
  60.5 0.0 collective-permute-done.rest_0_
  60.5 4.4 %collective-permute-start.9 = (bf16[384,1024]{1,0:T(8,128)(2,1)}, bf16[384,1024]{1,0:T(8,128)(2,1)}, u32[]{:S(2)}, u32[]{:S(2)}) collective-permute-start(bf16[384,1024]{1,0:T(8,128)(2,1)} %get-tuple-element.43), channel_id=1, source_target_pairs={{8,16},{16,8},{9,17},{17,9},{10,18},{18,10},{11,19},{19,11},{12,20... | collective-permute-start | bytes 2359304 | tf_op jit(solution)/shard_map/ppermute | solution.py:488
  64.9 0.0 collective-permute-done.1.rest_1_
  64.9 0.0 collective-permute-done.2.rest_2_
  64.9 0.0 collective-permute-done.7.rest_3_
  64.9 8.9 %columns_operator.3.x_ref = bf16[2048,1024]{1,0:T(8,128)(2,1)} custom-call(s32[15]{0:T(128)} %stack.63.where_ref, f32[7,8,128]{2,1,0:T(8,128)} %get-tuple-element.25.stencil_ref, f32[2048,1024]{1,0:T(8,128)} %p_ref.7, bf16[512,384]{1,0:T(8,128)(2,1)} %collective-permute-done.rest_0_, ...), custom_call_target="tpu_custom_call", output_to_operand_aliasing={{}: (10, {})} | custom-call | flops 9999999827968 | bytes 9999999827968 | tf_op jit(solution)/shard_map/columns_operator/pallas_call | solution.py:313
  73.8 0.0 collective-permute-done.8.even_ref
  73.8 0.9 collective-permute-done.9.odd_ref
  74.7 13.4 %rows_operator.3 = f32[2048,1024]{1,0:T(8,128)} custom-call(s32[15]{0:T(128)} %stack.63.where_ref, f32[7,16,128]{2,1,0:T(8,128)} %get-tuple-element.24.stencil_ref, bf16[2048,1024]{1,0:T(8,128)(2,1)} %columns_operator.3.x_ref, bf16[384,1024]{1,0:T(8,128)(2,1)} %collective-permute-done.8.even_ref, bf16[384,1024]{1,0:T(8,128)(2,1)} %collective-permute-done.9.odd_ref, ...), custom_call_target="tpu_custom_call" | custom-call | flops 1 | bytes 1 | tf_op jit(solution)/shard_map/rows_operator/pallas_call | solution.py:448
Async XLA Ops:
  6.6 39.6 %collective-permute-start.5 = (bf16[1040,384]{1,0:T(8,128)(2,1)}, bf16[1040,384]{1,0:T(8,128)(2,1)S(1)}, u32[]{:S(2)}, u32[]{:S(2)}) collective-permute-start(bf16[1040,384]{1,0:T(8,128)(2,1)} %get-tuple-element.32), channel_id=1, source_target_pairs={{0,1},{1,0},{2,3},{3,2},{4,5},{5,4},{6,7},{7,6},{8,9},{9,8},{10,11... | collective-permute-start | bytes 2396168 | tf_op jit(solution)/shard_map/ppermute | solution.py:488
  6.6 39.5 %collective-permute-start.6 = (bf16[1040,384]{1,0:T(8,128)(2,1)}, bf16[1040,384]{1,0:T(8,128)(2,1)}, u32[]{:S(2)}, u32[]{:S(2)}) collective-permute-start(bf16[1040,384]{1,0:T(8,128)(2,1)} %get-tuple-element.33), channel_id=1, source_target_pairs={{1,2},{2,1},{3,4},{4,3},{5,6},{6,5},{9,10},{10,9},{11,12},{12,11},... | collective-permute-start | bytes 2396168 | tf_op jit(solution)/shard_map/ppermute | solution.py:488
  11.0 13.0 %collective-permute-start.3 = (bf16[384,1024]{1,0:T(8,128)(2,1)}, bf16[384,1024]{1,0:T(8,128)(2,1)}, u32[]{:S(2)}, u32[]{:S(2)}) collective-permute-start(bf16[384,1024]{1,0:T(8,128)(2,1)} %get-tuple-element.29), channel_id=1, source_target_pairs={{0,8},{8,0},{16,24},{24,16},{1,9},{9,1},{17,25},{25,17},{2,10},{10... | collective-permute-start | bytes 2359304 | tf_op jit(solution)/shard_map/ppermute | solution.py:488
  12.3 14.7 %collective-permute-start.4 = (bf16[384,1024]{1,0:T(8,128)(2,1)}, bf16[384,1024]{1,0:T(8,128)(2,1)}, u32[]{:S(2)}, u32[]{:S(2)}) collective-permute-start(bf16[384,1024]{1,0:T(8,128)(2,1)} %get-tuple-element.30), channel_id=1, source_target_pairs={{8,16},{16,8},{9,17},{17,9},{10,18},{18,10},{11,19},{19,11},{12,20... | collective-permute-start | bytes 2359304 | tf_op jit(solution)/shard_map/ppermute | solution.py:488
  22.1 38.4 %collective-permute-start = (bf16[512,384]{1,0:T(8,128)(2,1)}, bf16[512,384]{1,0:T(8,128)(2,1)}, u32[]{:S(2)}, u32[]{:S(2)}) collective-permute-start(bf16[512,384]{1,0:T(8,128)(2,1)} %get-tuple-element.26), channel_id=1, source_target_pairs={{0,0},{1,1},{2,8},{3,9},{4,16},{5,17},{6,24},{7,25},{8,2},{9,3},{1... | collective-permute-start | bytes 1179656 | tf_op jit(solution)/shard_map/ppermute | solution.py:499
  24.0 40.9 %collective-permute-start.1 = (bf16[512,384]{1,0:T(8,128)(2,1)}, bf16[512,384]{1,0:T(8,128)(2,1)}, u32[]{:S(2)}, u32[]{:S(2)}) collective-permute-start(bf16[512,384]{1,0:T(8,128)(2,1)} %get-tuple-element.27), channel_id=1, source_target_pairs={{0,2},{2,10},{4,18},{6,26},{8,4},{9,1},{10,12},{11,9},{12,20},{13,... | collective-permute-start | bytes 1179656 | tf_op jit(solution)/shard_map/ppermute | solution.py:499
  27.0 37.9 %collective-permute-start.2 = (bf16[512,384]{1,0:T(8,128)(2,1)}, bf16[512,384]{1,0:T(8,128)(2,1)}, u32[]{:S(2)}, u32[]{:S(2)}) collective-permute-start(bf16[512,384]{1,0:T(8,128)(2,1)} %get-tuple-element.28), channel_id=1, source_target_pairs={{0,1},{1,0},{2,3},{3,2},{4,5},{5,4},{6,7},{7,6},{8,9},{9,8},{10,11... | collective-permute-start | bytes 1179656 | tf_op jit(solution)/shard_map/ppermute | solution.py:488
  46.2 5.0 %copy-start = (bf16[1040,384]{1,0:T(8,128)(2,1)}, bf16[1040,384]{1,0:T(8,128)(2,1)S(1)}, u32[]{:S(2)}) copy-start(bf16[1040,384]{1,0:T(8,128)(2,1)S(1)} %collective-permute-done.5.rest_0_) | copy-start | bytes 2396164
  46.2 18.7 %collective-permute-start.7 = (bf16[512,384]{1,0:T(8,128)(2,1)}, bf16[512,384]{1,0:T(8,128)(2,1)}, u32[]{:S(2)}, u32[]{:S(2)}) collective-permute-start(bf16[512,384]{1,0:T(8,128)(2,1)} %get-tuple-element.35), channel_id=1, source_target_pairs={{1,2},{2,1},{3,4},{4,3},{5,6},{6,5},{9,10},{10,9},{11,12},{12,11},... | collective-permute-start | bytes 1179656 | tf_op jit(solution)/shard_map/ppermute | solution.py:488
  60.4 13.3 %collective-permute-start.8 = (bf16[384,1024]{1,0:T(8,128)(2,1)}, bf16[384,1024]{1,0:T(8,128)(2,1)}, u32[]{:S(2)}, u32[]{:S(2)}) collective-permute-start(bf16[384,1024]{1,0:T(8,128)(2,1)} %get-tuple-element.42), channel_id=1, source_target_pairs={{0,8},{8,0},{16,24},{24,16},{1,9},{9,1},{17,25},{25,17},{2,10},{10... | collective-permute-start | bytes 2359304 | tf_op jit(solution)/shard_map/ppermute | solution.py:488
  60.5 14.2 %collective-permute-start.9 = (bf16[384,1024]{1,0:T(8,128)(2,1)}, bf16[384,1024]{1,0:T(8,128)(2,1)}, u32[]{:S(2)}, u32[]{:S(2)}) collective-permute-start(bf16[384,1024]{1,0:T(8,128)(2,1)} %get-tuple-element.43), channel_id=1, source_target_pairs={{8,16},{16,8},{9,17},{17,9},{10,18},{18,10},{11,19},{19,11},{12,20... | collective-permute-start | bytes 2359304 | tf_op jit(solution)/shard_map/ppermute | solution.py:488
